TPU v7x, 256 devices: a whole 4x4x8 slice. The times are simulated.
256 devices in a mesh: grp: 8 (over x, core), mem: 32 (over y, z).
Axes of the slice: x: 4, y: 4, z: 8, core: 2. Of those that a mesh axis runs over, the one named last changes fastest.
Arguments:
- amp_plus: bfloat16 [24576, 4096], P('mem', 'grp'), may hold values from -6 to 6
- amp_minus: bfloat16 [24576, 4096], P('mem', 'grp'), may hold values from -6 to 6
- ints_plus: bfloat16 [8192, 4096], P('grp', 'mem'), may hold values from -0.125 to 0.125
- ints_minus: bfloat16 [8192, 4096], P('grp', 'mem'), may hold values from -0.125 to 0.125
- sym_ij: int32 [192], P('mem'), may hold values from 0 to 1
- sym_ab: int32 [64], P('grp'), may hold values from 0 to 1
- sym_cd: int32 [32], replicated, may hold values from 0 to 1
- amp_mask: int32 [192, 32], P('mem'), may hold values 0 or 1
Outputs:
- ladder: bfloat16 [24576, 8192], P('mem', 'grp')
All inputs are finite; a program needn't handle non-finite values. No bound on the sum of `amp_mask` on one device may be relied on, other than what follows from the above.
Results may differ from a plain program's by a relative error of at most 0.001.
Values may be sent and summed in bfloat16 or wider, within the bound.
No kernel may reach another device: no remote copies, remote signals or barrier semaphores. Data moves between devices by JAX's collectives and lax.ppermute only.
A program may use at most 128 MiB of HBM per device.

v0:
```python
import jax
import jax.numpy as jnp
from jax import lax
from jax.sharding import PartitionSpec as P

BLK = 128


def tile_scale(values, flags):
    rows_t = values.shape[0] // BLK
    cols_t = values.shape[1] // BLK
    shaped = values.reshape(rows_t, BLK, cols_t, BLK) * flags.astype(values.dtype)[:, None, :, None]
    return shaped.reshape(values.shape)


def times_rows(left, right):
    return lax.dot_general(
        left, right, (((1,), (1,)), ((), ())), preferred_element_type=jnp.float32
    )


def body(amp_plus, amp_minus, ints_plus, ints_minus, sym_ij, sym_ab, sym_cd, amp_mask):
    amp_flags = (sym_ij[:, None] == sym_cd[None, :]) & (amp_mask == 1)

    def int_section(section):
        return tile_scale(section, sym_ab[:, None] == sym_cd[None, :])

    full_plus, full_minus = (
        lax.all_gather(amp_plus, "grp", axis=1, tiled=True),
        lax.all_gather(amp_minus, "grp", axis=1, tiled=True),
    )
    tplus = tile_scale(full_plus, amp_flags)
    tminus = tile_scale(full_minus, amp_flags)
    left = tplus
    zplus = times_rows(left, int_section(lax.all_gather(ints_plus, "mem", axis=1, tiled=True)))
    left = tminus
    zminus = times_rows(left, int_section(lax.all_gather(ints_minus, "mem", axis=1, tiled=True)))
    return (0.5 * (zplus + zminus)).astype(jnp.bfloat16)


def solution(mesh):
    placed = (
        P("mem", "grp"),
        P("mem", "grp"),
        P("grp", "mem"),
        P("grp", "mem"),
        P("mem"),
        P("grp"),
        P(),
        P("mem", None),
    )
    return jax.shard_map(
        body, mesh=mesh, in_specs=placed, out_specs=P("mem", "grp"), check_vma=False
    )
```

profile of v0, /device:TPU:24, one launch (start us, length us, event | category | flops | bytes accessed | tf_op | source)
XLA Modules:
  0.0 334.0 jit_solution(1514052840468070603)
XLA Ops:
  6.5 0.0 all-gather.5.cloned.1.call-start
  6.5 0.7 all-gather.5.cloned.1.call-update
  7.3 0.0 all-gather.7.cloned.1.call-start
  7.3 0.7 all-gather.7.cloned.1.call-update
  8.0 0.0 all-gather.9.cloned.1.call-start
  8.1 0.7 all-gather.9.cloned.1.call-update
  8.7 0.0 all-gather.11.cloned.1.call-start
  8.8 0.5 all-gather.11.cloned.1.call-update
  9.3 0.7 compare_convert_fusion
  10.1 0.8 and_convert_fusion
  10.8 44.5 %all-gather.5.cloned.1.call-done = bf16[768,4096]{1,0:T(8,128)(2,1)} async-done(((bf16[768,512]{1,0:T(8,128)(2,1)}), bf16[768,4096]{1,0:T(8,128)(2,1)}) %all-gather.5.cloned.1.call-update) | async-done | bytes 6291472 | tf_op jit(solution)/shard_map/all_gather | solution.py:29
  55.4 104.9 %all-gather.7.cloned.1.call-done = bf16[1024,4096]{1,0:T(8,128)(2,1)} async-done(((bf16[1024,128]{1,0:T(8,128)(2,1)}), bf16[1024,4096]{1,0:T(8,128)(2,1)}) %all-gather.7.cloned.1.call-update) | async-done | bytes 8388624 | tf_op jit(solution)/shard_map/all_gather | solution.py:35
  160.3 1.1 mul.45
  161.4 0.0 copy-start
  161.4 3.9 %mul.42 = bf16[6,128,32,128]{3,2,1,0:T(8,128)(2,1)} broadcast(bf16[6,32]{1,0:T(8,128)(2,1)S(1)} %and_convert_fusion), dimensions={0,2} | broadcast | bytes 6291840 | tf_op jit(solution)/shard_map/mul | solution.py:12
  165.4 1.2 copy-done
  166.5 16.6 %fusion = f32[768,1024]{1,0:T(8,128)} fusion(bf16[1024,4096]{1,0:T(8,128)(2,1)} %all-gather.7.cloned.1.call-done, bf16[128,8,32,128]{3,2,1,0:T(8,128)(2,1)S(1)} %bitcast.18, bf16[768,4096]{1,0:T(8,128)(2,1)} %all-gather.5.cloned.1.call-done, bf16[96,8,32,128]{3,2,1,0:T(8,128)(2,1)} %bitcast.20), kind=kOutput, calls=%fused_computation.2 | convolution fusion | flops 6449790976 | bytes 32505856 | tf_op jit(solution)/shard_map/dot_general | solution.py:17
  183.1 21.5 %all-gather.9.cloned.1.call-done = bf16[768,4096]{1,0:T(8,128)(2,1)} async-done(((bf16[768,512]{1,0:T(8,128)(2,1)}), bf16[768,4096]{1,0:T(8,128)(2,1)}) %all-gather.9.cloned.1.call-update) | async-done | bytes 6291472 | tf_op jit(solution)/shard_map/all_gather | solution.py:30
  204.6 104.8 %all-gather.11.cloned.1.call-done = bf16[1024,4096]{1,0:T(8,128)(2,1)} async-done(((bf16[1024,128]{1,0:T(8,128)(2,1)}), bf16[1024,4096]{1,0:T(8,128)(2,1)}) %all-gather.11.cloned.1.call-update) | async-done | bytes 8388624 | tf_op jit(solution)/shard_map/all_gather | solution.py:37
  309.3 18.1 %multiply_convert_fusion = bf16[768,1024]{1,0:T(8,128)(2,1)} fusion(f32[768,1024]{1,0:T(8,128)} %fusion, bf16[1024,4096]{1,0:T(8,128)(2,1)} %all-gather.11.cloned.1.call-done, bf16[128,8,32,128]{3,2,1,0:T(8,128)(2,1)} %bitcast.19, bf16[768,4096]{1,0:T(8,128)(2,1)} %all-gather.9.cloned.1.call-done, bf16[96,8,32,128]{3,2,1,0:T(8,128)(2,1)} %bitcast.21), kind=kOutput, calls=%fused_computation.10 | convolution fusion | flops 6452150272 | bytes 34078720 | tf_op jit(solution)/shard_map/dot_general | solution.py:17
Async XLA Ops:
  6.5 48.8 %all-gather.5.cloned.1.call-start = ((), (), s32[]{:S(2)}) async-start(), calls=%async_computation | async-start | bytes 7077888 | tf_op jit(solution)/shard_map/all_gather | solution.py:29
  7.3 153.0 %all-gather.7.cloned.1.call-start = ((), (), s32[]{:S(2)}) async-start(), calls=%async_computation.1 | async-start | bytes 8650752 | tf_op jit(solution)/shard_map/all_gather | solution.py:35
  8.0 196.6 %all-gather.9.cloned.1.call-start = ((), (), s32[]{:S(2)}) async-start(), calls=%async_computation.2 | async-start | bytes 7077888 | tf_op jit(solution)/shard_map/all_gather | solution.py:30
  8.7 300.6 %all-gather.11.cloned.1.call-start = ((), (), s32[]{:S(2)}) async-start(), calls=%async_computation.3 | async-start | bytes 8650752 | tf_op jit(solution)/shard_map/all_gather | solution.py:37
  161.4 5.1 %copy-start = (bf16[8,128,32,128]{3,2,1,0:T(8,128)(2,1)}, bf16[8,128,32,128]{3,2,1,0:T(8,128)(2,1)S(1)}, u32[]{:S(2)}) copy-start(bf16[8,128,32,128]{3,2,1,0:T(8,128)(2,1)S(1)} %mul.45) | copy-start | bytes 25165828
Sparse Core Ops, SparseCore 0:
  9.2 46.1 all-gather.4
  57.8 102.4 all-gather.6
  162.1 42.3 all-gather.8
  206.9 102.4 all-gather.10
where the time goes:
time: 336 us; the launch traced here: 334 us
  waiting for transfers between devices  278 us (83%)
  matrix products  34.7 us (10%)
  between operations  13.1 us (4%)
  local copies, waits for them, and re-layouts  6.25 us (2%)
    all_gather x1, waiting for transfers between devices, body(): lax.all_gather(ints_plus, 'mem', axis=1, tiled=True)  105 us
    all_gather x1, waiting for transfers between devices, body(): lax.all_gather(ints_minus, 'mem', axis=1, tiled=True)  105 us
    all_gather x1, waiting for transfers between devices, body(): lax.all_gather(amp_plus, 'grp', axis=1, tiled=True)  44.5 us
    dot_general x2, matrix products, times_rows(): lax.dot_general(left, right, (((1,), (1,)), ((), ())), preferred_element_...  34.7 us
    all_gather x1, waiting for transfers between devices, body(): lax.all_gather(amp_minus, 'grp', axis=1, tiled=True)  21.5 us
  transfers between devices with their start and end apart: 4, of which 4 were waited for; matrix products, arithmetic and copies ran while one was open for 7% of the time, Pallas kernels for 0%

commit v1 on v0

v1 whole, which is shorter than its diff:
```python
import jax
import jax.numpy as jnp
from jax import lax
from jax.experimental import pallas as pl
from jax.experimental.pallas import tpu as pltpu
from jax.sharding import PartitionSpec as P

BLK = 128
AXES = ("grp", "mem")
NX, NY, NZ = 4, 4, 8
BF16 = jnp.bfloat16
F32 = jnp.float32


def perm_of(dx, dy, dz, swap=0):
    pairs = []
    for x in range(NX):
        for core in range(2):
            sign = 1 if core == 0 else -1
            for y in range(NY):
                for z in range(NZ):
                    src = (2 * x + core) * 32 + 8 * y + z
                    x2, y2, z2 = (x + sign * dx) % NX, (y + sign * dy) % NY, (z + sign * dz) % NZ
                    core2 = core ^ swap
                    pairs.append((src, (2 * x2 + core2) * 32 + 8 * y2 + z2))
    return pairs


def move(values, dx=0, dy=0, dz=0, swap=0):
    return lax.ppermute(values, AXES, perm_of(dx, dy, dz, swap))


def after(value, *others):
    return lax.optimization_barrier((value,) + others)[0]


SMEM = pl.BlockSpec(memory_space=pltpu.SMEM)
VMEM = pl.BlockSpec(memory_space=pltpu.VMEM)
ANY = pl.BlockSpec(memory_space=pl.ANY)


def params(mib):
    return pltpu.CompilerParams(vmem_limit_bytes=mib * 2**20)


def cost(flops, moved):
    return pl.CostEstimate(flops=flops, bytes_accessed=moved, transcendentals=0)


def join_kernel(*refs):
    blocks, out = refs[:-1], refs[-1]
    width = blocks[0].shape[1]
    for b, block in enumerate(blocks):
        out[:, b * width:(b + 1) * width] = block[...]


def join(blocks):
    rows, width = blocks[0].shape
    full = width * len(blocks)
    return pl.pallas_call(
        join_kernel,
        out_shape=jax.ShapeDtypeStruct((rows, full), BF16),
        in_specs=[VMEM] * len(blocks),
        out_specs=VMEM,
        compiler_params=params(8),
        cost_estimate=cost(0, 4 * rows * full),
    )(*blocks)


def place_kernel(here_ref, ij_ref, cd_ref, mask_ref, *refs):
    blocks, (plus_out, minus_out) = refs[:-2], refs[-2:]
    sign, x, y, z, core = [here_ref[k] for k in range(5)]
    for b, block in enumerate(blocks):
        way = -sign if b % 2 == 0 else sign
        from_x = (x + way * (b // 2)) & (NX - 1)
        from_core = core if b % 2 == 0 else 1 - core
        step_y = (sign * (y - from_x)) & (NY - 1)
        for col in range(4):
            from_z = 4 * from_core + col
            step_z = (sign * (z - from_z)) & (NZ - 1)
            tile = 8 * from_x + from_z
            label = cd_ref[tile]
            places = ((0, plus_out, step_y * NZ + step_z), (1, minus_out, step_z * NY + step_y))
            for row in range(6):
                on = (ij_ref[row] == label) & (mask_ref[row, tile] == 1)
                rows = slice(row * BLK, (row + 1) * BLK)
                for panel, out, at in places:
                    kept = block[panel, rows, col * BLK:(col + 1) * BLK]
                    out[rows, pl.ds(pl.multiple_of(at * BLK, BLK), BLK)] = jnp.where(on, kept, jnp.zeros_like(kept))


def place(here, sym_ij, sym_cd, amp_mask, blocks):
    one = jax.ShapeDtypeStruct((768, 4096), BF16)
    return pl.pallas_call(
        place_kernel,
        out_shape=(one, one),
        in_specs=[SMEM] * 4 + [VMEM] * len(blocks),
        out_specs=(VMEM, VMEM),
        compiler_params=params(28),
        cost_estimate=cost(0, 25 * 2**20),
    )(here, sym_ij, sym_cd, amp_mask, *blocks)


def dot(left, right):
    return lax.dot_general(left, right, (((1,), (1,)), ((), ())), preferred_element_type=F32)


def product_kernel(places, ij_ref, ab_ref, plus_ref, minus_ref, *refs, first, last):
    blocks, rest = refs[:len(places)], refs[len(places):]
    out = rest[-1]

    def strip(n, carry):
        rows = pl.ds(pl.multiple_of(n * 256, 256), 256)
        total = None if first else rest[0][:, rows]
        for (panel, at), block in zip(places, blocks):
            left = (plus_ref, minus_ref)[panel]
            part = dot(left[:, at:at + block.shape[1]], block[rows, :])
            total = part if total is None else total + part
        if not last:
            out[:, rows] = total
            return carry
        for half in range(2):
            label = ab_ref[2 * n + half]
            for row in range(6):
                tile = total[row * BLK:(row + 1) * BLK, half * BLK:(half + 1) * BLK] * 0.5
                tile = jnp.where(ij_ref[row] == label, tile, jnp.zeros_like(tile))
                where = pl.ds(pl.multiple_of(n * 256 + half * BLK, BLK), BLK)
                out[row * BLK:(row + 1) * BLK, where] = tile.astype(BF16)
        return carry

    lax.fori_loop(0, 4, strip, 0)


def product(sym_ij, sym_ab, plus, minus, terms, so_far=None, last=False):
    first = so_far is None
    blocks = [block for _, _, block in terms]
    places = [(panel, at) for panel, at, _ in terms]
    extra = [] if first else [so_far]
    depth = sum(block.shape[1] for block in blocks)

    def kernel(*refs):
        product_kernel(places, *refs, first=first, last=last)

    return pl.pallas_call(
        kernel,
        out_shape=jax.ShapeDtypeStruct((768, 1024), BF16 if last else F32),
        in_specs=[SMEM] * 2 + [VMEM] * (2 + len(blocks) + len(extra)),
        out_specs=VMEM,
        compiler_params=params(36),
        cost_estimate=cost(2 * 768 * 1024 * depth, 12 * 2**20 + 2 * 1024 * depth),
    )(sym_ij, sym_ab, plus, minus, *blocks, *extra)


def body(amp_plus, amp_minus, ints_plus, ints_minus, sym_ij, sym_ab, sym_cd, amp_mask):
    grp, mem = lax.axis_index("grp"), lax.axis_index("mem")
    core, x, y, z = grp % 2, grp // 2, mem // 8, mem % 8
    here = jnp.stack([1 - 2 * core, x, y, z, core]).astype(jnp.int32)

    def go(value, *waits, **way):
        return move(after(value, *waits) if waits else value, **way)

    t0 = jnp.stack([amp_plus, amp_minus])
    z0, y0 = ints_plus, ints_minus
    z1 = go(z0, dz=1)
    y1, y2, y3 = [go(y0, dy=d) for d in (1, 2, 3)]
    t1 = go(t0, dx=1)
    z2 = go(z1, dz=1)
    z3 = go(z2, dz=1)
    a1, b1 = [[join(pair)] for pair in ((y0, y1), (y2, y3))]
    c1 = [join((z0, z1, z2, z3))]
    a1.append(go(a1[0], z3, dz=1))
    z4 = go(z3, y1, y2, y3, dz=1)
    c1.append(go(c1[0], dy=1))
    s0 = go(t0, z3, swap=1)
    t2 = go(t1, z3, dx=1)
    s1 = go(t1, s0, dx=0, swap=1)
    z5 = go(z4, dz=1)
    b1.append(go(b1[0], a1[1], z4, dz=1))
    z6 = go(z5, dz=1)
    c1.append(go(c1[1], z5, dy=1))
    a1.append(go(a1[1], b1[1], z5, dz=1))
    t3 = go(t2, z5, c1[1], dx=1)
    s2 = go(t2, s1, swap=1)
    z7 = go(z6, dz=1)
    b1.append(go(b1[1], a1[2], z6, dz=1))
    c1.append(go(c1[2], z6, dy=1))
    c2 = [join((z4, z5, z6, z7))]
    c2.append(go(c2[0], dy=1))
    a1.append(go(a1[2], b1[2], z7, dz=1))
    b1.append(go(b1[2], z7, dz=1))
    s3 = go(t3, s2, swap=1)
    a1.append(go(a1[3], dz=1))
    plus, minus = place(here, sym_ij, sym_cd, amp_mask, [t0, s0, t1, s1, t2, s2, t3, s3])
    c2.append(go(c2[1], c1[3], dy=1))
    for k in (4, 5, 6):
        b1.append(go(b1[k - 1], a1[k], dz=1))
        a1.append(go(a1[k], b1[k - 1], dz=1))
        if k == 5:
            c2.append(go(c2[2], dy=1))
    b1.append(go(b1[6], dz=1))

    def term(panel, step, part):
        if panel == 0:
            return panel, 1024 * step + 512 * part, (c1, c2)[part][step]
        return panel, 512 * step + 256 * part, (a1, b1)[part][step]

    early = [term(0, i, 0) for i in range(4)] + [term(0, i, 1) for i in range(2)]
    early += [term(1, t, part) for t in range(4) for part in range(2)]
    late = [term(0, i, 1) for i in (2, 3)] + [term(1, t, part) for t in (4, 5) for part in range(2)]
    rest = [term(1, t, part) for t in (6, 7) for part in range(2)]
    total = product(sym_ij, sym_ab, plus, minus, early)
    total = product(sym_ij, sym_ab, plus, minus, late, total)
    return product(sym_ij, sym_ab, plus, minus, rest, total, last=True)


def solution(mesh):
    placed = (
        P("mem", "grp"),
        P("mem", "grp"),
        P("grp", "mem"),
        P("grp", "mem"),
        P("mem"),
        P("grp"),
        P(),
        P("mem", None),
    )
    return jax.shard_map(
        body, mesh=mesh, in_specs=placed, out_specs=P("mem", "grp"), check_vma=False
    )
```

time: 336 us -> 208 us (0.62)
  waiting for transfers between devices: 278 us -> 110 us
  matrix products: 34.7 us -> 0 us
  Pallas kernels: 0 us -> 32.8 us
  local copies, waits for them, and re-layouts: 6.25 us -> 33.9 us
  starting transfers between devices: 0.12 us -> 26.7 us
  between operations: 13.1 us -> 0.48 us
    all_gather x4 -> x0, waiting for transfers between devices: 276 us -> none  [the longest x1 105 us: body(): lax.all_gather(ints_plus, 'mem', axis=1, tiled=True)]
    ppermute x0 -> x37, waiting for transfers between devices: none -> 110 us  [move(): return lax.ppermute(values, AXES, perm_of(dx, dy, dz, swap))]
    dot_general x2 -> x0, matrix products: 34.7 us -> none  [times_rows(): lax.dot_general(left, right, (((1,), (1,)), ((), ())), preferred_element_...]
    pallas_call x0 -> x8, Pallas kernels: none -> 32.8 us  [the longest x3 26.2 us: product(): pl.pallas_call(kernel, out_shape=jax.ShapeDtypeStruct((768, 1024), BF16 i...]
    unnamed x2 -> x108, local copies, waits for them, and re-layouts: 1.18 us -> 33.9 us
    ppermute x0 -> x37, starting transfers between devices: none -> 26.7 us  [move(): return lax.ppermute(values, AXES, perm_of(dx, dy, dz, swap))]
    mul x2 -> x0, local copies, waits for them, and re-layouts: 5.07 us -> none  [tile_scale(): values.reshape(rows_t, BLK, cols_t, BLK)]
  transfers between devices with their start and end apart: 4 -> 37, of which waited for: 4 -> 18; matrix products, arithmetic and copies ran while one was open for 7% -> 1% of each run, Pallas kernels for 0% -> 14%
where the time goes in v1:
time: 208 us; the launch traced here: 205 us
  waiting for transfers between devices  110 us (53%)
  local copies, waits for them, and re-layouts  33.9 us (16%)
  Pallas kernels  32.8 us (16%)
  starting transfers between devices  26.7 us (13%)
    ppermute x37, waiting for transfers between devices, move(): return lax.ppermute(values, AXES, perm_of(dx, dy, dz, swap))  110 us
    unnamed x108, local copies, waits for them, and re-layouts  33.9 us
    ppermute x37, starting transfers between devices, move(): return lax.ppermute(values, AXES, perm_of(dx, dy, dz, swap))  26.7 us
    pallas_call x3, Pallas kernels, product(): pl.pallas_call(kernel, out_shape=jax.ShapeDtypeStruct((768, 1024), BF16 i...  26.2 us
    pallas_call x1, Pallas kernels, place(): pl.pallas_call(place_kernel, out_shape=(one, one), in_specs=[SMEM] * 4 +...  6.06 us
  transfers between devices with their start and end apart: 37, of which 18 were waited for; matrix products, arithmetic and copies ran while one was open for 1% of the time, Pallas kernels for 14%

profile of v1, /device:TPU:24, one launch (start us, length us, event | category | flops | bytes accessed | tf_op | source)
XLA Modules:
  0.0 205.3 jit_solution(1281676180897122055)
XLA Ops:
  0.0 1.9 collective-permute-start
  1.9 8.5 %collective-permute-done.refs_1_ = bf16[1024,128]{1,0:T(8,128)(2,1)S(1)} collective-permute-done((bf16[1024,128]{1,0:T(8,128)(2,1)}, bf16[1024,128]{1,0:T(8,128)(2,1)S(1)}, u32[]{:S(2)}, u32[]{:S(2)}) %collective-permute-start) | collective-permute-done | bytes 262176 | tf_op jit(solution)/shard_map/ppermute | solution.py:30
  10.4 7.6 %collective-permute-done.1.refs_2_ = bf16[1024,128]{1,0:T(8,128)(2,1)S(1)} collective-permute-done((bf16[1024,128]{1,0:T(8,128)(2,1)S(1)}, bf16[1024,128]{1,0:T(8,128)(2,1)S(1)}, u32[]{:S(2)}, u32[]{:S(2)}) %collective-permute-start.1) | collective-permute-done | bytes 262176 | tf_op jit(solution)/shard_map/ppermute | solution.py:30
  18.0 1.6 pad_maximum_fusion.refs_0_
  19.6 1.6 collective-permute-start.4
  21.1 4.4 %collective-permute-done.2.refs_3_ = bf16[1024,128]{1,0:T(8,128)(2,1)S(1)} collective-permute-done((bf16[1024,128]{1,0:T(8,128)(2,1)S(1)}, bf16[1024,128]{1,0:T(8,128)(2,1)S(1)}, u32[]{:S(2)}, u32[]{:S(2)}) %collective-permute-start.2) | collective-permute-done | bytes 262176 | tf_op jit(solution)/shard_map/ppermute | solution.py:30
  25.8 1.8 collective-permute-start.10
  28.9 5.9 %collective-permute-done.8.refs_1_ = bf16[1024,128]{1,0:T(8,128)(2,1)S(1)} collective-permute-done((bf16[1024,128]{1,0:T(8,128)(2,1)S(1)}, bf16[1024,128]{1,0:T(8,128)(2,1)S(1)}, u32[]{:S(2)}, u32[]{:S(2)}) %collective-permute-start.8) | collective-permute-done | bytes 262176 | tf_op jit(solution)/shard_map/ppermute | solution.py:30
  35.7 5.4 %collective-permute-done.10.refs_1_ = bf16[1024,128]{1,0:T(8,128)(2,1)S(1)} collective-permute-done((bf16[1024,128]{1,0:T(8,128)(2,1)S(1)}, bf16[1024,128]{1,0:T(8,128)(2,1)S(1)}, u32[]{:S(2)}, u32[]{:S(2)}) %collective-permute-start.10) | collective-permute-done | bytes 262176 | tf_op jit(solution)/shard_map/ppermute | solution.py:30
  45.7 1.6 collective-permute-start.13
  50.1 11.8 %collective-permute-done.12.refs_1_ = bf16[1024,128]{1,0:T(8,128)(2,1)S(1)} collective-permute-done((bf16[1024,128]{1,0:T(8,128)(2,1)S(1)}, bf16[1024,128]{1,0:T(8,128)(2,1)S(1)}, u32[]{:S(2)}, u32[]{:S(2)}) %collective-permute-start.12) | collective-permute-done | bytes 262176 | tf_op jit(solution)/shard_map/ppermute | solution.py:30
  65.6 9.5 %collective-permute-done.19.refs_2_ = bf16[1024,128]{1,0:T(8,128)(2,1)S(1)} collective-permute-done((bf16[1024,128]{1,0:T(8,128)(2,1)S(1)}, bf16[1024,128]{1,0:T(8,128)(2,1)S(1)}, u32[]{:S(2)}, u32[]{:S(2)}) %collective-permute-start.19) | collective-permute-done | bytes 262176 | tf_op jit(solution)/shard_map/ppermute | solution.py:30
  78.6 2.8 %collective-permute-start.7 = (bf16[2,768,512]{2,1,0:T(8,128)(2,1)S(1)}, bf16[2,768,512]{2,1,0:T(8,128)(2,1)S(1)}, u32[]{:S(2)}, u32[]{:S(2)}) collective-permute-start(bf16[2,768,512]{2,1,0:T(8,128)(2,1)S(1)} %collective-permute-done.6.refs_4_), channel_id=1, source_target_pairs={{0,32},{1,33},{2,34},{3,35},{4,36},{5,37},{6,38},{7,39},{8,40},{9,... | collective-permute-start | bytes 4718600 | tf_op jit(solution)/shard_map/ppermute | solution.py:30
  82.6 5.8 %collective-permute-done.21.refs_3_ = bf16[1024,128]{1,0:T(8,128)(2,1)S(1)} collective-permute-done((bf16[1024,128]{1,0:T(8,128)(2,1)S(1)}, bf16[1024,128]{1,0:T(8,128)(2,1)S(1)}, u32[]{:S(2)}, u32[]{:S(2)}) %collective-permute-start.21) | collective-permute-done | bytes 262176 | tf_op jit(solution)/shard_map/ppermute | solution.py:30
  90.2 2.0 collective-permute-start.32
  93.1 5.6 %collective-permute-done.22.refs_16_ = bf16[1024,256]{1,0:T(8,128)(2,1)S(1)} collective-permute-done((bf16[1024,256]{1,0:T(8,128)(2,1)S(1)}, bf16[1024,256]{1,0:T(8,128)(2,1)S(1)}, u32[]{:S(2)}, u32[]{:S(2)}) %collective-permute-start.22) | collective-permute-done | bytes 524320 | tf_op jit(solution)/shard_map/ppermute | solution.py:30
  98.7 1.9 collective-permute-start.34
  101.7 2.7 %collective-permute-done.24.refs_17_ = bf16[1024,256]{1,0:T(8,128)(2,1)S(1)} collective-permute-done((bf16[1024,256]{1,0:T(8,128)(2,1)S(1)}, bf16[1024,256]{1,0:T(8,128)(2,1)S(1)}, u32[]{:S(2)}, u32[]{:S(2)}) %collective-permute-start.24) | collective-permute-done | bytes 524320 | tf_op jit(solution)/shard_map/ppermute | solution.py:30
  105.2 9.6 %collective-permute-done.23.refs_6_ = bf16[1024,256]{1,0:T(8,128)(2,1)S(1)} collective-permute-done((bf16[1024,256]{1,0:T(8,128)(2,1)S(1)}, bf16[1024,256]{1,0:T(8,128)(2,1)S(1)}, u32[]{:S(2)}, u32[]{:S(2)}) %collective-permute-start.23) | collective-permute-done | bytes 524320 | tf_op jit(solution)/shard_map/ppermute | solution.py:30
  118.6 1.9 collective-permute-start.35
  121.5 3.6 %collective-permute-done.26.refs_7_ = bf16[1024,256]{1,0:T(8,128)(2,1)S(1)} collective-permute-done((bf16[1024,256]{1,0:T(8,128)(2,1)S(1)}, bf16[1024,256]{1,0:T(8,128)(2,1)S(1)}, u32[]{:S(2)}, u32[]{:S(2)}) %collective-permute-start.26) | collective-permute-done | bytes 524320 | tf_op jit(solution)/shard_map/ppermute | solution.py:30
  125.1 5.6 %collective-permute-done.25.refs_8_ = bf16[1024,256]{1,0:T(8,128)(2,1)S(1)} collective-permute-done((bf16[1024,256]{1,0:T(8,128)(2,1)S(1)}, bf16[1024,256]{1,0:T(8,128)(2,1)S(1)}, u32[]{:S(2)}, u32[]{:S(2)}) %collective-permute-start.25) | collective-permute-done | bytes 524320 | tf_op jit(solution)/shard_map/ppermute | solution.py:30
  132.4 8.9 %collective-permute-done.28.refs_9_ = bf16[1024,256]{1,0:T(8,128)(2,1)} collective-permute-done((bf16[1024,256]{1,0:T(8,128)(2,1)S(1)}, bf16[1024,256]{1,0:T(8,128)(2,1)}, u32[]{:S(2)}, u32[]{:S(2)}) %collective-permute-start.28) | collective-permute-done | bytes 524320 | tf_op jit(solution)/shard_map/ppermute | solution.py:30
  141.3 5.5 %collective-permute-done.27.refs_4_ = bf16[1024,256]{1,0:T(8,128)(2,1)S(1)} collective-permute-done((bf16[1024,256]{1,0:T(8,128)(2,1)S(1)}, bf16[1024,256]{1,0:T(8,128)(2,1)S(1)}, u32[]{:S(2)}, u32[]{:S(2)}) %collective-permute-start.27) | collective-permute-done | bytes 524320 | tf_op jit(solution)/shard_map/ppermute | solution.py:30
  147.6 1.9 collective-permute-start.36
  149.6 8.7 %collective-permute-done.29.refs_5_ = bf16[1024,256]{1,0:T(8,128)(2,1)} collective-permute-done((bf16[1024,256]{1,0:T(8,128)(2,1)}, bf16[1024,256]{1,0:T(8,128)(2,1)}, u32[]{:S(2)}, u32[]{:S(2)}) %collective-permute-start.29) | collective-permute-done | bytes 524320 | tf_op jit(solution)/shard_map/ppermute | solution.py:30
  164.0 6.1 %shard_map.83 = (bf16[768,4096]{1,0:T(8,128)(2,1)S(1)}, bf16[768,4096]{1,0:T(8,128)(2,1)S(1)}) custom-call(s32[5]{0:T(128)S(1)} %stack.32.here_ref, s32[6]{0:T(128)S(1)} %copy-done.30, s32[32]{0:T(128)S(1)} %copy-done.33, s32[6,32]{1,0:T(8,128)S(1)} %copy-done.31, bf16[2,768,512]{2,1,0:T(8,128)(2,1)S(1)} %pad_maximum_fusion.refs_0_, ...), custom_call_target="tpu_custom_call" | custom-call | bytes 26214400 | tf_op jit(solution)/shard_map/pallas_call | solution.py:94
  170.1 2.7 %copy-done = bf16[768,4096]{1,0:T(8,128)(2,1)} copy-done((bf16[768,4096]{1,0:T(8,128)(2,1)}, bf16[768,4096]{1,0:T(8,128)(2,1)S(1)}, u32[]{:S(2)}) %copy-start) | copy-done | bytes 6291480
  172.8 2.6 %copy-done.2 = bf16[768,4096]{1,0:T(8,128)(2,1)} copy-done((bf16[768,4096]{1,0:T(8,128)(2,1)}, bf16[768,4096]{1,0:T(8,128)(2,1)S(1)}, u32[]{:S(2)}) %copy-start.2) | copy-done | bytes 6291480
  178.9 13.7 %shard_map.87.refs_10_ = f32[768,1024]{1,0:T(8,128)S(1)} custom-call(s32[6]{0:T(128)S(1)} %copy-done.30, s32[8]{0:T(128)S(1)} %copy-done.32, bf16[768,4096]{1,0:T(8,128)(2,1)} %copy-done, bf16[768,4096]{1,0:T(8,128)(2,1)} %copy-done.2, bf16[1024,512]{1,0:T(8,128)(2,1)S(1)} %copy-done.13, bf16[1024,512]{1,0:T(8,128)(2,1)S(1)} %copy-done.35, ...), custom_call_target="tpu_custom_call" | custom-call | flops 8053063680 | bytes 23068672 | tf_op jit(solution)/shard_map/pallas_call | solution.py:144
  192.6 7.7 %shard_map.88.refs_8_ = f32[768,1024]{1,0:T(8,128)S(1)} custom-call(s32[6]{0:T(128)S(1)} %copy-done.30, s32[8]{0:T(128)S(1)} %copy-done.32, bf16[768,4096]{1,0:T(8,128)(2,1)S(1)} %copy-done.1, bf16[768,4096]{1,0:T(8,128)(2,1)} %copy-done.2, bf16[1024,512]{1,0:T(8,128)(2,1)} %collective-permute-done.35.refs_4_, ...), custom_call_target="tpu_custom_call" | custom-call | flops 3221225472 | bytes 16777216 | tf_op jit(solution)/shard_map/pallas_call | solution.py:144
  200.4 4.9 %shard_map.89 = bf16[768,1024]{1,0:T(8,128)(2,1)} custom-call(s32[6]{0:T(128)S(1)} %copy-done.30, s32[8]{0:T(128)S(1)} %copy-done.32, bf16[768,4096]{1,0:T(8,128)(2,1)S(1)} %copy-done.1, bf16[768,4096]{1,0:T(8,128)(2,1)S(1)} %copy-done.3, bf16[1024,256]{1,0:T(8,128)(2,1)S(1)} %copy-done.23, bf16[1024,256]{1,0:T(8,128)(2,1)} %collective-permute-done.29.refs_5_, ...), custom_call_target="tpu_custom_call" | custom-call | flops 1610612736 | bytes 14680064 | tf_op jit(solution)/shard_map/pallas_call | solution.py:144
  (160 shorter events, 39.1 us)
Async XLA Ops:
  0.0 10.4 %collective-permute-start = (bf16[1024,128]{1,0:T(8,128)(2,1)}, bf16[1024,128]{1,0:T(8,128)(2,1)S(1)}, u32[]{:S(2)}, u32[]{:S(2)}) collective-permute-start(bf16[1024,128]{1,0:T(8,128)(2,1)} %refs_0_.5), channel_id=1, source_target_pairs={{0,1},{1,2},{2,3},{3,4},{4,5},{5,6},{6,7},{7,0},{8,9},{9,10},{10,1... | collective-permute-start | bytes 786440 | tf_op jit(solution)/shard_map/ppermute | solution.py:30
  19.6 21.7 %collective-permute-start.4 = (bf16[2,768,512]{2,1,0:T(8,128)(2,1)S(1)}, bf16[2,768,512]{2,1,0:T(8,128)(2,1)S(1)}, u32[]{:S(2)}, u32[]{:S(2)}) collective-permute-start(bf16[2,768,512]{2,1,0:T(8,128)(2,1)S(1)} %pad_maximum_fusion.refs_0_), channel_id=1, source_target_pairs={{0,64},{1,65},{2,66},{3,67},{4,68},{5,69},{6,70},{7,71},{8,72},{9,... | collective-permute-start | bytes 4718600 | tf_op jit(solution)/shard_map/ppermute | solution.py:30
  25.6 17.1 %collective-permute-start.3 = (bf16[2,768,512]{2,1,0:T(8,128)(2,1)S(1)}, bf16[2,768,512]{2,1,0:T(8,128)(2,1)S(1)}, u32[]{:S(2)}, u32[]{:S(2)}) collective-permute-start(bf16[2,768,512]{2,1,0:T(8,128)(2,1)S(1)} %pad_maximum_fusion.refs_0_), channel_id=1, source_target_pairs={{0,32},{1,33},{2,34},{3,35},{4,36},{5,37},{6,38},{7,39},{8,40},{9,... | collective-permute-start | bytes 4718600 | tf_op jit(solution)/shard_map/ppermute | solution.py:30
  25.8 15.3 %collective-permute-start.10 = (bf16[1024,128]{1,0:T(8,128)(2,1)S(1)}, bf16[1024,128]{1,0:T(8,128)(2,1)S(1)}, u32[]{:S(2)}, u32[]{:S(2)}) collective-permute-start(bf16[1024,128]{1,0:T(8,128)(2,1)S(1)} %copy-done.28), channel_id=1, source_target_pairs={{0,24},{1,25},{2,26},{3,27},{4,28},{5,29},{6,30},{7,31},{8,0},{9,1... | collective-permute-start | bytes 786440 | tf_op jit(solution)/shard_map/ppermute | solution.py:30
  27.6 13.5 %collective-permute-start.9 = (bf16[1024,128]{1,0:T(8,128)(2,1)S(1)}, bf16[1024,128]{1,0:T(8,128)(2,1)S(1)}, u32[]{:S(2)}, u32[]{:S(2)}) collective-permute-start(bf16[1024,128]{1,0:T(8,128)(2,1)S(1)} %copy-done.28), channel_id=1, source_target_pairs={{0,16},{1,17},{2,18},{3,19},{4,20},{5,21},{6,22},{7,23},{8,24},{9,... | collective-permute-start | bytes 786440 | tf_op jit(solution)/shard_map/ppermute | solution.py:30
  34.9 13.9 %collective-permute-start.16 = (bf16[1024,256]{1,0:T(8,128)(2,1)S(1)}, bf16[1024,256]{1,0:T(8,128)(2,1)S(1)}, u32[]{:S(2)}, u32[]{:S(2)}) collective-permute-start(bf16[1024,256]{1,0:T(8,128)(2,1)S(1)} %shard_map.84.refs_10_), channel_id=1, source_target_pairs={{0,1},{1,2},{2,3},{3,4},{4,5},{5,6},{6,7},{7,0},{8,9},{9,10},{10,1... | collective-permute-start | bytes 1572872 | tf_op jit(solution)/shard_map/ppermute | solution.py:30
  41.3 34.7 %collective-permute-start.6 = (bf16[2,768,512]{2,1,0:T(8,128)(2,1)S(1)}, bf16[2,768,512]{2,1,0:T(8,128)(2,1)S(1)}, u32[]{:S(2)}, u32[]{:S(2)}) collective-permute-start(bf16[2,768,512]{2,1,0:T(8,128)(2,1)S(1)} %collective-permute-done.4.refs_2_), channel_id=1, source_target_pairs={{0,64},{1,65},{2,66},{3,67},{4,68},{5,69},{6,70},{7,71},{8,72},{9,... | collective-permute-start | bytes 4718600 | tf_op jit(solution)/shard_map/ppermute | solution.py:30
  43.9 33.6 %collective-permute-start.5 = (bf16[2,768,512]{2,1,0:T(8,128)(2,1)S(1)}, bf16[2,768,512]{2,1,0:T(8,128)(2,1)S(1)}, u32[]{:S(2)}, u32[]{:S(2)}) collective-permute-start(bf16[2,768,512]{2,1,0:T(8,128)(2,1)S(1)} %collective-permute-done.4.refs_2_), channel_id=1, source_target_pairs={{0,32},{1,33},{2,34},{3,35},{4,36},{5,37},{6,38},{7,39},{8,40},{9,... | collective-permute-start | bytes 4718600 | tf_op jit(solution)/shard_map/ppermute | solution.py:30
  45.7 18.1 %collective-permute-start.13 = (bf16[1024,512]{1,0:T(8,128)(2,1)S(1)}, bf16[1024,512]{1,0:T(8,128)(2,1)S(1)}, u32[]{:S(2)}, u32[]{:S(2)}) collective-permute-start(bf16[1024,512]{1,0:T(8,128)(2,1)S(1)} %shard_map.82.refs_4_), channel_id=1, source_target_pairs={{0,8},{1,9},{2,10},{3,11},{4,12},{5,13},{6,14},{7,15},{8,16},{9,17... | collective-permute-start | bytes 3145736 | tf_op jit(solution)/shard_map/ppermute | solution.py:30
  48.7 13.2 %collective-permute-start.17 = (bf16[1024,256]{1,0:T(8,128)(2,1)S(1)}, bf16[1024,256]{1,0:T(8,128)(2,1)S(1)}, u32[]{:S(2)}, u32[]{:S(2)}) collective-permute-start(bf16[1024,256]{1,0:T(8,128)(2,1)S(1)} %shard_map.85.refs_11_), channel_id=1, source_target_pairs={{0,1},{1,2},{2,3},{3,4},{4,5},{5,6},{6,7},{7,0},{8,9},{9,10},{10,1... | collective-permute-start | bytes 1572872 | tf_op jit(solution)/shard_map/ppermute | solution.py:30
  50.0 11.9 %collective-permute-start.12 = (bf16[1024,128]{1,0:T(8,128)(2,1)S(1)}, bf16[1024,128]{1,0:T(8,128)(2,1)S(1)}, u32[]{:S(2)}, u32[]{:S(2)}) collective-permute-start(bf16[1024,128]{1,0:T(8,128)(2,1)S(1)} %collective-permute-done.11.refs_0_), channel_id=1, source_target_pairs={{0,1},{1,2},{2,3},{3,4},{4,5},{5,6},{6,7},{7,0},{8,9},{9,10},{10,1... | collective-permute-start | bytes 786440 | tf_op jit(solution)/shard_map/ppermute | solution.py:30
  61.9 13.2 %collective-permute-start.18 = (bf16[1024,256]{1,0:T(8,128)(2,1)S(1)}, bf16[1024,256]{1,0:T(8,128)(2,1)S(1)}, u32[]{:S(2)}, u32[]{:S(2)}) collective-permute-start(bf16[1024,256]{1,0:T(8,128)(2,1)S(1)} %collective-permute-done.16.refs_12_), channel_id=1, source_target_pairs={{0,1},{1,2},{2,3},{3,4},{4,5},{5,6},{6,7},{7,0},{8,9},{9,10},{10,1... | collective-permute-start | bytes 1572872 | tf_op jit(solution)/shard_map/ppermute | solution.py:30
  62.8 12.4 %collective-permute-start.19 = (bf16[1024,128]{1,0:T(8,128)(2,1)S(1)}, bf16[1024,128]{1,0:T(8,128)(2,1)S(1)}, u32[]{:S(2)}, u32[]{:S(2)}) collective-permute-start(bf16[1024,128]{1,0:T(8,128)(2,1)S(1)} %collective-permute-done.12.refs_1_), channel_id=1, source_target_pairs={{0,1},{1,2},{2,3},{3,4},{4,5},{5,6},{6,7},{7,0},{8,9},{9,10},{10,1... | collective-permute-start | bytes 786440 | tf_op jit(solution)/shard_map/ppermute | solution.py:30
  63.7 26.4 %collective-permute-start.33 = (bf16[1024,512]{1,0:T(8,128)(2,1)S(1)}, bf16[1024,512]{1,0:T(8,128)(2,1)S(1)}, u32[]{:S(2)}, u32[]{:S(2)}) collective-permute-start(bf16[1024,512]{1,0:T(8,128)(2,1)S(1)} %collective-permute-done.13.refs_5_), channel_id=1, source_target_pairs={{0,8},{1,9},{2,10},{3,11},{4,12},{5,13},{6,14},{7,15},{8,16},{9,17... | collective-permute-start | bytes 3145736 | tf_op jit(solution)/shard_map/ppermute | solution.py:30
  75.1 13.2 %collective-permute-start.20 = (bf16[1024,256]{1,0:T(8,128)(2,1)S(1)}, bf16[1024,256]{1,0:T(8,128)(2,1)S(1)}, u32[]{:S(2)}, u32[]{:S(2)}) collective-permute-start(bf16[1024,256]{1,0:T(8,128)(2,1)S(1)} %collective-permute-done.17.refs_13_), channel_id=1, source_target_pairs={{0,1},{1,2},{2,3},{3,4},{4,5},{5,6},{6,7},{7,0},{8,9},{9,10},{10,1... | collective-permute-start | bytes 1572872 | tf_op jit(solution)/shard_map/ppermute | solution.py:30
  75.9 12.4 %collective-permute-start.21 = (bf16[1024,128]{1,0:T(8,128)(2,1)S(1)}, bf16[1024,128]{1,0:T(8,128)(2,1)S(1)}, u32[]{:S(2)}, u32[]{:S(2)}) collective-permute-start(bf16[1024,128]{1,0:T(8,128)(2,1)S(1)} %collective-permute-done.19.refs_2_), channel_id=1, source_target_pairs={{0,1},{1,2},{2,3},{3,4},{4,5},{5,6},{6,7},{7,0},{8,9},{9,10},{10,1... | collective-permute-start | bytes 786440 | tf_op jit(solution)/shard_map/ppermute | solution.py:30
  76.0 39.6 %collective-permute-start.14 = (bf16[2,768,512]{2,1,0:T(8,128)(2,1)S(1)}, bf16[2,768,512]{2,1,0:T(8,128)(2,1)}, u32[]{:S(2)}, u32[]{:S(2)}) collective-permute-start(bf16[2,768,512]{2,1,0:T(8,128)(2,1)S(1)} %collective-permute-done.6.refs_4_), channel_id=1, source_target_pairs={{0,64},{1,65},{2,66},{3,67},{4,68},{5,69},{6,70},{7,71},{8,72},{9,... | collective-permute-start | bytes 4718600 | tf_op jit(solution)/shard_map/ppermute | solution.py:30
  78.6 37.8 %collective-permute-start.7 = (bf16[2,768,512]{2,1,0:T(8,128)(2,1)S(1)}, bf16[2,768,512]{2,1,0:T(8,128)(2,1)S(1)}, u32[]{:S(2)}, u32[]{:S(2)}) collective-permute-start(bf16[2,768,512]{2,1,0:T(8,128)(2,1)S(1)} %collective-permute-done.6.refs_4_), channel_id=1, source_target_pairs={{0,32},{1,33},{2,34},{3,35},{4,36},{5,37},{6,38},{7,39},{8,40},{9,... | collective-permute-start | bytes 4718600 | tf_op jit(solution)/shard_map/ppermute | solution.py:30
  88.3 10.4 %collective-permute-start.22 = (bf16[1024,256]{1,0:T(8,128)(2,1)S(1)}, bf16[1024,256]{1,0:T(8,128)(2,1)S(1)}, u32[]{:S(2)}, u32[]{:S(2)}) collective-permute-start(bf16[1024,256]{1,0:T(8,128)(2,1)S(1)} %collective-permute-done.18.refs_14_), channel_id=1, source_target_pairs={{0,1},{1,2},{2,3},{3,4},{4,5},{5,6},{6,7},{7,0},{8,9},{9,10},{10,1... | collective-permute-start | bytes 1572872 | tf_op jit(solution)/shard_map/ppermute | solution.py:30
  89.2 15.2 %collective-permute-start.24 = (bf16[1024,256]{1,0:T(8,128)(2,1)S(1)}, bf16[1024,256]{1,0:T(8,128)(2,1)S(1)}, u32[]{:S(2)}, u32[]{:S(2)}) collective-permute-start(bf16[1024,256]{1,0:T(8,128)(2,1)S(1)} %collective-permute-done.20.refs_15_), channel_id=1, source_target_pairs={{0,1},{1,2},{2,3},{3,4},{4,5},{5,6},{6,7},{7,0},{8,9},{9,10},{10,1... | collective-permute-start | bytes 1572872 | tf_op jit(solution)/shard_map/ppermute | solution.py:30
  90.2 27.5 %collective-permute-start.32 = (bf16[1024,512]{1,0:T(8,128)(2,1)S(1)}, bf16[1024,512]{1,0:T(8,128)(2,1)S(1)}, u32[]{:S(2)}, u32[]{:S(2)}) collective-permute-start(bf16[1024,512]{1,0:T(8,128)(2,1)S(1)} %shard_map.86.refs_8_), channel_id=1, source_target_pairs={{0,8},{1,9},{2,10},{3,11},{4,12},{5,13},{6,14},{7,15},{8,16},{9,17... | collective-permute-start | bytes 3145736 | tf_op jit(solution)/shard_map/ppermute | solution.py:30
  98.7 18.9 %collective-permute-start.34 = (bf16[1024,512]{1,0:T(8,128)(2,1)S(1)}, bf16[1024,512]{1,0:T(8,128)(2,1)S(1)}, u32[]{:S(2)}, u32[]{:S(2)}) collective-permute-start(bf16[1024,512]{1,0:T(8,128)(2,1)S(1)} %collective-permute-done.33.refs_6_), channel_id=1, source_target_pairs={{0,8},{1,9},{2,10},{3,11},{4,12},{5,13},{6,14},{7,15},{8,16},{9,17... | collective-permute-start | bytes 3145736 | tf_op jit(solution)/shard_map/ppermute | solution.py:30
  104.4 10.4 %collective-permute-start.23 = (bf16[1024,256]{1,0:T(8,128)(2,1)S(1)}, bf16[1024,256]{1,0:T(8,128)(2,1)S(1)}, u32[]{:S(2)}, u32[]{:S(2)}) collective-permute-start(bf16[1024,256]{1,0:T(8,128)(2,1)S(1)} %collective-permute-done.22.refs_16_), channel_id=1, source_target_pairs={{0,1},{1,2},{2,3},{3,4},{4,5},{5,6},{6,7},{7,0},{8,9},{9,10},{10,1... | collective-permute-start | bytes 1572872 | tf_op jit(solution)/shard_map/ppermute | solution.py:30
  115.5 15.2 %collective-permute-start.25 = (bf16[1024,256]{1,0:T(8,128)(2,1)S(1)}, bf16[1024,256]{1,0:T(8,128)(2,1)S(1)}, u32[]{:S(2)}, u32[]{:S(2)}) collective-permute-start(bf16[1024,256]{1,0:T(8,128)(2,1)S(1)} %collective-permute-done.23.refs_6_), channel_id=1, source_target_pairs={{0,1},{1,2},{2,3},{3,4},{4,5},{5,6},{6,7},{7,0},{8,9},{9,10},{10,1... | collective-permute-start | bytes 1572872 | tf_op jit(solution)/shard_map/ppermute | solution.py:30
  117.6 40.7 %collective-permute-start.15 = (bf16[2,768,512]{2,1,0:T(8,128)(2,1)}, bf16[2,768,512]{2,1,0:T(8,128)(2,1)}, u32[]{:S(2)}, u32[]{:S(2)}) collective-permute-start(bf16[2,768,512]{2,1,0:T(8,128)(2,1)} %collective-permute-done.14.refs_6_), channel_id=1, source_target_pairs={{0,32},{1,33},{2,34},{3,35},{4,36},{5,37},{6,38},{7,39},{8,40},{9,... | collective-permute-start | bytes 4718600 | tf_op jit(solution)/shard_map/ppermute | solution.py:30
  118.6 29.0 %collective-permute-start.35 = (bf16[1024,512]{1,0:T(8,128)(2,1)S(1)}, bf16[1024,512]{1,0:T(8,128)(2,1)}, u32[]{:S(2)}, u32[]{:S(2)}) collective-permute-start(bf16[1024,512]{1,0:T(8,128)(2,1)S(1)} %collective-permute-done.32.refs_9_), channel_id=1, source_target_pairs={{0,8},{1,9},{2,10},{3,11},{4,12},{5,13},{6,14},{7,15},{8,16},{9,17... | collective-permute-start | bytes 3145736 | tf_op jit(solution)/shard_map/ppermute | solution.py:30
  130.8 10.5 %collective-permute-start.28 = (bf16[1024,256]{1,0:T(8,128)(2,1)S(1)}, bf16[1024,256]{1,0:T(8,128)(2,1)}, u32[]{:S(2)}, u32[]{:S(2)}) collective-permute-start(bf16[1024,256]{1,0:T(8,128)(2,1)S(1)} %collective-permute-done.26.refs_7_), channel_id=1, source_target_pairs={{0,1},{1,2},{2,3},{3,4},{4,5},{5,6},{6,7},{7,0},{8,9},{9,10},{10,1... | collective-permute-start | bytes 1572872 | tf_op jit(solution)/shard_map/ppermute | solution.py:30
  131.6 15.2 %collective-permute-start.27 = (bf16[1024,256]{1,0:T(8,128)(2,1)S(1)}, bf16[1024,256]{1,0:T(8,128)(2,1)S(1)}, u32[]{:S(2)}, u32[]{:S(2)}) collective-permute-start(bf16[1024,256]{1,0:T(8,128)(2,1)S(1)} %collective-permute-done.25.refs_8_), channel_id=1, source_target_pairs={{0,1},{1,2},{2,3},{3,4},{4,5},{5,6},{6,7},{7,0},{8,9},{9,10},{10,1... | collective-permute-start | bytes 1572872 | tf_op jit(solution)/shard_map/ppermute | solution.py:30
  147.6 10.7 %collective-permute-start.29 = (bf16[1024,256]{1,0:T(8,128)(2,1)}, bf16[1024,256]{1,0:T(8,128)(2,1)}, u32[]{:S(2)}, u32[]{:S(2)}) collective-permute-start(bf16[1024,256]{1,0:T(8,128)(2,1)} %collective-permute-done.28.refs_9_), channel_id=1, source_target_pairs={{0,1},{1,2},{2,3},{3,4},{4,5},{5,6},{6,7},{7,0},{8,9},{9,10},{10,1... | collective-permute-start | bytes 1572872 | tf_op jit(solution)/shard_map/ppermute | solution.py:30
  147.6 45.0 %collective-permute-start.36 = (bf16[1024,512]{1,0:T(8,128)(2,1)}, bf16[1024,512]{1,0:T(8,128)(2,1)}, u32[]{:S(2)}, u32[]{:S(2)}) collective-permute-start(bf16[1024,512]{1,0:T(8,128)(2,1)} %collective-permute-done.35.refs_4_), channel_id=1, source_target_pairs={{0,8},{1,9},{2,10},{3,11},{4,12},{5,13},{6,14},{7,15},{8,16},{9,17... | collective-permute-start | bytes 3145736 | tf_op jit(solution)/shard_map/ppermute | solution.py:30
  149.6 50.7 %collective-permute-start.30 = (bf16[1024,256]{1,0:T(8,128)(2,1)}, bf16[1024,256]{1,0:T(8,128)(2,1)S(1)}, u32[]{:S(2)}, u32[]{:S(2)}) collective-permute-start(bf16[1024,256]{1,0:T(8,128)(2,1)} %copy-done.22), channel_id=1, source_target_pairs={{0,1},{1,2},{2,3},{3,4},{4,5},{5,6},{6,7},{7,0},{8,9},{9,10},{10,1... | collective-permute-start | bytes 1572872 | tf_op jit(solution)/shard_map/ppermute | solution.py:30
  158.3 42.0 %collective-permute-start.31 = (bf16[1024,256]{1,0:T(8,128)(2,1)}, bf16[1024,256]{1,0:T(8,128)(2,1)S(1)}, u32[]{:S(2)}, u32[]{:S(2)}) collective-permute-start(bf16[1024,256]{1,0:T(8,128)(2,1)} %collective-permute-done.29.refs_5_), channel_id=1, source_target_pairs={{0,1},{1,2},{2,3},{3,4},{4,5},{5,6},{6,7},{7,0},{8,9},{9,10},{10,1... | collective-permute-start | bytes 1572872 | tf_op jit(solution)/shard_map/ppermute | solution.py:30
  (59 other events, 715.4 us)

commit v2 on v0

v2 whole, which is shorter than its diff:
```python
import jax
import jax.numpy as jnp
from jax import lax
from jax.experimental import pallas as pl
from jax.experimental.pallas import tpu as pltpu
from jax.sharding import PartitionSpec as P

BLK = 128
AXES = ("grp", "mem")
NX, NY, NZ = 4, 4, 8
BF16 = jnp.bfloat16
F32 = jnp.float32


def perm_of(dx, dy, dz, swap=0):
    pairs = []
    for x in range(NX):
        for core in range(2):
            sign = 1 if core == 0 else -1
            for y in range(NY):
                for z in range(NZ):
                    src = (2 * x + core) * 32 + 8 * y + z
                    x2, y2, z2 = (x + sign * dx) % NX, (y + sign * dy) % NY, (z + sign * dz) % NZ
                    core2 = core ^ swap
                    pairs.append((src, (2 * x2 + core2) * 32 + 8 * y2 + z2))
    return pairs


def move(values, dx=0, dy=0, dz=0, swap=0):
    return lax.ppermute(values, AXES, perm_of(dx, dy, dz, swap))


def after(value, *others):
    return lax.optimization_barrier((value,) + others)[0]


SMEM = pl.BlockSpec(memory_space=pltpu.SMEM)
VMEM = pl.BlockSpec(memory_space=pltpu.VMEM)
ANY = pl.BlockSpec(memory_space=pl.ANY)


def params(mib):
    return pltpu.CompilerParams(vmem_limit_bytes=mib * 2**20)


def cost(flops, moved):
    return pl.CostEstimate(flops=flops, bytes_accessed=moved, transcendentals=0)


def join_kernel(*refs):
    blocks, out = refs[:-1], refs[-1]
    width = blocks[0].shape[1]
    for b, block in enumerate(blocks):
        out[:, b * width:(b + 1) * width] = block[...]


def join(blocks):
    rows, width = blocks[0].shape
    full = width * len(blocks)
    return pl.pallas_call(
        join_kernel,
        out_shape=jax.ShapeDtypeStruct((rows, full), BF16),
        in_specs=[VMEM] * len(blocks),
        out_specs=VMEM,
        compiler_params=params(8),
        cost_estimate=cost(0, 4 * rows * full),
    )(*blocks)


def dot(left, right):
    return lax.dot_general(left, right, (((1,), (1,)), ((), ())), preferred_element_type=F32)


def tiles_of(terms):
    return [tile for tiles, _ in terms for tile in tiles]


def early_kernel(terms, parts, here_ref, ij_ref, cd_ref, mask_ref, raw_hbm, *refs):
    n = len(terms)
    ints, outs, (raw, amps, rows_v, sem) = refs[:n], refs[n:-4], refs[-4:]
    copies = [pltpu.make_async_copy(raw_hbm, raw, sem.at[n])]
    at = 0
    for k, block in enumerate(ints):
        width = block.shape[1]
        copies.append(pltpu.make_async_copy(block, rows_v.at[:, pl.ds(at, width)], sem.at[k]))
        at += width
    for copy in copies:
        copy.start()
    sign, y, z = [here_ref[k] for k in range(3)]
    copies[0].wait()
    for target, tiles in zip((amps,) + tuple(outs[1:]), parts):
        for k, (panel, step_y, step_z) in enumerate(tiles):
            tile = 8 * ((y - sign * step_y) & (NY - 1)) + ((z - sign * step_z) & (NZ - 1))
            cols = pl.ds(pl.multiple_of(tile * BLK, BLK), BLK)
            label = cd_ref[tile]
            for row in range(6):
                on = (ij_ref[row] == label) & (mask_ref[row, tile] == 1)
                kept = raw[pl.ds(panel * 768 + row * BLK, BLK), cols]
                target[row * BLK:(row + 1) * BLK, k * BLK:(k + 1) * BLK] = jnp.where(on, kept, jnp.zeros_like(kept))
    for copy in copies[1:]:
        copy.wait()

    def strip(k, carry):
        m = pl.ds(pl.multiple_of((k // 4) * 256, 256), 256)
        c = pl.ds(pl.multiple_of((k % 4) * 256, 256), 256)
        outs[0][m, c] = dot(amps[m, :], rows_v[c, :])
        return carry

    lax.fori_loop(0, 12, strip, 0)


def early(here, sym_ij, sym_cd, amp_mask, raw, terms, later):
    parts = [tiles_of(terms)] + [tiles_of(more) for more in later]
    depth = [len(tiles) * BLK for tiles in parts]

    def kernel(*refs):
        early_kernel(terms, parts, *refs)

    return pl.pallas_call(
        kernel,
        out_shape=[jax.ShapeDtypeStruct((768, 1024), F32)]
        + [jax.ShapeDtypeStruct((768, size), BF16) for size in depth[1:]],
        in_specs=[SMEM] * 4 + [ANY] * (1 + len(terms)),
        out_specs=[VMEM] * len(depth),
        scratch_shapes=[
            pltpu.VMEM((1536, 4096), BF16),
            pltpu.VMEM((768, depth[0]), BF16),
            pltpu.VMEM((1024, depth[0]), BF16),
            pltpu.SemaphoreType.DMA((len(terms) + 1,)),
        ],
        compiler_params=params(46),
        cost_estimate=cost(2 * 768 * 1024 * depth[0], 32 * 2**20),
    )(here, sym_ij, sym_cd, amp_mask, raw, *[block for _, block in terms])


def more_kernel(n, last, ij_ref, ab_ref, amps, total, *refs):
    ints, (out, rows_v, sem) = refs[:n], refs[n:]
    copies = []
    at = 0
    for k, block in enumerate(ints):
        width = block.shape[1]
        copies.append(pltpu.make_async_copy(block, rows_v.at[:, pl.ds(at, width)], sem.at[k]))
        at += width
    for copy in copies:
        copy.start()
    for copy in copies:
        copy.wait()

    def strip(k, carry):
        m = pl.ds(pl.multiple_of((k // 4) * 256, 256), 256)
        c = pl.ds(pl.multiple_of((k % 4) * 256, 256), 256)
        value = total[m, c] + dot(amps[m, :], rows_v[c, :])
        if not last:
            out[m, c] = value
            return carry
        for i in range(2):
            for j in range(2):
                tile = value[i * BLK:(i + 1) * BLK, j * BLK:(j + 1) * BLK] * 0.5
                on = ij_ref[2 * (k // 4) + i] == ab_ref[2 * (k % 4) + j]
                where = (
                    pl.ds(pl.multiple_of((k // 4) * 256 + i * BLK, BLK), BLK),
                    pl.ds(pl.multiple_of((k % 4) * 256 + j * BLK, BLK), BLK),
                )
                out[where] = jnp.where(on, tile, jnp.zeros_like(tile)).astype(BF16)
        return carry

    lax.fori_loop(0, 12, strip, 0)


def more(sym_ij, sym_ab, amps, total, terms, last):
    depth = amps.shape[1]

    def kernel(*refs):
        more_kernel(len(terms), last, *refs)

    return pl.pallas_call(
        kernel,
        out_shape=jax.ShapeDtypeStruct((768, 1024), BF16 if last else F32),
        in_specs=[SMEM] * 2 + [VMEM] * 2 + [ANY] * len(terms),
        out_specs=VMEM,
        scratch_shapes=[pltpu.VMEM((1024, depth), BF16), pltpu.SemaphoreType.DMA((len(terms),))],
        compiler_params=params(20),
        cost_estimate=cost(2 * 768 * 1024 * depth, 8 * 2**20 + 3584 * depth),
    )(sym_ij, sym_ab, amps, total, *[block for _, block in terms])


def body(amp_plus, amp_minus, ints_plus, ints_minus, sym_ij, sym_ab, sym_cd, amp_mask):
    grp, mem = lax.axis_index("grp"), lax.axis_index("mem")
    here = jnp.stack([1 - 2 * (grp % 2), mem // 8, mem % 8]).astype(jnp.int32)

    def go(value, *waits, **way):
        return move(after(value, *waits) if waits else value, **way)

    raw = lax.all_gather(jnp.concatenate([amp_plus, amp_minus], axis=0), "grp", axis=1, tiled=True)

    z0, y0 = ints_plus, ints_minus
    z1, y1 = go(z0, dz=1), go(y0, dy=1)
    z2, y2 = go(z1, y1, dz=1), go(y1, z1, dy=1)
    z3, y3 = go(z2, y2, dz=1), go(y2, z2, dy=1)
    z4 = go(z3, y3, dz=1)
    a, b, c = [join((y0, y1))], [join((y2, y3))], [join((z0, z1, z2, z3))]
    a.append(go(a[0], dz=1))
    c.append(go(c[0], dy=1))
    b.append(go(b[0], dz=1))
    z5 = go(z4, dz=1)
    a.append(go(a[1], z4, dz=1))
    b.append(go(b[1], a[1], dz=1))
    d = [join((z4, z5))]
    z6 = go(z5, b[1], dz=1)
    c.append(go(c[1], b[1], dy=1))
    d.append(go(d[0], dy=1))
    a.append(go(a[2], z5, dz=1))
    b.append(go(b[2], a[2], dz=1))
    z7 = go(z6, b[2], dz=1)
    e = [join((z6, z7))]
    c.append(go(c[2], b[2], dy=1))
    d.append(go(d[1], b[2], dy=1))
    a.append(go(a[3], z6, dz=1))
    b.append(go(b[3], a[3], dz=1))
    e.append(go(e[0], b[3], dy=1))
    d.append(go(d[2], b[3], dy=1))
    a.append(go(a[4], z7, dz=1))
    b.append(go(b[4], a[4], dz=1))
    a.append(go(a[5], b[4], dz=1))
    e.append(go(e[1], a[5], dy=1))
    b.append(go(b[5], a[5], dz=1))
    a.append(go(a[6], b[5], dz=1))
    e.append(go(e[2], a[6], dy=1))
    b.append(go(b[6], a[6], dz=1))

    def plus(blocks, i, first):
        count = blocks[i].shape[1] // BLK
        return [(0, i, first + k) for k in range(count)], blocks[i]

    def minus(blocks, t, first):
        return [(1, first + k, t) for k in range(2)], blocks[t]

    now = [plus(c, i, 0) for i in range(4)] + [plus(d, i, 4) for i in range(2)] + [plus(e, 0, 6)]
    now += [term for t in range(5) for term in (minus(a, t, 0), minus(b, t, 2))]
    soon = [plus(d, 2, 4), plus(d, 3, 4), plus(e, 1, 6)]
    soon += [term for t in (5, 6) for term in (minus(a, t, 0), minus(b, t, 2))]
    rest = [plus(e, 2, 6), plus(e, 3, 6), minus(a, 7, 0), minus(b, 7, 2)]
    total, amps_soon, amps_rest = early(here, sym_ij, sym_cd, amp_mask, raw, now, (soon, rest))
    total = more(sym_ij, sym_ab, amps_soon, total, soon, False)
    return more(sym_ij, sym_ab, amps_rest, total, rest, True)


def solution(mesh):
    placed = (
        P("mem", "grp"),
        P("mem", "grp"),
        P("grp", "mem"),
        P("grp", "mem"),
        P("mem"),
        P("grp"),
        P(),
        P("mem", None),
    )
    return jax.shard_map(
        body, mesh=mesh, in_specs=placed, out_specs=P("mem", "grp"), check_vma=False
    )
```

time: 336 us -> 206 us (0.61)
  waiting for transfers between devices: 278 us -> 89.5 us
  starting transfers between devices: 0.12 us -> 40.5 us
  Pallas kernels: 0 us -> 37.4 us
  matrix products: 34.7 us -> 0 us
  local copies, waits for them, and re-layouts: 6.25 us -> 21 us
    all_gather x4 -> x1, waiting for transfers between devices: 276 us -> 0.01 us  [body(): lax.all_gather(jnp.concatenate([amp_plus, amp_minus], axis=0), 'grp', axi...]
    ppermute x0 -> x33, waiting for transfers between devices: none -> 89.5 us  [move(): return lax.ppermute(values, AXES, perm_of(dx, dy, dz, swap))]
    ppermute x0 -> x33, starting transfers between devices: none -> 40.5 us  [move(): return lax.ppermute(values, AXES, perm_of(dx, dy, dz, swap))]
    pallas_call x0 -> x8, Pallas kernels: none -> 37.4 us  [the longest x1 22 us: early(): pl.pallas_call(kernel, out_shape=[jax.ShapeDtypeStruct((768, 1024), F32)]...]
    dot_general x2 -> x0, matrix products: 34.7 us -> none  [times_rows(): lax.dot_general(left, right, (((1,), (1,)), ((), ())), preferred_element_...]
    unnamed x2 -> x68, local copies, waits for them, and re-layouts: 1.18 us -> 21 us
    mul x2 -> x0, local copies, waits for them, and re-layouts: 5.07 us -> none  [tile_scale(): values.reshape(rows_t, BLK, cols_t, BLK)]
  transfers between devices with their start and end apart: 4 -> 34, of which waited for: 4 -> 12; matrix products, arithmetic and copies ran while one was open for 7% -> 0% of each run, Pallas kernels for 0% -> 15%
where the time goes in v2:
time: 206 us; the launch traced here: 205 us
  waiting for transfers between devices  89.5 us (43%)
  starting transfers between devices  40.5 us (20%)
  Pallas kernels  37.4 us (18%)
  local copies, waits for them, and re-layouts  21 us (10%)
  between operations  13.7 us (7%)
  other arithmetic  2.75 us (1%)
    ppermute x33, waiting for transfers between devices, move(): return lax.ppermute(values, AXES, perm_of(dx, dy, dz, swap))  89.5 us
    ppermute x33, starting transfers between devices, move(): return lax.ppermute(values, AXES, perm_of(dx, dy, dz, swap))  40.5 us
    pallas_call x1, Pallas kernels, early(): pl.pallas_call(kernel, out_shape=[jax.ShapeDtypeStruct((768, 1024), F32)]...  22 us
    unnamed x68, local copies, waits for them, and re-layouts  21 us
    pallas_call x2, Pallas kernels, more(): pl.pallas_call(kernel, out_shape=jax.ShapeDtypeStruct((768, 1024), BF16 i...  14.9 us
  transfers between devices with their start and end apart: 34, of which 12 were waited for; matrix products, arithmetic and copies ran while one was open for 0% of the time, Pallas kernels for 15%

profile of v2, /device:TPU:24, one launch (start us, length us, event | category | flops | bytes accessed | tf_op | source)
XLA Modules:
  0.0 204.9 jit_solution(3945929280390235406)
XLA Ops:
  6.5 2.7 %pad_maximum_fusion = bf16[1536,512]{1,0:T(8,128)(2,1)} fusion(bf16[768,512]{1,0:T(8,128)(2,1)} %param.9, bf16[768,512]{1,0:T(8,128)(2,1)} %param.8), kind=kLoop, calls=%fused_computation | loop fusion | flops 3145728 | bytes 3145728 | tf_op jit(solution)/shard_map/concatenate | solution.py:194
  9.2 2.0 collective-permute-start
  11.5 8.1 %collective-permute-done.refs_1_ = bf16[1024,128]{1,0:T(8,128)(2,1)S(1)} collective-permute-done((bf16[1024,128]{1,0:T(8,128)(2,1)S(1)}, bf16[1024,128]{1,0:T(8,128)(2,1)S(1)}, u32[]{:S(2)}, u32[]{:S(2)}) %collective-permute-start) | collective-permute-done | bytes 262176 | tf_op jit(solution)/shard_map/ppermute | solution.py:30
  19.5 1.4 collective-permute-start.3
  21.0 6.2 %collective-permute-done.2.refs_2_ = bf16[1024,128]{1,0:T(8,128)(2,1)S(1)} collective-permute-done((bf16[1024,128]{1,0:T(8,128)(2,1)S(1)}, bf16[1024,128]{1,0:T(8,128)(2,1)S(1)}, u32[]{:S(2)}, u32[]{:S(2)}) %collective-permute-start.2) | collective-permute-done | bytes 262176 | tf_op jit(solution)/shard_map/ppermute | solution.py:30
  27.1 1.4 collective-permute-start.6
  28.6 1.9 collective-permute-start.4
  30.6 3.2 %collective-permute-start.9 = (bf16[1024,256]{1,0:T(8,128)(2,1)S(1)}, bf16[1024,256]{1,0:T(8,128)(2,1)S(1)}, u32[]{:S(2)}, u32[]{:S(2)}) collective-permute-start(bf16[1024,256]{1,0:T(8,128)(2,1)S(1)} %shard_map.84.refs_12_), channel_id=1, source_target_pairs={{0,1},{1,2},{2,3},{3,4},{4,5},{5,6},{6,7},{7,0},{8,9},{9,10},{10,1... | collective-permute-start | bytes 1572872 | tf_op jit(solution)/shard_map/ppermute | solution.py:30
  36.3 2.2 %collective-permute-start.5 = (bf16[1024,512]{1,0:T(8,128)(2,1)S(1)}, bf16[1024,512]{1,0:T(8,128)(2,1)S(1)}, u32[]{:S(2)}, u32[]{:S(2)}) collective-permute-start(bf16[1024,512]{1,0:T(8,128)(2,1)S(1)} %shard_map.82.refs_5_), channel_id=1, source_target_pairs={{0,8},{1,9},{2,10},{3,11},{4,12},{5,13},{6,14},{7,15},{8,16},{9,17... | collective-permute-start | bytes 3145736 | tf_op jit(solution)/shard_map/ppermute | solution.py:30
  38.5 3.1 %collective-permute-start.12 = (bf16[1024,128]{1,0:T(8,128)(2,1)S(1)}, bf16[1024,128]{1,0:T(8,128)(2,1)S(1)}, u32[]{:S(2)}, u32[]{:S(2)}) collective-permute-start(bf16[1024,128]{1,0:T(8,128)(2,1)S(1)} %collective-permute-done.4.refs_3_), channel_id=1, source_target_pairs={{0,1},{1,2},{2,3},{3,4},{4,5},{5,6},{6,7},{7,0},{8,9},{9,10},{10,1... | collective-permute-start | bytes 786440 | tf_op jit(solution)/shard_map/ppermute | solution.py:30
  41.8 8.4 %collective-permute-done.12.refs_0_ = bf16[1024,128]{1,0:T(8,128)(2,1)S(1)} collective-permute-done((bf16[1024,128]{1,0:T(8,128)(2,1)S(1)}, bf16[1024,128]{1,0:T(8,128)(2,1)S(1)}, u32[]{:S(2)}, u32[]{:S(2)}) %collective-permute-start.12) | collective-permute-done | bytes 262176 | tf_op jit(solution)/shard_map/ppermute | solution.py:30
  51.5 2.5 %collective-permute-start.10 = (bf16[1024,256]{1,0:T(8,128)(2,1)S(1)}, bf16[1024,256]{1,0:T(8,128)(2,1)S(1)}, u32[]{:S(2)}, u32[]{:S(2)}) collective-permute-start(bf16[1024,256]{1,0:T(8,128)(2,1)S(1)} %collective-permute-done.7.refs_15_), channel_id=1, source_target_pairs={{0,1},{1,2},{2,3},{3,4},{4,5},{5,6},{6,7},{7,0},{8,9},{9,10},{10,1... | collective-permute-start | bytes 1572872 | tf_op jit(solution)/shard_map/ppermute | solution.py:30
  55.0 14.0 %collective-permute-done.13.refs_1_ = bf16[1024,128]{1,0:T(8,128)(2,1)S(1)} collective-permute-done((bf16[1024,128]{1,0:T(8,128)(2,1)S(1)}, bf16[1024,128]{1,0:T(8,128)(2,1)S(1)}, u32[]{:S(2)}, u32[]{:S(2)}) %collective-permute-start.13) | collective-permute-done | bytes 262176 | tf_op jit(solution)/shard_map/ppermute | solution.py:30
  70.0 2.5 %collective-permute-start.19 = (bf16[1024,256]{1,0:T(8,128)(2,1)S(1)}, bf16[1024,256]{1,0:T(8,128)(2,1)S(1)}, u32[]{:S(2)}, u32[]{:S(2)}) collective-permute-start(bf16[1024,256]{1,0:T(8,128)(2,1)S(1)} %collective-permute-done.10.refs_17_), channel_id=1, source_target_pairs={{0,1},{1,2},{2,3},{3,4},{4,5},{5,6},{6,7},{7,0},{8,9},{9,10},{10,1... | collective-permute-start | bytes 1572872 | tf_op jit(solution)/shard_map/ppermute | solution.py:30
  73.6 14.3 %collective-permute-done.15.refs_0_ = bf16[1024,128]{1,0:T(8,128)(2,1)S(1)} collective-permute-done((bf16[1024,128]{1,0:T(8,128)(2,1)S(1)}, bf16[1024,128]{1,0:T(8,128)(2,1)S(1)}, u32[]{:S(2)}, u32[]{:S(2)}) %collective-permute-start.15) | collective-permute-done | bytes 262176 | tf_op jit(solution)/shard_map/ppermute | solution.py:30
  88.6 1.4 collective-permute-start.21
  90.8 2.0 collective-permute-start.16
  93.0 13.6 %collective-permute-done.16.refs_1_ = bf16[1024,128]{1,0:T(8,128)(2,1)S(1)} collective-permute-done((bf16[1024,128]{1,0:T(8,128)(2,1)S(1)}, bf16[1024,128]{1,0:T(8,128)(2,1)S(1)}, u32[]{:S(2)}, u32[]{:S(2)}) %collective-permute-start.16) | collective-permute-done | bytes 262176 | tf_op jit(solution)/shard_map/ppermute | solution.py:30
  109.6 1.6 collective-permute-start.11
  112.5 4.6 %collective-permute-done.25.refs_7_ = bf16[1024,256]{1,0:T(8,128)(2,1)S(1)} collective-permute-done((bf16[1024,256]{1,0:T(8,128)(2,1)S(1)}, bf16[1024,256]{1,0:T(8,128)(2,1)S(1)}, u32[]{:S(2)}, u32[]{:S(2)}) %collective-permute-start.25) | collective-permute-done | bytes 524320 | tf_op jit(solution)/shard_map/ppermute | solution.py:30
  117.0 1.4 collective-permute-start.29
  118.4 4.3 %collective-permute-done.26.refs_8_ = bf16[1024,256]{1,0:T(8,128)(2,1)S(1)} collective-permute-done((bf16[1024,256]{1,0:T(8,128)(2,1)S(1)}, bf16[1024,256]{1,0:T(8,128)(2,1)S(1)}, u32[]{:S(2)}, u32[]{:S(2)}) %collective-permute-start.26) | collective-permute-done | bytes 524320 | tf_op jit(solution)/shard_map/ppermute | solution.py:30
  122.8 11.0 %collective-permute-done.22.refs_4_ = bf16[1024,256]{1,0:T(8,128)(2,1)} collective-permute-done((bf16[1024,256]{1,0:T(8,128)(2,1)}, bf16[1024,256]{1,0:T(8,128)(2,1)}, u32[]{:S(2)}, u32[]{:S(2)}) %collective-permute-start.22) | collective-permute-done | bytes 524320 | tf_op jit(solution)/shard_map/ppermute | solution.py:30
  133.8 1.6 collective-permute-start.23
  135.4 3.9 %collective-permute-done.29.refs_4_ = bf16[1024,256]{1,0:T(8,128)(2,1)S(1)} collective-permute-done((bf16[1024,256]{1,0:T(8,128)(2,1)S(1)}, bf16[1024,256]{1,0:T(8,128)(2,1)S(1)}, u32[]{:S(2)}, u32[]{:S(2)}) %collective-permute-start.29) | collective-permute-done | bytes 524320 | tf_op jit(solution)/shard_map/ppermute | solution.py:30
  139.3 1.6 collective-permute-start.30
  141.2 3.7 %collective-permute-start.32 = (bf16[1024,256]{1,0:T(8,128)(2,1)}, bf16[1024,256]{1,0:T(8,128)(2,1)}, u32[]{:S(2)}, u32[]{:S(2)}) collective-permute-start(bf16[1024,256]{1,0:T(8,128)(2,1)} %collective-permute-done.28.refs_10_), channel_id=1, source_target_pairs={{0,1},{1,2},{2,3},{3,4},{4,5},{5,6},{6,7},{7,0},{8,9},{9,10},{10,1... | collective-permute-start | bytes 1572872 | tf_op jit(solution)/shard_map/ppermute | solution.py:30
  157.4 22.0 %shard_map.87 = (f32[768,1024]{1,0:T(8,128)}, bf16[768,1792]{1,0:T(8,128)(2,1)}, bf16[768,1024]{1,0:T(8,128)(2,1)}) custom-call(s32[3]{0:T(128)S(1)} %pad_add_fusion.refs_0_, s32[6]{0:T(128)S(1)} %copy-done.13, s32[32]{0:T(128)S(1)} %copy-done.32, s32[6,32]{1,0:T(8,128)S(1)} %copy-done.31, bf16[1536,4096]{1,0:T(8,128)(2,1)} %all-gather.2.cloned.1.call-done.refs_4_, ...), custom_call_target="tpu_custom_call" | custom-call | flops 8455716864 | bytes 33554432 | tf_op jit(solution)/shard_map/pallas_call | solution.py:119
  179.4 1.9 copy-done
  181.3 1.8 copy-done.1
  183.1 7.5 %shard_map.88.refs_3_ = f32[768,1024]{1,0:T(8,128)S(1)} custom-call(s32[6]{0:T(128)S(1)} %copy-done.13, s32[8]{0:T(128)S(1)} %copy-done.14, bf16[768,1792]{1,0:T(8,128)(2,1)S(1)} %copy-done.1, f32[768,1024]{1,0:T(8,128)S(1)} %copy-done, bf16[1024,256]{1,0:T(8,128)(2,1)} %collective-permute-done.22.refs_4_, ...), custom_call_target="tpu_custom_call" | custom-call | flops 2818572288 | bytes 14811136 | tf_op jit(solution)/shard_map/pallas_call | solution.py:176
  190.7 7.4 %shard_map.89 = bf16[768,1024]{1,0:T(8,128)(2,1)} custom-call(s32[6]{0:T(128)S(1)} %copy-done.13, s32[8]{0:T(128)S(1)} %copy-done.14, bf16[768,1024]{1,0:T(8,128)(2,1)S(1)} %copy-done.2, f32[768,1024]{1,0:T(8,128)S(1)} %shard_map.88.refs_3_, bf16[1024,256]{1,0:T(8,128)(2,1)S(1)} %collective-permute-done.29.refs_4_, ...), custom_call_target="tpu_custom_call" | custom-call | flops 1610612736 | bytes 12058624 | tf_op jit(solution)/shard_map/pallas_call | solution.py:176
  (115 shorter events, 26.4 us)
Async XLA Ops:
  6.5 138.4 %all-gather.2.cloned.1.call-start = ((), (), s32[]{:S(2)}) async-start(), calls=%async_computation | async-start | bytes 14155776 | tf_op jit(solution)/shard_map/all_gather | solution.py:194
  9.2 10.3 %collective-permute-start = (bf16[1024,128]{1,0:T(8,128)(2,1)S(1)}, bf16[1024,128]{1,0:T(8,128)(2,1)S(1)}, u32[]{:S(2)}, u32[]{:S(2)}) collective-permute-start(bf16[1024,128]{1,0:T(8,128)(2,1)S(1)} %copy-done.12), channel_id=1, source_target_pairs={{0,1},{1,2},{2,3},{3,4},{4,5},{5,6},{6,7},{7,0},{8,9},{9,10},{10,1... | collective-permute-start | bytes 786440 | tf_op jit(solution)/shard_map/ppermute | solution.py:30
  11.2 8.3 %collective-permute-start.1 = (bf16[1024,128]{1,0:T(8,128)(2,1)S(1)}, bf16[1024,128]{1,0:T(8,128)(2,1)S(1)}, u32[]{:S(2)}, u32[]{:S(2)}) collective-permute-start(bf16[1024,128]{1,0:T(8,128)(2,1)S(1)} %copy-done.11), channel_id=1, source_target_pairs={{0,8},{1,9},{2,10},{3,11},{4,12},{5,13},{6,14},{7,15},{8,16},{9,17... | collective-permute-start | bytes 786440 | tf_op jit(solution)/shard_map/ppermute | solution.py:30
  19.5 7.6 %collective-permute-start.2 = (bf16[1024,128]{1,0:T(8,128)(2,1)S(1)}, bf16[1024,128]{1,0:T(8,128)(2,1)S(1)}, u32[]{:S(2)}, u32[]{:S(2)}) collective-permute-start(bf16[1024,128]{1,0:T(8,128)(2,1)S(1)} %collective-permute-done.refs_1_), channel_id=1, source_target_pairs={{0,1},{1,2},{2,3},{3,4},{4,5},{5,6},{6,7},{7,0},{8,9},{9,10},{10,1... | collective-permute-start | bytes 786440 | tf_op jit(solution)/shard_map/ppermute | solution.py:30
  19.5 7.6 %collective-permute-start.3 = (bf16[1024,128]{1,0:T(8,128)(2,1)S(1)}, bf16[1024,128]{1,0:T(8,128)(2,1)S(1)}, u32[]{:S(2)}, u32[]{:S(2)}) collective-permute-start(bf16[1024,128]{1,0:T(8,128)(2,1)S(1)} %collective-permute-done.1.refs_1_), channel_id=1, source_target_pairs={{0,8},{1,9},{2,10},{3,11},{4,12},{5,13},{6,14},{7,15},{8,16},{9,17... | collective-permute-start | bytes 786440 | tf_op jit(solution)/shard_map/ppermute | solution.py:30
  30.6 11.1 %collective-permute-start.9 = (bf16[1024,256]{1,0:T(8,128)(2,1)S(1)}, bf16[1024,256]{1,0:T(8,128)(2,1)S(1)}, u32[]{:S(2)}, u32[]{:S(2)}) collective-permute-start(bf16[1024,256]{1,0:T(8,128)(2,1)S(1)} %shard_map.84.refs_12_), channel_id=1, source_target_pairs={{0,1},{1,2},{2,3},{3,4},{4,5},{5,6},{6,7},{7,0},{8,9},{9,10},{10,1... | collective-permute-start | bytes 1572872 | tf_op jit(solution)/shard_map/ppermute | solution.py:30
  33.9 17.6 %collective-permute-start.7 = (bf16[1024,256]{1,0:T(8,128)(2,1)S(1)}, bf16[1024,256]{1,0:T(8,128)(2,1)S(1)}, u32[]{:S(2)}, u32[]{:S(2)}) collective-permute-start(bf16[1024,256]{1,0:T(8,128)(2,1)S(1)} %shard_map.83.refs_13_), channel_id=1, source_target_pairs={{0,1},{1,2},{2,3},{3,4},{4,5},{5,6},{6,7},{7,0},{8,9},{9,10},{10,1... | collective-permute-start | bytes 1572872 | tf_op jit(solution)/shard_map/ppermute | solution.py:30
  36.3 36.1 %collective-permute-start.5 = (bf16[1024,512]{1,0:T(8,128)(2,1)S(1)}, bf16[1024,512]{1,0:T(8,128)(2,1)S(1)}, u32[]{:S(2)}, u32[]{:S(2)}) collective-permute-start(bf16[1024,512]{1,0:T(8,128)(2,1)S(1)} %shard_map.82.refs_5_), channel_id=1, source_target_pairs={{0,8},{1,9},{2,10},{3,11},{4,12},{5,13},{6,14},{7,15},{8,16},{9,17... | collective-permute-start | bytes 3145736 | tf_op jit(solution)/shard_map/ppermute | solution.py:30
  38.5 11.7 %collective-permute-start.12 = (bf16[1024,128]{1,0:T(8,128)(2,1)S(1)}, bf16[1024,128]{1,0:T(8,128)(2,1)S(1)}, u32[]{:S(2)}, u32[]{:S(2)}) collective-permute-start(bf16[1024,128]{1,0:T(8,128)(2,1)S(1)} %collective-permute-done.4.refs_3_), channel_id=1, source_target_pairs={{0,1},{1,2},{2,3},{3,4},{4,5},{5,6},{6,7},{7,0},{8,9},{9,10},{10,1... | collective-permute-start | bytes 786440 | tf_op jit(solution)/shard_map/ppermute | solution.py:30
  50.2 18.8 %collective-permute-start.17 = (bf16[1024,256]{1,0:T(8,128)(2,1)S(1)}, bf16[1024,256]{1,0:T(8,128)(2,1)S(1)}, u32[]{:S(2)}, u32[]{:S(2)}) collective-permute-start(bf16[1024,256]{1,0:T(8,128)(2,1)S(1)} %collective-permute-done.9.refs_14_), channel_id=1, source_target_pairs={{0,1},{1,2},{2,3},{3,4},{4,5},{5,6},{6,7},{7,0},{8,9},{9,10},{10,1... | collective-permute-start | bytes 1572872 | tf_op jit(solution)/shard_map/ppermute | solution.py:30
  51.5 18.4 %collective-permute-start.10 = (bf16[1024,256]{1,0:T(8,128)(2,1)S(1)}, bf16[1024,256]{1,0:T(8,128)(2,1)S(1)}, u32[]{:S(2)}, u32[]{:S(2)}) collective-permute-start(bf16[1024,256]{1,0:T(8,128)(2,1)S(1)} %collective-permute-done.7.refs_15_), channel_id=1, source_target_pairs={{0,1},{1,2},{2,3},{3,4},{4,5},{5,6},{6,7},{7,0},{8,9},{9,10},{10,1... | collective-permute-start | bytes 1572872 | tf_op jit(solution)/shard_map/ppermute | solution.py:30
  54.0 15.0 %collective-permute-start.13 = (bf16[1024,128]{1,0:T(8,128)(2,1)S(1)}, bf16[1024,128]{1,0:T(8,128)(2,1)S(1)}, u32[]{:S(2)}, u32[]{:S(2)}) collective-permute-start(bf16[1024,128]{1,0:T(8,128)(2,1)S(1)} %collective-permute-done.12.refs_0_), channel_id=1, source_target_pairs={{0,1},{1,2},{2,3},{3,4},{4,5},{5,6},{6,7},{7,0},{8,9},{9,10},{10,1... | collective-permute-start | bytes 786440 | tf_op jit(solution)/shard_map/ppermute | solution.py:30
  69.0 18.8 %collective-permute-start.18 = (bf16[1024,256]{1,0:T(8,128)(2,1)S(1)}, bf16[1024,256]{1,0:T(8,128)(2,1)S(1)}, u32[]{:S(2)}, u32[]{:S(2)}) collective-permute-start(bf16[1024,256]{1,0:T(8,128)(2,1)S(1)} %collective-permute-done.17.refs_16_), channel_id=1, source_target_pairs={{0,1},{1,2},{2,3},{3,4},{4,5},{5,6},{6,7},{7,0},{8,9},{9,10},{10,1... | collective-permute-start | bytes 1572872 | tf_op jit(solution)/shard_map/ppermute | solution.py:30
  70.0 18.7 %collective-permute-start.19 = (bf16[1024,256]{1,0:T(8,128)(2,1)S(1)}, bf16[1024,256]{1,0:T(8,128)(2,1)S(1)}, u32[]{:S(2)}, u32[]{:S(2)}) collective-permute-start(bf16[1024,256]{1,0:T(8,128)(2,1)S(1)} %collective-permute-done.10.refs_17_), channel_id=1, source_target_pairs={{0,1},{1,2},{2,3},{3,4},{4,5},{5,6},{6,7},{7,0},{8,9},{9,10},{10,1... | collective-permute-start | bytes 1572872 | tf_op jit(solution)/shard_map/ppermute | solution.py:30
  72.5 37.2 %collective-permute-start.8 = (bf16[1024,512]{1,0:T(8,128)(2,1)S(1)}, bf16[1024,512]{1,0:T(8,128)(2,1)}, u32[]{:S(2)}, u32[]{:S(2)}) collective-permute-start(bf16[1024,512]{1,0:T(8,128)(2,1)S(1)} %collective-permute-done.5.refs_6_), channel_id=1, source_target_pairs={{0,8},{1,9},{2,10},{3,11},{4,12},{5,13},{6,14},{7,15},{8,16},{9,17... | collective-permute-start | bytes 3145736 | tf_op jit(solution)/shard_map/ppermute | solution.py:30
  72.5 15.4 %collective-permute-start.15 = (bf16[1024,128]{1,0:T(8,128)(2,1)S(1)}, bf16[1024,128]{1,0:T(8,128)(2,1)S(1)}, u32[]{:S(2)}, u32[]{:S(2)}) collective-permute-start(bf16[1024,128]{1,0:T(8,128)(2,1)S(1)} %collective-permute-done.13.refs_1_), channel_id=1, source_target_pairs={{0,1},{1,2},{2,3},{3,4},{4,5},{5,6},{6,7},{7,0},{8,9},{9,10},{10,1... | collective-permute-start | bytes 786440 | tf_op jit(solution)/shard_map/ppermute | solution.py:30
  87.8 18.8 %collective-permute-start.20 = (bf16[1024,256]{1,0:T(8,128)(2,1)S(1)}, bf16[1024,256]{1,0:T(8,128)(2,1)S(1)}, u32[]{:S(2)}, u32[]{:S(2)}) collective-permute-start(bf16[1024,256]{1,0:T(8,128)(2,1)S(1)} %collective-permute-done.18.refs_18_), channel_id=1, source_target_pairs={{0,1},{1,2},{2,3},{3,4},{4,5},{5,6},{6,7},{7,0},{8,9},{9,10},{10,1... | collective-permute-start | bytes 1572872 | tf_op jit(solution)/shard_map/ppermute | solution.py:30
  88.6 20.2 %collective-permute-start.21 = (bf16[1024,256]{1,0:T(8,128)(2,1)S(1)}, bf16[1024,256]{1,0:T(8,128)(2,1)S(1)}, u32[]{:S(2)}, u32[]{:S(2)}) collective-permute-start(bf16[1024,256]{1,0:T(8,128)(2,1)S(1)} %collective-permute-done.19.refs_19_), channel_id=1, source_target_pairs={{0,1},{1,2},{2,3},{3,4},{4,5},{5,6},{6,7},{7,0},{8,9},{9,10},{10,1... | collective-permute-start | bytes 1572872 | tf_op jit(solution)/shard_map/ppermute | solution.py:30
  90.8 15.8 %collective-permute-start.16 = (bf16[1024,128]{1,0:T(8,128)(2,1)S(1)}, bf16[1024,128]{1,0:T(8,128)(2,1)S(1)}, u32[]{:S(2)}, u32[]{:S(2)}) collective-permute-start(bf16[1024,128]{1,0:T(8,128)(2,1)S(1)} %collective-permute-done.15.refs_0_), channel_id=1, source_target_pairs={{0,1},{1,2},{2,3},{3,4},{4,5},{5,6},{6,7},{7,0},{8,9},{9,10},{10,1... | collective-permute-start | bytes 786440 | tf_op jit(solution)/shard_map/ppermute | solution.py:30
  92.9 18.3 %collective-permute-start.14 = (bf16[1024,256]{1,0:T(8,128)(2,1)S(1)}, bf16[1024,256]{1,0:T(8,128)(2,1)}, u32[]{:S(2)}, u32[]{:S(2)}) collective-permute-start(bf16[1024,256]{1,0:T(8,128)(2,1)S(1)} %shard_map.85.refs_9_), channel_id=1, source_target_pairs={{0,8},{1,9},{2,10},{3,11},{4,12},{5,13},{6,14},{7,15},{8,16},{9,17... | collective-permute-start | bytes 1572872 | tf_op jit(solution)/shard_map/ppermute | solution.py:30
  106.6 10.4 %collective-permute-start.25 = (bf16[1024,256]{1,0:T(8,128)(2,1)S(1)}, bf16[1024,256]{1,0:T(8,128)(2,1)S(1)}, u32[]{:S(2)}, u32[]{:S(2)}) collective-permute-start(bf16[1024,256]{1,0:T(8,128)(2,1)S(1)} %collective-permute-done.20.refs_20_), channel_id=1, source_target_pairs={{0,1},{1,2},{2,3},{3,4},{4,5},{5,6},{6,7},{7,0},{8,9},{9,10},{10,1... | collective-permute-start | bytes 1572872 | tf_op jit(solution)/shard_map/ppermute | solution.py:30
  107.6 9.5 %collective-permute-start.24 = (bf16[1024,256]{1,0:T(8,128)(2,1)S(1)}, bf16[1024,256]{1,0:T(8,128)(2,1)S(1)}, u32[]{:S(2)}, u32[]{:S(2)}) collective-permute-start(bf16[1024,256]{1,0:T(8,128)(2,1)S(1)} %shard_map.86.refs_11_), channel_id=1, source_target_pairs={{0,8},{1,9},{2,10},{3,11},{4,12},{5,13},{6,14},{7,15},{8,16},{9,17... | collective-permute-start | bytes 1572872 | tf_op jit(solution)/shard_map/ppermute | solution.py:30
  108.8 13.8 %collective-permute-start.26 = (bf16[1024,256]{1,0:T(8,128)(2,1)S(1)}, bf16[1024,256]{1,0:T(8,128)(2,1)S(1)}, u32[]{:S(2)}, u32[]{:S(2)}) collective-permute-start(bf16[1024,256]{1,0:T(8,128)(2,1)S(1)} %collective-permute-done.21.refs_21_), channel_id=1, source_target_pairs={{0,1},{1,2},{2,3},{3,4},{4,5},{5,6},{6,7},{7,0},{8,9},{9,10},{10,1... | collective-permute-start | bytes 1572872 | tf_op jit(solution)/shard_map/ppermute | solution.py:30
  109.6 35.3 %collective-permute-start.11 = (bf16[1024,512]{1,0:T(8,128)(2,1)}, bf16[1024,512]{1,0:T(8,128)(2,1)}, u32[]{:S(2)}, u32[]{:S(2)}) collective-permute-start(bf16[1024,512]{1,0:T(8,128)(2,1)} %collective-permute-done.8.refs_7_), channel_id=1, source_target_pairs={{0,8},{1,9},{2,10},{3,11},{4,12},{5,13},{6,14},{7,15},{8,16},{9,17... | collective-permute-start | bytes 3145736 | tf_op jit(solution)/shard_map/ppermute | solution.py:30
  111.2 22.6 %collective-permute-start.22 = (bf16[1024,256]{1,0:T(8,128)(2,1)}, bf16[1024,256]{1,0:T(8,128)(2,1)}, u32[]{:S(2)}, u32[]{:S(2)}) collective-permute-start(bf16[1024,256]{1,0:T(8,128)(2,1)} %collective-permute-done.14.refs_10_), channel_id=1, source_target_pairs={{0,8},{1,9},{2,10},{3,11},{4,12},{5,13},{6,14},{7,15},{8,16},{9,17... | collective-permute-start | bytes 1572872 | tf_op jit(solution)/shard_map/ppermute | solution.py:30
  117.0 18.3 %collective-permute-start.27 = (bf16[1024,256]{1,0:T(8,128)(2,1)S(1)}, bf16[1024,256]{1,0:T(8,128)(2,1)}, u32[]{:S(2)}, u32[]{:S(2)}) collective-permute-start(bf16[1024,256]{1,0:T(8,128)(2,1)S(1)} %collective-permute-done.25.refs_7_), channel_id=1, source_target_pairs={{0,1},{1,2},{2,3},{3,4},{4,5},{5,6},{6,7},{7,0},{8,9},{9,10},{10,1... | collective-permute-start | bytes 1572872 | tf_op jit(solution)/shard_map/ppermute | solution.py:30
  117.0 22.2 %collective-permute-start.29 = (bf16[1024,256]{1,0:T(8,128)(2,1)S(1)}, bf16[1024,256]{1,0:T(8,128)(2,1)S(1)}, u32[]{:S(2)}, u32[]{:S(2)}) collective-permute-start(bf16[1024,256]{1,0:T(8,128)(2,1)S(1)} %collective-permute-done.24.refs_6_), channel_id=1, source_target_pairs={{0,8},{1,9},{2,10},{3,11},{4,12},{5,13},{6,14},{7,15},{8,16},{9,17... | collective-permute-start | bytes 1572872 | tf_op jit(solution)/shard_map/ppermute | solution.py:30
  122.7 18.5 %collective-permute-start.28 = (bf16[1024,256]{1,0:T(8,128)(2,1)S(1)}, bf16[1024,256]{1,0:T(8,128)(2,1)}, u32[]{:S(2)}, u32[]{:S(2)}) collective-permute-start(bf16[1024,256]{1,0:T(8,128)(2,1)S(1)} %collective-permute-done.26.refs_8_), channel_id=1, source_target_pairs={{0,1},{1,2},{2,3},{3,4},{4,5},{5,6},{6,7},{7,0},{8,9},{9,10},{10,1... | collective-permute-start | bytes 1572872 | tf_op jit(solution)/shard_map/ppermute | solution.py:30
  133.8 45.6 %collective-permute-start.23 = (bf16[1024,256]{1,0:T(8,128)(2,1)}, bf16[1024,256]{1,0:T(8,128)(2,1)}, u32[]{:S(2)}, u32[]{:S(2)}) collective-permute-start(bf16[1024,256]{1,0:T(8,128)(2,1)} %collective-permute-done.22.refs_4_), channel_id=1, source_target_pairs={{0,8},{1,9},{2,10},{3,11},{4,12},{5,13},{6,14},{7,15},{8,16},{9,17... | collective-permute-start | bytes 1572872 | tf_op jit(solution)/shard_map/ppermute | solution.py:30
  139.3 51.3 %collective-permute-start.30 = (bf16[1024,256]{1,0:T(8,128)(2,1)S(1)}, bf16[1024,256]{1,0:T(8,128)(2,1)}, u32[]{:S(2)}, u32[]{:S(2)}) collective-permute-start(bf16[1024,256]{1,0:T(8,128)(2,1)S(1)} %collective-permute-done.29.refs_4_), channel_id=1, source_target_pairs={{0,8},{1,9},{2,10},{3,11},{4,12},{5,13},{6,14},{7,15},{8,16},{9,17... | collective-permute-start | bytes 1572872 | tf_op jit(solution)/shard_map/ppermute | solution.py:30
  140.9 49.8 %collective-permute-start.31 = (bf16[1024,256]{1,0:T(8,128)(2,1)}, bf16[1024,256]{1,0:T(8,128)(2,1)}, u32[]{:S(2)}, u32[]{:S(2)}) collective-permute-start(bf16[1024,256]{1,0:T(8,128)(2,1)} %collective-permute-done.27.refs_9_), channel_id=1, source_target_pairs={{0,1},{1,2},{2,3},{3,4},{4,5},{5,6},{6,7},{7,0},{8,9},{9,10},{10,1... | collective-permute-start | bytes 1572872 | tf_op jit(solution)/shard_map/ppermute | solution.py:30
  141.2 49.4 %collective-permute-start.32 = (bf16[1024,256]{1,0:T(8,128)(2,1)}, bf16[1024,256]{1,0:T(8,128)(2,1)}, u32[]{:S(2)}, u32[]{:S(2)}) collective-permute-start(bf16[1024,256]{1,0:T(8,128)(2,1)} %collective-permute-done.28.refs_10_), channel_id=1, source_target_pairs={{0,1},{1,2},{2,3},{3,4},{4,5},{5,6},{6,7},{7,0},{8,9},{9,10},{10,1... | collective-permute-start | bytes 1572872 | tf_op jit(solution)/shard_map/ppermute | solution.py:30
  (36 other events, 868.8 us)
Sparse Core Ops, SparseCore 0:
  9.4 72.5 all-gather.1

commit v3 on v2

v3 whole, which is shorter than its diff:
```python
import jax
import jax.numpy as jnp
from jax import lax
from jax.experimental import pallas as pl
from jax.experimental.pallas import tpu as pltpu
from jax.sharding import PartitionSpec as P

BLK = 128
AXES = ("grp", "mem")
NX, NY, NZ = 4, 4, 8
BF16 = jnp.bfloat16
F32 = jnp.float32


def perm_of(dx, dy, dz, swap=0):
    pairs = []
    for x in range(NX):
        for core in range(2):
            sign = 1 if core == 0 else -1
            for y in range(NY):
                for z in range(NZ):
                    src = (2 * x + core) * 32 + 8 * y + z
                    x2, y2, z2 = (x + sign * dx) % NX, (y + sign * dy) % NY, (z + sign * dz) % NZ
                    core2 = core ^ swap
                    pairs.append((src, (2 * x2 + core2) * 32 + 8 * y2 + z2))
    return pairs


def move(values, dx=0, dy=0, dz=0, swap=0):
    return lax.ppermute(values, AXES, perm_of(dx, dy, dz, swap))


def after(value, *others):
    return lax.optimization_barrier((value,) + others)[0]


SMEM = pl.BlockSpec(memory_space=pltpu.SMEM)
VMEM = pl.BlockSpec(memory_space=pltpu.VMEM)
HBM = pl.BlockSpec(memory_space=pltpu.HBM)


def params(mib):
    return pltpu.CompilerParams(vmem_limit_bytes=mib * 2**20)


def cost(flops, moved):
    return pl.CostEstimate(flops=flops, bytes_accessed=moved, transcendentals=0)


def join_kernel(*refs):
    blocks, out = refs[:-1], refs[-1]
    width = blocks[0].shape[1]
    for b, block in enumerate(blocks):
        out[:, b * width:(b + 1) * width] = block[...]


def join(blocks):
    rows, width = blocks[0].shape
    full = width * len(blocks)
    return pl.pallas_call(
        join_kernel,
        out_shape=jax.ShapeDtypeStruct((rows, full), BF16),
        in_specs=[VMEM] * len(blocks),
        out_specs=VMEM,
        compiler_params=params(8),
        cost_estimate=cost(0, 4 * rows * full),
    )(*blocks)


def dot(left, right):
    return lax.dot_general(left, right, (((1,), (1,)), ((), ())), preferred_element_type=F32)


def tiles_of(terms):
    return [tile for tiles, _ in terms for tile in tiles]


def mask_kernel(parts, here_ref, ij_ref, cd_ref, mask_ref, raw_hbm, *refs):
    outs, raw, laid, sem = refs[:len(parts)], refs[-2 - len(parts)], refs[-1 - len(parts):-1], refs[-1]
    fetch = pltpu.make_async_copy(raw_hbm, raw, sem.at[len(parts)])
    fetch.start()
    sign, y, z = [here_ref[k] for k in range(3)]
    fetch.wait()
    copies = []
    for p, (target, tiles) in enumerate(zip(laid, parts)):
        for k, (panel, step_y, step_z) in enumerate(tiles):
            tile = 8 * ((y - sign * step_y) & (NY - 1)) + ((z - sign * step_z) & (NZ - 1))
            cols = pl.ds(pl.multiple_of(tile * BLK, BLK), BLK)
            label = cd_ref[tile]
            for row in range(6):
                on = (ij_ref[row] == label) & (mask_ref[row, tile] == 1)
                kept = raw[pl.ds(panel * 768 + row * BLK, BLK), cols]
                target[row * BLK:(row + 1) * BLK, k * BLK:(k + 1) * BLK] = jnp.where(on, kept, jnp.zeros_like(kept))
        copies.append(pltpu.make_async_copy(target, outs[p], sem.at[p]))
        copies[-1].start()
    for copy in copies:
        copy.wait()


def mask(here, sym_ij, sym_cd, amp_mask, raw, groups):
    parts = [tiles_of(terms) for terms in groups]
    shapes = [(768, len(tiles) * BLK) for tiles in parts]

    def kernel(*refs):
        mask_kernel(parts, *refs)

    return pl.pallas_call(
        kernel,
        out_shape=[jax.ShapeDtypeStruct(shape, BF16) for shape in shapes],
        in_specs=[SMEM] * 4 + [HBM],
        out_specs=[HBM] * len(shapes),
        scratch_shapes=[pltpu.VMEM((1536, 4096), BF16)]
        + [pltpu.VMEM(shape, BF16) for shape in shapes]
        + [pltpu.SemaphoreType.DMA((len(shapes) + 1,))],
        compiler_params=params(60),
        cost_estimate=cost(0, 25 * 2**20),
    )(here, sym_ij, sym_cd, amp_mask, raw)


def product_kernel(n, first, last, ij_ref, ab_ref, amps_hbm, *refs):
    ints, refs = refs[:n], refs[n:]
    if first:
        out, amps, rows_v, sem = refs
    else:
        total_hbm, out, amps, rows_v, sem, total = refs

    def fetch(c):
        rows = pl.ds(pl.multiple_of(c * 256, 256), 256)
        copies, at = [], 0
        for k, block in enumerate(ints):
            width = block.shape[1]
            copies.append(pltpu.make_async_copy(block.at[rows, :], rows_v.at[rows, pl.ds(at, width)], sem.at[c, k]))
            at += width
        if not first:
            copies.append(pltpu.make_async_copy(total_hbm.at[:, rows], total.at[:, rows], sem.at[c, n]))
        return copies

    whole = pltpu.make_async_copy(amps_hbm, amps, sem.at[4, 0])
    whole.start()
    for c in range(4):
        for copy in fetch(c):
            copy.start()
    whole.wait()

    def strip(c, carry):
        for copy in fetch(c):
            copy.wait()
        cols = pl.ds(pl.multiple_of(c * 256, 256), 256)

        def part(m, carry):
            rows = pl.ds(pl.multiple_of(m * 256, 256), 256)
            value = dot(amps[rows, :], rows_v[cols, :])
            if not first:
                value = value + total[rows, cols]
            if not last:
                out[rows, cols] = value
                return carry
            for i in range(2):
                for j in range(2):
                    tile = value[i * BLK:(i + 1) * BLK, j * BLK:(j + 1) * BLK] * 0.5
                    on = ij_ref[2 * m + i] == ab_ref[2 * c + j]
                    where = (
                        pl.ds(pl.multiple_of(m * 256 + i * BLK, BLK), BLK),
                        pl.ds(pl.multiple_of(c * 256 + j * BLK, BLK), BLK),
                    )
                    out[where] = jnp.where(on, tile, jnp.zeros_like(tile)).astype(BF16)
            return carry

        return lax.fori_loop(0, 3, part, carry)

    lax.fori_loop(0, 4, strip, 0)


def product(sym_ij, sym_ab, amps, terms, total=None, last=False):
    depth = amps.shape[1]
    first = total is None
    n = len(terms)

    def kernel(*refs):
        product_kernel(n, first, last, *refs)

    scratch = [
        pltpu.VMEM((768, depth), BF16), pltpu.VMEM((1024, depth), BF16), pltpu.SemaphoreType.DMA((5, n + 1))
    ]
    return pl.pallas_call(
        kernel,
        out_shape=jax.ShapeDtypeStruct((768, 1024), BF16 if last else F32),
        in_specs=[SMEM] * 2 + [HBM] * (1 + n + (not first)),
        out_specs=VMEM,
        scratch_shapes=scratch + ([] if first else [pltpu.VMEM((768, 1024), F32)]),
        compiler_params=params(60),
        cost_estimate=cost(2 * 768 * 1024 * depth, 8 * 2**20 + 3584 * depth),
    )(sym_ij, sym_ab, amps, *[block for _, block in terms], *([] if first else [total]))


def body(amp_plus, amp_minus, ints_plus, ints_minus, sym_ij, sym_ab, sym_cd, amp_mask):
    grp, mem = lax.axis_index("grp"), lax.axis_index("mem")
    here = jnp.stack([1 - 2 * (grp % 2), mem // 8, mem % 8]).astype(jnp.int32)

    def go(value, *waits, **way):
        return move(after(value, *waits) if waits else value, **way)

    raw = lax.all_gather(jnp.concatenate([amp_plus, amp_minus], axis=0), "grp", axis=1, tiled=True)

    z0, y0 = ints_plus, ints_minus
    z1, y1 = go(z0, dz=1), go(y0, dy=1)
    z2, y2 = go(z1, y1, dz=1), go(y1, z1, dy=1)
    z3, y3 = go(z2, y2, dz=1), go(y2, z2, dy=1)
    a, b, c = [join((y0, y1))], [join((y2, y3))], [join((z0, z1, z2, z3))]
    z4 = go(z3, y3, a[0], b[0], c[0], dz=1)
    a.append(go(a[0], dz=1))
    b.append(go(b[0], dz=1))
    c.append(go(c[0], dy=1))
    z5 = go(z4, a[1], dz=1)
    a.append(go(a[1], z4, dz=1))
    b.append(go(b[1], a[1], dz=1))
    d = [join((z4, z5))]
    c.append(go(c[1], b[1], dy=1))
    z6 = go(z5, a[2], dz=1)
    a.append(go(a[2], z5, dz=1))
    d.append(go(d[0], b[1], dy=1))
    b.append(go(b[2], a[2], dz=1))
    z7 = go(z6, a[3], dz=1)
    c.append(go(c[2], b[2], dy=1))
    a.append(go(a[3], z6, dz=1))
    d.append(go(d[1], b[2], dy=1))
    b.append(go(b[3], a[3], dz=1))
    e = [join((z6, z7))]
    d.append(go(d[2], b[3], dy=1))
    e.append(go(e[0], a[4], dy=1))

    def plus(blocks, i, first):
        count = blocks[i].shape[1] // BLK
        return [(0, i, first + k) for k in range(count)], blocks[i]

    def minus(blocks, t, first):
        return [(1, first + k, t) for k in range(2)], blocks[t]

    a.append(go(a[4], z7, dz=1))
    b.append(go(b[4], a[4], dz=1))
    now = [plus(c, i, 0) for i in range(4)] + [plus(d, i, 4) for i in range(4)] + [plus(e, 0, 6)]
    now += [term for t in range(5) for term in (minus(a, t, 0), minus(b, t, 2))]
    groups = [
        now,
        [([(0, i, 6), (0, i, 7)], None) for i in (1, 2)]
        + [([(1, first, t), (1, first + 1, t)], None) for t in (5, 6) for first in (0, 2)],
        [([(0, 3, 6), (0, 3, 7)], None)] + [([(1, first, 7), (1, first + 1, 7)], None) for first in (0, 2)],
    ]
    amps = mask(here, sym_ij, sym_cd, amp_mask, raw, groups)
    a.append(go(a[5], b[4], amps[0], dz=1))
    e.append(go(e[1], a[5], dy=1))
    b.append(go(b[5], a[5], dz=1))
    total = product(sym_ij, sym_ab, amps[0], now)
    a.append(go(a[6], b[5], total, dz=1))
    e.append(go(e[2], a[6], dy=1))
    b.append(go(b[6], a[6], dz=1))
    soon = [plus(e, 1, 6), plus(e, 2, 6)]
    soon += [term for t in (5, 6) for term in (minus(a, t, 0), minus(b, t, 2))]
    rest = [plus(e, 3, 6), minus(a, 7, 0), minus(b, 7, 2)]
    total = product(sym_ij, sym_ab, amps[1], soon, total)
    return product(sym_ij, sym_ab, amps[2], rest, total, True)


def solution(mesh):
    placed = (
        P("mem", "grp"),
        P("mem", "grp"),
        P("grp", "mem"),
        P("grp", "mem"),
        P("mem"),
        P("grp"),
        P(),
        P("mem", None),
    )
    return jax.shard_map(
        body, mesh=mesh, in_specs=placed, out_specs=P("mem", "grp"), check_vma=False
    )
```

time: 206 us -> 208 us (level)
  local copies, waits for them, and re-layouts: 21 us -> 1.19 us
  Pallas kernels: 37.4 us -> 49.3 us
  waiting for transfers between devices: 89.5 us -> 98.9 us
    unnamed x68 -> x38, local copies, waits for them, and re-layouts: 21 us -> 1.19 us
    pallas_call x3 -> x4, Pallas kernels: 36.9 us -> 48.8 us  [the longest x3 36.4 us: product(): pl.pallas_call(kernel, out_shape=jax.ShapeDtypeStruct((768, 1024), BF16 i...]
    ppermute x33, waiting for transfers between devices: 89.5 us -> 98.9 us  [move(): return lax.ppermute(values, AXES, perm_of(dx, dy, dz, swap))]
  transfers between devices with their start and end apart: 34 -> 34, of which waited for: 12 -> 11; matrix products, arithmetic and copies ran while one was open for 0% -> 0% of each run, Pallas kernels for 15% -> 20%
where the time goes in v3:
time: 208 us; the launch traced here: 206 us
  waiting for transfers between devices  98.9 us (48%)
  Pallas kernels  49.3 us (24%)
  starting transfers between devices  39.2 us (19%)
  between operations  13.8 us (7%)
  other arithmetic  3.31 us (2%)
    ppermute x33, waiting for transfers between devices, move(): return lax.ppermute(values, AXES, perm_of(dx, dy, dz, swap))  98.9 us
    ppermute x33, starting transfers between devices, move(): return lax.ppermute(values, AXES, perm_of(dx, dy, dz, swap))  39.2 us
    pallas_call x3, Pallas kernels, product(): pl.pallas_call(kernel, out_shape=jax.ShapeDtypeStruct((768, 1024), BF16 i...  36.4 us
    pallas_call x1, Pallas kernels, mask(): pl.pallas_call(kernel, out_shape=[jax.ShapeDtypeStruct(shape, BF16) for s...  12.4 us
  transfers between devices with their start and end apart: 34, of which 11 were waited for; matrix products, arithmetic and copies ran while one was open for 0% of the time, Pallas kernels for 20%

profile of v3, /device:TPU:24, one launch (start us, length us, event | category | flops | bytes accessed | tf_op | source)
XLA Modules:
  0.0 205.8 jit_solution(4654686164590306949)
XLA Ops:
  6.5 2.7 %pad_maximum_fusion = bf16[1536,512]{1,0:T(8,128)(2,1)} fusion(bf16[768,512]{1,0:T(8,128)(2,1)} %param.9, bf16[768,512]{1,0:T(8,128)(2,1)} %param.8), kind=kLoop, calls=%fused_computation | loop fusion | flops 3145728 | bytes 3145728 | tf_op jit(solution)/shard_map/concatenate | solution.py:203
  9.2 2.0 collective-permute-start
  11.5 8.1 %collective-permute-done.refs_1_ = bf16[1024,128]{1,0:T(8,128)(2,1)S(1)} collective-permute-done((bf16[1024,128]{1,0:T(8,128)(2,1)S(1)}, bf16[1024,128]{1,0:T(8,128)(2,1)S(1)}, u32[]{:S(2)}, u32[]{:S(2)}) %collective-permute-start) | collective-permute-done | bytes 262176 | tf_op jit(solution)/shard_map/ppermute | solution.py:30
  19.5 1.4 collective-permute-start.3
  21.0 6.2 %collective-permute-done.2.refs_2_ = bf16[1024,128]{1,0:T(8,128)(2,1)S(1)} collective-permute-done((bf16[1024,128]{1,0:T(8,128)(2,1)S(1)}, bf16[1024,128]{1,0:T(8,128)(2,1)S(1)}, u32[]{:S(2)}, u32[]{:S(2)}) %collective-permute-start.2) | collective-permute-done | bytes 262176 | tf_op jit(solution)/shard_map/ppermute | solution.py:30
  27.8 6.9 %collective-permute-done.4.refs_3_ = bf16[1024,128]{1,0:T(8,128)(2,1)S(1)} collective-permute-done((bf16[1024,128]{1,0:T(8,128)(2,1)S(1)}, bf16[1024,128]{1,0:T(8,128)(2,1)S(1)}, u32[]{:S(2)}, u32[]{:S(2)}) %collective-permute-start.4) | collective-permute-done | bytes 262176 | tf_op jit(solution)/shard_map/ppermute | solution.py:30
  34.9 1.5 collective-permute-start.24
  36.9 1.2 collective-permute-start.7
  38.0 14.6 %collective-permute-done.5.refs_1_ = bf16[1024,128]{1,0:T(8,128)(2,1)S(1)} collective-permute-done((bf16[1024,128]{1,0:T(8,128)(2,1)S(1)}, bf16[1024,128]{1,0:T(8,128)(2,1)S(1)}, u32[]{:S(2)}, u32[]{:S(2)}) %collective-permute-start.5) | collective-permute-done | bytes 262176 | tf_op jit(solution)/shard_map/ppermute | solution.py:30
  53.1 2.5 %collective-permute-start.6 = (bf16[1024,128]{1,0:T(8,128)(2,1)S(1)}, bf16[1024,128]{1,0:T(8,128)(2,1)S(1)}, u32[]{:S(2)}, u32[]{:S(2)}) collective-permute-start(bf16[1024,128]{1,0:T(8,128)(2,1)S(1)} %collective-permute-done.4.refs_3_), channel_id=1, source_target_pairs={{0,1},{1,2},{2,3},{3,4},{4,5},{5,6},{6,7},{7,0},{8,9},{9,10},{10,1... | collective-permute-start | bytes 786440 | tf_op jit(solution)/shard_map/ppermute | solution.py:30
  55.6 10.4 %collective-permute-done.6.refs_0_ = bf16[1024,128]{1,0:T(8,128)(2,1)S(1)} collective-permute-done((bf16[1024,128]{1,0:T(8,128)(2,1)S(1)}, bf16[1024,128]{1,0:T(8,128)(2,1)S(1)}, u32[]{:S(2)}, u32[]{:S(2)}) %collective-permute-start.6) | collective-permute-done | bytes 262176 | tf_op jit(solution)/shard_map/ppermute | solution.py:30
  66.0 1.6 collective-permute-start.18
  67.6 3.7 %collective-permute-start.25 = (bf16[1024,512]{1,0:T(8,128)(2,1)S(1)}, bf16[1024,512]{1,0:T(8,128)(2,1)}, u32[]{:S(2)}, u32[]{:S(2)}) collective-permute-start(bf16[1024,512]{1,0:T(8,128)(2,1)S(1)} %collective-permute-done.24.refs_4_), channel_id=1, source_target_pairs={{0,8},{1,9},{2,10},{3,11},{4,12},{5,13},{6,14},{7,15},{8,16},{9,17... | collective-permute-start | bytes 3145736 | tf_op jit(solution)/shard_map/ppermute | solution.py:30
  71.2 1.0 collective-permute-start.8
  72.3 12.5 %collective-permute-done.8.refs_1_ = bf16[1024,128]{1,0:T(8,128)(2,1)S(1)} collective-permute-done((bf16[1024,128]{1,0:T(8,128)(2,1)S(1)}, bf16[1024,128]{1,0:T(8,128)(2,1)S(1)}, u32[]{:S(2)}, u32[]{:S(2)}) %collective-permute-start.8) | collective-permute-done | bytes 262176 | tf_op jit(solution)/shard_map/ppermute | solution.py:30
  85.5 3.8 %collective-permute-start.27 = (bf16[1024,256]{1,0:T(8,128)(2,1)S(1)}, bf16[1024,256]{1,0:T(8,128)(2,1)S(1)}, u32[]{:S(2)}, u32[]{:S(2)}) collective-permute-start(bf16[1024,256]{1,0:T(8,128)(2,1)S(1)} %shard_map.87.refs_7_), channel_id=1, source_target_pairs={{0,8},{1,9},{2,10},{3,11},{4,12},{5,13},{6,14},{7,15},{8,16},{9,17... | collective-permute-start | bytes 1572872 | tf_op jit(solution)/shard_map/ppermute | solution.py:30
  89.3 2.0 collective-permute-start.10
  91.3 12.3 %collective-permute-done.10.refs_0_ = bf16[1024,128]{1,0:T(8,128)(2,1)S(1)} collective-permute-done((bf16[1024,128]{1,0:T(8,128)(2,1)S(1)}, bf16[1024,128]{1,0:T(8,128)(2,1)S(1)}, u32[]{:S(2)}, u32[]{:S(2)}) %collective-permute-start.10) | collective-permute-done | bytes 262176 | tf_op jit(solution)/shard_map/ppermute | solution.py:30
  103.8 2.7 %collective-permute-start.28 = (bf16[1024,256]{1,0:T(8,128)(2,1)S(1)}, bf16[1024,256]{1,0:T(8,128)(2,1)}, u32[]{:S(2)}, u32[]{:S(2)}) collective-permute-start(bf16[1024,256]{1,0:T(8,128)(2,1)S(1)} %collective-permute-done.27.refs_8_), channel_id=1, source_target_pairs={{0,8},{1,9},{2,10},{3,11},{4,12},{5,13},{6,14},{7,15},{8,16},{9,17... | collective-permute-start | bytes 1572872 | tf_op jit(solution)/shard_map/ppermute | solution.py:30
  106.6 3.2 %collective-permute-start.12 = (bf16[1024,128]{1,0:T(8,128)(2,1)S(1)}, bf16[1024,128]{1,0:T(8,128)(2,1)S(1)}, u32[]{:S(2)}, u32[]{:S(2)}) collective-permute-start(bf16[1024,128]{1,0:T(8,128)(2,1)S(1)} %collective-permute-done.10.refs_0_), channel_id=1, source_target_pairs={{0,1},{1,2},{2,3},{3,4},{4,5},{5,6},{6,7},{7,0},{8,9},{9,10},{10,1... | collective-permute-start | bytes 786440 | tf_op jit(solution)/shard_map/ppermute | solution.py:30
  109.8 12.7 %collective-permute-done.12.refs_1_ = bf16[1024,128]{1,0:T(8,128)(2,1)S(1)} collective-permute-done((bf16[1024,128]{1,0:T(8,128)(2,1)S(1)}, bf16[1024,128]{1,0:T(8,128)(2,1)S(1)}, u32[]{:S(2)}, u32[]{:S(2)}) %collective-permute-start.12) | collective-permute-done | bytes 262176 | tf_op jit(solution)/shard_map/ppermute | solution.py:30
  122.6 2.7 %collective-permute-start.14 = (bf16[1024,256]{1,0:T(8,128)(2,1)S(1)}, bf16[1024,256]{1,0:T(8,128)(2,1)}, u32[]{:S(2)}, u32[]{:S(2)}) collective-permute-start(bf16[1024,256]{1,0:T(8,128)(2,1)S(1)} %shard_map.86.refs_11_), channel_id=1, source_target_pairs={{0,8},{1,9},{2,10},{3,11},{4,12},{5,13},{6,14},{7,15},{8,16},{9,17... | collective-permute-start | bytes 1572872 | tf_op jit(solution)/shard_map/ppermute | solution.py:30
  126.3 5.7 %collective-permute-done.14.refs_3_ = bf16[1024,256]{1,0:T(8,128)(2,1)} collective-permute-done((bf16[1024,256]{1,0:T(8,128)(2,1)S(1)}, bf16[1024,256]{1,0:T(8,128)(2,1)}, u32[]{:S(2)}, u32[]{:S(2)}) %collective-permute-start.14) | collective-permute-done | bytes 524320 | tf_op jit(solution)/shard_map/ppermute | solution.py:30
  132.0 4.0 %collective-permute-done.15.refs_5_ = bf16[1024,256]{1,0:T(8,128)(2,1)} collective-permute-done((bf16[1024,256]{1,0:T(8,128)(2,1)}, bf16[1024,256]{1,0:T(8,128)(2,1)}, u32[]{:S(2)}, u32[]{:S(2)}) %collective-permute-start.15) | collective-permute-done | bytes 524320 | tf_op jit(solution)/shard_map/ppermute | solution.py:30
  136.1 5.5 %collective-permute-done.23.refs_6_ = bf16[1024,256]{1,0:T(8,128)(2,1)} collective-permute-done((bf16[1024,256]{1,0:T(8,128)(2,1)}, bf16[1024,256]{1,0:T(8,128)(2,1)}, u32[]{:S(2)}, u32[]{:S(2)}) %collective-permute-start.23) | collective-permute-done | bytes 524320 | tf_op jit(solution)/shard_map/ppermute | solution.py:30
  141.6 12.4 %shard_map.82 = (bf16[768,5888]{1,0:T(8,128)(2,1)}, bf16[768,1536]{1,0:T(8,128)(2,1)}, bf16[768,768]{1,0:T(8,128)(2,1)}) custom-call(s32[3]{0:T(128)} %pad_add_fusion.refs_0_, s32[6]{0:T(128)} %refs_0_.9, s32[32]{0:T(128)} %refs_2_.1, s32[6,32]{1,0:T(8,128)} %refs_3_.1, bf16[1536,4096]{1,0:T(8,128)(2,1)} %all-gather.2.cloned.1.call-done.refs_4_), custom_call_target="tpu_custom_call" | custom-call | bytes 26214400 | tf_op jit(solution)/shard_map/pallas_call | solution.py:107
  154.2 19.3 %shard_map.88.refs_9_ = f32[768,1024]{1,0:T(8,128)} custom-call(s32[6]{0:T(128)} %refs_0_.9, s32[8]{0:T(128)} %refs_1_.7, bf16[768,5888]{1,0:T(8,128)(2,1)} %get-tuple-element.54.refs_2_, bf16[1024,512]{1,0:T(8,128)(2,1)} %copy-done, bf16[1024,512]{1,0:T(8,128)(2,1)} %copy-done.11, bf16[1024,512]{1,0:T(8,128)(2,1)} %collective-permute-done.25.refs_5_, ...), custom_call_target="tpu_custom_call" | custom-call | flops 9261023232 | bytes 29491200 | tf_op jit(solution)/shard_map/pallas_call | solution.py:185
  173.7 3.3 %collective-permute-start.30 = (bf16[1024,256]{1,0:T(8,128)(2,1)S(1)}, bf16[1024,256]{1,0:T(8,128)(2,1)S(1)}, u32[]{:S(2)}, u32[]{:S(2)}) collective-permute-start(bf16[1024,256]{1,0:T(8,128)(2,1)S(1)} %collective-permute-done.21.refs_7_), channel_id=1, source_target_pairs={{0,1},{1,2},{2,3},{3,4},{4,5},{5,6},{6,7},{7,0},{8,9},{9,10},{10,1... | collective-permute-start | bytes 1572872 | tf_op jit(solution)/shard_map/ppermute | solution.py:30
  177.1 3.6 %collective-permute-start.32 = (bf16[1024,256]{1,0:T(8,128)(2,1)}, bf16[1024,256]{1,0:T(8,128)(2,1)S(1)}, u32[]{:S(2)}, u32[]{:S(2)}) collective-permute-start(bf16[1024,256]{1,0:T(8,128)(2,1)} %collective-permute-done.31.refs_8_), channel_id=1, source_target_pairs={{0,1},{1,2},{2,3},{3,4},{4,5},{5,6},{6,7},{7,0},{8,9},{9,10},{10,1... | collective-permute-start | bytes 1572872 | tf_op jit(solution)/shard_map/ppermute | solution.py:30
  180.7 9.6 %shard_map.89.refs_6_ = f32[768,1024]{1,0:T(8,128)} custom-call(s32[6]{0:T(128)} %refs_0_.9, s32[8]{0:T(128)} %refs_1_.7, bf16[768,1536]{1,0:T(8,128)(2,1)} %get-tuple-element.66.refs_2_, bf16[1024,256]{1,0:T(8,128)(2,1)} %collective-permute-done.14.refs_3_, bf16[1024,256]{1,0:T(8,128)(2,1)} %collective-permute-done.16.refs_4_, ...), custom_call_target="tpu_custom_call" | custom-call | flops 2415919104 | bytes 13893632 | tf_op jit(solution)/shard_map/pallas_call | solution.py:185
  190.4 0.7 copy-done.8
  191.5 7.5 %shard_map.90 = bf16[768,1024]{1,0:T(8,128)(2,1)} custom-call(s32[6]{0:T(128)} %refs_0_.9, s32[8]{0:T(128)} %refs_1_.7, bf16[768,768]{1,0:T(8,128)(2,1)} %get-tuple-element.36.refs_2_, bf16[1024,256]{1,0:T(8,128)(2,1)} %copy-done.8, bf16[1024,256]{1,0:T(8,128)(2,1)} %copy-done.9, bf16[1024,256]{1,0:T(8,128)(2,1)} %copy-done.10, f32[768,1024]{1,0:T(8,128)} %shard_map.89.refs_6_), custom_call_target="tpu_custom_call" | custom-call | flops 1207959552 | bytes 11141120 | tf_op jit(solution)/shard_map/pallas_call | solution.py:185
  (86 shorter events, 4.8 us)
Async XLA Ops:
  6.5 135.1 %all-gather.2.cloned.1.call-start = ((), (), s32[]{:S(2)}) async-start(), calls=%async_computation | async-start | bytes 14155776 | tf_op jit(solution)/shard_map/all_gather | solution.py:203
  9.2 10.3 %collective-permute-start = (bf16[1024,128]{1,0:T(8,128)(2,1)S(1)}, bf16[1024,128]{1,0:T(8,128)(2,1)S(1)}, u32[]{:S(2)}, u32[]{:S(2)}) collective-permute-start(bf16[1024,128]{1,0:T(8,128)(2,1)S(1)} %copy-done.6), channel_id=1, source_target_pairs={{0,1},{1,2},{2,3},{3,4},{4,5},{5,6},{6,7},{7,0},{8,9},{9,10},{10,1... | collective-permute-start | bytes 786440 | tf_op jit(solution)/shard_map/ppermute | solution.py:30
  11.2 8.3 %collective-permute-start.1 = (bf16[1024,128]{1,0:T(8,128)(2,1)S(1)}, bf16[1024,128]{1,0:T(8,128)(2,1)S(1)}, u32[]{:S(2)}, u32[]{:S(2)}) collective-permute-start(bf16[1024,128]{1,0:T(8,128)(2,1)S(1)} %copy-done.5), channel_id=1, source_target_pairs={{0,8},{1,9},{2,10},{3,11},{4,12},{5,13},{6,14},{7,15},{8,16},{9,17... | collective-permute-start | bytes 786440 | tf_op jit(solution)/shard_map/ppermute | solution.py:30
  19.5 7.6 %collective-permute-start.2 = (bf16[1024,128]{1,0:T(8,128)(2,1)S(1)}, bf16[1024,128]{1,0:T(8,128)(2,1)S(1)}, u32[]{:S(2)}, u32[]{:S(2)}) collective-permute-start(bf16[1024,128]{1,0:T(8,128)(2,1)S(1)} %collective-permute-done.refs_1_), channel_id=1, source_target_pairs={{0,1},{1,2},{2,3},{3,4},{4,5},{5,6},{6,7},{7,0},{8,9},{9,10},{10,1... | collective-permute-start | bytes 786440 | tf_op jit(solution)/shard_map/ppermute | solution.py:30
  34.9 32.6 %collective-permute-start.24 = (bf16[1024,512]{1,0:T(8,128)(2,1)S(1)}, bf16[1024,512]{1,0:T(8,128)(2,1)S(1)}, u32[]{:S(2)}, u32[]{:S(2)}) collective-permute-start(bf16[1024,512]{1,0:T(8,128)(2,1)S(1)} %shard_map.85.refs_3_), channel_id=1, source_target_pairs={{0,8},{1,9},{2,10},{3,11},{4,12},{5,13},{6,14},{7,15},{8,16},{9,17... | collective-permute-start | bytes 3145736 | tf_op jit(solution)/shard_map/ppermute | solution.py:30
  36.4 16.2 %collective-permute-start.5 = (bf16[1024,128]{1,0:T(8,128)(2,1)S(1)}, bf16[1024,128]{1,0:T(8,128)(2,1)S(1)}, u32[]{:S(2)}, u32[]{:S(2)}) collective-permute-start(bf16[1024,128]{1,0:T(8,128)(2,1)S(1)} %collective-permute-done.3.refs_0_), channel_id=1, source_target_pairs={{0,8},{1,9},{2,10},{3,11},{4,12},{5,13},{6,14},{7,15},{8,16},{9,17... | collective-permute-start | bytes 786440 | tf_op jit(solution)/shard_map/ppermute | solution.py:30
  36.9 18.7 %collective-permute-start.7 = (bf16[1024,256]{1,0:T(8,128)(2,1)S(1)}, bf16[1024,256]{1,0:T(8,128)(2,1)S(1)}, u32[]{:S(2)}, u32[]{:S(2)}) collective-permute-start(bf16[1024,256]{1,0:T(8,128)(2,1)S(1)} %shard_map.83.refs_12_), channel_id=1, source_target_pairs={{0,1},{1,2},{2,3},{3,4},{4,5},{5,6},{6,7},{7,0},{8,9},{9,10},{10,1... | collective-permute-start | bytes 1572872 | tf_op jit(solution)/shard_map/ppermute | solution.py:30
  52.7 13.3 %collective-permute-start.17 = (bf16[1024,256]{1,0:T(8,128)(2,1)S(1)}, bf16[1024,256]{1,0:T(8,128)(2,1)S(1)}, u32[]{:S(2)}, u32[]{:S(2)}) collective-permute-start(bf16[1024,256]{1,0:T(8,128)(2,1)S(1)} %shard_map.84.refs_13_), channel_id=1, source_target_pairs={{0,1},{1,2},{2,3},{3,4},{4,5},{5,6},{6,7},{7,0},{8,9},{9,10},{10,1... | collective-permute-start | bytes 1572872 | tf_op jit(solution)/shard_map/ppermute | solution.py:30
  53.1 12.9 %collective-permute-start.6 = (bf16[1024,128]{1,0:T(8,128)(2,1)S(1)}, bf16[1024,128]{1,0:T(8,128)(2,1)S(1)}, u32[]{:S(2)}, u32[]{:S(2)}) collective-permute-start(bf16[1024,128]{1,0:T(8,128)(2,1)S(1)} %collective-permute-done.4.refs_3_), channel_id=1, source_target_pairs={{0,1},{1,2},{2,3},{3,4},{4,5},{5,6},{6,7},{7,0},{8,9},{9,10},{10,1... | collective-permute-start | bytes 786440 | tf_op jit(solution)/shard_map/ppermute | solution.py:30
  66.0 18.8 %collective-permute-start.9 = (bf16[1024,256]{1,0:T(8,128)(2,1)S(1)}, bf16[1024,256]{1,0:T(8,128)(2,1)S(1)}, u32[]{:S(2)}, u32[]{:S(2)}) collective-permute-start(bf16[1024,256]{1,0:T(8,128)(2,1)S(1)} %collective-permute-done.7.refs_14_), channel_id=1, source_target_pairs={{0,1},{1,2},{2,3},{3,4},{4,5},{5,6},{6,7},{7,0},{8,9},{9,10},{10,1... | collective-permute-start | bytes 1572872 | tf_op jit(solution)/shard_map/ppermute | solution.py:30
  66.0 18.8 %collective-permute-start.18 = (bf16[1024,256]{1,0:T(8,128)(2,1)S(1)}, bf16[1024,256]{1,0:T(8,128)(2,1)S(1)}, u32[]{:S(2)}, u32[]{:S(2)}) collective-permute-start(bf16[1024,256]{1,0:T(8,128)(2,1)S(1)} %collective-permute-done.17.refs_15_), channel_id=1, source_target_pairs={{0,1},{1,2},{2,3},{3,4},{4,5},{5,6},{6,7},{7,0},{8,9},{9,10},{10,1... | collective-permute-start | bytes 1572872 | tf_op jit(solution)/shard_map/ppermute | solution.py:30
  67.6 38.9 %collective-permute-start.25 = (bf16[1024,512]{1,0:T(8,128)(2,1)S(1)}, bf16[1024,512]{1,0:T(8,128)(2,1)}, u32[]{:S(2)}, u32[]{:S(2)}) collective-permute-start(bf16[1024,512]{1,0:T(8,128)(2,1)S(1)} %collective-permute-done.24.refs_4_), channel_id=1, source_target_pairs={{0,8},{1,9},{2,10},{3,11},{4,12},{5,13},{6,14},{7,15},{8,16},{9,17... | collective-permute-start | bytes 3145736 | tf_op jit(solution)/shard_map/ppermute | solution.py:30
  71.2 13.5 %collective-permute-start.8 = (bf16[1024,128]{1,0:T(8,128)(2,1)S(1)}, bf16[1024,128]{1,0:T(8,128)(2,1)S(1)}, u32[]{:S(2)}, u32[]{:S(2)}) collective-permute-start(bf16[1024,128]{1,0:T(8,128)(2,1)S(1)} %collective-permute-done.6.refs_0_), channel_id=1, source_target_pairs={{0,1},{1,2},{2,3},{3,4},{4,5},{5,6},{6,7},{7,0},{8,9},{9,10},{10,1... | collective-permute-start | bytes 786440 | tf_op jit(solution)/shard_map/ppermute | solution.py:30
  84.8 18.8 %collective-permute-start.11 = (bf16[1024,256]{1,0:T(8,128)(2,1)S(1)}, bf16[1024,256]{1,0:T(8,128)(2,1)S(1)}, u32[]{:S(2)}, u32[]{:S(2)}) collective-permute-start(bf16[1024,256]{1,0:T(8,128)(2,1)S(1)} %collective-permute-done.9.refs_16_), channel_id=1, source_target_pairs={{0,1},{1,2},{2,3},{3,4},{4,5},{5,6},{6,7},{7,0},{8,9},{9,10},{10,1... | collective-permute-start | bytes 1572872 | tf_op jit(solution)/shard_map/ppermute | solution.py:30
  84.8 18.8 %collective-permute-start.19 = (bf16[1024,256]{1,0:T(8,128)(2,1)S(1)}, bf16[1024,256]{1,0:T(8,128)(2,1)S(1)}, u32[]{:S(2)}, u32[]{:S(2)}) collective-permute-start(bf16[1024,256]{1,0:T(8,128)(2,1)S(1)} %collective-permute-done.18.refs_17_), channel_id=1, source_target_pairs={{0,1},{1,2},{2,3},{3,4},{4,5},{5,6},{6,7},{7,0},{8,9},{9,10},{10,1... | collective-permute-start | bytes 1572872 | tf_op jit(solution)/shard_map/ppermute | solution.py:30
  85.5 18.2 %collective-permute-start.27 = (bf16[1024,256]{1,0:T(8,128)(2,1)S(1)}, bf16[1024,256]{1,0:T(8,128)(2,1)S(1)}, u32[]{:S(2)}, u32[]{:S(2)}) collective-permute-start(bf16[1024,256]{1,0:T(8,128)(2,1)S(1)} %shard_map.87.refs_7_), channel_id=1, source_target_pairs={{0,8},{1,9},{2,10},{3,11},{4,12},{5,13},{6,14},{7,15},{8,16},{9,17... | collective-permute-start | bytes 1572872 | tf_op jit(solution)/shard_map/ppermute | solution.py:30
  89.3 14.3 %collective-permute-start.10 = (bf16[1024,128]{1,0:T(8,128)(2,1)S(1)}, bf16[1024,128]{1,0:T(8,128)(2,1)S(1)}, u32[]{:S(2)}, u32[]{:S(2)}) collective-permute-start(bf16[1024,128]{1,0:T(8,128)(2,1)S(1)} %collective-permute-done.8.refs_1_), channel_id=1, source_target_pairs={{0,1},{1,2},{2,3},{3,4},{4,5},{5,6},{6,7},{7,0},{8,9},{9,10},{10,1... | collective-permute-start | bytes 786440 | tf_op jit(solution)/shard_map/ppermute | solution.py:30
  103.6 18.9 %collective-permute-start.13 = (bf16[1024,256]{1,0:T(8,128)(2,1)S(1)}, bf16[1024,256]{1,0:T(8,128)(2,1)}, u32[]{:S(2)}, u32[]{:S(2)}) collective-permute-start(bf16[1024,256]{1,0:T(8,128)(2,1)S(1)} %collective-permute-done.11.refs_18_), channel_id=1, source_target_pairs={{0,1},{1,2},{2,3},{3,4},{4,5},{5,6},{6,7},{7,0},{8,9},{9,10},{10,1... | collective-permute-start | bytes 1572872 | tf_op jit(solution)/shard_map/ppermute | solution.py:30
  103.6 21.7 %collective-permute-start.20 = (bf16[1024,256]{1,0:T(8,128)(2,1)S(1)}, bf16[1024,256]{1,0:T(8,128)(2,1)}, u32[]{:S(2)}, u32[]{:S(2)}) collective-permute-start(bf16[1024,256]{1,0:T(8,128)(2,1)S(1)} %collective-permute-done.19.refs_19_), channel_id=1, source_target_pairs={{0,1},{1,2},{2,3},{3,4},{4,5},{5,6},{6,7},{7,0},{8,9},{9,10},{10,1... | collective-permute-start | bytes 1572872 | tf_op jit(solution)/shard_map/ppermute | solution.py:30
  103.8 21.7 %collective-permute-start.28 = (bf16[1024,256]{1,0:T(8,128)(2,1)S(1)}, bf16[1024,256]{1,0:T(8,128)(2,1)}, u32[]{:S(2)}, u32[]{:S(2)}) collective-permute-start(bf16[1024,256]{1,0:T(8,128)(2,1)S(1)} %collective-permute-done.27.refs_8_), channel_id=1, source_target_pairs={{0,8},{1,9},{2,10},{3,11},{4,12},{5,13},{6,14},{7,15},{8,16},{9,17... | collective-permute-start | bytes 1572872 | tf_op jit(solution)/shard_map/ppermute | solution.py:30
  106.5 47.7 %collective-permute-start.26 = (bf16[1024,512]{1,0:T(8,128)(2,1)}, bf16[1024,512]{1,0:T(8,128)(2,1)}, u32[]{:S(2)}, u32[]{:S(2)}) collective-permute-start(bf16[1024,512]{1,0:T(8,128)(2,1)} %collective-permute-done.25.refs_5_), channel_id=1, source_target_pairs={{0,8},{1,9},{2,10},{3,11},{4,12},{5,13},{6,14},{7,15},{8,16},{9,17... | collective-permute-start | bytes 3145736 | tf_op jit(solution)/shard_map/ppermute | solution.py:30
  106.6 15.9 %collective-permute-start.12 = (bf16[1024,128]{1,0:T(8,128)(2,1)S(1)}, bf16[1024,128]{1,0:T(8,128)(2,1)S(1)}, u32[]{:S(2)}, u32[]{:S(2)}) collective-permute-start(bf16[1024,128]{1,0:T(8,128)(2,1)S(1)} %collective-permute-done.10.refs_0_), channel_id=1, source_target_pairs={{0,1},{1,2},{2,3},{3,4},{4,5},{5,6},{6,7},{7,0},{8,9},{9,10},{10,1... | collective-permute-start | bytes 786440 | tf_op jit(solution)/shard_map/ppermute | solution.py:30
  122.6 9.4 %collective-permute-start.14 = (bf16[1024,256]{1,0:T(8,128)(2,1)S(1)}, bf16[1024,256]{1,0:T(8,128)(2,1)}, u32[]{:S(2)}, u32[]{:S(2)}) collective-permute-start(bf16[1024,256]{1,0:T(8,128)(2,1)S(1)} %shard_map.86.refs_11_), channel_id=1, source_target_pairs={{0,8},{1,9},{2,10},{3,11},{4,12},{5,13},{6,14},{7,15},{8,16},{9,17... | collective-permute-start | bytes 1572872 | tf_op jit(solution)/shard_map/ppermute | solution.py:30
  125.3 10.7 %collective-permute-start.15 = (bf16[1024,256]{1,0:T(8,128)(2,1)}, bf16[1024,256]{1,0:T(8,128)(2,1)}, u32[]{:S(2)}, u32[]{:S(2)}) collective-permute-start(bf16[1024,256]{1,0:T(8,128)(2,1)} %collective-permute-done.13.refs_20_), channel_id=1, source_target_pairs={{0,1},{1,2},{2,3},{3,4},{4,5},{5,6},{6,7},{7,0},{8,9},{9,10},{10,1... | collective-permute-start | bytes 1572872 | tf_op jit(solution)/shard_map/ppermute | solution.py:30
  125.3 16.3 %collective-permute-start.23 = (bf16[1024,256]{1,0:T(8,128)(2,1)}, bf16[1024,256]{1,0:T(8,128)(2,1)}, u32[]{:S(2)}, u32[]{:S(2)}) collective-permute-start(bf16[1024,256]{1,0:T(8,128)(2,1)} %collective-permute-done.20.refs_21_), channel_id=1, source_target_pairs={{0,1},{1,2},{2,3},{3,4},{4,5},{5,6},{6,7},{7,0},{8,9},{9,10},{10,1... | collective-permute-start | bytes 1572872 | tf_op jit(solution)/shard_map/ppermute | solution.py:30
  125.4 28.7 %collective-permute-start.29 = (bf16[1024,256]{1,0:T(8,128)(2,1)}, bf16[1024,256]{1,0:T(8,128)(2,1)}, u32[]{:S(2)}, u32[]{:S(2)}) collective-permute-start(bf16[1024,256]{1,0:T(8,128)(2,1)} %collective-permute-done.28.refs_9_), channel_id=1, source_target_pairs={{0,8},{1,9},{2,10},{3,11},{4,12},{5,13},{6,14},{7,15},{8,16},{9,17... | collective-permute-start | bytes 1572872 | tf_op jit(solution)/shard_map/ppermute | solution.py:30
  136.0 37.5 %collective-permute-start.16 = (bf16[1024,256]{1,0:T(8,128)(2,1)}, bf16[1024,256]{1,0:T(8,128)(2,1)}, u32[]{:S(2)}, u32[]{:S(2)}) collective-permute-start(bf16[1024,256]{1,0:T(8,128)(2,1)} %collective-permute-done.14.refs_3_), channel_id=1, source_target_pairs={{0,8},{1,9},{2,10},{3,11},{4,12},{5,13},{6,14},{7,15},{8,16},{9,17... | collective-permute-start | bytes 1572872 | tf_op jit(solution)/shard_map/ppermute | solution.py:30
  141.6 35.5 %collective-permute-start.31 = (bf16[1024,256]{1,0:T(8,128)(2,1)}, bf16[1024,256]{1,0:T(8,128)(2,1)}, u32[]{:S(2)}, u32[]{:S(2)}) collective-permute-start(bf16[1024,256]{1,0:T(8,128)(2,1)} %collective-permute-done.23.refs_6_), channel_id=1, source_target_pairs={{0,1},{1,2},{2,3},{3,4},{4,5},{5,6},{6,7},{7,0},{8,9},{9,10},{10,1... | collective-permute-start | bytes 1572872 | tf_op jit(solution)/shard_map/ppermute | solution.py:30
  154.1 19.5 %collective-permute-start.21 = (bf16[1024,256]{1,0:T(8,128)(2,1)}, bf16[1024,256]{1,0:T(8,128)(2,1)S(1)}, u32[]{:S(2)}, u32[]{:S(2)}) collective-permute-start(bf16[1024,256]{1,0:T(8,128)(2,1)} %collective-permute-done.15.refs_5_), channel_id=1, source_target_pairs={{0,1},{1,2},{2,3},{3,4},{4,5},{5,6},{6,7},{7,0},{8,9},{9,10},{10,1... | collective-permute-start | bytes 1572872 | tf_op jit(solution)/shard_map/ppermute | solution.py:30
  173.6 16.7 %collective-permute-start.22 = (bf16[1024,256]{1,0:T(8,128)(2,1)}, bf16[1024,256]{1,0:T(8,128)(2,1)S(1)}, u32[]{:S(2)}, u32[]{:S(2)}) collective-permute-start(bf16[1024,256]{1,0:T(8,128)(2,1)} %collective-permute-done.16.refs_4_), channel_id=1, source_target_pairs={{0,8},{1,9},{2,10},{3,11},{4,12},{5,13},{6,14},{7,15},{8,16},{9,17... | collective-permute-start | bytes 1572872 | tf_op jit(solution)/shard_map/ppermute | solution.py:30
  173.7 16.6 %collective-permute-start.30 = (bf16[1024,256]{1,0:T(8,128)(2,1)S(1)}, bf16[1024,256]{1,0:T(8,128)(2,1)S(1)}, u32[]{:S(2)}, u32[]{:S(2)}) collective-permute-start(bf16[1024,256]{1,0:T(8,128)(2,1)S(1)} %collective-permute-done.21.refs_7_), channel_id=1, source_target_pairs={{0,1},{1,2},{2,3},{3,4},{4,5},{5,6},{6,7},{7,0},{8,9},{9,10},{10,1... | collective-permute-start | bytes 1572872 | tf_op jit(solution)/shard_map/ppermute | solution.py:30
  177.1 13.3 %collective-permute-start.32 = (bf16[1024,256]{1,0:T(8,128)(2,1)}, bf16[1024,256]{1,0:T(8,128)(2,1)S(1)}, u32[]{:S(2)}, u32[]{:S(2)}) collective-permute-start(bf16[1024,256]{1,0:T(8,128)(2,1)} %collective-permute-done.31.refs_8_), channel_id=1, source_target_pairs={{0,1},{1,2},{2,3},{3,4},{4,5},{5,6},{6,7},{7,0},{8,9},{9,10},{10,1... | collective-permute-start | bytes 1572872 | tf_op jit(solution)/shard_map/ppermute | solution.py:30
  (21 other events, 757.4 us)
Sparse Core Ops, SparseCore 0:
  9.4 72.5 all-gather.1

commit v4 on v3

v4 whole, which is shorter than its diff:
```python
import jax
import jax.numpy as jnp
from jax import lax
from jax.experimental import pallas as pl
from jax.experimental.pallas import tpu as pltpu
from jax.sharding import PartitionSpec as P

BLK = 128
NY, NZ = 4, 8
HALF = 512
BF16 = jnp.bfloat16
F32 = jnp.float32


def perm_of(dy, dz):
    return [
        (8 * y + z, 8 * ((y + dy) % NY) + (z + dz) % NZ) for y in range(NY) for z in range(NZ)
    ]


def move(values, dy=0, dz=0):
    return lax.ppermute(values, "mem", perm_of(dy, dz))


def after(value, *others):
    return lax.optimization_barrier((value,) + others)[0]


SMEM = pl.BlockSpec(memory_space=pltpu.SMEM)
VMEM = pl.BlockSpec(memory_space=pltpu.VMEM)
HBM = pl.BlockSpec(memory_space=pltpu.HBM)


def params(mib):
    return pltpu.CompilerParams(vmem_limit_bytes=mib * 2**20)


def cost(flops, moved):
    return pl.CostEstimate(flops=flops, bytes_accessed=moved, transcendentals=0)


def join_kernel(blocks, *refs):
    out, at, k = refs[-1], 0, 0
    for block in blocks:
        width = block[0].shape[1]
        if len(block) == 1:
            out[:, at:at + width] = refs[k][...]
        else:
            out[:HALF, at:at + width] = refs[k][...]
            out[HALF:, at:at + width] = refs[k + 1][...]
        at += width
        k += len(block)


def join(blocks):
    arrays = [array for block in blocks for array in block]
    full = sum(block[0].shape[1] for block in blocks)

    def kernel(*refs):
        join_kernel(blocks, *refs)

    return pl.pallas_call(
        kernel,
        out_shape=jax.ShapeDtypeStruct((2 * HALF, full), BF16),
        in_specs=[VMEM] * len(arrays),
        out_specs=VMEM,
        compiler_params=params(8),
        cost_estimate=cost(0, 8 * HALF * full),
    )(*arrays)


def dot(left, right):
    return lax.dot_general(left, right, (((1,), (1,)), ((), ())), preferred_element_type=F32)


def tiles_of(terms):
    return [tile for tiles, _ in terms for tile in tiles]


def mask_kernel(parts, here_ref, ij_ref, cd_ref, mask_ref, raw_hbm, *refs):
    outs, raw, laid, sem = refs[:len(parts)], refs[-2 - len(parts)], refs[-1 - len(parts):-1], refs[-1]
    fetch = pltpu.make_async_copy(raw_hbm, raw, sem.at[len(parts)])
    fetch.start()
    y, z = here_ref[0], here_ref[1]
    fetch.wait()
    copies = []
    for p, (target, tiles) in enumerate(zip(laid, parts)):
        for k, (panel, off_y, off_z) in enumerate(tiles):
            tile = 8 * ((y + off_y) & (NY - 1)) + ((z + off_z) & (NZ - 1))
            cols = pl.ds(pl.multiple_of(tile * BLK, BLK), BLK)
            label = cd_ref[tile]
            for row in range(6):
                on = (ij_ref[row] == label) & (mask_ref[row, tile] == 1)
                kept = raw[pl.ds(panel * 768 + row * BLK, BLK), cols]
                target[row * BLK:(row + 1) * BLK, k * BLK:(k + 1) * BLK] = jnp.where(on, kept, jnp.zeros_like(kept))
        copies.append(pltpu.make_async_copy(target, outs[p], sem.at[p]))
        copies[-1].start()
    for copy in copies:
        copy.wait()


def mask(here, sym_ij, sym_cd, amp_mask, raw, groups):
    parts = [tiles_of(terms) for terms in groups]
    shapes = [(768, len(tiles) * BLK) for tiles in parts]

    def kernel(*refs):
        mask_kernel(parts, *refs)

    return pl.pallas_call(
        kernel,
        out_shape=[jax.ShapeDtypeStruct(shape, BF16) for shape in shapes],
        in_specs=[SMEM] * 4 + [HBM],
        out_specs=[HBM] * len(shapes),
        scratch_shapes=[pltpu.VMEM((1536, 4096), BF16)]
        + [pltpu.VMEM(shape, BF16) for shape in shapes]
        + [pltpu.SemaphoreType.DMA((len(shapes) + 1,))],
        compiler_params=params(60),
        cost_estimate=cost(0, 25 * 2**20),
    )(here, sym_ij, sym_cd, amp_mask, raw)


def product_kernel(sizes, first, last, ij_ref, ab_ref, amps_hbm, *refs):
    n = sum(sizes)
    ints, refs = refs[:n], refs[n:]
    if first:
        out, amps, rows_v, sem = refs
    else:
        total_hbm, out, amps, rows_v, sem, total = refs

    def fetch(c, act):
        rows = pl.ds(pl.multiple_of(c * 256, 256), 256)
        at, k = 0, 0
        for b, size in enumerate(sizes):
            width = ints[k].shape[1]
            to = rows_v.at[rows, pl.ds(at, width)]
            if size == 1:
                act(pltpu.make_async_copy(ints[k].at[rows, :], to, sem.at[c, b]))
            else:
                part = pl.ds(pl.multiple_of((c & 1) * 256, 256), 256)

                @pl.when(c < 2)
                def _():
                    act(pltpu.make_async_copy(ints[k].at[part, :], to, sem.at[c, b]))

                @pl.when(c >= 2)
                def _():
                    act(pltpu.make_async_copy(ints[k + 1].at[part, :], to, sem.at[c, b]))
            at += width
            k += size
        if not first:
            act(pltpu.make_async_copy(total_hbm.at[:, rows], total.at[:, rows], sem.at[c, len(sizes)]))

    whole = pltpu.make_async_copy(amps_hbm, amps, sem.at[4, 0])
    whole.start()
    for c in range(4):
        fetch(jnp.int32(c), lambda copy: copy.start())
    whole.wait()

    def strip(c, carry):
        fetch(c, lambda copy: copy.wait())
        cols = pl.ds(pl.multiple_of(c * 256, 256), 256)

        def part(m, carry):
            rows = pl.ds(pl.multiple_of(m * 256, 256), 256)
            value = dot(amps[rows, :], rows_v[cols, :])
            if not first:
                value = value + total[rows, cols]
            if not last:
                out[rows, cols] = value
                return carry
            for i in range(2):
                for j in range(2):
                    tile = value[i * BLK:(i + 1) * BLK, j * BLK:(j + 1) * BLK] * 0.5
                    on = ij_ref[2 * m + i] == ab_ref[2 * c + j]
                    where = (
                        pl.ds(pl.multiple_of(m * 256 + i * BLK, BLK), BLK),
                        pl.ds(pl.multiple_of(c * 256 + j * BLK, BLK), BLK),
                    )
                    out[where] = jnp.where(on, tile, jnp.zeros_like(tile)).astype(BF16)
            return carry

        return lax.fori_loop(0, 3, part, carry)

    lax.fori_loop(0, 4, strip, 0)


def product(sym_ij, sym_ab, amps, terms, total=None, last=False):
    depth = amps.shape[1]
    first = total is None
    sizes = [len(block) for _, block in terms]
    n = sum(sizes)

    def kernel(*refs):
        product_kernel(sizes, first, last, *refs)

    scratch = [
        pltpu.VMEM((768, depth), BF16), pltpu.VMEM((1024, depth), BF16), pltpu.SemaphoreType.DMA((5, len(sizes) + 1))
    ]
    return pl.pallas_call(
        kernel,
        out_shape=jax.ShapeDtypeStruct((768, 1024), BF16 if last else F32),
        in_specs=[SMEM] * 2 + [HBM] * (1 + n + (not first)),
        out_specs=VMEM,
        scratch_shapes=scratch + ([] if first else [pltpu.VMEM((768, 1024), F32)]),
        compiler_params=params(60),
        cost_estimate=cost(2 * 768 * 1024 * depth, 8 * 2**20 + 3584 * depth),
    )(sym_ij, sym_ab, amps, *[array for _, block in terms for array in block], *([] if first else [total]))


def body(amp_plus, amp_minus, ints_plus, ints_minus, sym_ij, sym_ab, sym_cd, amp_mask):
    mem = lax.axis_index("mem")
    here = jnp.stack([mem // NZ, mem % NZ]).astype(jnp.int32)

    def go(value, *waits, **way):
        return move(after(value, *waits) if waits else value, **way)

    raw = lax.all_gather(jnp.concatenate([amp_plus, amp_minus], axis=0), "grp", axis=1, tiled=True)

    z0, y0 = ints_plus, ints_minus
    zu, zd, yu, yd = [go(z0, dz=1)], [go(z0, dz=-1)], [go(y0, dy=1)], [go(y0, dy=-1)]
    ones = (zu[0], zd[0], yu[0], yd[0])
    zu.append(go(zu[0], *ones, dz=1))
    zd.append(go(zd[0], *ones, dz=-1))
    y2 = (go(yu[0][:HALF], *ones, dy=1), go(yd[0][HALF:], *ones, dy=-1))
    twos = (zu[1], zd[1]) + y2
    zu.append(go(zu[1], *twos, dz=1))
    zd.append(go(zd[1], *twos, dz=-1))
    c0 = join([(z0,), (zu[0],), (zd[0],), (zu[1],), (zd[1],)])
    c1 = (go(c0, *twos, dy=1), go(c0, *twos, dy=-1))
    w0 = join([(y0,), (yu[0],), (yd[0],), y2])
    threes = (zu[2], zd[2])
    z4 = (go(zu[2][:HALF], *threes, dz=1), go(zd[2][HALF:], *threes, dz=-1))
    d0 = join([(zu[2],), (zd[2],), z4])
    wu, wd = [go(w0, *z4, dz=1)], [go(w0, *z4, dz=-1)]
    c2 = (go(c1[0][:HALF], *c1, dy=1), go(c1[1][HALF:], *c1, dy=-1))
    wu.append(go(wu[0], wd[0], dz=1))
    wd.append(go(wd[0], wu[0], dz=-1))
    d1 = (go(d0, *c2, dy=1), go(d0, *c2, dy=-1))
    wu.append(go(wu[1], wd[1], dz=1))
    wd.append(go(wd[1], wu[1], dz=-1))

    def plus(offs, y, block):
        return [(0, y, z) for z in offs], block

    def minus(z, block):
        return [(1, y, z) for y in (0, -1, 1, 2)], block

    near, far = (0, -1, 1, -2, 2), (-3, 3, 4)
    now = [plus(near, 0, (c0,)), plus(near, -1, c1[:1]), plus(near, 1, c1[1:]), plus(near, 2, c2)]
    now += [minus(0, (w0,)), minus(-1, (wu[0],)), minus(1, (wd[0],))]
    far4 = [(0, y, z) for y in (0, -1, 1, 2) for z in far]
    tiles = [(far4, None)] + [minus(z, None) for z in (-2, 2, -3, 3)]
    amps = mask(here, sym_ij, sym_cd, amp_mask, raw, (now, tiles, [minus(4, None)]))
    total = product(sym_ij, sym_ab, amps[0], now)
    d2 = (go(d1[0][:HALF], *d1, total, dy=1), go(d1[1][HALF:], *d1, total, dy=-1))
    soon = [plus(far, 0, (d0,)), plus(far, -1, d1[:1]), plus(far, 1, d1[1:]), plus(far, 2, d2)]
    soon += [minus(-2, (wu[1],)), minus(2, (wd[1],)), minus(-3, (wu[2],)), minus(3, (wd[2],))]
    w4 = (go(wu[2][:HALF], wd[2], *d2, dz=1), go(wd[2][HALF:], wu[2], *d2, dz=-1))
    total = product(sym_ij, sym_ab, amps[1], soon, total)
    return product(sym_ij, sym_ab, amps[2], [minus(4, w4)], total, True)


def solution(mesh):
    placed = (
        P("mem", "grp"),
        P("mem", "grp"),
        P("grp", "mem"),
        P("grp", "mem"),
        P("mem"),
        P("grp"),
        P(),
        P("mem", None),
    )
    return jax.shard_map(
        body, mesh=mesh, in_specs=placed, out_specs=P("mem", "grp"), check_vma=False
    )
```

time: 208 us -> 173 us (0.83); the launches traced: 206 us -> 173 us
  waiting for transfers between devices: 98.9 us -> 59.6 us
  local copies, waits for them, and re-layouts: 1.19 us -> 5.38 us
  starting transfers between devices: 39.2 us -> 43.1 us
    ppermute x33 -> x28, waiting for transfers between devices: 98.9 us -> 59.5 us  [move(): return lax.ppermute(values, 'mem', perm_of(dy, dz))]
    slice x0 -> x10, local copies, waits for them, and re-layouts: none -> 4.38 us  [the longest x1 1.08 us: body(): wd[2][HALF:]]
    ppermute x33 -> x28, starting transfers between devices: 39.2 us -> 43.1 us  [move(): return lax.ppermute(values, 'mem', perm_of(dy, dz))]
  transfers between devices with their start and end apart: 34 -> 29, of which waited for: 11 -> 14; matrix products, arithmetic and copies ran while one was open for 0% -> 3% of each run, Pallas kernels for 20% -> 24%
where the time goes in v4:
time: 173 us
  waiting for transfers between devices  59.6 us (34%)
  Pallas kernels  47.9 us (28%)
  starting transfers between devices  43.1 us (25%)
  between operations  13.7 us (8%)
  local copies, waits for them, and re-layouts  5.38 us (3%)
  other arithmetic  3.28 us (2%)
    ppermute x28, waiting for transfers between devices, move(): return lax.ppermute(values, 'mem', perm_of(dy, dz))  59.5 us
    ppermute x28, starting transfers between devices, move(): return lax.ppermute(values, 'mem', perm_of(dy, dz))  43.1 us
    pallas_call x3, Pallas kernels, product(): pl.pallas_call(kernel, out_shape=jax.ShapeDtypeStruct((768, 1024), BF16 i...  35.7 us
    pallas_call x1, Pallas kernels, mask(): pl.pallas_call(kernel, out_shape=[jax.ShapeDtypeStruct(shape, BF16) for s...  11.6 us
  transfers between devices with their start and end apart: 29, of which 14 were waited for; matrix products, arithmetic and copies ran while one was open for 3% of the time, Pallas kernels for 24%

profile of v4, /device:TPU:24, one launch (start us, length us, event | category | flops | bytes accessed | tf_op | source)
XLA Modules:
  0.0 172.9 jit_solution(5541865784615819837)
XLA Ops:
  6.5 2.7 %pad_maximum_fusion = bf16[1536,512]{1,0:T(8,128)(2,1)} fusion(bf16[768,512]{1,0:T(8,128)(2,1)} %param.9, bf16[768,512]{1,0:T(8,128)(2,1)} %param.8), kind=kLoop, calls=%fused_computation | loop fusion | flops 3145728 | bytes 3145728 | tf_op jit(solution)/shard_map/concatenate | solution.py:217
  9.2 2.0 %collective-permute-start = (bf16[1024,128]{1,0:T(8,128)(2,1)S(1)}, bf16[1024,128]{1,0:T(8,128)(2,1)S(1)}, u32[]{:S(2)}, u32[]{:S(2)}) collective-permute-start(bf16[1024,128]{1,0:T(8,128)(2,1)S(1)} %copy-done.4), channel_id=1, source_target_pairs={{0,8},{1,9},{2,10},{3,11},{4,12},{5,13},{6,14},{7,15},{8,16},{9,17... | collective-permute-start | bytes 786440 | tf_op jit(solution)/shard_map/ppermute | solution.py:22
  11.4 1.9 %collective-permute-start.2 = (bf16[1024,128]{1,0:T(8,128)(2,1)S(1)}, bf16[1024,128]{1,0:T(8,128)(2,1)S(1)}, u32[]{:S(2)}, u32[]{:S(2)}) collective-permute-start(bf16[1024,128]{1,0:T(8,128)(2,1)S(1)} %copy-done.3), channel_id=1, source_target_pairs={{0,1},{1,2},{2,3},{3,4},{4,5},{5,6},{6,7},{7,0},{8,9},{9,10},{10,1... | collective-permute-start | bytes 786440 | tf_op jit(solution)/shard_map/ppermute | solution.py:22
  13.3 3.9 %collective-permute-start.3 = (bf16[1024,128]{1,0:T(8,128)(2,1)S(1)}, bf16[1024,128]{1,0:T(8,128)(2,1)S(1)}, u32[]{:S(2)}, u32[]{:S(2)}) collective-permute-start(bf16[1024,128]{1,0:T(8,128)(2,1)S(1)} %copy-done.3), channel_id=1, source_target_pairs={{0,7},{1,0},{2,1},{3,2},{4,3},{5,4},{6,5},{7,6},{8,15},{9,8},{10,9... | collective-permute-start | bytes 786440 | tf_op jit(solution)/shard_map/ppermute | solution.py:22
  17.4 1.5 collective-permute-done.1.refs_2_
  18.9 4.1 %collective-permute-done.2.refs_1_ = bf16[1024,128]{1,0:T(8,128)(2,1)S(1)} collective-permute-done((bf16[1024,128]{1,0:T(8,128)(2,1)S(1)}, bf16[1024,128]{1,0:T(8,128)(2,1)S(1)}, u32[]{:S(2)}, u32[]{:S(2)}) %collective-permute-start.2) | collective-permute-done | bytes 262176 | tf_op jit(solution)/shard_map/ppermute | solution.py:22
  23.0 3.2 %collective-permute-start.7 = (bf16[1024,128]{1,0:T(8,128)(2,1)S(1)}, bf16[1024,128]{1,0:T(8,128)(2,1)S(1)}, u32[]{:S(2)}, u32[]{:S(2)}) collective-permute-start(bf16[1024,128]{1,0:T(8,128)(2,1)S(1)} %collective-permute-done.3.refs_2_), channel_id=1, source_target_pairs={{0,7},{1,0},{2,1},{3,2},{4,3},{5,4},{6,5},{7,6},{8,15},{9,8},{10,9... | collective-permute-start | bytes 786440 | tf_op jit(solution)/shard_map/ppermute | solution.py:22
  26.2 1.7 collective-permute-start.4
  28.4 2.6 %collective-permute-done.6.refs_3_ = bf16[1024,128]{1,0:T(8,128)(2,1)S(1)} collective-permute-done((bf16[1024,128]{1,0:T(8,128)(2,1)S(1)}, bf16[1024,128]{1,0:T(8,128)(2,1)S(1)}, u32[]{:S(2)}, u32[]{:S(2)}) %collective-permute-start.6) | collective-permute-done | bytes 262176 | tf_op jit(solution)/shard_map/ppermute | solution.py:22
  31.3 2.9 %collective-permute-done.5.refs_4_ = bf16[512,128]{1,0:T(8,128)(2,1)S(1)} collective-permute-done((bf16[512,128]{1,0:T(8,128)(2,1)S(1)}, bf16[512,128]{1,0:T(8,128)(2,1)S(1)}, u32[]{:S(2)}, u32[]{:S(2)}) %collective-permute-start.5) | collective-permute-done | bytes 131104 | tf_op jit(solution)/shard_map/ppermute | solution.py:22
  34.1 2.0 %collective-permute-start.19 = (bf16[1024,640]{1,0:T(8,128)(2,1)S(1)}, bf16[1024,640]{1,0:T(8,128)(2,1)S(1)}, u32[]{:S(2)}, u32[]{:S(2)}) collective-permute-start(bf16[1024,640]{1,0:T(8,128)(2,1)S(1)} %shard_map.85.refs_3_), channel_id=1, source_target_pairs={{0,24},{1,25},{2,26},{3,27},{4,28},{5,29},{6,30},{7,31},{8,0},{9,1... | collective-permute-start | bytes 3932168 | tf_op jit(solution)/shard_map/ppermute | solution.py:22
  36.2 3.2 %collective-permute-start.9 = (bf16[1024,128]{1,0:T(8,128)(2,1)S(1)}, bf16[1024,128]{1,0:T(8,128)(2,1)S(1)}, u32[]{:S(2)}, u32[]{:S(2)}) collective-permute-start(bf16[1024,128]{1,0:T(8,128)(2,1)S(1)} %collective-permute-done.7.refs_4_), channel_id=1, source_target_pairs={{0,7},{1,0},{2,1},{3,2},{4,3},{5,4},{6,5},{7,6},{8,15},{9,8},{10,9... | collective-permute-start | bytes 786440 | tf_op jit(solution)/shard_map/ppermute | solution.py:22
  39.4 4.5 %collective-permute-done.8.refs_0_ = bf16[1024,128]{1,0:T(8,128)(2,1)S(1)} collective-permute-done((bf16[1024,128]{1,0:T(8,128)(2,1)S(1)}, bf16[1024,128]{1,0:T(8,128)(2,1)S(1)}, u32[]{:S(2)}, u32[]{:S(2)}) %collective-permute-start.8) | collective-permute-done | bytes 262176 | tf_op jit(solution)/shard_map/ppermute | solution.py:22
  45.0 2.4 %collective-permute-start.11 = (bf16[512,128]{1,0:T(8,128)(2,1)S(1)}, bf16[512,128]{1,0:T(8,128)(2,1)S(1)}, u32[]{:S(2)}, u32[]{:S(2)}) collective-permute-start(bf16[512,128]{1,0:T(8,128)(2,1)S(1)} %slice.43), channel_id=1, source_target_pairs={{0,7},{1,0},{2,1},{3,2},{4,3},{5,4},{6,5},{7,6},{8,15},{9,8},{10,9... | collective-permute-start | bytes 393224 | tf_op jit(solution)/shard_map/ppermute | solution.py:22
  47.6 3.5 %collective-permute-done.10.refs_2_ = bf16[512,128]{1,0:T(8,128)(2,1)S(1)} collective-permute-done((bf16[512,128]{1,0:T(8,128)(2,1)S(1)}, bf16[512,128]{1,0:T(8,128)(2,1)S(1)}, u32[]{:S(2)}, u32[]{:S(2)}) %collective-permute-start.10) | collective-permute-done | bytes 131104 | tf_op jit(solution)/shard_map/ppermute | solution.py:22
  51.1 3.9 %collective-permute-start.12 = (bf16[1024,512]{1,0:T(8,128)(2,1)S(1)}, bf16[1024,512]{1,0:T(8,128)(2,1)}, u32[]{:S(2)}, u32[]{:S(2)}) collective-permute-start(bf16[1024,512]{1,0:T(8,128)(2,1)S(1)} %shard_map.83.refs_8_), channel_id=1, source_target_pairs={{0,1},{1,2},{2,3},{3,4},{4,5},{5,6},{6,7},{7,0},{8,9},{9,10},{10,1... | collective-permute-start | bytes 3145736 | tf_op jit(solution)/shard_map/ppermute | solution.py:22
  55.0 7.0 %collective-permute-done.18.refs_4_ = bf16[1024,640]{1,0:T(8,128)(2,1)S(1)} collective-permute-done((bf16[1024,640]{1,0:T(8,128)(2,1)S(1)}, bf16[1024,640]{1,0:T(8,128)(2,1)S(1)}, u32[]{:S(2)}, u32[]{:S(2)}) %collective-permute-start.18) | collective-permute-done | bytes 1310752 | tf_op jit(solution)/shard_map/ppermute | solution.py:22
  63.3 1.4 collective-permute-start.20
  65.4 9.0 %collective-permute-done.12.refs_9_ = bf16[1024,512]{1,0:T(8,128)(2,1)} collective-permute-done((bf16[1024,512]{1,0:T(8,128)(2,1)S(1)}, bf16[1024,512]{1,0:T(8,128)(2,1)}, u32[]{:S(2)}, u32[]{:S(2)}) %collective-permute-start.12) | collective-permute-done | bytes 1048608 | tf_op jit(solution)/shard_map/ppermute | solution.py:22
  74.4 3.7 %collective-permute-start.14 = (bf16[1024,512]{1,0:T(8,128)(2,1)}, bf16[1024,512]{1,0:T(8,128)(2,1)}, u32[]{:S(2)}, u32[]{:S(2)}) collective-permute-start(bf16[1024,512]{1,0:T(8,128)(2,1)} %collective-permute-done.12.refs_9_), channel_id=1, source_target_pairs={{0,1},{1,2},{2,3},{3,4},{4,5},{5,6},{6,7},{7,0},{8,9},{9,10},{10,1... | collective-permute-start | bytes 3145736 | tf_op jit(solution)/shard_map/ppermute | solution.py:22
  79.4 1.9 %collective-permute-start.23 = (bf16[1024,384]{1,0:T(8,128)(2,1)S(1)}, bf16[1024,384]{1,0:T(8,128)(2,1)}, u32[]{:S(2)}, u32[]{:S(2)}) collective-permute-start(bf16[1024,384]{1,0:T(8,128)(2,1)S(1)} %shard_map.84.refs_3_), channel_id=1, source_target_pairs={{0,24},{1,25},{2,26},{3,27},{4,28},{5,29},{6,30},{7,31},{8,0},{9,1... | collective-permute-start | bytes 2359304 | tf_op jit(solution)/shard_map/ppermute | solution.py:22
  81.3 16.4 %collective-permute-done.14.refs_8_ = bf16[1024,512]{1,0:T(8,128)(2,1)} collective-permute-done((bf16[1024,512]{1,0:T(8,128)(2,1)}, bf16[1024,512]{1,0:T(8,128)(2,1)}, u32[]{:S(2)}, u32[]{:S(2)}) %collective-permute-start.14) | collective-permute-done | bytes 1048608 | tf_op jit(solution)/shard_map/ppermute | solution.py:22
  97.7 3.7 %collective-permute-start.16 = (bf16[1024,512]{1,0:T(8,128)(2,1)}, bf16[1024,512]{1,0:T(8,128)(2,1)}, u32[]{:S(2)}, u32[]{:S(2)}) collective-permute-start(bf16[1024,512]{1,0:T(8,128)(2,1)} %collective-permute-done.14.refs_8_), channel_id=1, source_target_pairs={{0,1},{1,2},{2,3},{3,4},{4,5},{5,6},{6,7},{7,0},{8,9},{9,10},{10,1... | collective-permute-start | bytes 3145736 | tf_op jit(solution)/shard_map/ppermute | solution.py:22
  104.2 11.6 %shard_map.82 = (bf16[768,4096]{1,0:T(8,128)(2,1)}, bf16[768,3584]{1,0:T(8,128)(2,1)}, bf16[768,512]{1,0:T(8,128)(2,1)}) custom-call(s32[2]{0:T(128)} %pad_add_fusion.refs_0_, s32[6]{0:T(128)} %refs_0_.9, s32[32]{0:T(128)} %refs_2_.1, s32[6,32]{1,0:T(8,128)} %refs_3_.1, bf16[1536,4096]{1,0:T(8,128)(2,1)} %all-gather.2.cloned.1.call-done.refs_4_), custom_call_target="tpu_custom_call" | custom-call | bytes 26214400 | tf_op jit(solution)/shard_map/pallas_call | solution.py:109
  115.8 14.9 %shard_map.86.refs_12_ = f32[768,1024]{1,0:T(8,128)} custom-call(s32[6]{0:T(128)} %refs_0_.9, s32[8]{0:T(128)} %refs_1_.7, bf16[768,4096]{1,0:T(8,128)(2,1)} %get-tuple-element.47.refs_2_, bf16[1024,640]{1,0:T(8,128)(2,1)} %copy-done, bf16[1024,640]{1,0:T(8,128)(2,1)} %copy-done.7, bf16[1024,640]{1,0:T(8,128)(2,1)} %copy-done.8, bf16[512,640]{1,0:T(8,128)(2,1)} %copy-done.9, ...), custom_call_target="tpu_custom_call" | custom-call | flops 6442450944 | bytes 23068672 | tf_op jit(solution)/shard_map/pallas_call | solution.py:199
  130.7 1.3 collective-permute-start.24
  135.2 3.6 %collective-permute-done.24.refs_6_ = bf16[512,384]{1,0:T(8,128)(2,1)S(1)} collective-permute-done((bf16[512,384]{1,0:T(8,128)(2,1)S(1)}, bf16[512,384]{1,0:T(8,128)(2,1)S(1)}, u32[]{:S(2)}, u32[]{:S(2)}) %collective-permute-start.24) | collective-permute-done | bytes 393248 | tf_op jit(solution)/shard_map/ppermute | solution.py:22
  138.8 2.2 %collective-permute-done.25.refs_7_ = bf16[512,384]{1,0:T(8,128)(2,1)S(1)} collective-permute-done((bf16[512,384]{1,0:T(8,128)(2,1)S(1)}, bf16[512,384]{1,0:T(8,128)(2,1)S(1)}, u32[]{:S(2)}, u32[]{:S(2)}) %collective-permute-start.25) | collective-permute-done | bytes 393248 | tf_op jit(solution)/shard_map/ppermute | solution.py:22
  140.9 2.0 %collective-permute-start.26 = (bf16[512,512]{1,0:T(8,128)(2,1)S(1)}, bf16[512,512]{1,0:T(8,128)(2,1)S(1)}, u32[]{:S(2)}, u32[]{:S(2)}) collective-permute-start(bf16[512,512]{1,0:T(8,128)(2,1)S(1)} %slice.44), channel_id=1, source_target_pairs={{0,1},{1,2},{2,3},{3,4},{4,5},{5,6},{6,7},{7,0},{8,9},{9,10},{10,1... | collective-permute-start | bytes 1572872 | tf_op jit(solution)/shard_map/ppermute | solution.py:22
  143.0 1.2 collective-permute-start.27
  144.2 14.2 %shard_map.87.refs_5_ = f32[768,1024]{1,0:T(8,128)} custom-call(s32[6]{0:T(128)} %refs_0_.9, s32[8]{0:T(128)} %refs_1_.7, bf16[768,3584]{1,0:T(8,128)(2,1)} %get-tuple-element.52.refs_2_, bf16[1024,384]{1,0:T(8,128)(2,1)} %copy-done.2, bf16[1024,384]{1,0:T(8,128)(2,1)} %collective-permute-done.22.refs_4_, bf16[1024,384]{1,0:T(8,128)(2,1)} %collective-permute-done.23.refs_5_, ...), custom_call_target="tpu_custom_call" | custom-call | flops 5637144576 | bytes 21233664 | tf_op jit(solution)/shard_map/pallas_call | solution.py:199
  159.4 6.7 %shard_map.88 = bf16[768,1024]{1,0:T(8,128)(2,1)} custom-call(s32[6]{0:T(128)} %refs_0_.9, s32[8]{0:T(128)} %refs_1_.7, bf16[768,512]{1,0:T(8,128)(2,1)} %get-tuple-element.29.refs_2_, bf16[512,512]{1,0:T(8,128)(2,1)} %copy-done.5, bf16[512,512]{1,0:T(8,128)(2,1)} %copy-done.6, f32[768,1024]{1,0:T(8,128)} %shard_map.87.refs_5_), custom_call_target="tpu_custom_call" | custom-call | flops 805306368 | bytes 10223616 | tf_op jit(solution)/shard_map/pallas_call | solution.py:199
  (72 shorter events, 12.6 us)
Async XLA Ops:
  6.5 97.6 %all-gather.2.cloned.1.call-start = ((), (), s32[]{:S(2)}) async-start(), calls=%async_computation | async-start | bytes 14155776 | tf_op jit(solution)/shard_map/all_gather | solution.py:217
  9.2 8.1 %collective-permute-start = (bf16[1024,128]{1,0:T(8,128)(2,1)S(1)}, bf16[1024,128]{1,0:T(8,128)(2,1)S(1)}, u32[]{:S(2)}, u32[]{:S(2)}) collective-permute-start(bf16[1024,128]{1,0:T(8,128)(2,1)S(1)} %copy-done.4), channel_id=1, source_target_pairs={{0,8},{1,9},{2,10},{3,11},{4,12},{5,13},{6,14},{7,15},{8,16},{9,17... | collective-permute-start | bytes 786440 | tf_op jit(solution)/shard_map/ppermute | solution.py:22
  11.3 7.6 %collective-permute-start.1 = (bf16[1024,128]{1,0:T(8,128)(2,1)S(1)}, bf16[1024,128]{1,0:T(8,128)(2,1)S(1)}, u32[]{:S(2)}, u32[]{:S(2)}) collective-permute-start(bf16[1024,128]{1,0:T(8,128)(2,1)S(1)} %copy-done.4), channel_id=1, source_target_pairs={{0,24},{1,25},{2,26},{3,27},{4,28},{5,29},{6,30},{7,31},{8,0},{9,1... | collective-permute-start | bytes 786440 | tf_op jit(solution)/shard_map/ppermute | solution.py:22
  11.4 11.6 %collective-permute-start.2 = (bf16[1024,128]{1,0:T(8,128)(2,1)S(1)}, bf16[1024,128]{1,0:T(8,128)(2,1)S(1)}, u32[]{:S(2)}, u32[]{:S(2)}) collective-permute-start(bf16[1024,128]{1,0:T(8,128)(2,1)S(1)} %copy-done.3), channel_id=1, source_target_pairs={{0,1},{1,2},{2,3},{3,4},{4,5},{5,6},{6,7},{7,0},{8,9},{9,10},{10,1... | collective-permute-start | bytes 786440 | tf_op jit(solution)/shard_map/ppermute | solution.py:22
  13.3 9.7 %collective-permute-start.3 = (bf16[1024,128]{1,0:T(8,128)(2,1)S(1)}, bf16[1024,128]{1,0:T(8,128)(2,1)S(1)}, u32[]{:S(2)}, u32[]{:S(2)}) collective-permute-start(bf16[1024,128]{1,0:T(8,128)(2,1)S(1)} %copy-done.3), channel_id=1, source_target_pairs={{0,7},{1,0},{2,1},{3,2},{4,3},{5,4},{6,5},{7,6},{8,15},{9,8},{10,9... | collective-permute-start | bytes 786440 | tf_op jit(solution)/shard_map/ppermute | solution.py:22
  23.0 8.1 %collective-permute-start.6 = (bf16[1024,128]{1,0:T(8,128)(2,1)S(1)}, bf16[1024,128]{1,0:T(8,128)(2,1)S(1)}, u32[]{:S(2)}, u32[]{:S(2)}) collective-permute-start(bf16[1024,128]{1,0:T(8,128)(2,1)S(1)} %collective-permute-done.2.refs_1_), channel_id=1, source_target_pairs={{0,1},{1,2},{2,3},{3,4},{4,5},{5,6},{6,7},{7,0},{8,9},{9,10},{10,1... | collective-permute-start | bytes 786440 | tf_op jit(solution)/shard_map/ppermute | solution.py:22
  23.0 8.1 %collective-permute-start.7 = (bf16[1024,128]{1,0:T(8,128)(2,1)S(1)}, bf16[1024,128]{1,0:T(8,128)(2,1)S(1)}, u32[]{:S(2)}, u32[]{:S(2)}) collective-permute-start(bf16[1024,128]{1,0:T(8,128)(2,1)S(1)} %collective-permute-done.3.refs_2_), channel_id=1, source_target_pairs={{0,7},{1,0},{2,1},{3,2},{4,3},{5,4},{6,5},{7,6},{8,15},{9,8},{10,9... | collective-permute-start | bytes 786440 | tf_op jit(solution)/shard_map/ppermute | solution.py:22
  26.2 5.1 %collective-permute-start.4 = (bf16[512,128]{1,0:T(8,128)(2,1)S(1)}, bf16[512,128]{1,0:T(8,128)(2,1)S(1)}, u32[]{:S(2)}, u32[]{:S(2)}) collective-permute-start(bf16[512,128]{1,0:T(8,128)(2,1)S(1)} %slice.40), channel_id=1, source_target_pairs={{0,8},{1,9},{2,10},{3,11},{4,12},{5,13},{6,14},{7,15},{8,16},{9,17... | collective-permute-start | bytes 393224 | tf_op jit(solution)/shard_map/ppermute | solution.py:22
  27.9 6.3 %collective-permute-start.5 = (bf16[512,128]{1,0:T(8,128)(2,1)S(1)}, bf16[512,128]{1,0:T(8,128)(2,1)S(1)}, u32[]{:S(2)}, u32[]{:S(2)}) collective-permute-start(bf16[512,128]{1,0:T(8,128)(2,1)S(1)} %slice.41), channel_id=1, source_target_pairs={{0,24},{1,25},{2,26},{3,27},{4,28},{5,29},{6,30},{7,31},{8,0},{9,1... | collective-permute-start | bytes 393224 | tf_op jit(solution)/shard_map/ppermute | solution.py:22
  31.3 47.0 %copy-start = (bf16[1024,640]{1,0:T(8,128)(2,1)}, bf16[1024,640]{1,0:T(8,128)(2,1)S(1)}, u32[]{:S(2)}) copy-start(bf16[1024,640]{1,0:T(8,128)(2,1)S(1)} %shard_map.85.refs_3_) | copy-start | bytes 3932164
  34.1 27.9 %collective-permute-start.18 = (bf16[1024,640]{1,0:T(8,128)(2,1)S(1)}, bf16[1024,640]{1,0:T(8,128)(2,1)S(1)}, u32[]{:S(2)}, u32[]{:S(2)}) collective-permute-start(bf16[1024,640]{1,0:T(8,128)(2,1)S(1)} %shard_map.85.refs_3_), channel_id=1, source_target_pairs={{0,8},{1,9},{2,10},{3,11},{4,12},{5,13},{6,14},{7,15},{8,16},{9,17... | collective-permute-start | bytes 3932168 | tf_op jit(solution)/shard_map/ppermute | solution.py:22
  34.1 29.1 %collective-permute-start.19 = (bf16[1024,640]{1,0:T(8,128)(2,1)S(1)}, bf16[1024,640]{1,0:T(8,128)(2,1)S(1)}, u32[]{:S(2)}, u32[]{:S(2)}) collective-permute-start(bf16[1024,640]{1,0:T(8,128)(2,1)S(1)} %shard_map.85.refs_3_), channel_id=1, source_target_pairs={{0,24},{1,25},{2,26},{3,27},{4,28},{5,29},{6,30},{7,31},{8,0},{9,1... | collective-permute-start | bytes 3932168 | tf_op jit(solution)/shard_map/ppermute | solution.py:22
  36.2 7.7 %collective-permute-start.8 = (bf16[1024,128]{1,0:T(8,128)(2,1)S(1)}, bf16[1024,128]{1,0:T(8,128)(2,1)S(1)}, u32[]{:S(2)}, u32[]{:S(2)}) collective-permute-start(bf16[1024,128]{1,0:T(8,128)(2,1)S(1)} %collective-permute-done.6.refs_3_), channel_id=1, source_target_pairs={{0,1},{1,2},{2,3},{3,4},{4,5},{5,6},{6,7},{7,0},{8,9},{9,10},{10,1... | collective-permute-start | bytes 786440 | tf_op jit(solution)/shard_map/ppermute | solution.py:22
  36.2 7.7 %collective-permute-start.9 = (bf16[1024,128]{1,0:T(8,128)(2,1)S(1)}, bf16[1024,128]{1,0:T(8,128)(2,1)S(1)}, u32[]{:S(2)}, u32[]{:S(2)}) collective-permute-start(bf16[1024,128]{1,0:T(8,128)(2,1)S(1)} %collective-permute-done.7.refs_4_), channel_id=1, source_target_pairs={{0,7},{1,0},{2,1},{3,2},{4,3},{5,4},{6,5},{7,6},{8,15},{9,8},{10,9... | collective-permute-start | bytes 786440 | tf_op jit(solution)/shard_map/ppermute | solution.py:22
  43.9 7.2 %collective-permute-start.10 = (bf16[512,128]{1,0:T(8,128)(2,1)S(1)}, bf16[512,128]{1,0:T(8,128)(2,1)S(1)}, u32[]{:S(2)}, u32[]{:S(2)}) collective-permute-start(bf16[512,128]{1,0:T(8,128)(2,1)S(1)} %slice.42), channel_id=1, source_target_pairs={{0,1},{1,2},{2,3},{3,4},{4,5},{5,6},{6,7},{7,0},{8,9},{9,10},{10,1... | collective-permute-start | bytes 393224 | tf_op jit(solution)/shard_map/ppermute | solution.py:22
  45.0 6.1 %collective-permute-start.11 = (bf16[512,128]{1,0:T(8,128)(2,1)S(1)}, bf16[512,128]{1,0:T(8,128)(2,1)S(1)}, u32[]{:S(2)}, u32[]{:S(2)}) collective-permute-start(bf16[512,128]{1,0:T(8,128)(2,1)S(1)} %slice.43), channel_id=1, source_target_pairs={{0,7},{1,0},{2,1},{3,2},{4,3},{5,4},{6,5},{7,6},{8,15},{9,8},{10,9... | collective-permute-start | bytes 393224 | tf_op jit(solution)/shard_map/ppermute | solution.py:22
  47.6 68.2 %copy-start.1 = (bf16[1024,512]{1,0:T(8,128)(2,1)}, bf16[1024,512]{1,0:T(8,128)(2,1)S(1)}, u32[]{:S(2)}) copy-start(bf16[1024,512]{1,0:T(8,128)(2,1)S(1)} %shard_map.83.refs_8_) | copy-start | bytes 3145732
  51.1 23.3 %collective-permute-start.12 = (bf16[1024,512]{1,0:T(8,128)(2,1)S(1)}, bf16[1024,512]{1,0:T(8,128)(2,1)}, u32[]{:S(2)}, u32[]{:S(2)}) collective-permute-start(bf16[1024,512]{1,0:T(8,128)(2,1)S(1)} %shard_map.83.refs_8_), channel_id=1, source_target_pairs={{0,1},{1,2},{2,3},{3,4},{4,5},{5,6},{6,7},{7,0},{8,9},{9,10},{10,1... | collective-permute-start | bytes 3145736 | tf_op jit(solution)/shard_map/ppermute | solution.py:22
  55.0 19.4 %collective-permute-start.13 = (bf16[1024,512]{1,0:T(8,128)(2,1)S(1)}, bf16[1024,512]{1,0:T(8,128)(2,1)}, u32[]{:S(2)}, u32[]{:S(2)}) collective-permute-start(bf16[1024,512]{1,0:T(8,128)(2,1)S(1)} %shard_map.83.refs_8_), channel_id=1, source_target_pairs={{0,7},{1,0},{2,1},{3,2},{4,3},{5,4},{6,5},{7,6},{8,15},{9,8},{10,9... | collective-permute-start | bytes 3145736 | tf_op jit(solution)/shard_map/ppermute | solution.py:22
  63.3 15.0 %collective-permute-start.20 = (bf16[512,640]{1,0:T(8,128)(2,1)S(1)}, bf16[512,640]{1,0:T(8,128)(2,1)S(1)}, u32[]{:S(2)}, u32[]{:S(2)}) collective-permute-start(bf16[512,640]{1,0:T(8,128)(2,1)S(1)} %slice.45), channel_id=1, source_target_pairs={{0,8},{1,9},{2,10},{3,11},{4,12},{5,13},{6,14},{7,15},{8,16},{9,17... | collective-permute-start | bytes 1966088 | tf_op jit(solution)/shard_map/ppermute | solution.py:22
  64.7 14.6 %collective-permute-start.21 = (bf16[512,640]{1,0:T(8,128)(2,1)S(1)}, bf16[512,640]{1,0:T(8,128)(2,1)S(1)}, u32[]{:S(2)}, u32[]{:S(2)}) collective-permute-start(bf16[512,640]{1,0:T(8,128)(2,1)S(1)} %slice.46), channel_id=1, source_target_pairs={{0,24},{1,25},{2,26},{3,27},{4,28},{5,29},{6,30},{7,31},{8,0},{9,1... | collective-permute-start | bytes 1966088 | tf_op jit(solution)/shard_map/ppermute | solution.py:22
  74.4 23.3 %collective-permute-start.14 = (bf16[1024,512]{1,0:T(8,128)(2,1)}, bf16[1024,512]{1,0:T(8,128)(2,1)}, u32[]{:S(2)}, u32[]{:S(2)}) collective-permute-start(bf16[1024,512]{1,0:T(8,128)(2,1)} %collective-permute-done.12.refs_9_), channel_id=1, source_target_pairs={{0,1},{1,2},{2,3},{3,4},{4,5},{5,6},{6,7},{7,0},{8,9},{9,10},{10,1... | collective-permute-start | bytes 3145736 | tf_op jit(solution)/shard_map/ppermute | solution.py:22
  78.1 19.6 %collective-permute-start.15 = (bf16[1024,512]{1,0:T(8,128)(2,1)}, bf16[1024,512]{1,0:T(8,128)(2,1)}, u32[]{:S(2)}, u32[]{:S(2)}) collective-permute-start(bf16[1024,512]{1,0:T(8,128)(2,1)} %collective-permute-done.13.refs_10_), channel_id=1, source_target_pairs={{0,7},{1,0},{2,1},{3,2},{4,3},{5,4},{6,5},{7,6},{8,15},{9,8},{10,9... | collective-permute-start | bytes 3145736 | tf_op jit(solution)/shard_map/ppermute | solution.py:22
  78.3 37.5 %copy-start.2 = (bf16[1024,384]{1,0:T(8,128)(2,1)}, bf16[1024,384]{1,0:T(8,128)(2,1)S(1)}, u32[]{:S(2)}) copy-start(bf16[1024,384]{1,0:T(8,128)(2,1)S(1)} %shard_map.84.refs_3_) | copy-start | bytes 2359300
  79.3 22.7 %collective-permute-start.22 = (bf16[1024,384]{1,0:T(8,128)(2,1)S(1)}, bf16[1024,384]{1,0:T(8,128)(2,1)}, u32[]{:S(2)}, u32[]{:S(2)}) collective-permute-start(bf16[1024,384]{1,0:T(8,128)(2,1)S(1)} %shard_map.84.refs_3_), channel_id=1, source_target_pairs={{0,8},{1,9},{2,10},{3,11},{4,12},{5,13},{6,14},{7,15},{8,16},{9,17... | collective-permute-start | bytes 2359304 | tf_op jit(solution)/shard_map/ppermute | solution.py:22
  79.4 23.7 %collective-permute-start.23 = (bf16[1024,384]{1,0:T(8,128)(2,1)S(1)}, bf16[1024,384]{1,0:T(8,128)(2,1)}, u32[]{:S(2)}, u32[]{:S(2)}) collective-permute-start(bf16[1024,384]{1,0:T(8,128)(2,1)S(1)} %shard_map.84.refs_3_), channel_id=1, source_target_pairs={{0,24},{1,25},{2,26},{3,27},{4,28},{5,29},{6,30},{7,31},{8,0},{9,1... | collective-permute-start | bytes 2359304 | tf_op jit(solution)/shard_map/ppermute | solution.py:22
  97.7 35.3 %collective-permute-start.16 = (bf16[1024,512]{1,0:T(8,128)(2,1)}, bf16[1024,512]{1,0:T(8,128)(2,1)}, u32[]{:S(2)}, u32[]{:S(2)}) collective-permute-start(bf16[1024,512]{1,0:T(8,128)(2,1)} %collective-permute-done.14.refs_8_), channel_id=1, source_target_pairs={{0,1},{1,2},{2,3},{3,4},{4,5},{5,6},{6,7},{7,0},{8,9},{9,10},{10,1... | collective-permute-start | bytes 3145736 | tf_op jit(solution)/shard_map/ppermute | solution.py:22
  101.4 32.7 %collective-permute-start.17 = (bf16[1024,512]{1,0:T(8,128)(2,1)}, bf16[1024,512]{1,0:T(8,128)(2,1)}, u32[]{:S(2)}, u32[]{:S(2)}) collective-permute-start(bf16[1024,512]{1,0:T(8,128)(2,1)} %collective-permute-done.15.refs_9_), channel_id=1, source_target_pairs={{0,7},{1,0},{2,1},{3,2},{4,3},{5,4},{6,5},{7,6},{8,15},{9,8},{10,9... | collective-permute-start | bytes 3145736 | tf_op jit(solution)/shard_map/ppermute | solution.py:22
  130.7 8.1 %collective-permute-start.24 = (bf16[512,384]{1,0:T(8,128)(2,1)S(1)}, bf16[512,384]{1,0:T(8,128)(2,1)S(1)}, u32[]{:S(2)}, u32[]{:S(2)}) collective-permute-start(bf16[512,384]{1,0:T(8,128)(2,1)S(1)} %slice.47), channel_id=1, source_target_pairs={{0,8},{1,9},{2,10},{3,11},{4,12},{5,13},{6,14},{7,15},{8,16},{9,17... | collective-permute-start | bytes 1179656 | tf_op jit(solution)/shard_map/ppermute | solution.py:22
  132.0 9.0 %collective-permute-start.25 = (bf16[512,384]{1,0:T(8,128)(2,1)S(1)}, bf16[512,384]{1,0:T(8,128)(2,1)S(1)}, u32[]{:S(2)}, u32[]{:S(2)}) collective-permute-start(bf16[512,384]{1,0:T(8,128)(2,1)S(1)} %slice.48), channel_id=1, source_target_pairs={{0,24},{1,25},{2,26},{3,27},{4,28},{5,29},{6,30},{7,31},{8,0},{9,1... | collective-permute-start | bytes 1179656 | tf_op jit(solution)/shard_map/ppermute | solution.py:22
  140.9 17.4 %collective-permute-start.26 = (bf16[512,512]{1,0:T(8,128)(2,1)S(1)}, bf16[512,512]{1,0:T(8,128)(2,1)S(1)}, u32[]{:S(2)}, u32[]{:S(2)}) collective-permute-start(bf16[512,512]{1,0:T(8,128)(2,1)S(1)} %slice.44), channel_id=1, source_target_pairs={{0,1},{1,2},{2,3},{3,4},{4,5},{5,6},{6,7},{7,0},{8,9},{9,10},{10,1... | collective-permute-start | bytes 1572872 | tf_op jit(solution)/shard_map/ppermute | solution.py:22
  143.0 15.4 %collective-permute-start.27 = (bf16[512,512]{1,0:T(8,128)(2,1)S(1)}, bf16[512,512]{1,0:T(8,128)(2,1)S(1)}, u32[]{:S(2)}, u32[]{:S(2)}) collective-permute-start(bf16[512,512]{1,0:T(8,128)(2,1)S(1)} %slice.49), channel_id=1, source_target_pairs={{0,7},{1,0},{2,1},{3,2},{4,3},{5,4},{6,5},{7,6},{8,15},{9,8},{10,9... | collective-permute-start | bytes 1572872 | tf_op jit(solution)/shard_map/ppermute | solution.py:22
  (10 other events, 38.4 us)
Sparse Core Ops, SparseCore 0:
  9.4 72.5 all-gather.1

commit v5 on v4

--- a/solution.py
+++ b/solution.py
@@ -160,26 +160,20 @@
         fetch(c, lambda copy: copy.wait())
         cols = pl.ds(pl.multiple_of(c * 256, 256), 256)
 
-        def part(m, carry):
-            rows = pl.ds(pl.multiple_of(m * 256, 256), 256)
-            value = dot(amps[rows, :], rows_v[cols, :])
-            if not first:
-                value = value + total[rows, cols]
-            if not last:
-                out[rows, cols] = value
-                return carry
-            for i in range(2):
-                for j in range(2):
-                    tile = value[i * BLK:(i + 1) * BLK, j * BLK:(j + 1) * BLK] * 0.5
-                    on = ij_ref[2 * m + i] == ab_ref[2 * c + j]
-                    where = (
-                        pl.ds(pl.multiple_of(m * 256 + i * BLK, BLK), BLK),
-                        pl.ds(pl.multiple_of(c * 256 + j * BLK, BLK), BLK),
-                    )
-                    out[where] = jnp.where(on, tile, jnp.zeros_like(tile)).astype(BF16)
+        value = dot(amps[...], rows_v[cols, :])
+        if not first:
+            value = value + total[:, cols]
+        if not last:
+            out[:, cols] = value
             return carry
-
-        return lax.fori_loop(0, 3, part, carry)
+        for i in range(6):
+            for j in range(2):
+                rows = slice(i * BLK, (i + 1) * BLK)
+                tile = value[rows, j * BLK:(j + 1) * BLK] * 0.5
+                on = ij_ref[i] == ab_ref[2 * c + j]
+                where = pl.ds(pl.multiple_of(c * 256 + j * BLK, BLK), BLK)
+                out[rows, where] = jnp.where(on, tile, jnp.zeros_like(tile)).astype(BF16)
+        return carry
 
     lax.fori_loop(0, 4, strip, 0)
 
@@ -236,28 +230,32 @@
     wu.append(go(wu[0], wd[0], dz=1))
     wd.append(go(wd[0], wu[0], dz=-1))
     d1 = (go(d0, *c2, dy=1), go(d0, *c2, dy=-1))
-    wu.append(go(wu[1], wd[1], dz=1))
-    wd.append(go(wd[1], wu[1], dz=-1))
-
-    def plus(offs, y, block):
+
+    def plus(offs, y, block=None):
         return [(0, y, z) for z in offs], block
 
-    def minus(z, block):
+    def minus(z, block=None):
         return [(1, y, z) for y in (0, -1, 1, 2)], block
 
     near, far = (0, -1, 1, -2, 2), (-3, 3, 4)
-    now = [plus(near, 0, (c0,)), plus(near, -1, c1[:1]), plus(near, 1, c1[1:]), plus(near, 2, c2)]
-    now += [minus(0, (w0,)), minus(-1, (wu[0],)), minus(1, (wd[0],))]
-    far4 = [(0, y, z) for y in (0, -1, 1, 2) for z in far]
-    tiles = [(far4, None)] + [minus(z, None) for z in (-2, 2, -3, 3)]
-    amps = mask(here, sym_ij, sym_cd, amp_mask, raw, (now, tiles, [minus(4, None)]))
-    total = product(sym_ij, sym_ab, amps[0], now)
+    groups = [
+        [plus(near, y) for y in (0, -1, 1, 2)] + [minus(z) for z in (0, -1, 1)],
+        [plus(far, y) for y in (0, -1, 1)] + [minus(z) for z in (-2, 2)],
+        [plus(far, 2)] + [minus(z) for z in (-3, 3)],
+        [minus(4)],
+    ]
+    amps = mask(here, sym_ij, sym_cd, amp_mask, raw, groups)
+    wu.append(go(wu[1], wd[1], amps[0], dz=1))
+    wd.append(go(wd[1], wu[1], amps[0], dz=-1))
+    blocks = [(c0,), c1[:1], c1[1:], c2, (w0,), (wu[0],), (wd[0],)]
+    total = product(sym_ij, sym_ab, amps[0], [(None, block) for block in blocks])
     d2 = (go(d1[0][:HALF], *d1, total, dy=1), go(d1[1][HALF:], *d1, total, dy=-1))
-    soon = [plus(far, 0, (d0,)), plus(far, -1, d1[:1]), plus(far, 1, d1[1:]), plus(far, 2, d2)]
-    soon += [minus(-2, (wu[1],)), minus(2, (wd[1],)), minus(-3, (wu[2],)), minus(3, (wd[2],))]
+    blocks = [(d0,), d1[:1], d1[1:], (wu[1],), (wd[1],)]
+    total = product(sym_ij, sym_ab, amps[1], [(None, block) for block in blocks], total)
     w4 = (go(wu[2][:HALF], wd[2], *d2, dz=1), go(wd[2][HALF:], wu[2], *d2, dz=-1))
-    total = product(sym_ij, sym_ab, amps[1], soon, total)
-    return product(sym_ij, sym_ab, amps[2], [minus(4, w4)], total, True)
+    blocks = [d2, (wu[2],), (wd[2],)]
+    total = product(sym_ij, sym_ab, amps[2], [(None, block) for block in blocks], total)
+    return product(sym_ij, sym_ab, amps[3], [(None, w4)], total, True)
 
 
 def solution(mesh):

time: 173 us -> 161 us (0.931)
  waiting for transfers between devices: 59.6 us -> 48.4 us
    ppermute x28, waiting for transfers between devices: 59.5 us -> 48.4 us  [move(): return lax.ppermute(values, 'mem', perm_of(dy, dz))]
    pallas_call x3 -> x4, Pallas kernels: 35.7 us -> 35.6 us  [product(): pl.pallas_call(kernel, out_shape=jax.ShapeDtypeStruct((768, 1024), BF16 i...]
  transfers between devices with their start and end apart: 29 -> 29, of which waited for: 14 -> 15; matrix products, arithmetic and copies ran while one was open for 3% -> 2% of each run, Pallas kernels for 24% -> 27%
where the time goes in v5:
time: 161 us; the launch traced here: 160 us
  waiting for transfers between devices  48.4 us (30%)
  Pallas kernels  47.8 us (30%)
  starting transfers between devices  42.6 us (26%)
  between operations  13.7 us (9%)
  local copies, waits for them, and re-layouts  4.61 us (3%)
  other arithmetic  3.31 us (2%)
    ppermute x28, waiting for transfers between devices, move(): return lax.ppermute(values, 'mem', perm_of(dy, dz))  48.4 us
    ppermute x28, starting transfers between devices, move(): return lax.ppermute(values, 'mem', perm_of(dy, dz))  42.6 us
    pallas_call x4, Pallas kernels, product(): pl.pallas_call(kernel, out_shape=jax.ShapeDtypeStruct((768, 1024), BF16 i...  35.6 us
    pallas_call x1, Pallas kernels, mask(): pl.pallas_call(kernel, out_shape=[jax.ShapeDtypeStruct(shape, BF16) for s...  11.6 us
  transfers between devices with their start and end apart: 29, of which 15 were waited for; matrix products, arithmetic and copies ran while one was open for 2% of the time, Pallas kernels for 27%

profile of v5, /device:TPU:24, one launch (start us, length us, event | category | flops | bytes accessed | tf_op | source)
XLA Modules:
  0.0 160.4 jit_solution(13429349357205990408)
XLA Ops:
  6.5 2.7 %pad_maximum_fusion = bf16[1536,512]{1,0:T(8,128)(2,1)} fusion(bf16[768,512]{1,0:T(8,128)(2,1)} %param.9, bf16[768,512]{1,0:T(8,128)(2,1)} %param.8), kind=kLoop, calls=%fused_computation | loop fusion | flops 3145728 | bytes 3145728 | tf_op jit(solution)/shard_map/concatenate | solution.py:211
  9.2 2.0 %collective-permute-start = (bf16[1024,128]{1,0:T(8,128)(2,1)S(1)}, bf16[1024,128]{1,0:T(8,128)(2,1)S(1)}, u32[]{:S(2)}, u32[]{:S(2)}) collective-permute-start(bf16[1024,128]{1,0:T(8,128)(2,1)S(1)} %copy-done.4), channel_id=1, source_target_pairs={{0,8},{1,9},{2,10},{3,11},{4,12},{5,13},{6,14},{7,15},{8,16},{9,17... | collective-permute-start | bytes 786440 | tf_op jit(solution)/shard_map/ppermute | solution.py:22
  11.4 1.9 %collective-permute-start.2 = (bf16[1024,128]{1,0:T(8,128)(2,1)S(1)}, bf16[1024,128]{1,0:T(8,128)(2,1)S(1)}, u32[]{:S(2)}, u32[]{:S(2)}) collective-permute-start(bf16[1024,128]{1,0:T(8,128)(2,1)S(1)} %copy-done.3), channel_id=1, source_target_pairs={{0,1},{1,2},{2,3},{3,4},{4,5},{5,6},{6,7},{7,0},{8,9},{9,10},{10,1... | collective-permute-start | bytes 786440 | tf_op jit(solution)/shard_map/ppermute | solution.py:22
  13.3 3.9 %collective-permute-start.3 = (bf16[1024,128]{1,0:T(8,128)(2,1)S(1)}, bf16[1024,128]{1,0:T(8,128)(2,1)S(1)}, u32[]{:S(2)}, u32[]{:S(2)}) collective-permute-start(bf16[1024,128]{1,0:T(8,128)(2,1)S(1)} %copy-done.3), channel_id=1, source_target_pairs={{0,7},{1,0},{2,1},{3,2},{4,3},{5,4},{6,5},{7,6},{8,15},{9,8},{10,9... | collective-permute-start | bytes 786440 | tf_op jit(solution)/shard_map/ppermute | solution.py:22
  17.4 1.5 collective-permute-done.1.refs_2_
  18.9 4.1 %collective-permute-done.2.refs_1_ = bf16[1024,128]{1,0:T(8,128)(2,1)S(1)} collective-permute-done((bf16[1024,128]{1,0:T(8,128)(2,1)S(1)}, bf16[1024,128]{1,0:T(8,128)(2,1)S(1)}, u32[]{:S(2)}, u32[]{:S(2)}) %collective-permute-start.2) | collective-permute-done | bytes 262176 | tf_op jit(solution)/shard_map/ppermute | solution.py:22
  23.0 3.2 %collective-permute-start.7 = (bf16[1024,128]{1,0:T(8,128)(2,1)S(1)}, bf16[1024,128]{1,0:T(8,128)(2,1)S(1)}, u32[]{:S(2)}, u32[]{:S(2)}) collective-permute-start(bf16[1024,128]{1,0:T(8,128)(2,1)S(1)} %collective-permute-done.3.refs_2_), channel_id=1, source_target_pairs={{0,7},{1,0},{2,1},{3,2},{4,3},{5,4},{6,5},{7,6},{8,15},{9,8},{10,9... | collective-permute-start | bytes 786440 | tf_op jit(solution)/shard_map/ppermute | solution.py:22
  26.2 1.7 %collective-permute-start.4 = (bf16[512,128]{1,0:T(8,128)(2,1)S(1)}, bf16[512,128]{1,0:T(8,128)(2,1)S(1)}, u32[]{:S(2)}, u32[]{:S(2)}) collective-permute-start(bf16[512,128]{1,0:T(8,128)(2,1)S(1)} %slice.40), channel_id=1, source_target_pairs={{0,8},{1,9},{2,10},{3,11},{4,12},{5,13},{6,14},{7,15},{8,16},{9,17... | collective-permute-start | bytes 393224 | tf_op jit(solution)/shard_map/ppermute | solution.py:22
  28.4 2.6 %collective-permute-done.6.refs_3_ = bf16[1024,128]{1,0:T(8,128)(2,1)S(1)} collective-permute-done((bf16[1024,128]{1,0:T(8,128)(2,1)S(1)}, bf16[1024,128]{1,0:T(8,128)(2,1)S(1)}, u32[]{:S(2)}, u32[]{:S(2)}) %collective-permute-start.6) | collective-permute-done | bytes 262176 | tf_op jit(solution)/shard_map/ppermute | solution.py:22
  31.3 2.9 %collective-permute-done.5.refs_4_ = bf16[512,128]{1,0:T(8,128)(2,1)S(1)} collective-permute-done((bf16[512,128]{1,0:T(8,128)(2,1)S(1)}, bf16[512,128]{1,0:T(8,128)(2,1)S(1)}, u32[]{:S(2)}, u32[]{:S(2)}) %collective-permute-start.5) | collective-permute-done | bytes 131104 | tf_op jit(solution)/shard_map/ppermute | solution.py:22
  34.1 2.0 %collective-permute-start.19 = (bf16[1024,640]{1,0:T(8,128)(2,1)S(1)}, bf16[1024,640]{1,0:T(8,128)(2,1)S(1)}, u32[]{:S(2)}, u32[]{:S(2)}) collective-permute-start(bf16[1024,640]{1,0:T(8,128)(2,1)S(1)} %shard_map.85.refs_3_), channel_id=1, source_target_pairs={{0,24},{1,25},{2,26},{3,27},{4,28},{5,29},{6,30},{7,31},{8,0},{9,1... | collective-permute-start | bytes 3932168 | tf_op jit(solution)/shard_map/ppermute | solution.py:22
  36.2 3.2 %collective-permute-start.9 = (bf16[1024,128]{1,0:T(8,128)(2,1)S(1)}, bf16[1024,128]{1,0:T(8,128)(2,1)S(1)}, u32[]{:S(2)}, u32[]{:S(2)}) collective-permute-start(bf16[1024,128]{1,0:T(8,128)(2,1)S(1)} %collective-permute-done.7.refs_4_), channel_id=1, source_target_pairs={{0,7},{1,0},{2,1},{3,2},{4,3},{5,4},{6,5},{7,6},{8,15},{9,8},{10,9... | collective-permute-start | bytes 786440 | tf_op jit(solution)/shard_map/ppermute | solution.py:22
  39.4 4.5 %collective-permute-done.8.refs_0_ = bf16[1024,128]{1,0:T(8,128)(2,1)S(1)} collective-permute-done((bf16[1024,128]{1,0:T(8,128)(2,1)S(1)}, bf16[1024,128]{1,0:T(8,128)(2,1)S(1)}, u32[]{:S(2)}, u32[]{:S(2)}) %collective-permute-start.8) | collective-permute-done | bytes 262176 | tf_op jit(solution)/shard_map/ppermute | solution.py:22
  45.0 2.4 %collective-permute-start.11 = (bf16[512,128]{1,0:T(8,128)(2,1)S(1)}, bf16[512,128]{1,0:T(8,128)(2,1)S(1)}, u32[]{:S(2)}, u32[]{:S(2)}) collective-permute-start(bf16[512,128]{1,0:T(8,128)(2,1)S(1)} %slice.43), channel_id=1, source_target_pairs={{0,7},{1,0},{2,1},{3,2},{4,3},{5,4},{6,5},{7,6},{8,15},{9,8},{10,9... | collective-permute-start | bytes 393224 | tf_op jit(solution)/shard_map/ppermute | solution.py:22
  47.6 3.5 %collective-permute-done.10.refs_2_ = bf16[512,128]{1,0:T(8,128)(2,1)S(1)} collective-permute-done((bf16[512,128]{1,0:T(8,128)(2,1)S(1)}, bf16[512,128]{1,0:T(8,128)(2,1)S(1)}, u32[]{:S(2)}, u32[]{:S(2)}) %collective-permute-start.10) | collective-permute-done | bytes 131104 | tf_op jit(solution)/shard_map/ppermute | solution.py:22
  51.1 3.9 %collective-permute-start.12 = (bf16[1024,512]{1,0:T(8,128)(2,1)S(1)}, bf16[1024,512]{1,0:T(8,128)(2,1)}, u32[]{:S(2)}, u32[]{:S(2)}) collective-permute-start(bf16[1024,512]{1,0:T(8,128)(2,1)S(1)} %shard_map.83.refs_8_), channel_id=1, source_target_pairs={{0,1},{1,2},{2,3},{3,4},{4,5},{5,6},{6,7},{7,0},{8,9},{9,10},{10,1... | collective-permute-start | bytes 3145736 | tf_op jit(solution)/shard_map/ppermute | solution.py:22
  55.0 7.0 %collective-permute-done.18.refs_4_ = bf16[1024,640]{1,0:T(8,128)(2,1)S(1)} collective-permute-done((bf16[1024,640]{1,0:T(8,128)(2,1)S(1)}, bf16[1024,640]{1,0:T(8,128)(2,1)S(1)}, u32[]{:S(2)}, u32[]{:S(2)}) %collective-permute-start.18) | collective-permute-done | bytes 1310752 | tf_op jit(solution)/shard_map/ppermute | solution.py:22
  65.4 9.0 %collective-permute-done.12.refs_9_ = bf16[1024,512]{1,0:T(8,128)(2,1)} collective-permute-done((bf16[1024,512]{1,0:T(8,128)(2,1)S(1)}, bf16[1024,512]{1,0:T(8,128)(2,1)}, u32[]{:S(2)}, u32[]{:S(2)}) %collective-permute-start.12) | collective-permute-done | bytes 1048608 | tf_op jit(solution)/shard_map/ppermute | solution.py:22
  74.4 3.7 %collective-permute-start.14 = (bf16[1024,512]{1,0:T(8,128)(2,1)}, bf16[1024,512]{1,0:T(8,128)(2,1)}, u32[]{:S(2)}, u32[]{:S(2)}) collective-permute-start(bf16[1024,512]{1,0:T(8,128)(2,1)} %collective-permute-done.12.refs_9_), channel_id=1, source_target_pairs={{0,1},{1,2},{2,3},{3,4},{4,5},{5,6},{6,7},{7,0},{8,9},{9,10},{10,1... | collective-permute-start | bytes 3145736 | tf_op jit(solution)/shard_map/ppermute | solution.py:22
  79.4 1.9 %collective-permute-start.23 = (bf16[1024,384]{1,0:T(8,128)(2,1)S(1)}, bf16[1024,384]{1,0:T(8,128)(2,1)}, u32[]{:S(2)}, u32[]{:S(2)}) collective-permute-start(bf16[1024,384]{1,0:T(8,128)(2,1)S(1)} %shard_map.84.refs_3_), channel_id=1, source_target_pairs={{0,24},{1,25},{2,26},{3,27},{4,28},{5,29},{6,30},{7,31},{8,0},{9,1... | collective-permute-start | bytes 2359304 | tf_op jit(solution)/shard_map/ppermute | solution.py:22
  82.0 11.6 %shard_map.82 = (bf16[768,4096]{1,0:T(8,128)(2,1)}, bf16[768,2176]{1,0:T(8,128)(2,1)}, bf16[768,1408]{1,0:T(8,128)(2,1)}, bf16[768,512]{1,0:T(8,128)(2,1)}) custom-call(s32[2]{0:T(128)} %pad_add_fusion.refs_0_, s32[6]{0:T(128)} %refs_0_.11, s32[32]{0:T(128)} %refs_2_.1, s32[6,32]{1,0:T(8,128)} %refs_3_.1, bf16[1536,4096]{1,0:T(8,128)(2,1)} %all-gather.2.cloned.1.call-done.refs_4_), custom_call_target="tpu_custom_call" | custom-call | bytes 26214400 | tf_op jit(solution)/shard_map/pallas_call | solution.py:109
  93.7 1.6 %collective-permute-done.14.refs_6_ = bf16[1024,512]{1,0:T(8,128)(2,1)} collective-permute-done((bf16[1024,512]{1,0:T(8,128)(2,1)}, bf16[1024,512]{1,0:T(8,128)(2,1)}, u32[]{:S(2)}, u32[]{:S(2)}) %collective-permute-start.14) | collective-permute-done | bytes 1048608 | tf_op jit(solution)/shard_map/ppermute | solution.py:22
  95.3 3.1 %collective-permute-start.16 = (bf16[1024,512]{1,0:T(8,128)(2,1)}, bf16[1024,512]{1,0:T(8,128)(2,1)S(1)}, u32[]{:S(2)}, u32[]{:S(2)}) collective-permute-start(bf16[1024,512]{1,0:T(8,128)(2,1)} %collective-permute-done.14.refs_6_), channel_id=1, source_target_pairs={{0,1},{1,2},{2,3},{3,4},{4,5},{5,6},{6,7},{7,0},{8,9},{9,10},{10,1... | collective-permute-start | bytes 3145736 | tf_op jit(solution)/shard_map/ppermute | solution.py:22
  99.7 1.8 %slice.48 = bf16[512,384]{1,0:T(8,128)(2,1)} slice(bf16[1024,384]{1,0:T(8,128)(2,1)} %collective-permute-done.23.refs_5_), slice={[512:1024], [0:384]} | slice | bytes 786432 | tf_op jit(solution)/shard_map/slice | solution.py:252
  101.5 13.3 %shard_map.86.refs_8_ = f32[768,1024]{1,0:T(8,128)} custom-call(s32[6]{0:T(128)} %refs_0_.11, s32[8]{0:T(128)} %refs_1_.9, bf16[768,4096]{1,0:T(8,128)(2,1)} %get-tuple-element.42.refs_2_, bf16[1024,640]{1,0:T(8,128)(2,1)} %copy-done.1, bf16[1024,640]{1,0:T(8,128)(2,1)} %copy-done.10, bf16[1024,640]{1,0:T(8,128)(2,1)} %copy-done.11, ...), custom_call_target="tpu_custom_call" | custom-call | flops 6442450944 | bytes 23068672 | tf_op jit(solution)/shard_map/pallas_call | solution.py:193
  116.9 4.1 %collective-permute-done.16.refs_5_ = bf16[1024,512]{1,0:T(8,128)(2,1)S(1)} collective-permute-done((bf16[1024,512]{1,0:T(8,128)(2,1)}, bf16[1024,512]{1,0:T(8,128)(2,1)S(1)}, u32[]{:S(2)}, u32[]{:S(2)}) %collective-permute-start.16) | collective-permute-done | bytes 1048608 | tf_op jit(solution)/shard_map/ppermute | solution.py:22
  121.0 3.7 %collective-permute-done.24.refs_3_ = bf16[512,384]{1,0:T(8,128)(2,1)S(1)} collective-permute-done((bf16[512,384]{1,0:T(8,128)(2,1)S(1)}, bf16[512,384]{1,0:T(8,128)(2,1)S(1)}, u32[]{:S(2)}, u32[]{:S(2)}) %collective-permute-start.24) | collective-permute-done | bytes 393248 | tf_op jit(solution)/shard_map/ppermute | solution.py:22
  124.7 1.6 collective-permute-done.25.refs_4_
  127.8 2.6 %collective-permute-start.27 = (bf16[512,512]{1,0:T(8,128)(2,1)S(1)}, bf16[512,512]{1,0:T(8,128)(2,1)}, u32[]{:S(2)}, u32[]{:S(2)}) collective-permute-start(bf16[512,512]{1,0:T(8,128)(2,1)S(1)} %slice.49), channel_id=1, source_target_pairs={{0,7},{1,0},{2,1},{3,2},{4,3},{5,4},{6,5},{7,6},{8,15},{9,8},{10,9... | collective-permute-start | bytes 1572872 | tf_op jit(solution)/shard_map/ppermute | solution.py:22
  130.4 9.6 %shard_map.87.refs_7_ = f32[768,1024]{1,0:T(8,128)} custom-call(s32[6]{0:T(128)} %refs_0_.11, s32[8]{0:T(128)} %refs_1_.9, bf16[768,2176]{1,0:T(8,128)(2,1)} %get-tuple-element.54.refs_2_, bf16[1024,384]{1,0:T(8,128)(2,1)} %copy-done, bf16[1024,384]{1,0:T(8,128)(2,1)} %collective-permute-done.22.refs_4_, bf16[1024,384]{1,0:T(8,128)(2,1)} %collective-permute-done.23.refs_5_, ...), custom_call_target="tpu_custom_call" | custom-call | flops 3422552064 | bytes 16187392 | tf_op jit(solution)/shard_map/pallas_call | solution.py:193
  140.0 7.7 %shard_map.88.refs_5_ = f32[768,1024]{1,0:T(8,128)} custom-call(s32[6]{0:T(128)} %refs_0_.11, s32[8]{0:T(128)} %refs_1_.9, bf16[768,1408]{1,0:T(8,128)(2,1)} %get-tuple-element.53.refs_2_, bf16[512,384]{1,0:T(8,128)(2,1)} %copy-done.8, bf16[512,384]{1,0:T(8,128)(2,1)} %copy-done.9, bf16[1024,512]{1,0:T(8,128)(2,1)} %copy-done.5, ...), custom_call_target="tpu_custom_call" | custom-call | flops 2214592512 | bytes 13434880 | tf_op jit(solution)/shard_map/pallas_call | solution.py:193
  148.5 5.0 %shard_map.89 = bf16[768,1024]{1,0:T(8,128)(2,1)} custom-call(s32[6]{0:T(128)} %refs_0_.11, s32[8]{0:T(128)} %refs_1_.9, bf16[768,512]{1,0:T(8,128)(2,1)} %get-tuple-element.30.refs_2_, bf16[512,512]{1,0:T(8,128)(2,1)} %copy-done.7, bf16[512,512]{1,0:T(8,128)(2,1)} %collective-permute-done.27.refs_4_, f32[768,1024]{1,0:T(8,128)} %shard_map.88.refs_5_), custom_call_target="tpu_custom_call" | custom-call | flops 805306368 | bytes 10223616 | tf_op jit(solution)/shard_map/pallas_call | solution.py:193
  (75 shorter events, 13.4 us)
Async XLA Ops:
  6.5 75.4 %all-gather.2.cloned.1.call-start = ((), (), s32[]{:S(2)}) async-start(), calls=%async_computation | async-start | bytes 14155776 | tf_op jit(solution)/shard_map/all_gather | solution.py:211
  9.2 8.1 %collective-permute-start = (bf16[1024,128]{1,0:T(8,128)(2,1)S(1)}, bf16[1024,128]{1,0:T(8,128)(2,1)S(1)}, u32[]{:S(2)}, u32[]{:S(2)}) collective-permute-start(bf16[1024,128]{1,0:T(8,128)(2,1)S(1)} %copy-done.4), channel_id=1, source_target_pairs={{0,8},{1,9},{2,10},{3,11},{4,12},{5,13},{6,14},{7,15},{8,16},{9,17... | collective-permute-start | bytes 786440 | tf_op jit(solution)/shard_map/ppermute | solution.py:22
  11.3 7.6 %collective-permute-start.1 = (bf16[1024,128]{1,0:T(8,128)(2,1)S(1)}, bf16[1024,128]{1,0:T(8,128)(2,1)S(1)}, u32[]{:S(2)}, u32[]{:S(2)}) collective-permute-start(bf16[1024,128]{1,0:T(8,128)(2,1)S(1)} %copy-done.4), channel_id=1, source_target_pairs={{0,24},{1,25},{2,26},{3,27},{4,28},{5,29},{6,30},{7,31},{8,0},{9,1... | collective-permute-start | bytes 786440 | tf_op jit(solution)/shard_map/ppermute | solution.py:22
  11.4 11.6 %collective-permute-start.2 = (bf16[1024,128]{1,0:T(8,128)(2,1)S(1)}, bf16[1024,128]{1,0:T(8,128)(2,1)S(1)}, u32[]{:S(2)}, u32[]{:S(2)}) collective-permute-start(bf16[1024,128]{1,0:T(8,128)(2,1)S(1)} %copy-done.3), channel_id=1, source_target_pairs={{0,1},{1,2},{2,3},{3,4},{4,5},{5,6},{6,7},{7,0},{8,9},{9,10},{10,1... | collective-permute-start | bytes 786440 | tf_op jit(solution)/shard_map/ppermute | solution.py:22
  13.3 9.7 %collective-permute-start.3 = (bf16[1024,128]{1,0:T(8,128)(2,1)S(1)}, bf16[1024,128]{1,0:T(8,128)(2,1)S(1)}, u32[]{:S(2)}, u32[]{:S(2)}) collective-permute-start(bf16[1024,128]{1,0:T(8,128)(2,1)S(1)} %copy-done.3), channel_id=1, source_target_pairs={{0,7},{1,0},{2,1},{3,2},{4,3},{5,4},{6,5},{7,6},{8,15},{9,8},{10,9... | collective-permute-start | bytes 786440 | tf_op jit(solution)/shard_map/ppermute | solution.py:22
  23.0 8.1 %collective-permute-start.6 = (bf16[1024,128]{1,0:T(8,128)(2,1)S(1)}, bf16[1024,128]{1,0:T(8,128)(2,1)S(1)}, u32[]{:S(2)}, u32[]{:S(2)}) collective-permute-start(bf16[1024,128]{1,0:T(8,128)(2,1)S(1)} %collective-permute-done.2.refs_1_), channel_id=1, source_target_pairs={{0,1},{1,2},{2,3},{3,4},{4,5},{5,6},{6,7},{7,0},{8,9},{9,10},{10,1... | collective-permute-start | bytes 786440 | tf_op jit(solution)/shard_map/ppermute | solution.py:22
  23.0 8.1 %collective-permute-start.7 = (bf16[1024,128]{1,0:T(8,128)(2,1)S(1)}, bf16[1024,128]{1,0:T(8,128)(2,1)S(1)}, u32[]{:S(2)}, u32[]{:S(2)}) collective-permute-start(bf16[1024,128]{1,0:T(8,128)(2,1)S(1)} %collective-permute-done.3.refs_2_), channel_id=1, source_target_pairs={{0,7},{1,0},{2,1},{3,2},{4,3},{5,4},{6,5},{7,6},{8,15},{9,8},{10,9... | collective-permute-start | bytes 786440 | tf_op jit(solution)/shard_map/ppermute | solution.py:22
  26.2 5.1 %collective-permute-start.4 = (bf16[512,128]{1,0:T(8,128)(2,1)S(1)}, bf16[512,128]{1,0:T(8,128)(2,1)S(1)}, u32[]{:S(2)}, u32[]{:S(2)}) collective-permute-start(bf16[512,128]{1,0:T(8,128)(2,1)S(1)} %slice.40), channel_id=1, source_target_pairs={{0,8},{1,9},{2,10},{3,11},{4,12},{5,13},{6,14},{7,15},{8,16},{9,17... | collective-permute-start | bytes 393224 | tf_op jit(solution)/shard_map/ppermute | solution.py:22
  27.9 6.3 %collective-permute-start.5 = (bf16[512,128]{1,0:T(8,128)(2,1)S(1)}, bf16[512,128]{1,0:T(8,128)(2,1)S(1)}, u32[]{:S(2)}, u32[]{:S(2)}) collective-permute-start(bf16[512,128]{1,0:T(8,128)(2,1)S(1)} %slice.41), channel_id=1, source_target_pairs={{0,24},{1,25},{2,26},{3,27},{4,28},{5,29},{6,30},{7,31},{8,0},{9,1... | collective-permute-start | bytes 393224 | tf_op jit(solution)/shard_map/ppermute | solution.py:22
  31.3 47.0 %copy-start.1 = (bf16[1024,640]{1,0:T(8,128)(2,1)}, bf16[1024,640]{1,0:T(8,128)(2,1)S(1)}, u32[]{:S(2)}) copy-start(bf16[1024,640]{1,0:T(8,128)(2,1)S(1)} %shard_map.85.refs_3_) | copy-start | bytes 3932164
  34.1 27.9 %collective-permute-start.18 = (bf16[1024,640]{1,0:T(8,128)(2,1)S(1)}, bf16[1024,640]{1,0:T(8,128)(2,1)S(1)}, u32[]{:S(2)}, u32[]{:S(2)}) collective-permute-start(bf16[1024,640]{1,0:T(8,128)(2,1)S(1)} %shard_map.85.refs_3_), channel_id=1, source_target_pairs={{0,8},{1,9},{2,10},{3,11},{4,12},{5,13},{6,14},{7,15},{8,16},{9,17... | collective-permute-start | bytes 3932168 | tf_op jit(solution)/shard_map/ppermute | solution.py:22
  34.1 29.1 %collective-permute-start.19 = (bf16[1024,640]{1,0:T(8,128)(2,1)S(1)}, bf16[1024,640]{1,0:T(8,128)(2,1)S(1)}, u32[]{:S(2)}, u32[]{:S(2)}) collective-permute-start(bf16[1024,640]{1,0:T(8,128)(2,1)S(1)} %shard_map.85.refs_3_), channel_id=1, source_target_pairs={{0,24},{1,25},{2,26},{3,27},{4,28},{5,29},{6,30},{7,31},{8,0},{9,1... | collective-permute-start | bytes 3932168 | tf_op jit(solution)/shard_map/ppermute | solution.py:22
  36.2 7.7 %collective-permute-start.8 = (bf16[1024,128]{1,0:T(8,128)(2,1)S(1)}, bf16[1024,128]{1,0:T(8,128)(2,1)S(1)}, u32[]{:S(2)}, u32[]{:S(2)}) collective-permute-start(bf16[1024,128]{1,0:T(8,128)(2,1)S(1)} %collective-permute-done.6.refs_3_), channel_id=1, source_target_pairs={{0,1},{1,2},{2,3},{3,4},{4,5},{5,6},{6,7},{7,0},{8,9},{9,10},{10,1... | collective-permute-start | bytes 786440 | tf_op jit(solution)/shard_map/ppermute | solution.py:22
  36.2 7.7 %collective-permute-start.9 = (bf16[1024,128]{1,0:T(8,128)(2,1)S(1)}, bf16[1024,128]{1,0:T(8,128)(2,1)S(1)}, u32[]{:S(2)}, u32[]{:S(2)}) collective-permute-start(bf16[1024,128]{1,0:T(8,128)(2,1)S(1)} %collective-permute-done.7.refs_4_), channel_id=1, source_target_pairs={{0,7},{1,0},{2,1},{3,2},{4,3},{5,4},{6,5},{7,6},{8,15},{9,8},{10,9... | collective-permute-start | bytes 786440 | tf_op jit(solution)/shard_map/ppermute | solution.py:22
  43.9 7.2 %collective-permute-start.10 = (bf16[512,128]{1,0:T(8,128)(2,1)S(1)}, bf16[512,128]{1,0:T(8,128)(2,1)S(1)}, u32[]{:S(2)}, u32[]{:S(2)}) collective-permute-start(bf16[512,128]{1,0:T(8,128)(2,1)S(1)} %slice.42), channel_id=1, source_target_pairs={{0,1},{1,2},{2,3},{3,4},{4,5},{5,6},{6,7},{7,0},{8,9},{9,10},{10,1... | collective-permute-start | bytes 393224 | tf_op jit(solution)/shard_map/ppermute | solution.py:22
  45.0 6.1 %collective-permute-start.11 = (bf16[512,128]{1,0:T(8,128)(2,1)S(1)}, bf16[512,128]{1,0:T(8,128)(2,1)S(1)}, u32[]{:S(2)}, u32[]{:S(2)}) collective-permute-start(bf16[512,128]{1,0:T(8,128)(2,1)S(1)} %slice.43), channel_id=1, source_target_pairs={{0,7},{1,0},{2,1},{3,2},{4,3},{5,4},{6,5},{7,6},{8,15},{9,8},{10,9... | collective-permute-start | bytes 393224 | tf_op jit(solution)/shard_map/ppermute | solution.py:22
  47.6 46.1 %copy-start.2 = (bf16[1024,512]{1,0:T(8,128)(2,1)}, bf16[1024,512]{1,0:T(8,128)(2,1)S(1)}, u32[]{:S(2)}) copy-start(bf16[1024,512]{1,0:T(8,128)(2,1)S(1)} %shard_map.83.refs_8_) | copy-start | bytes 3145732
  51.1 23.3 %collective-permute-start.12 = (bf16[1024,512]{1,0:T(8,128)(2,1)S(1)}, bf16[1024,512]{1,0:T(8,128)(2,1)}, u32[]{:S(2)}, u32[]{:S(2)}) collective-permute-start(bf16[1024,512]{1,0:T(8,128)(2,1)S(1)} %shard_map.83.refs_8_), channel_id=1, source_target_pairs={{0,1},{1,2},{2,3},{3,4},{4,5},{5,6},{6,7},{7,0},{8,9},{9,10},{10,1... | collective-permute-start | bytes 3145736 | tf_op jit(solution)/shard_map/ppermute | solution.py:22
  55.0 19.4 %collective-permute-start.13 = (bf16[1024,512]{1,0:T(8,128)(2,1)S(1)}, bf16[1024,512]{1,0:T(8,128)(2,1)}, u32[]{:S(2)}, u32[]{:S(2)}) collective-permute-start(bf16[1024,512]{1,0:T(8,128)(2,1)S(1)} %shard_map.83.refs_8_), channel_id=1, source_target_pairs={{0,7},{1,0},{2,1},{3,2},{4,3},{5,4},{6,5},{7,6},{8,15},{9,8},{10,9... | collective-permute-start | bytes 3145736 | tf_op jit(solution)/shard_map/ppermute | solution.py:22
  63.3 15.0 %collective-permute-start.20 = (bf16[512,640]{1,0:T(8,128)(2,1)S(1)}, bf16[512,640]{1,0:T(8,128)(2,1)S(1)}, u32[]{:S(2)}, u32[]{:S(2)}) collective-permute-start(bf16[512,640]{1,0:T(8,128)(2,1)S(1)} %slice.45), channel_id=1, source_target_pairs={{0,8},{1,9},{2,10},{3,11},{4,12},{5,13},{6,14},{7,15},{8,16},{9,17... | collective-permute-start | bytes 1966088 | tf_op jit(solution)/shard_map/ppermute | solution.py:22
  64.7 14.6 %collective-permute-start.21 = (bf16[512,640]{1,0:T(8,128)(2,1)S(1)}, bf16[512,640]{1,0:T(8,128)(2,1)S(1)}, u32[]{:S(2)}, u32[]{:S(2)}) collective-permute-start(bf16[512,640]{1,0:T(8,128)(2,1)S(1)} %slice.46), channel_id=1, source_target_pairs={{0,24},{1,25},{2,26},{3,27},{4,28},{5,29},{6,30},{7,31},{8,0},{9,1... | collective-permute-start | bytes 1966088 | tf_op jit(solution)/shard_map/ppermute | solution.py:22
  74.4 20.9 %collective-permute-start.14 = (bf16[1024,512]{1,0:T(8,128)(2,1)}, bf16[1024,512]{1,0:T(8,128)(2,1)}, u32[]{:S(2)}, u32[]{:S(2)}) collective-permute-start(bf16[1024,512]{1,0:T(8,128)(2,1)} %collective-permute-done.12.refs_9_), channel_id=1, source_target_pairs={{0,1},{1,2},{2,3},{3,4},{4,5},{5,6},{6,7},{7,0},{8,9},{9,10},{10,1... | collective-permute-start | bytes 3145736 | tf_op jit(solution)/shard_map/ppermute | solution.py:22
  78.1 17.2 %collective-permute-start.15 = (bf16[1024,512]{1,0:T(8,128)(2,1)}, bf16[1024,512]{1,0:T(8,128)(2,1)}, u32[]{:S(2)}, u32[]{:S(2)}) collective-permute-start(bf16[1024,512]{1,0:T(8,128)(2,1)} %collective-permute-done.13.refs_10_), channel_id=1, source_target_pairs={{0,7},{1,0},{2,1},{3,2},{4,3},{5,4},{6,5},{7,6},{8,15},{9,8},{10,9... | collective-permute-start | bytes 3145736 | tf_op jit(solution)/shard_map/ppermute | solution.py:22
  79.3 19.3 %collective-permute-start.22 = (bf16[1024,384]{1,0:T(8,128)(2,1)S(1)}, bf16[1024,384]{1,0:T(8,128)(2,1)}, u32[]{:S(2)}, u32[]{:S(2)}) collective-permute-start(bf16[1024,384]{1,0:T(8,128)(2,1)S(1)} %shard_map.84.refs_3_), channel_id=1, source_target_pairs={{0,8},{1,9},{2,10},{3,11},{4,12},{5,13},{6,14},{7,15},{8,16},{9,17... | collective-permute-start | bytes 2359304 | tf_op jit(solution)/shard_map/ppermute | solution.py:22
  79.4 20.2 %collective-permute-start.23 = (bf16[1024,384]{1,0:T(8,128)(2,1)S(1)}, bf16[1024,384]{1,0:T(8,128)(2,1)}, u32[]{:S(2)}, u32[]{:S(2)}) collective-permute-start(bf16[1024,384]{1,0:T(8,128)(2,1)S(1)} %shard_map.84.refs_3_), channel_id=1, source_target_pairs={{0,24},{1,25},{2,26},{3,27},{4,28},{5,29},{6,30},{7,31},{8,0},{9,1... | collective-permute-start | bytes 2359304 | tf_op jit(solution)/shard_map/ppermute | solution.py:22
  95.3 25.7 %collective-permute-start.16 = (bf16[1024,512]{1,0:T(8,128)(2,1)}, bf16[1024,512]{1,0:T(8,128)(2,1)S(1)}, u32[]{:S(2)}, u32[]{:S(2)}) collective-permute-start(bf16[1024,512]{1,0:T(8,128)(2,1)} %collective-permute-done.14.refs_6_), channel_id=1, source_target_pairs={{0,1},{1,2},{2,3},{3,4},{4,5},{5,6},{6,7},{7,0},{8,9},{9,10},{10,1... | collective-permute-start | bytes 3145736 | tf_op jit(solution)/shard_map/ppermute | solution.py:22
  98.4 27.9 %collective-permute-start.17 = (bf16[1024,512]{1,0:T(8,128)(2,1)}, bf16[1024,512]{1,0:T(8,128)(2,1)S(1)}, u32[]{:S(2)}, u32[]{:S(2)}) collective-permute-start(bf16[1024,512]{1,0:T(8,128)(2,1)} %collective-permute-done.15.refs_7_), channel_id=1, source_target_pairs={{0,7},{1,0},{2,1},{3,2},{4,3},{5,4},{6,5},{7,6},{8,15},{9,8},{10,9... | collective-permute-start | bytes 3145736 | tf_op jit(solution)/shard_map/ppermute | solution.py:22
  114.8 9.9 %collective-permute-start.24 = (bf16[512,384]{1,0:T(8,128)(2,1)S(1)}, bf16[512,384]{1,0:T(8,128)(2,1)S(1)}, u32[]{:S(2)}, u32[]{:S(2)}) collective-permute-start(bf16[512,384]{1,0:T(8,128)(2,1)S(1)} %slice.47), channel_id=1, source_target_pairs={{0,8},{1,9},{2,10},{3,11},{4,12},{5,13},{6,14},{7,15},{8,16},{9,17... | collective-permute-start | bytes 1179656 | tf_op jit(solution)/shard_map/ppermute | solution.py:22
  116.1 10.2 %collective-permute-start.25 = (bf16[512,384]{1,0:T(8,128)(2,1)}, bf16[512,384]{1,0:T(8,128)(2,1)S(1)}, u32[]{:S(2)}, u32[]{:S(2)}) collective-permute-start(bf16[512,384]{1,0:T(8,128)(2,1)} %slice.48), channel_id=1, source_target_pairs={{0,24},{1,25},{2,26},{3,27},{4,28},{5,29},{6,30},{7,31},{8,0},{9,1... | collective-permute-start | bytes 1179656 | tf_op jit(solution)/shard_map/ppermute | solution.py:22
  121.0 19.0 %copy-start.5 = (bf16[1024,512]{1,0:T(8,128)(2,1)}, bf16[1024,512]{1,0:T(8,128)(2,1)S(1)}, u32[]{:S(2)}) copy-start(bf16[1024,512]{1,0:T(8,128)(2,1)S(1)} %collective-permute-done.16.refs_5_) | copy-start | bytes 3145732
  127.0 20.7 %collective-permute-start.26 = (bf16[512,512]{1,0:T(8,128)(2,1)S(1)}, bf16[512,512]{1,0:T(8,128)(2,1)S(1)}, u32[]{:S(2)}, u32[]{:S(2)}) collective-permute-start(bf16[512,512]{1,0:T(8,128)(2,1)S(1)} %slice.44), channel_id=1, source_target_pairs={{0,1},{1,2},{2,3},{3,4},{4,5},{5,6},{6,7},{7,0},{8,9},{9,10},{10,1... | collective-permute-start | bytes 1572872 | tf_op jit(solution)/shard_map/ppermute | solution.py:22
  127.8 20.0 %collective-permute-start.27 = (bf16[512,512]{1,0:T(8,128)(2,1)S(1)}, bf16[512,512]{1,0:T(8,128)(2,1)}, u32[]{:S(2)}, u32[]{:S(2)}) collective-permute-start(bf16[512,512]{1,0:T(8,128)(2,1)S(1)} %slice.49), channel_id=1, source_target_pairs={{0,7},{1,0},{2,1},{3,2},{4,3},{5,4},{6,5},{7,6},{8,15},{9,8},{10,9... | collective-permute-start | bytes 1572872 | tf_op jit(solution)/shard_map/ppermute | solution.py:22
  (11 other events, 59.4 us)
Sparse Core Ops, SparseCore 0:
  9.4 72.5 all-gather.1

commit v6 on v5

--- a/solution.py
+++ b/solution.py
@@ -212,23 +212,23 @@
 
     z0, y0 = ints_plus, ints_minus
     zu, zd, yu, yd = [go(z0, dz=1)], [go(z0, dz=-1)], [go(y0, dy=1)], [go(y0, dy=-1)]
-    ones = (zu[0], zd[0], yu[0], yd[0])
+    ones = (zu[0], zd[0], yu[0])
     zu.append(go(zu[0], *ones, dz=1))
     zd.append(go(zd[0], *ones, dz=-1))
-    y2 = (go(yu[0][:HALF], *ones, dy=1), go(yd[0][HALF:], *ones, dy=-1))
-    twos = (zu[1], zd[1]) + y2
+    y2 = (go(yu[0], *ones, yd[0], dy=1),)
+    twos = (zu[1], zd[1])
     zu.append(go(zu[1], *twos, dz=1))
     zd.append(go(zd[1], *twos, dz=-1))
     c0 = join([(z0,), (zu[0],), (zd[0],), (zu[1],), (zd[1],)])
-    c1 = (go(c0, *twos, dy=1), go(c0, *twos, dy=-1))
+    c1 = (go(c0, *y2, dy=1), go(c0, *y2, dy=-1))
     w0 = join([(y0,), (yu[0],), (yd[0],), y2])
     threes = (zu[2], zd[2])
-    z4 = (go(zu[2][:HALF], *threes, dz=1), go(zd[2][HALF:], *threes, dz=-1))
+    wu, wd = [go(w0, *threes, dz=1)], [go(w0, *threes, dz=-1)]
+    z4 = (go(zu[2], dz=1),)
     d0 = join([(zu[2],), (zd[2],), z4])
-    wu, wd = [go(w0, *z4, dz=1)], [go(w0, *z4, dz=-1)]
     c2 = (go(c1[0][:HALF], *c1, dy=1), go(c1[1][HALF:], *c1, dy=-1))
-    wu.append(go(wu[0], wd[0], dz=1))
-    wd.append(go(wd[0], wu[0], dz=-1))
+    wu.append(go(wu[0], wd[0], *z4, dz=1))
+    wd.append(go(wd[0], wu[0], *z4, dz=-1))
     d1 = (go(d0, *c2, dy=1), go(d0, *c2, dy=-1))
 
     def plus(offs, y, block=None):
@@ -239,20 +239,20 @@
 
     near, far = (0, -1, 1, -2, 2), (-3, 3, 4)
     groups = [
-        [plus(near, y) for y in (0, -1, 1, 2)] + [minus(z) for z in (0, -1, 1)],
-        [plus(far, y) for y in (0, -1, 1)] + [minus(z) for z in (-2, 2)],
+        [plus(near, y) for y in (0, -1, 1)],
+        [plus(near, 2)] + [plus(far, y) for y in (0, -1, 1)] + [minus(z) for z in (0, -1, 1, -2, 2)],
         [plus(far, 2)] + [minus(z) for z in (-3, 3)],
         [minus(4)],
     ]
     amps = mask(here, sym_ij, sym_cd, amp_mask, raw, groups)
     wu.append(go(wu[1], wd[1], amps[0], dz=1))
     wd.append(go(wd[1], wu[1], amps[0], dz=-1))
-    blocks = [(c0,), c1[:1], c1[1:], c2, (w0,), (wu[0],), (wd[0],)]
+    blocks = [(c0,), c1[:1], c1[1:]]
     total = product(sym_ij, sym_ab, amps[0], [(None, block) for block in blocks])
     d2 = (go(d1[0][:HALF], *d1, total, dy=1), go(d1[1][HALF:], *d1, total, dy=-1))
-    blocks = [(d0,), d1[:1], d1[1:], (wu[1],), (wd[1],)]
+    blocks = [c2, (d0,), d1[:1], d1[1:], (w0,), (wu[0],), (wd[0],), (wu[1],), (wd[1],)]
     total = product(sym_ij, sym_ab, amps[1], [(None, block) for block in blocks], total)
-    w4 = (go(wu[2][:HALF], wd[2], *d2, dz=1), go(wd[2][HALF:], wu[2], *d2, dz=-1))
+    w4 = (go(wu[2][:HALF], wd[2], *d2, total, dz=1), go(wd[2][HALF:], wu[2], *d2, total, dz=-1))
     blocks = [d2, (wu[2],), (wd[2],)]
     total = product(sym_ij, sym_ab, amps[2], [(None, block) for block in blocks], total)
     return product(sym_ij, sym_ab, amps[3], [(None, w4)], total, True)

time: 161 us -> 157 us (0.975)
  starting transfers between devices: 42.6 us -> 36.6 us
  waiting for transfers between devices: 48.4 us -> 50.9 us
    ppermute x28 -> x26, starting transfers between devices: 42.6 us -> 36.6 us  [move(): return lax.ppermute(values, 'mem', perm_of(dy, dz))]
    ppermute x28 -> x26, waiting for transfers between devices: 48.4 us -> 50.9 us  [move(): return lax.ppermute(values, 'mem', perm_of(dy, dz))]
  transfers between devices with their start and end apart: 29 -> 27, of which waited for: 15 -> 14; matrix products, arithmetic and copies ran while one was open for 2% -> 2% of each run, Pallas kernels for 27% -> 27%
where the time goes in v6:
time: 157 us; the launch traced here: 156 us
  waiting for transfers between devices  50.9 us (32%)
  Pallas kernels  47.8 us (30%)
  starting transfers between devices  36.6 us (23%)
  between operations  13.6 us (9%)
  local copies, waits for them, and re-layouts  3.93 us (3%)
  other arithmetic  3.32 us (2%)
    ppermute x26, waiting for transfers between devices, move(): return lax.ppermute(values, 'mem', perm_of(dy, dz))  50.9 us
    ppermute x26, starting transfers between devices, move(): return lax.ppermute(values, 'mem', perm_of(dy, dz))  36.6 us
    pallas_call x4, Pallas kernels, product(): pl.pallas_call(kernel, out_shape=jax.ShapeDtypeStruct((768, 1024), BF16 i...  35.7 us
    pallas_call x1, Pallas kernels, mask(): pl.pallas_call(kernel, out_shape=[jax.ShapeDtypeStruct(shape, BF16) for s...  11.6 us
  transfers between devices with their start and end apart: 27, of which 14 were waited for; matrix products, arithmetic and copies ran while one was open for 2% of the time, Pallas kernels for 27%

profile of v6, /device:TPU:24, one launch (start us, length us, event | category | flops | bytes accessed | tf_op | source)
XLA Modules:
  0.0 156.2 jit_solution(11493969183809566585)
XLA Ops:
  6.5 2.7 %pad_maximum_fusion = bf16[1536,512]{1,0:T(8,128)(2,1)} fusion(bf16[768,512]{1,0:T(8,128)(2,1)} %param.9, bf16[768,512]{1,0:T(8,128)(2,1)} %param.8), kind=kLoop, calls=%fused_computation | loop fusion | flops 3145728 | bytes 3145728 | tf_op jit(solution)/shard_map/concatenate | solution.py:211
  9.2 2.0 %collective-permute-start = (bf16[1024,128]{1,0:T(8,128)(2,1)S(1)}, bf16[1024,128]{1,0:T(8,128)(2,1)S(1)}, u32[]{:S(2)}, u32[]{:S(2)}) collective-permute-start(bf16[1024,128]{1,0:T(8,128)(2,1)S(1)} %copy-done.4), channel_id=1, source_target_pairs={{0,8},{1,9},{2,10},{3,11},{4,12},{5,13},{6,14},{7,15},{8,16},{9,17... | collective-permute-start | bytes 786440 | tf_op jit(solution)/shard_map/ppermute | solution.py:22
  11.5 3.9 %collective-permute-start.3 = (bf16[1024,128]{1,0:T(8,128)(2,1)S(1)}, bf16[1024,128]{1,0:T(8,128)(2,1)S(1)}, u32[]{:S(2)}, u32[]{:S(2)}) collective-permute-start(bf16[1024,128]{1,0:T(8,128)(2,1)S(1)} %copy-done.3), channel_id=1, source_target_pairs={{0,7},{1,0},{2,1},{3,2},{4,3},{5,4},{6,5},{7,6},{8,15},{9,8},{10,9... | collective-permute-start | bytes 786440 | tf_op jit(solution)/shard_map/ppermute | solution.py:22
  15.4 1.8 %collective-permute-start.1 = (bf16[1024,128]{1,0:T(8,128)(2,1)S(1)}, bf16[1024,128]{1,0:T(8,128)(2,1)S(1)}, u32[]{:S(2)}, u32[]{:S(2)}) collective-permute-start(bf16[1024,128]{1,0:T(8,128)(2,1)S(1)} %copy-done.4), channel_id=1, source_target_pairs={{0,24},{1,25},{2,26},{3,27},{4,28},{5,29},{6,30},{7,31},{8,0},{9,1... | collective-permute-start | bytes 786440 | tf_op jit(solution)/shard_map/ppermute | solution.py:22
  17.4 4.2 %collective-permute-done.2.refs_1_ = bf16[1024,128]{1,0:T(8,128)(2,1)S(1)} collective-permute-done((bf16[1024,128]{1,0:T(8,128)(2,1)S(1)}, bf16[1024,128]{1,0:T(8,128)(2,1)S(1)}, u32[]{:S(2)}, u32[]{:S(2)}) %collective-permute-start.2) | collective-permute-done | bytes 262176 | tf_op jit(solution)/shard_map/ppermute | solution.py:22
  21.6 3.2 %collective-permute-start.6 = (bf16[1024,128]{1,0:T(8,128)(2,1)S(1)}, bf16[1024,128]{1,0:T(8,128)(2,1)S(1)}, u32[]{:S(2)}, u32[]{:S(2)}) collective-permute-start(bf16[1024,128]{1,0:T(8,128)(2,1)S(1)} %collective-permute-done.3.refs_2_), channel_id=1, source_target_pairs={{0,7},{1,0},{2,1},{3,2},{4,3},{5,4},{6,5},{7,6},{8,15},{9,8},{10,9... | collective-permute-start | bytes 786440 | tf_op jit(solution)/shard_map/ppermute | solution.py:22
  24.8 1.4 collective-permute-start.4
  26.3 3.9 %collective-permute-done.5.refs_3_ = bf16[1024,128]{1,0:T(8,128)(2,1)S(1)} collective-permute-done((bf16[1024,128]{1,0:T(8,128)(2,1)S(1)}, bf16[1024,128]{1,0:T(8,128)(2,1)S(1)}, u32[]{:S(2)}, u32[]{:S(2)}) %collective-permute-start.5) | collective-permute-done | bytes 262176 | tf_op jit(solution)/shard_map/ppermute | solution.py:22
  30.4 1.2 collective-permute-done.4.refs_3_
  31.6 2.5 %collective-permute-start.16 = (bf16[1024,640]{1,0:T(8,128)(2,1)S(1)}, bf16[1024,640]{1,0:T(8,128)(2,1)S(1)}, u32[]{:S(2)}, u32[]{:S(2)}) collective-permute-start(bf16[1024,640]{1,0:T(8,128)(2,1)S(1)} %shard_map.85.refs_3_), channel_id=1, source_target_pairs={{0,8},{1,9},{2,10},{3,11},{4,12},{5,13},{6,14},{7,15},{8,16},{9,17... | collective-permute-start | bytes 3932168 | tf_op jit(solution)/shard_map/ppermute | solution.py:22
  34.3 3.0 %collective-permute-start.8 = (bf16[1024,128]{1,0:T(8,128)(2,1)S(1)}, bf16[1024,128]{1,0:T(8,128)(2,1)S(1)}, u32[]{:S(2)}, u32[]{:S(2)}) collective-permute-start(bf16[1024,128]{1,0:T(8,128)(2,1)S(1)} %collective-permute-done.6.refs_4_), channel_id=1, source_target_pairs={{0,7},{1,0},{2,1},{3,2},{4,3},{5,4},{6,5},{7,6},{8,15},{9,8},{10,9... | collective-permute-start | bytes 786440 | tf_op jit(solution)/shard_map/ppermute | solution.py:22
  37.5 4.2 %collective-permute-done.7.refs_0_ = bf16[1024,128]{1,0:T(8,128)(2,1)S(1)} collective-permute-done((bf16[1024,128]{1,0:T(8,128)(2,1)S(1)}, bf16[1024,128]{1,0:T(8,128)(2,1)S(1)}, u32[]{:S(2)}, u32[]{:S(2)}) %collective-permute-start.7) | collective-permute-done | bytes 262176 | tf_op jit(solution)/shard_map/ppermute | solution.py:22
  41.7 3.2 %collective-permute-start.10 = (bf16[1024,512]{1,0:T(8,128)(2,1)S(1)}, bf16[1024,512]{1,0:T(8,128)(2,1)}, u32[]{:S(2)}, u32[]{:S(2)}) collective-permute-start(bf16[1024,512]{1,0:T(8,128)(2,1)S(1)} %shard_map.83.refs_8_), channel_id=1, source_target_pairs={{0,7},{1,0},{2,1},{3,2},{4,3},{5,4},{6,5},{7,6},{8,15},{9,8},{10,9... | collective-permute-start | bytes 3145736 | tf_op jit(solution)/shard_map/ppermute | solution.py:22
  44.9 15.1 %collective-permute-done.16.refs_4_ = bf16[1024,640]{1,0:T(8,128)(2,1)S(1)} collective-permute-done((bf16[1024,640]{1,0:T(8,128)(2,1)S(1)}, bf16[1024,640]{1,0:T(8,128)(2,1)S(1)}, u32[]{:S(2)}, u32[]{:S(2)}) %collective-permute-start.16) | collective-permute-done | bytes 1310752 | tf_op jit(solution)/shard_map/ppermute | solution.py:22
  60.0 3.2 %collective-permute-done.17.refs_5_ = bf16[1024,640]{1,0:T(8,128)(2,1)S(1)} collective-permute-done((bf16[1024,640]{1,0:T(8,128)(2,1)S(1)}, bf16[1024,640]{1,0:T(8,128)(2,1)S(1)}, u32[]{:S(2)}, u32[]{:S(2)}) %collective-permute-start.17) | collective-permute-done | bytes 1310752 | tf_op jit(solution)/shard_map/ppermute | solution.py:22
  63.3 1.4 collective-permute-start.18
  65.6 7.6 %collective-permute-done.11.refs_2_ = bf16[1024,128]{1,0:T(8,128)(2,1)S(1)} collective-permute-done((bf16[1024,128]{1,0:T(8,128)(2,1)S(1)}, bf16[1024,128]{1,0:T(8,128)(2,1)S(1)}, u32[]{:S(2)}, u32[]{:S(2)}) %collective-permute-start.11) | collective-permute-done | bytes 262176 | tf_op jit(solution)/shard_map/ppermute | solution.py:22
  73.2 2.0 %collective-permute-start.12 = (bf16[1024,512]{1,0:T(8,128)(2,1)}, bf16[1024,512]{1,0:T(8,128)(2,1)}, u32[]{:S(2)}, u32[]{:S(2)}) collective-permute-start(bf16[1024,512]{1,0:T(8,128)(2,1)} %collective-permute-done.9.refs_9_), channel_id=1, source_target_pairs={{0,1},{1,2},{2,3},{3,4},{4,5},{5,6},{6,7},{7,0},{8,9},{9,10},{10,1... | collective-permute-start | bytes 3145736 | tf_op jit(solution)/shard_map/ppermute | solution.py:22
  76.4 3.3 %collective-permute-done.19.refs_4_ = bf16[512,640]{1,0:T(8,128)(2,1)S(1)} collective-permute-done((bf16[512,640]{1,0:T(8,128)(2,1)S(1)}, bf16[512,640]{1,0:T(8,128)(2,1)S(1)}, u32[]{:S(2)}, u32[]{:S(2)}) %collective-permute-start.19) | collective-permute-done | bytes 655392 | tf_op jit(solution)/shard_map/ppermute | solution.py:22
  79.7 3.2 %collective-permute-start.20 = (bf16[1024,384]{1,0:T(8,128)(2,1)S(1)}, bf16[1024,384]{1,0:T(8,128)(2,1)}, u32[]{:S(2)}, u32[]{:S(2)}) collective-permute-start(bf16[1024,384]{1,0:T(8,128)(2,1)S(1)} %shard_map.84.refs_5_), channel_id=1, source_target_pairs={{0,8},{1,9},{2,10},{3,11},{4,12},{5,13},{6,14},{7,15},{8,16},{9,17... | collective-permute-start | bytes 2359304 | tf_op jit(solution)/shard_map/ppermute | solution.py:22
  83.6 11.6 %shard_map.82 = (bf16[768,1920]{1,0:T(8,128)(2,1)}, bf16[768,4352]{1,0:T(8,128)(2,1)}, bf16[768,1408]{1,0:T(8,128)(2,1)}, bf16[768,512]{1,0:T(8,128)(2,1)}) custom-call(s32[2]{0:T(128)} %pad_add_fusion.refs_0_, s32[6]{0:T(128)} %refs_0_.11, s32[32]{0:T(128)} %refs_2_.1, s32[6,32]{1,0:T(8,128)} %refs_3_.1, bf16[1536,4096]{1,0:T(8,128)(2,1)} %all-gather.2.cloned.1.call-done.refs_4_), custom_call_target="tpu_custom_call" | custom-call | bytes 26214400 | tf_op jit(solution)/shard_map/pallas_call | solution.py:109
  95.6 1.3 collective-permute-done.12.refs_11_
  97.1 1.8 %collective-permute-start.14 = (bf16[1024,512]{1,0:T(8,128)(2,1)}, bf16[1024,512]{1,0:T(8,128)(2,1)S(1)}, u32[]{:S(2)}, u32[]{:S(2)}) collective-permute-start(bf16[1024,512]{1,0:T(8,128)(2,1)} %collective-permute-done.12.refs_11_), channel_id=1, source_target_pairs={{0,1},{1,2},{2,3},{3,4},{4,5},{5,6},{6,7},{7,0},{8,9},{9,10},{10,1... | collective-permute-start | bytes 3145736 | tf_op jit(solution)/shard_map/ppermute | solution.py:22
  98.9 1.8 %slice.28 = bf16[512,384]{1,0:T(8,128)(2,1)} slice(bf16[1024,384]{1,0:T(8,128)(2,1)} %collective-permute-done.21.refs_7_), slice={[512:1024], [0:384]} | slice | bytes 786432 | tf_op jit(solution)/shard_map/slice | solution.py:252
  101.7 8.7 %shard_map.86.refs_13_ = f32[768,1024]{1,0:T(8,128)} custom-call(s32[6]{0:T(128)} %refs_0_.11, s32[8]{0:T(128)} %refs_1_.9, bf16[768,1920]{1,0:T(8,128)(2,1)} %get-tuple-element.36.refs_2_, bf16[1024,640]{1,0:T(8,128)(2,1)} %copy-done, bf16[1024,640]{1,0:T(8,128)(2,1)} %copy-done.10, bf16[1024,640]{1,0:T(8,128)(2,1)} %copy-done.11), custom_call_target="tpu_custom_call" | custom-call | flops 3019898880 | bytes 15269888 | tf_op jit(solution)/shard_map/pallas_call | solution.py:193
  111.5 2.3 %collective-permute-start.22 = (bf16[512,384]{1,0:T(8,128)(2,1)S(1)}, bf16[512,384]{1,0:T(8,128)(2,1)S(1)}, u32[]{:S(2)}, u32[]{:S(2)}) collective-permute-start(bf16[512,384]{1,0:T(8,128)(2,1)S(1)} %slice.27), channel_id=1, source_target_pairs={{0,8},{1,9},{2,10},{3,11},{4,12},{5,13},{6,14},{7,15},{8,16},{9,17... | collective-permute-start | bytes 1179656 | tf_op jit(solution)/shard_map/ppermute | solution.py:22
  113.7 14.2 %shard_map.87.refs_7_ = f32[768,1024]{1,0:T(8,128)} custom-call(s32[6]{0:T(128)} %refs_0_.11, s32[8]{0:T(128)} %refs_1_.9, bf16[768,4352]{1,0:T(8,128)(2,1)} %get-tuple-element.45.refs_2_, bf16[512,640]{1,0:T(8,128)(2,1)} %copy-done.12, bf16[512,640]{1,0:T(8,128)(2,1)} %copy-done.13, bf16[1024,384]{1,0:T(8,128)(2,1)} %copy-done.2, ...), custom_call_target="tpu_custom_call" | custom-call | flops 6845104128 | bytes 23986176 | tf_op jit(solution)/shard_map/pallas_call | solution.py:193
  128.9 1.4 collective-permute-start.25
  131.1 7.8 %shard_map.88.refs_5_ = f32[768,1024]{1,0:T(8,128)} custom-call(s32[6]{0:T(128)} %refs_0_.11, s32[8]{0:T(128)} %refs_1_.9, bf16[768,1408]{1,0:T(8,128)(2,1)} %get-tuple-element.48.refs_2_, bf16[512,384]{1,0:T(8,128)(2,1)} %copy-done.9, bf16[512,384]{1,0:T(8,128)(2,1)} %copy-done.8, bf16[1024,512]{1,0:T(8,128)(2,1)} %copy-done.6, ...), custom_call_target="tpu_custom_call" | custom-call | flops 2214592512 | bytes 13434880 | tf_op jit(solution)/shard_map/pallas_call | solution.py:193
  138.9 1.8 %collective-permute-done.25.refs_4_ = bf16[512,512]{1,0:T(8,128)(2,1)S(1)} collective-permute-done((bf16[512,512]{1,0:T(8,128)(2,1)S(1)}, bf16[512,512]{1,0:T(8,128)(2,1)S(1)}, u32[]{:S(2)}, u32[]{:S(2)}) %collective-permute-start.25) | collective-permute-done | bytes 524320 | tf_op jit(solution)/shard_map/ppermute | solution.py:22
  140.7 3.6 %collective-permute-done.24.refs_3_ = bf16[512,512]{1,0:T(8,128)(2,1)} collective-permute-done((bf16[512,512]{1,0:T(8,128)(2,1)S(1)}, bf16[512,512]{1,0:T(8,128)(2,1)}, u32[]{:S(2)}, u32[]{:S(2)}) %collective-permute-start.24) | collective-permute-done | bytes 524320 | tf_op jit(solution)/shard_map/ppermute | solution.py:22
  144.3 5.0 %shard_map.89 = bf16[768,1024]{1,0:T(8,128)(2,1)} custom-call(s32[6]{0:T(128)} %refs_0_.11, s32[8]{0:T(128)} %refs_1_.9, bf16[768,512]{1,0:T(8,128)(2,1)} %get-tuple-element.27.refs_2_, bf16[512,512]{1,0:T(8,128)(2,1)} %collective-permute-done.24.refs_3_, bf16[512,512]{1,0:T(8,128)(2,1)} %copy-done.7, f32[768,1024]{1,0:T(8,128)} %shard_map.88.refs_5_), custom_call_target="tpu_custom_call" | custom-call | flops 805306368 | bytes 10223616 | tf_op jit(solution)/shard_map/pallas_call | solution.py:193
  (67 shorter events, 8.2 us)
Async XLA Ops:
  6.5 4.7 %copy-start.3 = (bf16[1024,128]{1,0:T(8,128)(2,1)S(1)}, bf16[1024,128]{1,0:T(8,128)(2,1)}, u32[]{:S(2)}) copy-start(bf16[1024,128]{1,0:T(8,128)(2,1)} %refs_0_.7) | copy-start | bytes 786436
  6.5 77.1 %all-gather.2.cloned.1.call-start = ((), (), s32[]{:S(2)}) async-start(), calls=%async_computation | async-start | bytes 14155776 | tf_op jit(solution)/shard_map/all_gather | solution.py:211
  9.2 8.1 %collective-permute-start = (bf16[1024,128]{1,0:T(8,128)(2,1)S(1)}, bf16[1024,128]{1,0:T(8,128)(2,1)S(1)}, u32[]{:S(2)}, u32[]{:S(2)}) collective-permute-start(bf16[1024,128]{1,0:T(8,128)(2,1)S(1)} %copy-done.4), channel_id=1, source_target_pairs={{0,8},{1,9},{2,10},{3,11},{4,12},{5,13},{6,14},{7,15},{8,16},{9,17... | collective-permute-start | bytes 786440 | tf_op jit(solution)/shard_map/ppermute | solution.py:22
  11.3 10.3 %collective-permute-start.2 = (bf16[1024,128]{1,0:T(8,128)(2,1)S(1)}, bf16[1024,128]{1,0:T(8,128)(2,1)S(1)}, u32[]{:S(2)}, u32[]{:S(2)}) collective-permute-start(bf16[1024,128]{1,0:T(8,128)(2,1)S(1)} %copy-done.3), channel_id=1, source_target_pairs={{0,1},{1,2},{2,3},{3,4},{4,5},{5,6},{6,7},{7,0},{8,9},{9,10},{10,1... | collective-permute-start | bytes 786440 | tf_op jit(solution)/shard_map/ppermute | solution.py:22
  11.5 10.1 %collective-permute-start.3 = (bf16[1024,128]{1,0:T(8,128)(2,1)S(1)}, bf16[1024,128]{1,0:T(8,128)(2,1)S(1)}, u32[]{:S(2)}, u32[]{:S(2)}) collective-permute-start(bf16[1024,128]{1,0:T(8,128)(2,1)S(1)} %copy-done.3), channel_id=1, source_target_pairs={{0,7},{1,0},{2,1},{3,2},{4,3},{5,4},{6,5},{7,6},{8,15},{9,8},{10,9... | collective-permute-start | bytes 786440 | tf_op jit(solution)/shard_map/ppermute | solution.py:22
  15.4 9.4 %collective-permute-start.1 = (bf16[1024,128]{1,0:T(8,128)(2,1)S(1)}, bf16[1024,128]{1,0:T(8,128)(2,1)S(1)}, u32[]{:S(2)}, u32[]{:S(2)}) collective-permute-start(bf16[1024,128]{1,0:T(8,128)(2,1)S(1)} %copy-done.4), channel_id=1, source_target_pairs={{0,24},{1,25},{2,26},{3,27},{4,28},{5,29},{6,30},{7,31},{8,0},{9,1... | collective-permute-start | bytes 786440 | tf_op jit(solution)/shard_map/ppermute | solution.py:22
  21.6 8.6 %collective-permute-start.5 = (bf16[1024,128]{1,0:T(8,128)(2,1)S(1)}, bf16[1024,128]{1,0:T(8,128)(2,1)S(1)}, u32[]{:S(2)}, u32[]{:S(2)}) collective-permute-start(bf16[1024,128]{1,0:T(8,128)(2,1)S(1)} %collective-permute-done.2.refs_1_), channel_id=1, source_target_pairs={{0,1},{1,2},{2,3},{3,4},{4,5},{5,6},{6,7},{7,0},{8,9},{9,10},{10,1... | collective-permute-start | bytes 786440 | tf_op jit(solution)/shard_map/ppermute | solution.py:22
  21.6 8.6 %collective-permute-start.6 = (bf16[1024,128]{1,0:T(8,128)(2,1)S(1)}, bf16[1024,128]{1,0:T(8,128)(2,1)S(1)}, u32[]{:S(2)}, u32[]{:S(2)}) collective-permute-start(bf16[1024,128]{1,0:T(8,128)(2,1)S(1)} %collective-permute-done.3.refs_2_), channel_id=1, source_target_pairs={{0,7},{1,0},{2,1},{3,2},{4,3},{5,4},{6,5},{7,6},{8,15},{9,8},{10,9... | collective-permute-start | bytes 786440 | tf_op jit(solution)/shard_map/ppermute | solution.py:22
  24.8 6.8 %collective-permute-start.4 = (bf16[1024,128]{1,0:T(8,128)(2,1)S(1)}, bf16[1024,128]{1,0:T(8,128)(2,1)S(1)}, u32[]{:S(2)}, u32[]{:S(2)}) collective-permute-start(bf16[1024,128]{1,0:T(8,128)(2,1)S(1)} %collective-permute-done.refs_1_), channel_id=1, source_target_pairs={{0,8},{1,9},{2,10},{3,11},{4,12},{5,13},{6,14},{7,15},{8,16},{9,17... | collective-permute-start | bytes 786440 | tf_op jit(solution)/shard_map/ppermute | solution.py:22
  30.4 45.0 %copy-start = (bf16[1024,640]{1,0:T(8,128)(2,1)}, bf16[1024,640]{1,0:T(8,128)(2,1)S(1)}, u32[]{:S(2)}) copy-start(bf16[1024,640]{1,0:T(8,128)(2,1)S(1)} %shard_map.85.refs_3_) | copy-start | bytes 3932164
  31.6 28.3 %collective-permute-start.16 = (bf16[1024,640]{1,0:T(8,128)(2,1)S(1)}, bf16[1024,640]{1,0:T(8,128)(2,1)S(1)}, u32[]{:S(2)}, u32[]{:S(2)}) collective-permute-start(bf16[1024,640]{1,0:T(8,128)(2,1)S(1)} %shard_map.85.refs_3_), channel_id=1, source_target_pairs={{0,8},{1,9},{2,10},{3,11},{4,12},{5,13},{6,14},{7,15},{8,16},{9,17... | collective-permute-start | bytes 3932168 | tf_op jit(solution)/shard_map/ppermute | solution.py:22
  34.1 29.2 %collective-permute-start.17 = (bf16[1024,640]{1,0:T(8,128)(2,1)S(1)}, bf16[1024,640]{1,0:T(8,128)(2,1)S(1)}, u32[]{:S(2)}, u32[]{:S(2)}) collective-permute-start(bf16[1024,640]{1,0:T(8,128)(2,1)S(1)} %shard_map.85.refs_3_), channel_id=1, source_target_pairs={{0,24},{1,25},{2,26},{3,27},{4,28},{5,29},{6,30},{7,31},{8,0},{9,1... | collective-permute-start | bytes 3932168 | tf_op jit(solution)/shard_map/ppermute | solution.py:22
  34.1 7.6 %collective-permute-start.7 = (bf16[1024,128]{1,0:T(8,128)(2,1)S(1)}, bf16[1024,128]{1,0:T(8,128)(2,1)S(1)}, u32[]{:S(2)}, u32[]{:S(2)}) collective-permute-start(bf16[1024,128]{1,0:T(8,128)(2,1)S(1)} %collective-permute-done.5.refs_3_), channel_id=1, source_target_pairs={{0,1},{1,2},{2,3},{3,4},{4,5},{5,6},{6,7},{7,0},{8,9},{9,10},{10,1... | collective-permute-start | bytes 786440 | tf_op jit(solution)/shard_map/ppermute | solution.py:22
  34.3 7.3 %collective-permute-start.8 = (bf16[1024,128]{1,0:T(8,128)(2,1)S(1)}, bf16[1024,128]{1,0:T(8,128)(2,1)S(1)}, u32[]{:S(2)}, u32[]{:S(2)}) collective-permute-start(bf16[1024,128]{1,0:T(8,128)(2,1)S(1)} %collective-permute-done.6.refs_4_), channel_id=1, source_target_pairs={{0,7},{1,0},{2,1},{3,2},{4,3},{5,4},{6,5},{7,6},{8,15},{9,8},{10,9... | collective-permute-start | bytes 786440 | tf_op jit(solution)/shard_map/ppermute | solution.py:22
  37.5 57.8 %copy-start.1 = (bf16[1024,512]{1,0:T(8,128)(2,1)}, bf16[1024,512]{1,0:T(8,128)(2,1)S(1)}, u32[]{:S(2)}) copy-start(bf16[1024,512]{1,0:T(8,128)(2,1)S(1)} %shard_map.83.refs_8_) | copy-start | bytes 3145732
  41.7 31.5 %collective-permute-start.10 = (bf16[1024,512]{1,0:T(8,128)(2,1)S(1)}, bf16[1024,512]{1,0:T(8,128)(2,1)}, u32[]{:S(2)}, u32[]{:S(2)}) collective-permute-start(bf16[1024,512]{1,0:T(8,128)(2,1)S(1)} %shard_map.83.refs_8_), channel_id=1, source_target_pairs={{0,7},{1,0},{2,1},{3,2},{4,3},{5,4},{6,5},{7,6},{8,15},{9,8},{10,9... | collective-permute-start | bytes 3145736 | tf_op jit(solution)/shard_map/ppermute | solution.py:22
  44.9 28.3 %collective-permute-start.9 = (bf16[1024,512]{1,0:T(8,128)(2,1)S(1)}, bf16[1024,512]{1,0:T(8,128)(2,1)}, u32[]{:S(2)}, u32[]{:S(2)}) collective-permute-start(bf16[1024,512]{1,0:T(8,128)(2,1)S(1)} %shard_map.83.refs_8_), channel_id=1, source_target_pairs={{0,1},{1,2},{2,3},{3,4},{4,5},{5,6},{6,7},{7,0},{8,9},{9,10},{10,1... | collective-permute-start | bytes 3145736 | tf_op jit(solution)/shard_map/ppermute | solution.py:22
  63.3 16.5 %copy-start.11 = (bf16[1024,640]{1,0:T(8,128)(2,1)}, bf16[1024,640]{1,0:T(8,128)(2,1)S(1)}, u32[]{:S(2)}) copy-start(bf16[1024,640]{1,0:T(8,128)(2,1)S(1)} %collective-permute-done.17.refs_5_) | copy-start | bytes 3932164
  63.3 13.1 %collective-permute-start.18 = (bf16[512,640]{1,0:T(8,128)(2,1)S(1)}, bf16[512,640]{1,0:T(8,128)(2,1)S(1)}, u32[]{:S(2)}, u32[]{:S(2)}) collective-permute-start(bf16[512,640]{1,0:T(8,128)(2,1)S(1)} %slice.25), channel_id=1, source_target_pairs={{0,8},{1,9},{2,10},{3,11},{4,12},{5,13},{6,14},{7,15},{8,16},{9,17... | collective-permute-start | bytes 1966088 | tf_op jit(solution)/shard_map/ppermute | solution.py:22
  64.7 15.0 %collective-permute-start.19 = (bf16[512,640]{1,0:T(8,128)(2,1)S(1)}, bf16[512,640]{1,0:T(8,128)(2,1)S(1)}, u32[]{:S(2)}, u32[]{:S(2)}) collective-permute-start(bf16[512,640]{1,0:T(8,128)(2,1)S(1)} %slice.26), channel_id=1, source_target_pairs={{0,24},{1,25},{2,26},{3,27},{4,28},{5,29},{6,30},{7,31},{8,0},{9,1... | collective-permute-start | bytes 1966088 | tf_op jit(solution)/shard_map/ppermute | solution.py:22
  65.6 7.6 %collective-permute-start.11 = (bf16[1024,128]{1,0:T(8,128)(2,1)S(1)}, bf16[1024,128]{1,0:T(8,128)(2,1)S(1)}, u32[]{:S(2)}, u32[]{:S(2)}) collective-permute-start(bf16[1024,128]{1,0:T(8,128)(2,1)S(1)} %collective-permute-done.7.refs_0_), channel_id=1, source_target_pairs={{0,1},{1,2},{2,3},{3,4},{4,5},{5,6},{6,7},{7,0},{8,9},{9,10},{10,1... | collective-permute-start | bytes 786440 | tf_op jit(solution)/shard_map/ppermute | solution.py:22
  73.2 22.4 %collective-permute-start.13 = (bf16[1024,512]{1,0:T(8,128)(2,1)}, bf16[1024,512]{1,0:T(8,128)(2,1)}, u32[]{:S(2)}, u32[]{:S(2)}) collective-permute-start(bf16[1024,512]{1,0:T(8,128)(2,1)} %collective-permute-done.10.refs_10_), channel_id=1, source_target_pairs={{0,7},{1,0},{2,1},{3,2},{4,3},{5,4},{6,5},{7,6},{8,15},{9,8},{10,9... | collective-permute-start | bytes 3145736 | tf_op jit(solution)/shard_map/ppermute | solution.py:22
  73.2 23.7 %collective-permute-start.12 = (bf16[1024,512]{1,0:T(8,128)(2,1)}, bf16[1024,512]{1,0:T(8,128)(2,1)}, u32[]{:S(2)}, u32[]{:S(2)}) collective-permute-start(bf16[1024,512]{1,0:T(8,128)(2,1)} %collective-permute-done.9.refs_9_), channel_id=1, source_target_pairs={{0,1},{1,2},{2,3},{3,4},{4,5},{5,6},{6,7},{7,0},{8,9},{9,10},{10,1... | collective-permute-start | bytes 3145736 | tf_op jit(solution)/shard_map/ppermute | solution.py:22
  75.4 19.9 %copy-start.2 = (bf16[1024,384]{1,0:T(8,128)(2,1)}, bf16[1024,384]{1,0:T(8,128)(2,1)S(1)}, u32[]{:S(2)}) copy-start(bf16[1024,384]{1,0:T(8,128)(2,1)S(1)} %shard_map.84.refs_5_) | copy-start | bytes 2359300
  79.7 19.2 %collective-permute-start.21 = (bf16[1024,384]{1,0:T(8,128)(2,1)S(1)}, bf16[1024,384]{1,0:T(8,128)(2,1)}, u32[]{:S(2)}, u32[]{:S(2)}) collective-permute-start(bf16[1024,384]{1,0:T(8,128)(2,1)S(1)} %shard_map.84.refs_5_), channel_id=1, source_target_pairs={{0,24},{1,25},{2,26},{3,27},{4,28},{5,29},{6,30},{7,31},{8,0},{9,1... | collective-permute-start | bytes 2359304 | tf_op jit(solution)/shard_map/ppermute | solution.py:22
  79.7 20.9 %collective-permute-start.20 = (bf16[1024,384]{1,0:T(8,128)(2,1)S(1)}, bf16[1024,384]{1,0:T(8,128)(2,1)}, u32[]{:S(2)}, u32[]{:S(2)}) collective-permute-start(bf16[1024,384]{1,0:T(8,128)(2,1)S(1)} %shard_map.84.refs_5_), channel_id=1, source_target_pairs={{0,8},{1,9},{2,10},{3,11},{4,12},{5,13},{6,14},{7,15},{8,16},{9,17... | collective-permute-start | bytes 2359304 | tf_op jit(solution)/shard_map/ppermute | solution.py:22
  96.9 31.1 %collective-permute-start.15 = (bf16[1024,512]{1,0:T(8,128)(2,1)}, bf16[1024,512]{1,0:T(8,128)(2,1)S(1)}, u32[]{:S(2)}, u32[]{:S(2)}) collective-permute-start(bf16[1024,512]{1,0:T(8,128)(2,1)} %collective-permute-done.13.refs_12_), channel_id=1, source_target_pairs={{0,7},{1,0},{2,1},{3,2},{4,3},{5,4},{6,5},{7,6},{8,15},{9,8},{10,9... | collective-permute-start | bytes 3145736 | tf_op jit(solution)/shard_map/ppermute | solution.py:22
  97.1 31.0 %collective-permute-start.14 = (bf16[1024,512]{1,0:T(8,128)(2,1)}, bf16[1024,512]{1,0:T(8,128)(2,1)S(1)}, u32[]{:S(2)}, u32[]{:S(2)}) collective-permute-start(bf16[1024,512]{1,0:T(8,128)(2,1)} %collective-permute-done.12.refs_11_), channel_id=1, source_target_pairs={{0,1},{1,2},{2,3},{3,4},{4,5},{5,6},{6,7},{7,0},{8,9},{9,10},{10,1... | collective-permute-start | bytes 3145736 | tf_op jit(solution)/shard_map/ppermute | solution.py:22
  110.4 17.6 %collective-permute-start.23 = (bf16[512,384]{1,0:T(8,128)(2,1)}, bf16[512,384]{1,0:T(8,128)(2,1)S(1)}, u32[]{:S(2)}, u32[]{:S(2)}) collective-permute-start(bf16[512,384]{1,0:T(8,128)(2,1)} %slice.28), channel_id=1, source_target_pairs={{0,24},{1,25},{2,26},{3,27},{4,28},{5,29},{6,30},{7,31},{8,0},{9,1... | collective-permute-start | bytes 1179656 | tf_op jit(solution)/shard_map/ppermute | solution.py:22
  111.5 16.6 %collective-permute-start.22 = (bf16[512,384]{1,0:T(8,128)(2,1)S(1)}, bf16[512,384]{1,0:T(8,128)(2,1)S(1)}, u32[]{:S(2)}, u32[]{:S(2)}) collective-permute-start(bf16[512,384]{1,0:T(8,128)(2,1)S(1)} %slice.27), channel_id=1, source_target_pairs={{0,8},{1,9},{2,10},{3,11},{4,12},{5,13},{6,14},{7,15},{8,16},{9,17... | collective-permute-start | bytes 1179656 | tf_op jit(solution)/shard_map/ppermute | solution.py:22
  128.9 11.8 %collective-permute-start.25 = (bf16[512,512]{1,0:T(8,128)(2,1)S(1)}, bf16[512,512]{1,0:T(8,128)(2,1)S(1)}, u32[]{:S(2)}, u32[]{:S(2)}) collective-permute-start(bf16[512,512]{1,0:T(8,128)(2,1)S(1)} %slice.29), channel_id=1, source_target_pairs={{0,7},{1,0},{2,1},{3,2},{4,3},{5,4},{6,5},{7,6},{8,15},{9,8},{10,9... | collective-permute-start | bytes 1572872 | tf_op jit(solution)/shard_map/ppermute | solution.py:22
  130.4 14.0 %collective-permute-start.24 = (bf16[512,512]{1,0:T(8,128)(2,1)S(1)}, bf16[512,512]{1,0:T(8,128)(2,1)}, u32[]{:S(2)}, u32[]{:S(2)}) collective-permute-start(bf16[512,512]{1,0:T(8,128)(2,1)S(1)} %slice.24), channel_id=1, source_target_pairs={{0,1},{1,2},{2,3},{3,4},{4,5},{5,6},{6,7},{7,0},{8,9},{9,10},{10,1... | collective-permute-start | bytes 1572872 | tf_op jit(solution)/shard_map/ppermute | solution.py:22
  (9 other events, 25.5 us)
Sparse Core Ops, SparseCore 0:
  9.4 72.5 all-gather.1

commit v7 on v6

--- a/solution.py
+++ b/solution.py
@@ -73,10 +73,6 @@
     return lax.dot_general(left, right, (((1,), (1,)), ((), ())), preferred_element_type=F32)
 
 
-def tiles_of(terms):
-    return [tile for tiles, _ in terms for tile in tiles]
-
-
 def mask_kernel(parts, here_ref, ij_ref, cd_ref, mask_ref, raw_hbm, *refs):
     outs, raw, laid, sem = refs[:len(parts)], refs[-2 - len(parts)], refs[-1 - len(parts):-1], refs[-1]
     fetch = pltpu.make_async_copy(raw_hbm, raw, sem.at[len(parts)])
@@ -85,13 +81,13 @@
     fetch.wait()
     copies = []
     for p, (target, tiles) in enumerate(zip(laid, parts)):
-        for k, (panel, off_y, off_z) in enumerate(tiles):
+        for k, (off_y, off_z) in enumerate(tiles):
             tile = 8 * ((y + off_y) & (NY - 1)) + ((z + off_z) & (NZ - 1))
             cols = pl.ds(pl.multiple_of(tile * BLK, BLK), BLK)
             label = cd_ref[tile]
             for row in range(6):
                 on = (ij_ref[row] == label) & (mask_ref[row, tile] == 1)
-                kept = raw[pl.ds(panel * 768 + row * BLK, BLK), cols]
+                kept = raw[row * BLK:(row + 1) * BLK, cols]
                 target[row * BLK:(row + 1) * BLK, k * BLK:(k + 1) * BLK] = jnp.where(on, kept, jnp.zeros_like(kept))
         copies.append(pltpu.make_async_copy(target, outs[p], sem.at[p]))
         copies[-1].start()
@@ -99,8 +95,7 @@
         copy.wait()
 
 
-def mask(here, sym_ij, sym_cd, amp_mask, raw, groups):
-    parts = [tiles_of(terms) for terms in groups]
+def mask(here, sym_ij, sym_cd, amp_mask, raw, *parts):
     shapes = [(768, len(tiles) * BLK) for tiles in parts]
 
     def kernel(*refs):
@@ -111,11 +106,11 @@
         out_shape=[jax.ShapeDtypeStruct(shape, BF16) for shape in shapes],
         in_specs=[SMEM] * 4 + [HBM],
         out_specs=[HBM] * len(shapes),
-        scratch_shapes=[pltpu.VMEM((1536, 4096), BF16)]
+        scratch_shapes=[pltpu.VMEM((768, 4096), BF16)]
         + [pltpu.VMEM(shape, BF16) for shape in shapes]
         + [pltpu.SemaphoreType.DMA((len(shapes) + 1,))],
         compiler_params=params(60),
-        cost_estimate=cost(0, 25 * 2**20),
+        cost_estimate=cost(0, 12 * 2**20),
     )(here, sym_ij, sym_cd, amp_mask, raw)
 
 
@@ -178,10 +173,10 @@
     lax.fori_loop(0, 4, strip, 0)
 
 
-def product(sym_ij, sym_ab, amps, terms, total=None, last=False):
+def product(sym_ij, sym_ab, amps, blocks, total=None, last=False):
     depth = amps.shape[1]
     first = total is None
-    sizes = [len(block) for _, block in terms]
+    sizes = [len(block) for block in blocks]
     n = sum(sizes)
 
     def kernel(*refs):
@@ -198,7 +193,7 @@
         scratch_shapes=scratch + ([] if first else [pltpu.VMEM((768, 1024), F32)]),
         compiler_params=params(60),
         cost_estimate=cost(2 * 768 * 1024 * depth, 8 * 2**20 + 3584 * depth),
-    )(sym_ij, sym_ab, amps, *[array for _, block in terms for array in block], *([] if first else [total]))
+    )(sym_ij, sym_ab, amps, *[array for block in blocks for array in block], *([] if first else [total]))
 
 
 def body(amp_plus, amp_minus, ints_plus, ints_minus, sym_ij, sym_ab, sym_cd, amp_mask):
@@ -208,7 +203,8 @@
     def go(value, *waits, **way):
         return move(after(value, *waits) if waits else value, **way)
 
-    raw = lax.all_gather(jnp.concatenate([amp_plus, amp_minus], axis=0), "grp", axis=1, tiled=True)
+    raw_plus = lax.all_gather(amp_plus, "grp", axis=1, tiled=True)
+    raw_minus = lax.all_gather(amp_minus, "grp", axis=1, tiled=True)
 
     z0, y0 = ints_plus, ints_minus
     zu, zd, yu, yd = [go(z0, dz=1)], [go(z0, dz=-1)], [go(y0, dy=1)], [go(y0, dy=-1)]
@@ -227,35 +223,33 @@
     z4 = (go(zu[2], dz=1),)
     d0 = join([(zu[2],), (zd[2],), z4])
     c2 = (go(c1[0][:HALF], *c1, dy=1), go(c1[1][HALF:], *c1, dy=-1))
-    wu.append(go(wu[0], wd[0], *z4, dz=1))
-    wd.append(go(wd[0], wu[0], *z4, dz=-1))
-    d1 = (go(d0, *c2, dy=1), go(d0, *c2, dy=-1))
-
-    def plus(offs, y, block=None):
-        return [(0, y, z) for z in offs], block
-
-    def minus(z, block=None):
-        return [(1, y, z) for y in (0, -1, 1, 2)], block
-
+    wu.append(go(wu[0], wd[0], *z4, *c1, dz=1))
+    wd.append(go(wd[0], wu[0], *z4, *c1, dz=-1))
+
+    def plus(offs, *ys):
+        return [(y, z) for y in ys for z in offs]
+
+    def minus(*zs):
+        return [(y, z) for z in zs for y in (0, -1, 1, 2)]
+
+    def add(amps, blocks, *rest):
+        return product(sym_ij, sym_ab, amps, blocks, *rest)
+
+    labels = (here, sym_ij, sym_cd, amp_mask)
     near, far = (0, -1, 1, -2, 2), (-3, 3, 4)
-    groups = [
-        [plus(near, y) for y in (0, -1, 1)],
-        [plus(near, 2)] + [plus(far, y) for y in (0, -1, 1)] + [minus(z) for z in (0, -1, 1, -2, 2)],
-        [plus(far, 2)] + [minus(z) for z in (-3, 3)],
-        [minus(4)],
-    ]
-    amps = mask(here, sym_ij, sym_cd, amp_mask, raw, groups)
-    wu.append(go(wu[1], wd[1], amps[0], dz=1))
-    wd.append(go(wd[1], wu[1], amps[0], dz=-1))
-    blocks = [(c0,), c1[:1], c1[1:]]
-    total = product(sym_ij, sym_ab, amps[0], [(None, block) for block in blocks])
-    d2 = (go(d1[0][:HALF], *d1, total, dy=1), go(d1[1][HALF:], *d1, total, dy=-1))
-    blocks = [c2, (d0,), d1[:1], d1[1:], (w0,), (wu[0],), (wd[0],), (wu[1],), (wd[1],)]
-    total = product(sym_ij, sym_ab, amps[1], [(None, block) for block in blocks], total)
+    tp = mask(*labels, raw_plus, plus(near, 0, -1, 1), plus(near, 2) + plus(far, 0), plus(far, -1, 1, 2))
+    total = add(tp[0], [(c0,), c1[:1], c1[1:]])
+    d1 = (go(d0, *c2, total, dy=1), go(d0, *c2, total, dy=-1))
+    total = add(tp[1], [c2, (d0,)], total)
+    wu.append(go(wu[1], wd[1], total, dz=1))
+    wd.append(go(wd[1], wu[1], total, dz=-1))
+    tm = mask(*labels, raw_minus, minus(0, -1, 1, -2, 2), minus(-3, 3), minus(4))
+    d2 = (go(d1[0][:HALF], *d1, tm[0], dy=1), go(d1[1][HALF:], *d1, tm[0], dy=-1))
+    total = add(tm[0], [(w0,), (wu[0],), (wd[0],), (wu[1],), (wd[1],)], total)
     w4 = (go(wu[2][:HALF], wd[2], *d2, total, dz=1), go(wd[2][HALF:], wu[2], *d2, total, dz=-1))
-    blocks = [d2, (wu[2],), (wd[2],)]
-    total = product(sym_ij, sym_ab, amps[2], [(None, block) for block in blocks], total)
-    return product(sym_ij, sym_ab, amps[3], [(None, w4)], total, True)
+    total = add(tp[2], [d1[:1], d1[1:], d2], total)
+    total = add(tm[1], [(wu[2],), (wd[2],)], total)
+    return add(tm[2], [w4], total, True)
 
 
 def solution(mesh):

time: 157 us -> 165 us (1.051); the launches traced: 156 us -> 162 us
  waiting for transfers between devices: 50.9 us -> 37.7 us
  Pallas kernels: 47.8 us -> 59.5 us
  local copies, waits for them, and re-layouts: 3.93 us -> 10.9 us
  starting transfers between devices: 36.6 us -> 39.7 us
  other arithmetic: 3.32 us -> 0.59 us
    ppermute x26, waiting for transfers between devices: 50.9 us -> 36.3 us  [move(): return lax.ppermute(values, 'mem', perm_of(dy, dz))]
    pallas_call x4 -> x6, Pallas kernels: 35.7 us -> 44.5 us  [product(): pl.pallas_call(kernel, out_shape=jax.ShapeDtypeStruct((768, 1024), BF16 i...]
    unnamed x28 -> x30, local copies, waits for them, and re-layouts: 0.93 us -> 5.37 us
    ppermute x26, starting transfers between devices: 36.6 us -> 39.6 us  [move(): return lax.ppermute(values, 'mem', perm_of(dy, dz))]
    pallas_call x1 -> x2, Pallas kernels: 11.6 us -> 14.5 us  [mask(): pl.pallas_call(kernel, out_shape=[jax.ShapeDtypeStruct(shape, BF16) for s...]
    concatenate x1 -> x0, other arithmetic: 2.67 us -> none  [body(): jnp.concatenate([amp_plus, amp_minus], axis=0)]
    slice x2, local copies, waits for them, and re-layouts: 0.11 us -> 1.84 us  [body(): c2 = (go(c1[0][:HALF], *c1, dy=1), go(c1[1][HALF:], *c1, dy=-1))]
  transfers between devices with their start and end apart: 27 -> 28, of which waited for: 14 -> 4; matrix products, arithmetic and copies ran while one was open for 2% -> 4% of each run, Pallas kernels for 27% -> 34%
where the time goes in v7:
time: 165 us; the launch traced here: 162 us
  Pallas kernels  59.5 us (36%)
  starting transfers between devices  39.7 us (24%)
  waiting for transfers between devices  37.7 us (23%)
  between operations  13.8 us (8%)
  local copies, waits for them, and re-layouts  10.9 us (7%)
    pallas_call x6, Pallas kernels, product(): pl.pallas_call(kernel, out_shape=jax.ShapeDtypeStruct((768, 1024), BF16 i...  44.5 us
    ppermute x26, starting transfers between devices, move(): return lax.ppermute(values, 'mem', perm_of(dy, dz))  39.6 us
    ppermute x26, waiting for transfers between devices, move(): return lax.ppermute(values, 'mem', perm_of(dy, dz))  36.3 us
    pallas_call x2, Pallas kernels, mask(): pl.pallas_call(kernel, out_shape=[jax.ShapeDtypeStruct(shape, BF16) for s...  14.5 us
    unnamed x30, local copies, waits for them, and re-layouts  5.37 us
  transfers between devices with their start and end apart: 28, of which 4 were waited for; matrix products, arithmetic and copies ran while one was open for 4% of the time, Pallas kernels for 34%

profile of v7, /device:TPU:24, one launch (start us, length us, event | category | flops | bytes accessed | tf_op | source)
XLA Modules:
  0.0 162.2 jit_solution(11975920220517789793)
XLA Ops:
  8.0 2.0 %collective-permute-start.2 = (bf16[1024,128]{1,0:T(8,128)(2,1)}, bf16[1024,128]{1,0:T(8,128)(2,1)S(1)}, u32[]{:S(2)}, u32[]{:S(2)}) collective-permute-start(bf16[1024,128]{1,0:T(8,128)(2,1)} %refs_0_.9), channel_id=1, source_target_pairs={{0,1},{1,2},{2,3},{3,4},{4,5},{5,6},{6,7},{7,0},{8,9},{9,10},{10,1... | collective-permute-start | bytes 786440 | tf_op jit(solution)/shard_map/ppermute | solution.py:22
  10.0 4.0 %collective-permute-start.3 = (bf16[1024,128]{1,0:T(8,128)(2,1)}, bf16[1024,128]{1,0:T(8,128)(2,1)S(1)}, u32[]{:S(2)}, u32[]{:S(2)}) collective-permute-start(bf16[1024,128]{1,0:T(8,128)(2,1)} %refs_0_.9), channel_id=1, source_target_pairs={{0,7},{1,0},{2,1},{3,2},{4,3},{5,4},{6,5},{7,6},{8,15},{9,8},{10,9... | collective-permute-start | bytes 786440 | tf_op jit(solution)/shard_map/ppermute | solution.py:22
  14.3 1.8 %collective-permute-start.1 = (bf16[1024,128]{1,0:T(8,128)(2,1)}, bf16[1024,128]{1,0:T(8,128)(2,1)S(1)}, u32[]{:S(2)}, u32[]{:S(2)}) collective-permute-start(bf16[1024,128]{1,0:T(8,128)(2,1)} %refs_0_.8), channel_id=1, source_target_pairs={{0,24},{1,25},{2,26},{3,27},{4,28},{5,29},{6,30},{7,31},{8,0},{9,1... | collective-permute-start | bytes 786440 | tf_op jit(solution)/shard_map/ppermute | solution.py:22
  16.1 4.4 %collective-permute-done.2.refs_1_ = bf16[1024,128]{1,0:T(8,128)(2,1)S(1)} collective-permute-done((bf16[1024,128]{1,0:T(8,128)(2,1)}, bf16[1024,128]{1,0:T(8,128)(2,1)S(1)}, u32[]{:S(2)}, u32[]{:S(2)}) %collective-permute-start.2) | collective-permute-done | bytes 262176 | tf_op jit(solution)/shard_map/ppermute | solution.py:22
  20.5 1.5 collective-permute-done.refs_1_
  22.0 3.2 %collective-permute-start.6 = (bf16[1024,128]{1,0:T(8,128)(2,1)S(1)}, bf16[1024,128]{1,0:T(8,128)(2,1)S(1)}, u32[]{:S(2)}, u32[]{:S(2)}) collective-permute-start(bf16[1024,128]{1,0:T(8,128)(2,1)S(1)} %collective-permute-done.3.refs_2_), channel_id=1, source_target_pairs={{0,7},{1,0},{2,1},{3,2},{4,3},{5,4},{6,5},{7,6},{8,15},{9,8},{10,9... | collective-permute-start | bytes 786440 | tf_op jit(solution)/shard_map/ppermute | solution.py:22
  25.2 1.5 collective-permute-start.4
  26.7 3.3 %collective-permute-done.5.refs_3_ = bf16[1024,128]{1,0:T(8,128)(2,1)S(1)} collective-permute-done((bf16[1024,128]{1,0:T(8,128)(2,1)S(1)}, bf16[1024,128]{1,0:T(8,128)(2,1)S(1)}, u32[]{:S(2)}, u32[]{:S(2)}) %collective-permute-start.5) | collective-permute-done | bytes 262176 | tf_op jit(solution)/shard_map/ppermute | solution.py:22
  31.0 2.3 %collective-permute-start.8 = (bf16[1024,128]{1,0:T(8,128)(2,1)S(1)}, bf16[1024,128]{1,0:T(8,128)(2,1)S(1)}, u32[]{:S(2)}, u32[]{:S(2)}) collective-permute-start(bf16[1024,128]{1,0:T(8,128)(2,1)S(1)} %collective-permute-done.6.refs_4_), channel_id=1, source_target_pairs={{0,7},{1,0},{2,1},{3,2},{4,3},{5,4},{6,5},{7,6},{8,15},{9,8},{10,9... | collective-permute-start | bytes 786440 | tf_op jit(solution)/shard_map/ppermute | solution.py:22
  33.3 1.0 copy-done.3
  35.4 2.4 %collective-permute-start.12 = (bf16[1024,640]{1,0:T(8,128)(2,1)S(1)}, bf16[1024,640]{1,0:T(8,128)(2,1)S(1)}, u32[]{:S(2)}, u32[]{:S(2)}) collective-permute-start(bf16[1024,640]{1,0:T(8,128)(2,1)S(1)} %shard_map.84.refs_3_), channel_id=1, source_target_pairs={{0,8},{1,9},{2,10},{3,11},{4,12},{5,13},{6,14},{7,15},{8,16},{9,17... | collective-permute-start | bytes 3932168 | tf_op jit(solution)/shard_map/ppermute | solution.py:22
  38.8 2.8 %collective-permute-start.10 = (bf16[1024,512]{1,0:T(8,128)(2,1)S(1)}, bf16[1024,512]{1,0:T(8,128)(2,1)}, u32[]{:S(2)}, u32[]{:S(2)}) collective-permute-start(bf16[1024,512]{1,0:T(8,128)(2,1)S(1)} %shard_map.83.refs_3_), channel_id=1, source_target_pairs={{0,7},{1,0},{2,1},{3,2},{4,3},{5,4},{6,5},{7,6},{8,15},{9,8},{10,9... | collective-permute-start | bytes 3145736 | tf_op jit(solution)/shard_map/ppermute | solution.py:22
  41.6 1.5 collective-permute-start.11
  43.1 27.0 %collective-permute-done.11.refs_2_ = bf16[1024,128]{1,0:T(8,128)(2,1)S(1)} collective-permute-done((bf16[1024,128]{1,0:T(8,128)(2,1)S(1)}, bf16[1024,128]{1,0:T(8,128)(2,1)S(1)}, u32[]{:S(2)}, u32[]{:S(2)}) %collective-permute-start.11) | collective-permute-done | bytes 262176 | tf_op jit(solution)/shard_map/ppermute | solution.py:22
  70.2 3.2 %collective-permute-start.15 = (bf16[1024,512]{1,0:T(8,128)(2,1)}, bf16[1024,512]{1,0:T(8,128)(2,1)}, u32[]{:S(2)}, u32[]{:S(2)}) collective-permute-start(bf16[1024,512]{1,0:T(8,128)(2,1)} %collective-permute-done.10.refs_5_), channel_id=1, source_target_pairs={{0,7},{1,0},{2,1},{3,2},{4,3},{5,4},{6,5},{7,6},{8,15},{9,8},{10,9... | collective-permute-start | bytes 3145736 | tf_op jit(solution)/shard_map/ppermute | solution.py:22
  75.3 1.6 collective-permute-start.16
  77.9 0.9 copy-done.5
  78.9 1.0 copy-done.7
  80.0 7.2 %shard_map.85 = (bf16[768,1920]{1,0:T(8,128)(2,1)}, bf16[768,1024]{1,0:T(8,128)(2,1)}, bf16[768,1152]{1,0:T(8,128)(2,1)}) custom-call(s32[2]{0:T(128)} %pad_add_fusion.refs_0_, s32[6]{0:T(128)} %refs_0_.15, s32[32]{0:T(128)} %refs_2_.3, s32[6,32]{1,0:T(8,128)} %refs_3_.3, bf16[768,4096]{1,0:T(8,128)(2,1)} %all-gather.5.cloned.1.call-done.refs_4_), custom_call_target="tpu_custom_call" | custom-call | bytes 12582912 | tf_op jit(solution)/shard_map/pallas_call | solution.py:104
  87.2 8.7 %shard_map.87.refs_6_ = f32[768,1024]{1,0:T(8,128)} custom-call(s32[6]{0:T(128)} %refs_0_.15, s32[8]{0:T(128)} %refs_1_.15, bf16[768,1920]{1,0:T(8,128)(2,1)} %get-tuple-element.42.refs_2_, bf16[1024,640]{1,0:T(8,128)(2,1)} %copy-done.2, bf16[1024,640]{1,0:T(8,128)(2,1)} %copy-done.14, bf16[1024,640]{1,0:T(8,128)(2,1)} %copy-done.13), custom_call_target="tpu_custom_call" | custom-call | flops 3019898880 | bytes 15269888 | tf_op jit(solution)/shard_map/pallas_call | solution.py:188
  96.8 2.5 %collective-permute-start.20 = (bf16[1024,384]{1,0:T(8,128)(2,1)S(1)}, bf16[1024,384]{1,0:T(8,128)(2,1)}, u32[]{:S(2)}, u32[]{:S(2)}) collective-permute-start(bf16[1024,384]{1,0:T(8,128)(2,1)S(1)} %shard_map.86.refs_5_), channel_id=1, source_target_pairs={{0,8},{1,9},{2,10},{3,11},{4,12},{5,13},{6,14},{7,15},{8,16},{9,17... | collective-permute-start | bytes 2359304 | tf_op jit(solution)/shard_map/ppermute | solution.py:22
  99.2 6.8 %shard_map.88.refs_8_ = f32[768,1024]{1,0:T(8,128)} custom-call(s32[6]{0:T(128)} %refs_0_.15, s32[8]{0:T(128)} %refs_1_.15, bf16[768,1024]{1,0:T(8,128)(2,1)} %get-tuple-element.39.refs_2_, bf16[512,640]{1,0:T(8,128)(2,1)} %collective-permute-done.16.refs_3_, bf16[512,640]{1,0:T(8,128)(2,1)} %collective-permute-done.17.refs_4_, bf16[1024,384]{1,0:T(8,128)(2,1)} %copy-done.1, ...), custom_call_target="tpu_custom_call" | custom-call | flops 1610612736 | bytes 12058624 | tf_op jit(solution)/shard_map/pallas_call | solution.py:188
  106.1 3.2 %collective-permute-start.19 = (bf16[1024,512]{1,0:T(8,128)(2,1)}, bf16[1024,512]{1,0:T(8,128)(2,1)S(1)}, u32[]{:S(2)}, u32[]{:S(2)}) collective-permute-start(bf16[1024,512]{1,0:T(8,128)(2,1)} %collective-permute-done.15.refs_7_), channel_id=1, source_target_pairs={{0,7},{1,0},{2,1},{3,2},{4,3},{5,4},{6,5},{7,6},{8,15},{9,8},{10,9... | collective-permute-start | bytes 3145736 | tf_op jit(solution)/shard_map/ppermute | solution.py:22
  109.4 7.3 %shard_map.82 = (bf16[768,2560]{1,0:T(8,128)(2,1)}, bf16[768,1024]{1,0:T(8,128)(2,1)}, bf16[768,512]{1,0:T(8,128)(2,1)}) custom-call(s32[2]{0:T(128)} %pad_add_fusion.refs_0_, s32[6]{0:T(128)} %refs_0_.15, s32[32]{0:T(128)} %refs_2_.3, s32[6,32]{1,0:T(8,128)} %refs_3_.3, bf16[768,4096]{1,0:T(8,128)(2,1)} %all-gather.3.cloned.1.call-done.refs_4_), custom_call_target="tpu_custom_call" | custom-call | bytes 12582912 | tf_op jit(solution)/shard_map/pallas_call | solution.py:104
  116.7 1.8 %slice.28 = bf16[512,384]{1,0:T(8,128)(2,1)} slice(bf16[1024,384]{1,0:T(8,128)(2,1)} %collective-permute-done.21.refs_4_), slice={[512:1024], [0:384]} | slice | bytes 786432 | tf_op jit(solution)/shard_map/slice | solution.py:247
  118.5 1.8 %slice.27 = bf16[512,384]{1,0:T(8,128)(2,1)} slice(bf16[1024,384]{1,0:T(8,128)(2,1)} %collective-permute-done.20.refs_3_), slice={[0:512], [0:384]} | slice | bytes 786432 | tf_op jit(solution)/shard_map/slice | solution.py:247
  120.3 1.6 collective-permute-start.22
  122.3 10.2 %shard_map.89.refs_7_ = f32[768,1024]{1,0:T(8,128)} custom-call(s32[6]{0:T(128)} %refs_0_.15, s32[8]{0:T(128)} %refs_1_.15, bf16[768,2560]{1,0:T(8,128)(2,1)} %get-tuple-element.46.refs_2_, bf16[1024,512]{1,0:T(8,128)(2,1)} %copy-done, bf16[1024,512]{1,0:T(8,128)(2,1)} %collective-permute-done.9.refs_4_, bf16[1024,512]{1,0:T(8,128)(2,1)} %collective-permute-done.10.refs_5_, ...), custom_call_target="tpu_custom_call" | custom-call | flops 4026531840 | bytes 17563648 | tf_op jit(solution)/shard_map/pallas_call | solution.py:188
  133.5 2.0 %collective-permute-start.24 = (bf16[512,512]{1,0:T(8,128)(2,1)S(1)}, bf16[512,512]{1,0:T(8,128)(2,1)}, u32[]{:S(2)}, u32[]{:S(2)}) collective-permute-start(bf16[512,512]{1,0:T(8,128)(2,1)S(1)} %slice.26), channel_id=1, source_target_pairs={{0,1},{1,2},{2,3},{3,4},{4,5},{5,6},{6,7},{7,0},{8,9},{9,10},{10,1... | collective-permute-start | bytes 1572872 | tf_op jit(solution)/shard_map/ppermute | solution.py:22
  135.6 7.2 %shard_map.90.refs_5_ = f32[768,1024]{1,0:T(8,128)} custom-call(s32[6]{0:T(128)} %refs_0_.15, s32[8]{0:T(128)} %refs_1_.15, bf16[768,1152]{1,0:T(8,128)(2,1)} %get-tuple-element.52.refs_2_, bf16[1024,384]{1,0:T(8,128)(2,1)} %collective-permute-done.20.refs_3_, bf16[1024,384]{1,0:T(8,128)(2,1)} %collective-permute-done.21.refs_4_, ...), custom_call_target="tpu_custom_call" | custom-call | flops 1811939328 | bytes 12517376 | tf_op jit(solution)/shard_map/pallas_call | solution.py:188
  142.8 6.6 %shard_map.91.refs_5_ = f32[768,1024]{1,0:T(8,128)} custom-call(s32[6]{0:T(128)} %refs_0_.15, s32[8]{0:T(128)} %refs_1_.15, bf16[768,1024]{1,0:T(8,128)(2,1)} %get-tuple-element.51.refs_2_, bf16[1024,512]{1,0:T(8,128)(2,1)} %copy-done.9, bf16[1024,512]{1,0:T(8,128)(2,1)} %copy-done.10, f32[768,1024]{1,0:T(8,128)} %shard_map.90.refs_5_), custom_call_target="tpu_custom_call" | custom-call | flops 1610612736 | bytes 12058624 | tf_op jit(solution)/shard_map/pallas_call | solution.py:188
  150.3 5.0 %shard_map.92 = bf16[768,1024]{1,0:T(8,128)(2,1)} custom-call(s32[6]{0:T(128)} %refs_0_.15, s32[8]{0:T(128)} %refs_1_.15, bf16[768,512]{1,0:T(8,128)(2,1)} %get-tuple-element.29.refs_2_, bf16[512,512]{1,0:T(8,128)(2,1)} %collective-permute-done.24.refs_3_, bf16[512,512]{1,0:T(8,128)(2,1)} %copy-done.11, f32[768,1024]{1,0:T(8,128)} %shard_map.91.refs_5_), custom_call_target="tpu_custom_call" | custom-call | flops 805306368 | bytes 10223616 | tf_op jit(solution)/shard_map/pallas_call | solution.py:188
  (74 shorter events, 11.0 us)
Async XLA Ops:
  6.5 31.3 %copy-start.8 = (bf16[1024,128]{1,0:T(8,128)(2,1)S(1)}, bf16[1024,128]{1,0:T(8,128)(2,1)}, u32[]{:S(2)}) copy-start(bf16[1024,128]{1,0:T(8,128)(2,1)} %refs_0_.8) | copy-start | bytes 786436
  6.5 73.5 %all-gather.5.cloned.1.call-start = ((), (), s32[]{:S(2)}) async-start(), calls=%async_computation.1 | async-start | bytes 7077888 | tf_op jit(solution)/shard_map/all_gather | solution.py:206
  7.3 102.1 %all-gather.3.cloned.1.call-start = ((), (), s32[]{:S(2)}) async-start(), calls=%async_computation | async-start | bytes 7077888 | tf_op jit(solution)/shard_map/all_gather | solution.py:207
  8.0 12.4 %collective-permute-start.2 = (bf16[1024,128]{1,0:T(8,128)(2,1)}, bf16[1024,128]{1,0:T(8,128)(2,1)S(1)}, u32[]{:S(2)}, u32[]{:S(2)}) collective-permute-start(bf16[1024,128]{1,0:T(8,128)(2,1)} %refs_0_.9), channel_id=1, source_target_pairs={{0,1},{1,2},{2,3},{3,4},{4,5},{5,6},{6,7},{7,0},{8,9},{9,10},{10,1... | collective-permute-start | bytes 786440 | tf_op jit(solution)/shard_map/ppermute | solution.py:22
  10.0 10.5 %collective-permute-start.3 = (bf16[1024,128]{1,0:T(8,128)(2,1)}, bf16[1024,128]{1,0:T(8,128)(2,1)S(1)}, u32[]{:S(2)}, u32[]{:S(2)}) collective-permute-start(bf16[1024,128]{1,0:T(8,128)(2,1)} %refs_0_.9), channel_id=1, source_target_pairs={{0,7},{1,0},{2,1},{3,2},{4,3},{5,4},{6,5},{7,6},{8,15},{9,8},{10,9... | collective-permute-start | bytes 786440 | tf_op jit(solution)/shard_map/ppermute | solution.py:22
  14.0 8.0 %collective-permute-start = (bf16[1024,128]{1,0:T(8,128)(2,1)}, bf16[1024,128]{1,0:T(8,128)(2,1)S(1)}, u32[]{:S(2)}, u32[]{:S(2)}) collective-permute-start(bf16[1024,128]{1,0:T(8,128)(2,1)} %refs_0_.8), channel_id=1, source_target_pairs={{0,8},{1,9},{2,10},{3,11},{4,12},{5,13},{6,14},{7,15},{8,16},{9,17... | collective-permute-start | bytes 786440 | tf_op jit(solution)/shard_map/ppermute | solution.py:22
  14.3 11.0 %collective-permute-start.1 = (bf16[1024,128]{1,0:T(8,128)(2,1)}, bf16[1024,128]{1,0:T(8,128)(2,1)S(1)}, u32[]{:S(2)}, u32[]{:S(2)}) collective-permute-start(bf16[1024,128]{1,0:T(8,128)(2,1)} %refs_0_.8), channel_id=1, source_target_pairs={{0,24},{1,25},{2,26},{3,27},{4,28},{5,29},{6,30},{7,31},{8,0},{9,1... | collective-permute-start | bytes 786440 | tf_op jit(solution)/shard_map/ppermute | solution.py:22
  22.0 8.1 %collective-permute-start.5 = (bf16[1024,128]{1,0:T(8,128)(2,1)S(1)}, bf16[1024,128]{1,0:T(8,128)(2,1)S(1)}, u32[]{:S(2)}, u32[]{:S(2)}) collective-permute-start(bf16[1024,128]{1,0:T(8,128)(2,1)S(1)} %collective-permute-done.2.refs_1_), channel_id=1, source_target_pairs={{0,1},{1,2},{2,3},{3,4},{4,5},{5,6},{6,7},{7,0},{8,9},{9,10},{10,1... | collective-permute-start | bytes 786440 | tf_op jit(solution)/shard_map/ppermute | solution.py:22
  22.0 8.1 %collective-permute-start.6 = (bf16[1024,128]{1,0:T(8,128)(2,1)S(1)}, bf16[1024,128]{1,0:T(8,128)(2,1)S(1)}, u32[]{:S(2)}, u32[]{:S(2)}) collective-permute-start(bf16[1024,128]{1,0:T(8,128)(2,1)S(1)} %collective-permute-done.3.refs_2_), channel_id=1, source_target_pairs={{0,7},{1,0},{2,1},{3,2},{4,3},{5,4},{6,5},{7,6},{8,15},{9,8},{10,9... | collective-permute-start | bytes 786440 | tf_op jit(solution)/shard_map/ppermute | solution.py:22
  25.2 9.3 %collective-permute-start.4 = (bf16[1024,128]{1,0:T(8,128)(2,1)S(1)}, bf16[1024,128]{1,0:T(8,128)(2,1)S(1)}, u32[]{:S(2)}, u32[]{:S(2)}) collective-permute-start(bf16[1024,128]{1,0:T(8,128)(2,1)S(1)} %collective-permute-done.refs_1_), channel_id=1, source_target_pairs={{0,8},{1,9},{2,10},{3,11},{4,12},{5,13},{6,14},{7,15},{8,16},{9,17... | collective-permute-start | bytes 786440 | tf_op jit(solution)/shard_map/ppermute | solution.py:22
  30.1 8.0 %collective-permute-start.7 = (bf16[1024,128]{1,0:T(8,128)(2,1)S(1)}, bf16[1024,128]{1,0:T(8,128)(2,1)S(1)}, u32[]{:S(2)}, u32[]{:S(2)}) collective-permute-start(bf16[1024,128]{1,0:T(8,128)(2,1)S(1)} %collective-permute-done.5.refs_3_), channel_id=1, source_target_pairs={{0,1},{1,2},{2,3},{3,4},{4,5},{5,6},{6,7},{7,0},{8,9},{9,10},{10,1... | collective-permute-start | bytes 786440 | tf_op jit(solution)/shard_map/ppermute | solution.py:22
  31.0 7.1 %collective-permute-start.8 = (bf16[1024,128]{1,0:T(8,128)(2,1)S(1)}, bf16[1024,128]{1,0:T(8,128)(2,1)S(1)}, u32[]{:S(2)}, u32[]{:S(2)}) collective-permute-start(bf16[1024,128]{1,0:T(8,128)(2,1)S(1)} %collective-permute-done.6.refs_4_), channel_id=1, source_target_pairs={{0,7},{1,0},{2,1},{3,2},{4,3},{5,4},{6,5},{7,6},{8,15},{9,8},{10,9... | collective-permute-start | bytes 786440 | tf_op jit(solution)/shard_map/ppermute | solution.py:22
  34.5 45.5 %copy-start.2 = (bf16[1024,640]{1,0:T(8,128)(2,1)}, bf16[1024,640]{1,0:T(8,128)(2,1)S(1)}, u32[]{:S(2)}) copy-start(bf16[1024,640]{1,0:T(8,128)(2,1)S(1)} %shard_map.84.refs_3_) | copy-start | bytes 3932164
  34.5 35.6 %collective-permute-start.13 = (bf16[1024,640]{1,0:T(8,128)(2,1)S(1)}, bf16[1024,640]{1,0:T(8,128)(2,1)S(1)}, u32[]{:S(2)}, u32[]{:S(2)}) collective-permute-start(bf16[1024,640]{1,0:T(8,128)(2,1)S(1)} %shard_map.84.refs_3_), channel_id=1, source_target_pairs={{0,24},{1,25},{2,26},{3,27},{4,28},{5,29},{6,30},{7,31},{8,0},{9,1... | collective-permute-start | bytes 3932168 | tf_op jit(solution)/shard_map/ppermute | solution.py:22
  35.4 34.7 %collective-permute-start.12 = (bf16[1024,640]{1,0:T(8,128)(2,1)S(1)}, bf16[1024,640]{1,0:T(8,128)(2,1)S(1)}, u32[]{:S(2)}, u32[]{:S(2)}) collective-permute-start(bf16[1024,640]{1,0:T(8,128)(2,1)S(1)} %shard_map.84.refs_3_), channel_id=1, source_target_pairs={{0,8},{1,9},{2,10},{3,11},{4,12},{5,13},{6,14},{7,15},{8,16},{9,17... | collective-permute-start | bytes 3932168 | tf_op jit(solution)/shard_map/ppermute | solution.py:22
  38.0 49.2 %copy-start = (bf16[1024,512]{1,0:T(8,128)(2,1)}, bf16[1024,512]{1,0:T(8,128)(2,1)S(1)}, u32[]{:S(2)}) copy-start(bf16[1024,512]{1,0:T(8,128)(2,1)S(1)} %shard_map.83.refs_3_) | copy-start | bytes 3145732
  38.8 31.3 %collective-permute-start.10 = (bf16[1024,512]{1,0:T(8,128)(2,1)S(1)}, bf16[1024,512]{1,0:T(8,128)(2,1)}, u32[]{:S(2)}, u32[]{:S(2)}) collective-permute-start(bf16[1024,512]{1,0:T(8,128)(2,1)S(1)} %shard_map.83.refs_3_), channel_id=1, source_target_pairs={{0,7},{1,0},{2,1},{3,2},{4,3},{5,4},{6,5},{7,6},{8,15},{9,8},{10,9... | collective-permute-start | bytes 3145736 | tf_op jit(solution)/shard_map/ppermute | solution.py:22
  41.6 28.5 %collective-permute-start.9 = (bf16[1024,512]{1,0:T(8,128)(2,1)S(1)}, bf16[1024,512]{1,0:T(8,128)(2,1)}, u32[]{:S(2)}, u32[]{:S(2)}) collective-permute-start(bf16[1024,512]{1,0:T(8,128)(2,1)S(1)} %shard_map.83.refs_3_), channel_id=1, source_target_pairs={{0,1},{1,2},{2,3},{3,4},{4,5},{5,6},{6,7},{7,0},{8,9},{9,10},{10,1... | collective-permute-start | bytes 3145736 | tf_op jit(solution)/shard_map/ppermute | solution.py:22
  41.6 28.5 %collective-permute-start.11 = (bf16[1024,128]{1,0:T(8,128)(2,1)S(1)}, bf16[1024,128]{1,0:T(8,128)(2,1)S(1)}, u32[]{:S(2)}, u32[]{:S(2)}) collective-permute-start(bf16[1024,128]{1,0:T(8,128)(2,1)S(1)} %collective-permute-done.7.refs_0_), channel_id=1, source_target_pairs={{0,1},{1,2},{2,3},{3,4},{4,5},{5,6},{6,7},{7,0},{8,9},{9,10},{10,1... | collective-permute-start | bytes 786440 | tf_op jit(solution)/shard_map/ppermute | solution.py:22
  70.2 35.9 %collective-permute-start.14 = (bf16[1024,512]{1,0:T(8,128)(2,1)}, bf16[1024,512]{1,0:T(8,128)(2,1)}, u32[]{:S(2)}, u32[]{:S(2)}) collective-permute-start(bf16[1024,512]{1,0:T(8,128)(2,1)} %collective-permute-done.9.refs_4_), channel_id=1, source_target_pairs={{0,1},{1,2},{2,3},{3,4},{4,5},{5,6},{6,7},{7,0},{8,9},{9,10},{10,1... | collective-permute-start | bytes 3145736 | tf_op jit(solution)/shard_map/ppermute | solution.py:22
  70.2 35.8 %collective-permute-start.15 = (bf16[1024,512]{1,0:T(8,128)(2,1)}, bf16[1024,512]{1,0:T(8,128)(2,1)}, u32[]{:S(2)}, u32[]{:S(2)}) collective-permute-start(bf16[1024,512]{1,0:T(8,128)(2,1)} %collective-permute-done.10.refs_5_), channel_id=1, source_target_pairs={{0,7},{1,0},{2,1},{3,2},{4,3},{5,4},{6,5},{7,6},{8,15},{9,8},{10,9... | collective-permute-start | bytes 3145736 | tf_op jit(solution)/shard_map/ppermute | solution.py:22
  75.3 20.6 %collective-permute-start.16 = (bf16[512,640]{1,0:T(8,128)(2,1)}, bf16[512,640]{1,0:T(8,128)(2,1)}, u32[]{:S(2)}, u32[]{:S(2)}) collective-permute-start(bf16[512,640]{1,0:T(8,128)(2,1)} %slice.24), channel_id=1, source_target_pairs={{0,8},{1,9},{2,10},{3,11},{4,12},{5,13},{6,14},{7,15},{8,16},{9,17... | collective-permute-start | bytes 1966088 | tf_op jit(solution)/shard_map/ppermute | solution.py:22
  76.9 19.0 %collective-permute-start.17 = (bf16[512,640]{1,0:T(8,128)(2,1)}, bf16[512,640]{1,0:T(8,128)(2,1)}, u32[]{:S(2)}, u32[]{:S(2)}) collective-permute-start(bf16[512,640]{1,0:T(8,128)(2,1)} %slice.25), channel_id=1, source_target_pairs={{0,24},{1,25},{2,26},{3,27},{4,28},{5,29},{6,30},{7,31},{8,0},{9,1... | collective-permute-start | bytes 1966088 | tf_op jit(solution)/shard_map/ppermute | solution.py:22
  80.0 16.8 %copy-start.1 = (bf16[1024,384]{1,0:T(8,128)(2,1)}, bf16[1024,384]{1,0:T(8,128)(2,1)S(1)}, u32[]{:S(2)}) copy-start(bf16[1024,384]{1,0:T(8,128)(2,1)S(1)} %shard_map.86.refs_5_) | copy-start | bytes 2359300
  95.9 20.8 %collective-permute-start.21 = (bf16[1024,384]{1,0:T(8,128)(2,1)S(1)}, bf16[1024,384]{1,0:T(8,128)(2,1)}, u32[]{:S(2)}, u32[]{:S(2)}) collective-permute-start(bf16[1024,384]{1,0:T(8,128)(2,1)S(1)} %shard_map.86.refs_5_), channel_id=1, source_target_pairs={{0,24},{1,25},{2,26},{3,27},{4,28},{5,29},{6,30},{7,31},{8,0},{9,1... | collective-permute-start | bytes 2359304 | tf_op jit(solution)/shard_map/ppermute | solution.py:22
  96.8 21.7 %collective-permute-start.20 = (bf16[1024,384]{1,0:T(8,128)(2,1)S(1)}, bf16[1024,384]{1,0:T(8,128)(2,1)}, u32[]{:S(2)}, u32[]{:S(2)}) collective-permute-start(bf16[1024,384]{1,0:T(8,128)(2,1)S(1)} %shard_map.86.refs_5_), channel_id=1, source_target_pairs={{0,8},{1,9},{2,10},{3,11},{4,12},{5,13},{6,14},{7,15},{8,16},{9,17... | collective-permute-start | bytes 2359304 | tf_op jit(solution)/shard_map/ppermute | solution.py:22
  106.0 26.4 %collective-permute-start.18 = (bf16[1024,512]{1,0:T(8,128)(2,1)}, bf16[1024,512]{1,0:T(8,128)(2,1)S(1)}, u32[]{:S(2)}, u32[]{:S(2)}) collective-permute-start(bf16[1024,512]{1,0:T(8,128)(2,1)} %collective-permute-done.14.refs_6_), channel_id=1, source_target_pairs={{0,1},{1,2},{2,3},{3,4},{4,5},{5,6},{6,7},{7,0},{8,9},{9,10},{10,1... | collective-permute-start | bytes 3145736 | tf_op jit(solution)/shard_map/ppermute | solution.py:22
  106.1 26.4 %collective-permute-start.19 = (bf16[1024,512]{1,0:T(8,128)(2,1)}, bf16[1024,512]{1,0:T(8,128)(2,1)S(1)}, u32[]{:S(2)}, u32[]{:S(2)}) collective-permute-start(bf16[1024,512]{1,0:T(8,128)(2,1)} %collective-permute-done.15.refs_7_), channel_id=1, source_target_pairs={{0,7},{1,0},{2,1},{3,2},{4,3},{5,4},{6,5},{7,6},{8,15},{9,8},{10,9... | collective-permute-start | bytes 3145736 | tf_op jit(solution)/shard_map/ppermute | solution.py:22
  120.3 12.3 %collective-permute-start.22 = (bf16[512,384]{1,0:T(8,128)(2,1)}, bf16[512,384]{1,0:T(8,128)(2,1)S(1)}, u32[]{:S(2)}, u32[]{:S(2)}) collective-permute-start(bf16[512,384]{1,0:T(8,128)(2,1)} %slice.27), channel_id=1, source_target_pairs={{0,8},{1,9},{2,10},{3,11},{4,12},{5,13},{6,14},{7,15},{8,16},{9,17... | collective-permute-start | bytes 1179656 | tf_op jit(solution)/shard_map/ppermute | solution.py:22
  121.8 11.7 %collective-permute-start.23 = (bf16[512,384]{1,0:T(8,128)(2,1)}, bf16[512,384]{1,0:T(8,128)(2,1)}, u32[]{:S(2)}, u32[]{:S(2)}) collective-permute-start(bf16[512,384]{1,0:T(8,128)(2,1)} %slice.28), channel_id=1, source_target_pairs={{0,24},{1,25},{2,26},{3,27},{4,28},{5,29},{6,30},{7,31},{8,0},{9,1... | collective-permute-start | bytes 1179656 | tf_op jit(solution)/shard_map/ppermute | solution.py:22
  133.5 15.9 %collective-permute-start.25 = (bf16[512,512]{1,0:T(8,128)(2,1)S(1)}, bf16[512,512]{1,0:T(8,128)(2,1)S(1)}, u32[]{:S(2)}, u32[]{:S(2)}) collective-permute-start(bf16[512,512]{1,0:T(8,128)(2,1)S(1)} %slice.29), channel_id=1, source_target_pairs={{0,7},{1,0},{2,1},{3,2},{4,3},{5,4},{6,5},{7,6},{8,15},{9,8},{10,9... | collective-permute-start | bytes 1572872 | tf_op jit(solution)/shard_map/ppermute | solution.py:22
  133.5 16.0 %collective-permute-start.24 = (bf16[512,512]{1,0:T(8,128)(2,1)S(1)}, bf16[512,512]{1,0:T(8,128)(2,1)}, u32[]{:S(2)}, u32[]{:S(2)}) collective-permute-start(bf16[512,512]{1,0:T(8,128)(2,1)S(1)} %slice.26), channel_id=1, source_target_pairs={{0,1},{1,2},{2,3},{3,4},{4,5},{5,6},{6,7},{7,0},{8,9},{9,10},{10,1... | collective-permute-start | bytes 1572872 | tf_op jit(solution)/shard_map/ppermute | solution.py:22
  (11 other events, 40.8 us)
Sparse Core Ops, SparseCore 0:
  9.2 46.1 all-gather.4
  57.2 43.5 all-gather.2

commit v8 on v7

--- a/solution.py
+++ b/solution.py
@@ -114,9 +114,9 @@
     )(here, sym_ij, sym_cd, amp_mask, raw)
 
 
-def product_kernel(sizes, first, last, ij_ref, ab_ref, amps_hbm, *refs):
+def product_kernel(pieces, sizes, first, last, ij_ref, ab_ref, *refs):
     n = sum(sizes)
-    ints, refs = refs[:n], refs[n:]
+    amps_hbm, ints, refs = refs[:pieces], refs[pieces:pieces + n], refs[pieces + n:]
     if first:
         out, amps, rows_v, sem = refs
     else:
@@ -145,11 +145,16 @@
         if not first:
             act(pltpu.make_async_copy(total_hbm.at[:, rows], total.at[:, rows], sem.at[c, len(sizes)]))
 
-    whole = pltpu.make_async_copy(amps_hbm, amps, sem.at[4, 0])
-    whole.start()
+    whole, at = [], 0
+    for k, piece in enumerate(amps_hbm):
+        width = piece.shape[1]
+        whole.append(pltpu.make_async_copy(piece, amps.at[:, pl.ds(at, width)], sem.at[4, k]))
+        whole[-1].start()
+        at += width
     for c in range(4):
         fetch(jnp.int32(c), lambda copy: copy.start())
-    whole.wait()
+    for copy in whole:
+        copy.wait()
 
     def strip(c, carry):
         fetch(c, lambda copy: copy.wait())
@@ -174,13 +179,13 @@
 
 
 def product(sym_ij, sym_ab, amps, blocks, total=None, last=False):
-    depth = amps.shape[1]
+    depth = sum(piece.shape[1] for piece in amps)
     first = total is None
     sizes = [len(block) for block in blocks]
     n = sum(sizes)
 
     def kernel(*refs):
-        product_kernel(sizes, first, last, *refs)
+        product_kernel(len(amps), sizes, first, last, *refs)
 
     scratch = [
         pltpu.VMEM((768, depth), BF16), pltpu.VMEM((1024, depth), BF16), pltpu.SemaphoreType.DMA((5, len(sizes) + 1))
@@ -188,12 +193,12 @@
     return pl.pallas_call(
         kernel,
         out_shape=jax.ShapeDtypeStruct((768, 1024), BF16 if last else F32),
-        in_specs=[SMEM] * 2 + [HBM] * (1 + n + (not first)),
+        in_specs=[SMEM] * 2 + [HBM] * (len(amps) + n + (not first)),
         out_specs=VMEM,
         scratch_shapes=scratch + ([] if first else [pltpu.VMEM((768, 1024), F32)]),
         compiler_params=params(60),
         cost_estimate=cost(2 * 768 * 1024 * depth, 8 * 2**20 + 3584 * depth),
-    )(sym_ij, sym_ab, amps, *[array for block in blocks for array in block], *([] if first else [total]))
+    )(sym_ij, sym_ab, *amps, *[array for block in blocks for array in block], *([] if first else [total]))
 
 
 def body(amp_plus, amp_minus, ints_plus, ints_minus, sym_ij, sym_ab, sym_cd, amp_mask):
@@ -220,36 +225,36 @@
     w0 = join([(y0,), (yu[0],), (yd[0],), y2])
     threes = (zu[2], zd[2])
     wu, wd = [go(w0, *threes, dz=1)], [go(w0, *threes, dz=-1)]
-    z4 = (go(zu[2], dz=1),)
+
+    def plus(offs, *ys):
+        return [(y, z) for y in ys for z in offs]
+
+    def minus(*zs):
+        return [(y, z) for z in zs for y in (0, -1, 1, 2)]
+
+    def add(amps, blocks, *rest):
+        return product(sym_ij, sym_ab, amps, blocks, *rest)
+
+    labels = (here, sym_ij, sym_cd, amp_mask)
+    near, far = (0, -1, 1, -2, 2), (-3, 3, 4)
+    tp = mask(*labels, raw_plus, plus(near, 0, -1, 1) + plus(far, 0), plus(far, -1, 1), plus(near, 2) + plus(far, 2))
+    z4 = (go(zu[2], tp[0], dz=1),)
     d0 = join([(zu[2],), (zd[2],), z4])
-    c2 = (go(c1[0][:HALF], *c1, dy=1), go(c1[1][HALF:], *c1, dy=-1))
+    c2 = (go(c1[0][:HALF], *c1, tp[0], dy=1), go(c1[1][HALF:], *c1, tp[0], dy=-1))
     wu.append(go(wu[0], wd[0], *z4, *c1, dz=1))
     wd.append(go(wd[0], wu[0], *z4, *c1, dz=-1))
-
-    def plus(offs, *ys):
-        return [(y, z) for y in ys for z in offs]
-
-    def minus(*zs):
-        return [(y, z) for z in zs for y in (0, -1, 1, 2)]
-
-    def add(amps, blocks, *rest):
-        return product(sym_ij, sym_ab, amps, blocks, *rest)
-
-    labels = (here, sym_ij, sym_cd, amp_mask)
-    near, far = (0, -1, 1, -2, 2), (-3, 3, 4)
-    tp = mask(*labels, raw_plus, plus(near, 0, -1, 1), plus(near, 2) + plus(far, 0), plus(far, -1, 1, 2))
-    total = add(tp[0], [(c0,), c1[:1], c1[1:]])
+    total = add(tp[:1], [(c0,), c1[:1], c1[1:], (d0,)])
     d1 = (go(d0, *c2, total, dy=1), go(d0, *c2, total, dy=-1))
-    total = add(tp[1], [c2, (d0,)], total)
-    wu.append(go(wu[1], wd[1], total, dz=1))
-    wd.append(go(wd[1], wu[1], total, dz=-1))
+    wu.append(go(wu[1], wd[1], dz=1))
+    wd.append(go(wd[1], wu[1], dz=-1))
     tm = mask(*labels, raw_minus, minus(0, -1, 1, -2, 2), minus(-3, 3), minus(4))
     d2 = (go(d1[0][:HALF], *d1, tm[0], dy=1), go(d1[1][HALF:], *d1, tm[0], dy=-1))
-    total = add(tm[0], [(w0,), (wu[0],), (wd[0],), (wu[1],), (wd[1],)], total)
+    total = add(
+        [tm[0], tp[1]], [(w0,), (wu[0],), (wd[0],), (wu[1],), (wd[1],), d1[:1], d1[1:]], total
+    )
     w4 = (go(wu[2][:HALF], wd[2], *d2, total, dz=1), go(wd[2][HALF:], wu[2], *d2, total, dz=-1))
-    total = add(tp[2], [d1[:1], d1[1:], d2], total)
-    total = add(tm[1], [(wu[2],), (wd[2],)], total)
-    return add(tm[2], [w4], total, True)
+    total = add([tp[2], tm[1]], [c2, d2, (wu[2],), (wd[2],)], total)
+    return add(tm[2:], [w4], total, True)
 
 
 def solution(mesh):

time: 165 us -> 159 us (0.964); the launches traced: 162 us -> 158 us
  waiting for transfers between devices: 37.7 us -> 48.4 us
  Pallas kernels: 59.5 us -> 50.5 us
  local copies, waits for them, and re-layouts: 10.9 us -> 7.9 us
  starting transfers between devices: 39.7 us -> 37.1 us
    all_gather x1, waiting for transfers between devices: 0.02 us -> 14.8 us  [body(): raw_plus = lax.all_gather(amp_plus, 'grp', axis=1, tiled=True)]
    pallas_call x6 -> x4, Pallas kernels: 44.5 us -> 35.5 us  [product(): pl.pallas_call(kernel, out_shape=jax.ShapeDtypeStruct((768, 1024), BF16 i...]
    ppermute x26, waiting for transfers between devices: 36.3 us -> 32.2 us  [move(): return lax.ppermute(values, 'mem', perm_of(dy, dz))]
    unnamed x30 -> x24, local copies, waits for them, and re-layouts: 5.37 us -> 2.72 us
    ppermute x26, starting transfers between devices: 39.6 us -> 37.1 us  [move(): return lax.ppermute(values, 'mem', perm_of(dy, dz))]
  transfers between devices with their start and end apart: 28 -> 28, of which waited for: 4 -> 13; matrix products, arithmetic and copies ran while one was open for 4% -> 4% of each run, Pallas kernels for 34% -> 29%
where the time goes in v8:
time: 159 us; the launch traced here: 158 us
  Pallas kernels  50.5 us (32%)
  waiting for transfers between devices  48.4 us (30%)
  starting transfers between devices  37.1 us (23%)
  between operations  13.7 us (9%)
  local copies, waits for them, and re-layouts  7.9 us (5%)
    ppermute x26, starting transfers between devices, move(): return lax.ppermute(values, 'mem', perm_of(dy, dz))  37.1 us
    pallas_call x4, Pallas kernels, product(): pl.pallas_call(kernel, out_shape=jax.ShapeDtypeStruct((768, 1024), BF16 i...  35.5 us
    ppermute x26, waiting for transfers between devices, move(): return lax.ppermute(values, 'mem', perm_of(dy, dz))  32.2 us
    all_gather x1, waiting for transfers between devices, body(): raw_plus = lax.all_gather(amp_plus, 'grp', axis=1, tiled=True)  14.8 us
    pallas_call x2, Pallas kernels, mask(): pl.pallas_call(kernel, out_shape=[jax.ShapeDtypeStruct(shape, BF16) for s...  14.5 us
  transfers between devices with their start and end apart: 28, of which 13 were waited for; matrix products, arithmetic and copies ran while one was open for 4% of the time, Pallas kernels for 29%

profile of v8, /device:TPU:24, one launch (start us, length us, event | category | flops | bytes accessed | tf_op | source)
XLA Modules:
  0.0 158.2 jit_solution(5564357776230561735)
XLA Ops:
  8.0 2.0 %collective-permute-start = (bf16[1024,128]{1,0:T(8,128)(2,1)}, bf16[1024,128]{1,0:T(8,128)(2,1)S(1)}, u32[]{:S(2)}, u32[]{:S(2)}) collective-permute-start(bf16[1024,128]{1,0:T(8,128)(2,1)} %refs_0_.6), channel_id=1, source_target_pairs={{0,8},{1,9},{2,10},{3,11},{4,12},{5,13},{6,14},{7,15},{8,16},{9,17... | collective-permute-start | bytes 786440 | tf_op jit(solution)/shard_map/ppermute | solution.py:22
  10.2 3.9 %collective-permute-start.3 = (bf16[1024,128]{1,0:T(8,128)(2,1)}, bf16[1024,128]{1,0:T(8,128)(2,1)S(1)}, u32[]{:S(2)}, u32[]{:S(2)}) collective-permute-start(bf16[1024,128]{1,0:T(8,128)(2,1)} %refs_0_.7), channel_id=1, source_target_pairs={{0,7},{1,0},{2,1},{3,2},{4,3},{5,4},{6,5},{7,6},{8,15},{9,8},{10,9... | collective-permute-start | bytes 786440 | tf_op jit(solution)/shard_map/ppermute | solution.py:22
  14.2 1.8 %collective-permute-start.1 = (bf16[1024,128]{1,0:T(8,128)(2,1)}, bf16[1024,128]{1,0:T(8,128)(2,1)S(1)}, u32[]{:S(2)}, u32[]{:S(2)}) collective-permute-start(bf16[1024,128]{1,0:T(8,128)(2,1)} %refs_0_.6), channel_id=1, source_target_pairs={{0,24},{1,25},{2,26},{3,27},{4,28},{5,29},{6,30},{7,31},{8,0},{9,1... | collective-permute-start | bytes 786440 | tf_op jit(solution)/shard_map/ppermute | solution.py:22
  16.3 4.2 %collective-permute-done.2.refs_1_ = bf16[1024,128]{1,0:T(8,128)(2,1)S(1)} collective-permute-done((bf16[1024,128]{1,0:T(8,128)(2,1)}, bf16[1024,128]{1,0:T(8,128)(2,1)S(1)}, u32[]{:S(2)}, u32[]{:S(2)}) %collective-permute-start.2) | collective-permute-done | bytes 262176 | tf_op jit(solution)/shard_map/ppermute | solution.py:22
  20.6 3.2 %collective-permute-start.6 = (bf16[1024,128]{1,0:T(8,128)(2,1)S(1)}, bf16[1024,128]{1,0:T(8,128)(2,1)S(1)}, u32[]{:S(2)}, u32[]{:S(2)}) collective-permute-start(bf16[1024,128]{1,0:T(8,128)(2,1)S(1)} %collective-permute-done.3.refs_2_), channel_id=1, source_target_pairs={{0,7},{1,0},{2,1},{3,2},{4,3},{5,4},{6,5},{7,6},{8,15},{9,8},{10,9... | collective-permute-start | bytes 786440 | tf_op jit(solution)/shard_map/ppermute | solution.py:22
  23.8 1.4 collective-permute-start.4
  25.2 3.9 %collective-permute-done.5.refs_3_ = bf16[1024,128]{1,0:T(8,128)(2,1)S(1)} collective-permute-done((bf16[1024,128]{1,0:T(8,128)(2,1)S(1)}, bf16[1024,128]{1,0:T(8,128)(2,1)S(1)}, u32[]{:S(2)}, u32[]{:S(2)}) %collective-permute-start.5) | collective-permute-done | bytes 262176 | tf_op jit(solution)/shard_map/ppermute | solution.py:22
  29.1 1.8 %collective-permute-start.7 = (bf16[1024,128]{1,0:T(8,128)(2,1)S(1)}, bf16[1024,128]{1,0:T(8,128)(2,1)S(1)}, u32[]{:S(2)}, u32[]{:S(2)}) collective-permute-start(bf16[1024,128]{1,0:T(8,128)(2,1)S(1)} %collective-permute-done.5.refs_3_), channel_id=1, source_target_pairs={{0,1},{1,2},{2,3},{3,4},{4,5},{5,6},{6,7},{7,0},{8,9},{9,10},{10,1... | collective-permute-start | bytes 786440 | tf_op jit(solution)/shard_map/ppermute | solution.py:22
  30.9 1.4 collective-permute-start.8
  33.5 1.3 collective-permute-start.12
  37.8 2.1 %collective-permute-start.10 = (bf16[1024,512]{1,0:T(8,128)(2,1)S(1)}, bf16[1024,512]{1,0:T(8,128)(2,1)}, u32[]{:S(2)}, u32[]{:S(2)}) collective-permute-start(bf16[1024,512]{1,0:T(8,128)(2,1)S(1)} %shard_map.83.refs_4_), channel_id=1, source_target_pairs={{0,7},{1,0},{2,1},{3,2},{4,3},{5,4},{6,5},{7,6},{8,15},{9,8},{10,9... | collective-permute-start | bytes 3145736 | tf_op jit(solution)/shard_map/ppermute | solution.py:22
  40.6 14.8 %all-gather.5.cloned.1.call-done.refs_4_ = bf16[768,4096]{1,0:T(8,128)(2,1)} async-done(((bf16[768,512]{1,0:T(8,128)(2,1)}), bf16[768,4096]{1,0:T(8,128)(2,1)}) %all-gather.5.cloned.1.call-update) | async-done | bytes 6291472 | tf_op jit(solution)/shard_map/all_gather | solution.py:211
  55.4 7.1 %shard_map.84 = (bf16[768,2304]{1,0:T(8,128)(2,1)}, bf16[768,768]{1,0:T(8,128)(2,1)}, bf16[768,1024]{1,0:T(8,128)(2,1)}) custom-call(s32[2]{0:T(128)} %pad_add_fusion.refs_0_, s32[6]{0:T(128)} %refs_0_.11, s32[32]{0:T(128)} %refs_2_.3, s32[6,32]{1,0:T(8,128)} %refs_3_.3, bf16[768,4096]{1,0:T(8,128)(2,1)} %all-gather.5.cloned.1.call-done.refs_4_), custom_call_target="tpu_custom_call" | custom-call | bytes 12582912 | tf_op jit(solution)/shard_map/pallas_call | solution.py:104
  62.5 1.6 %collective-permute-start.11 = (bf16[1024,128]{1,0:T(8,128)(2,1)S(1)}, bf16[1024,128]{1,0:T(8,128)(2,1)S(1)}, u32[]{:S(2)}, u32[]{:S(2)}) collective-permute-start(bf16[1024,128]{1,0:T(8,128)(2,1)S(1)} %collective-permute-done.7.refs_0_), channel_id=1, source_target_pairs={{0,1},{1,2},{2,3},{3,4},{4,5},{5,6},{6,7},{7,0},{8,9},{9,10},{10,1... | collective-permute-start | bytes 786440 | tf_op jit(solution)/shard_map/ppermute | solution.py:22
  64.2 8.5 %collective-permute-done.11.refs_2_ = bf16[1024,128]{1,0:T(8,128)(2,1)S(1)} collective-permute-done((bf16[1024,128]{1,0:T(8,128)(2,1)S(1)}, bf16[1024,128]{1,0:T(8,128)(2,1)S(1)}, u32[]{:S(2)}, u32[]{:S(2)}) %collective-permute-start.11) | collective-permute-done | bytes 262176 | tf_op jit(solution)/shard_map/ppermute | solution.py:22
  72.7 1.7 %collective-permute-start.15 = (bf16[1024,512]{1,0:T(8,128)(2,1)}, bf16[1024,512]{1,0:T(8,128)(2,1)}, u32[]{:S(2)}, u32[]{:S(2)}) collective-permute-start(bf16[1024,512]{1,0:T(8,128)(2,1)} %collective-permute-done.10.refs_6_), channel_id=1, source_target_pairs={{0,7},{1,0},{2,1},{3,2},{4,3},{5,4},{6,5},{7,6},{8,15},{9,8},{10,9... | collective-permute-start | bytes 3145736 | tf_op jit(solution)/shard_map/ppermute | solution.py:22
  77.6 1.5 collective-permute-start.19
  80.1 9.4 %shard_map.87.refs_11_ = f32[768,1024]{1,0:T(8,128)} custom-call(s32[6]{0:T(128)} %refs_0_.11, s32[8]{0:T(128)} %refs_1_.11, bf16[768,2304]{1,0:T(8,128)(2,1)} %get-tuple-element.37.refs_2_, bf16[1024,640]{1,0:T(8,128)(2,1)} %copy-done, bf16[1024,640]{1,0:T(8,128)(2,1)} %collective-permute-done.12.refs_4_, ...), custom_call_target="tpu_custom_call" | custom-call | flops 3623878656 | bytes 16646144 | tf_op jit(solution)/shard_map/pallas_call | solution.py:193
  89.5 3.4 %collective-permute-done.18.refs_4_ = bf16[512,640]{1,0:T(8,128)(2,1)S(1)} collective-permute-done((bf16[512,640]{1,0:T(8,128)(2,1)S(1)}, bf16[512,640]{1,0:T(8,128)(2,1)S(1)}, u32[]{:S(2)}, u32[]{:S(2)}) %collective-permute-start.18) | collective-permute-done | bytes 655392 | tf_op jit(solution)/shard_map/ppermute | solution.py:22
  92.9 1.4 collective-permute-done.19.refs_5_
  94.6 2.9 %collective-permute-start.20 = (bf16[1024,384]{1,0:T(8,128)(2,1)}, bf16[1024,384]{1,0:T(8,128)(2,1)}, u32[]{:S(2)}, u32[]{:S(2)}) collective-permute-start(bf16[1024,384]{1,0:T(8,128)(2,1)} %copy-done.2), channel_id=1, source_target_pairs={{0,8},{1,9},{2,10},{3,11},{4,12},{5,13},{6,14},{7,15},{8,16},{9,17... | collective-permute-start | bytes 2359304 | tf_op jit(solution)/shard_map/ppermute | solution.py:22
  97.8 2.3 %collective-permute-done.14.refs_7_ = bf16[1024,512]{1,0:T(8,128)(2,1)} collective-permute-done((bf16[1024,512]{1,0:T(8,128)(2,1)}, bf16[1024,512]{1,0:T(8,128)(2,1)}, u32[]{:S(2)}, u32[]{:S(2)}) %collective-permute-start.14) | collective-permute-done | bytes 1048608 | tf_op jit(solution)/shard_map/ppermute | solution.py:22
  100.4 1.7 %collective-permute-start.16 = (bf16[1024,512]{1,0:T(8,128)(2,1)}, bf16[1024,512]{1,0:T(8,128)(2,1)S(1)}, u32[]{:S(2)}, u32[]{:S(2)}) collective-permute-start(bf16[1024,512]{1,0:T(8,128)(2,1)} %collective-permute-done.14.refs_7_), channel_id=1, source_target_pairs={{0,1},{1,2},{2,3},{3,4},{4,5},{5,6},{6,7},{7,0},{8,9},{9,10},{10,1... | collective-permute-start | bytes 3145736 | tf_op jit(solution)/shard_map/ppermute | solution.py:22
  102.2 7.3 %shard_map.82 = (bf16[768,2560]{1,0:T(8,128)(2,1)}, bf16[768,1024]{1,0:T(8,128)(2,1)}, bf16[768,512]{1,0:T(8,128)(2,1)}) custom-call(s32[2]{0:T(128)} %pad_add_fusion.refs_0_, s32[6]{0:T(128)} %refs_0_.11, s32[32]{0:T(128)} %refs_2_.3, s32[6,32]{1,0:T(8,128)} %refs_3_.3, bf16[768,4096]{1,0:T(8,128)(2,1)} %all-gather.3.cloned.1.call-done.refs_4_), custom_call_target="tpu_custom_call" | custom-call | bytes 12582912 | tf_op jit(solution)/shard_map/pallas_call | solution.py:104
  109.5 3.9 %collective-permute-done.21.refs_10_ = bf16[1024,384]{1,0:T(8,128)(2,1)} collective-permute-done((bf16[1024,384]{1,0:T(8,128)(2,1)}, bf16[1024,384]{1,0:T(8,128)(2,1)}, u32[]{:S(2)}, u32[]{:S(2)}) %collective-permute-start.21) | collective-permute-done | bytes 786464 | tf_op jit(solution)/shard_map/ppermute | solution.py:22
  114.8 1.8 %slice.27 = bf16[512,384]{1,0:T(8,128)(2,1)} slice(bf16[1024,384]{1,0:T(8,128)(2,1)} %collective-permute-done.20.refs_9_), slice={[0:512], [0:384]} | slice | bytes 786432 | tf_op jit(solution)/shard_map/slice | solution.py:251
  116.5 3.2 %collective-permute-start.22 = (bf16[512,384]{1,0:T(8,128)(2,1)}, bf16[512,384]{1,0:T(8,128)(2,1)S(1)}, u32[]{:S(2)}, u32[]{:S(2)}) collective-permute-start(bf16[512,384]{1,0:T(8,128)(2,1)} %slice.27), channel_id=1, source_target_pairs={{0,8},{1,9},{2,10},{3,11},{4,12},{5,13},{6,14},{7,15},{8,16},{9,17... | collective-permute-start | bytes 1179656 | tf_op jit(solution)/shard_map/ppermute | solution.py:22
  119.8 12.0 %shard_map.88.refs_10_ = f32[768,1024]{1,0:T(8,128)} custom-call(s32[6]{0:T(128)} %refs_0_.11, s32[8]{0:T(128)} %refs_1_.11, bf16[768,2560]{1,0:T(8,128)(2,1)} %get-tuple-element.47.refs_2_, bf16[768,768]{1,0:T(8,128)(2,1)} %get-tuple-element.50.refs_3_, bf16[1024,512]{1,0:T(8,128)(2,1)} %copy-done.1, bf16[1024,512]{1,0:T(8,128)(2,1)} %collective-permute-done.9.refs_5_, ...), custom_call_target="tpu_custom_call" | custom-call | flops 5234491392 | bytes 20316160 | tf_op jit(solution)/shard_map/pallas_call | solution.py:193
  132.7 2.3 %collective-permute-start.25 = (bf16[512,512]{1,0:T(8,128)(2,1)S(1)}, bf16[512,512]{1,0:T(8,128)(2,1)S(1)}, u32[]{:S(2)}, u32[]{:S(2)}) collective-permute-start(bf16[512,512]{1,0:T(8,128)(2,1)S(1)} %slice.29), channel_id=1, source_target_pairs={{0,7},{1,0},{2,1},{3,2},{4,3},{5,4},{6,5},{7,6},{8,15},{9,8},{10,9... | collective-permute-start | bytes 1572872 | tf_op jit(solution)/shard_map/ppermute | solution.py:22
  135.2 9.1 %shard_map.89.refs_5_ = f32[768,1024]{1,0:T(8,128)} custom-call(s32[6]{0:T(128)} %refs_0_.11, s32[8]{0:T(128)} %refs_1_.11, bf16[768,1024]{1,0:T(8,128)(2,1)} %get-tuple-element.53.refs_2_, bf16[768,1024]{1,0:T(8,128)(2,1)} %get-tuple-element.54.refs_3_, bf16[512,640]{1,0:T(8,128)(2,1)} %copy-done.7, bf16[512,640]{1,0:T(8,128)(2,1)} %copy-done.8, ...), custom_call_target="tpu_custom_call" | custom-call | flops 3221225472 | bytes 15728640 | tf_op jit(solution)/shard_map/pallas_call | solution.py:193
  144.3 2.0 %collective-permute-done.24.refs_3_ = bf16[512,512]{1,0:T(8,128)(2,1)} collective-permute-done((bf16[512,512]{1,0:T(8,128)(2,1)S(1)}, bf16[512,512]{1,0:T(8,128)(2,1)}, u32[]{:S(2)}, u32[]{:S(2)}) %collective-permute-start.24) | collective-permute-done | bytes 524320 | tf_op jit(solution)/shard_map/ppermute | solution.py:22
  146.3 5.0 %shard_map.90 = bf16[768,1024]{1,0:T(8,128)(2,1)} custom-call(s32[6]{0:T(128)} %refs_0_.11, s32[8]{0:T(128)} %refs_1_.11, bf16[768,512]{1,0:T(8,128)(2,1)} %get-tuple-element.30.refs_2_, bf16[512,512]{1,0:T(8,128)(2,1)} %collective-permute-done.24.refs_3_, bf16[512,512]{1,0:T(8,128)(2,1)} %copy-done.9, f32[768,1024]{1,0:T(8,128)} %shard_map.89.refs_5_), custom_call_target="tpu_custom_call" | custom-call | flops 805306368 | bytes 10223616 | tf_op jit(solution)/shard_map/pallas_call | solution.py:193
  (66 shorter events, 14.1 us)
Async XLA Ops:
  6.5 29.1 %copy-start.4 = (bf16[1024,128]{1,0:T(8,128)(2,1)S(1)}, bf16[1024,128]{1,0:T(8,128)(2,1)}, u32[]{:S(2)}) copy-start(bf16[1024,128]{1,0:T(8,128)(2,1)} %refs_0_.6) | copy-start | bytes 786436
  6.5 48.8 %all-gather.5.cloned.1.call-start = ((), (), s32[]{:S(2)}) async-start(), calls=%async_computation.1 | async-start | bytes 7077888 | tf_op jit(solution)/shard_map/all_gather | solution.py:211
  7.3 94.9 %all-gather.3.cloned.1.call-start = ((), (), s32[]{:S(2)}) async-start(), calls=%async_computation | async-start | bytes 7077888 | tf_op jit(solution)/shard_map/all_gather | solution.py:212
  8.0 8.3 %collective-permute-start = (bf16[1024,128]{1,0:T(8,128)(2,1)}, bf16[1024,128]{1,0:T(8,128)(2,1)S(1)}, u32[]{:S(2)}, u32[]{:S(2)}) collective-permute-start(bf16[1024,128]{1,0:T(8,128)(2,1)} %refs_0_.6), channel_id=1, source_target_pairs={{0,8},{1,9},{2,10},{3,11},{4,12},{5,13},{6,14},{7,15},{8,16},{9,17... | collective-permute-start | bytes 786440 | tf_op jit(solution)/shard_map/ppermute | solution.py:22
  10.0 10.5 %collective-permute-start.2 = (bf16[1024,128]{1,0:T(8,128)(2,1)}, bf16[1024,128]{1,0:T(8,128)(2,1)S(1)}, u32[]{:S(2)}, u32[]{:S(2)}) collective-permute-start(bf16[1024,128]{1,0:T(8,128)(2,1)} %refs_0_.7), channel_id=1, source_target_pairs={{0,1},{1,2},{2,3},{3,4},{4,5},{5,6},{6,7},{7,0},{8,9},{9,10},{10,1... | collective-permute-start | bytes 786440 | tf_op jit(solution)/shard_map/ppermute | solution.py:22
  10.2 10.3 %collective-permute-start.3 = (bf16[1024,128]{1,0:T(8,128)(2,1)}, bf16[1024,128]{1,0:T(8,128)(2,1)S(1)}, u32[]{:S(2)}, u32[]{:S(2)}) collective-permute-start(bf16[1024,128]{1,0:T(8,128)(2,1)} %refs_0_.7), channel_id=1, source_target_pairs={{0,7},{1,0},{2,1},{3,2},{4,3},{5,4},{6,5},{7,6},{8,15},{9,8},{10,9... | collective-permute-start | bytes 786440 | tf_op jit(solution)/shard_map/ppermute | solution.py:22
  14.2 9.6 %collective-permute-start.1 = (bf16[1024,128]{1,0:T(8,128)(2,1)}, bf16[1024,128]{1,0:T(8,128)(2,1)S(1)}, u32[]{:S(2)}, u32[]{:S(2)}) collective-permute-start(bf16[1024,128]{1,0:T(8,128)(2,1)} %refs_0_.6), channel_id=1, source_target_pairs={{0,24},{1,25},{2,26},{3,27},{4,28},{5,29},{6,30},{7,31},{8,0},{9,1... | collective-permute-start | bytes 786440 | tf_op jit(solution)/shard_map/ppermute | solution.py:22
  20.5 8.6 %collective-permute-start.5 = (bf16[1024,128]{1,0:T(8,128)(2,1)S(1)}, bf16[1024,128]{1,0:T(8,128)(2,1)S(1)}, u32[]{:S(2)}, u32[]{:S(2)}) collective-permute-start(bf16[1024,128]{1,0:T(8,128)(2,1)S(1)} %collective-permute-done.2.refs_1_), channel_id=1, source_target_pairs={{0,1},{1,2},{2,3},{3,4},{4,5},{5,6},{6,7},{7,0},{8,9},{9,10},{10,1... | collective-permute-start | bytes 786440 | tf_op jit(solution)/shard_map/ppermute | solution.py:22
  20.6 8.6 %collective-permute-start.6 = (bf16[1024,128]{1,0:T(8,128)(2,1)S(1)}, bf16[1024,128]{1,0:T(8,128)(2,1)S(1)}, u32[]{:S(2)}, u32[]{:S(2)}) collective-permute-start(bf16[1024,128]{1,0:T(8,128)(2,1)S(1)} %collective-permute-done.3.refs_2_), channel_id=1, source_target_pairs={{0,7},{1,0},{2,1},{3,2},{4,3},{5,4},{6,5},{7,6},{8,15},{9,8},{10,9... | collective-permute-start | bytes 786440 | tf_op jit(solution)/shard_map/ppermute | solution.py:22
  23.8 9.7 %collective-permute-start.4 = (bf16[1024,128]{1,0:T(8,128)(2,1)S(1)}, bf16[1024,128]{1,0:T(8,128)(2,1)S(1)}, u32[]{:S(2)}, u32[]{:S(2)}) collective-permute-start(bf16[1024,128]{1,0:T(8,128)(2,1)S(1)} %collective-permute-done.refs_1_), channel_id=1, source_target_pairs={{0,8},{1,9},{2,10},{3,11},{4,12},{5,13},{6,14},{7,15},{8,16},{9,17... | collective-permute-start | bytes 786440 | tf_op jit(solution)/shard_map/ppermute | solution.py:22
  29.1 7.6 %collective-permute-start.7 = (bf16[1024,128]{1,0:T(8,128)(2,1)S(1)}, bf16[1024,128]{1,0:T(8,128)(2,1)S(1)}, u32[]{:S(2)}, u32[]{:S(2)}) collective-permute-start(bf16[1024,128]{1,0:T(8,128)(2,1)S(1)} %collective-permute-done.5.refs_3_), channel_id=1, source_target_pairs={{0,1},{1,2},{2,3},{3,4},{4,5},{5,6},{6,7},{7,0},{8,9},{9,10},{10,1... | collective-permute-start | bytes 786440 | tf_op jit(solution)/shard_map/ppermute | solution.py:22
  30.9 6.9 %collective-permute-start.8 = (bf16[1024,128]{1,0:T(8,128)(2,1)S(1)}, bf16[1024,128]{1,0:T(8,128)(2,1)S(1)}, u32[]{:S(2)}, u32[]{:S(2)}) collective-permute-start(bf16[1024,128]{1,0:T(8,128)(2,1)S(1)} %collective-permute-done.6.refs_4_), channel_id=1, source_target_pairs={{0,7},{1,0},{2,1},{3,2},{4,3},{5,4},{6,5},{7,6},{8,15},{9,8},{10,9... | collective-permute-start | bytes 786440 | tf_op jit(solution)/shard_map/ppermute | solution.py:22
  33.5 29.0 %copy-start = (bf16[1024,640]{1,0:T(8,128)(2,1)}, bf16[1024,640]{1,0:T(8,128)(2,1)S(1)}, u32[]{:S(2)}) copy-start(bf16[1024,640]{1,0:T(8,128)(2,1)S(1)} %shard_map.85.refs_3_) | copy-start | bytes 3932164
  33.5 30.6 %collective-permute-start.12 = (bf16[1024,640]{1,0:T(8,128)(2,1)S(1)}, bf16[1024,640]{1,0:T(8,128)(2,1)}, u32[]{:S(2)}, u32[]{:S(2)}) collective-permute-start(bf16[1024,640]{1,0:T(8,128)(2,1)S(1)} %shard_map.85.refs_3_), channel_id=1, source_target_pairs={{0,8},{1,9},{2,10},{3,11},{4,12},{5,13},{6,14},{7,15},{8,16},{9,17... | collective-permute-start | bytes 3932168 | tf_op jit(solution)/shard_map/ppermute | solution.py:22
  34.9 29.3 %collective-permute-start.13 = (bf16[1024,640]{1,0:T(8,128)(2,1)S(1)}, bf16[1024,640]{1,0:T(8,128)(2,1)}, u32[]{:S(2)}, u32[]{:S(2)}) collective-permute-start(bf16[1024,640]{1,0:T(8,128)(2,1)S(1)} %shard_map.85.refs_3_), channel_id=1, source_target_pairs={{0,24},{1,25},{2,26},{3,27},{4,28},{5,29},{6,30},{7,31},{8,0},{9,1... | collective-permute-start | bytes 3932168 | tf_op jit(solution)/shard_map/ppermute | solution.py:22
  35.8 26.7 %copy-start.1 = (bf16[1024,512]{1,0:T(8,128)(2,1)}, bf16[1024,512]{1,0:T(8,128)(2,1)S(1)}, u32[]{:S(2)}) copy-start(bf16[1024,512]{1,0:T(8,128)(2,1)S(1)} %shard_map.83.refs_4_) | copy-start | bytes 3145732
  37.8 26.4 %collective-permute-start.10 = (bf16[1024,512]{1,0:T(8,128)(2,1)S(1)}, bf16[1024,512]{1,0:T(8,128)(2,1)}, u32[]{:S(2)}, u32[]{:S(2)}) collective-permute-start(bf16[1024,512]{1,0:T(8,128)(2,1)S(1)} %shard_map.83.refs_4_), channel_id=1, source_target_pairs={{0,7},{1,0},{2,1},{3,2},{4,3},{5,4},{6,5},{7,6},{8,15},{9,8},{10,9... | collective-permute-start | bytes 3145736 | tf_op jit(solution)/shard_map/ppermute | solution.py:22
  39.9 24.3 %collective-permute-start.9 = (bf16[1024,512]{1,0:T(8,128)(2,1)S(1)}, bf16[1024,512]{1,0:T(8,128)(2,1)}, u32[]{:S(2)}, u32[]{:S(2)}) collective-permute-start(bf16[1024,512]{1,0:T(8,128)(2,1)S(1)} %shard_map.83.refs_4_), channel_id=1, source_target_pairs={{0,1},{1,2},{2,3},{3,4},{4,5},{5,6},{6,7},{7,0},{8,9},{9,10},{10,1... | collective-permute-start | bytes 3145736 | tf_op jit(solution)/shard_map/ppermute | solution.py:22
  62.5 10.1 %collective-permute-start.11 = (bf16[1024,128]{1,0:T(8,128)(2,1)S(1)}, bf16[1024,128]{1,0:T(8,128)(2,1)S(1)}, u32[]{:S(2)}, u32[]{:S(2)}) collective-permute-start(bf16[1024,128]{1,0:T(8,128)(2,1)S(1)} %collective-permute-done.7.refs_0_), channel_id=1, source_target_pairs={{0,1},{1,2},{2,3},{3,4},{4,5},{5,6},{6,7},{7,0},{8,9},{9,10},{10,1... | collective-permute-start | bytes 786440 | tf_op jit(solution)/shard_map/ppermute | solution.py:22
  72.7 25.1 %collective-permute-start.15 = (bf16[1024,512]{1,0:T(8,128)(2,1)}, bf16[1024,512]{1,0:T(8,128)(2,1)}, u32[]{:S(2)}, u32[]{:S(2)}) collective-permute-start(bf16[1024,512]{1,0:T(8,128)(2,1)} %collective-permute-done.10.refs_6_), channel_id=1, source_target_pairs={{0,7},{1,0},{2,1},{3,2},{4,3},{5,4},{6,5},{7,6},{8,15},{9,8},{10,9... | collective-permute-start | bytes 3145736 | tf_op jit(solution)/shard_map/ppermute | solution.py:22
  74.4 25.8 %collective-permute-start.14 = (bf16[1024,512]{1,0:T(8,128)(2,1)}, bf16[1024,512]{1,0:T(8,128)(2,1)}, u32[]{:S(2)}, u32[]{:S(2)}) collective-permute-start(bf16[1024,512]{1,0:T(8,128)(2,1)} %collective-permute-done.9.refs_5_), channel_id=1, source_target_pairs={{0,1},{1,2},{2,3},{3,4},{4,5},{5,6},{6,7},{7,0},{8,9},{9,10},{10,1... | collective-permute-start | bytes 3145736 | tf_op jit(solution)/shard_map/ppermute | solution.py:22
  77.0 15.9 %collective-permute-start.18 = (bf16[512,640]{1,0:T(8,128)(2,1)S(1)}, bf16[512,640]{1,0:T(8,128)(2,1)S(1)}, u32[]{:S(2)}, u32[]{:S(2)}) collective-permute-start(bf16[512,640]{1,0:T(8,128)(2,1)S(1)} %slice.25), channel_id=1, source_target_pairs={{0,8},{1,9},{2,10},{3,11},{4,12},{5,13},{6,14},{7,15},{8,16},{9,17... | collective-permute-start | bytes 1966088 | tf_op jit(solution)/shard_map/ppermute | solution.py:22
  77.6 16.8 %collective-permute-start.19 = (bf16[512,640]{1,0:T(8,128)(2,1)S(1)}, bf16[512,640]{1,0:T(8,128)(2,1)S(1)}, u32[]{:S(2)}, u32[]{:S(2)}) collective-permute-start(bf16[512,640]{1,0:T(8,128)(2,1)S(1)} %slice.26), channel_id=1, source_target_pairs={{0,24},{1,25},{2,26},{3,27},{4,28},{5,29},{6,30},{7,31},{8,0},{9,1... | collective-permute-start | bytes 1966088 | tf_op jit(solution)/shard_map/ppermute | solution.py:22
  92.9 16.6 %copy-start.7 = (bf16[512,640]{1,0:T(8,128)(2,1)}, bf16[512,640]{1,0:T(8,128)(2,1)S(1)}, u32[]{:S(2)}) copy-start(bf16[512,640]{1,0:T(8,128)(2,1)S(1)} %collective-permute-done.18.refs_4_) | copy-start | bytes 1966084
  94.3 19.1 %collective-permute-start.21 = (bf16[1024,384]{1,0:T(8,128)(2,1)}, bf16[1024,384]{1,0:T(8,128)(2,1)}, u32[]{:S(2)}, u32[]{:S(2)}) collective-permute-start(bf16[1024,384]{1,0:T(8,128)(2,1)} %copy-done.2), channel_id=1, source_target_pairs={{0,24},{1,25},{2,26},{3,27},{4,28},{5,29},{6,30},{7,31},{8,0},{9,1... | collective-permute-start | bytes 2359304 | tf_op jit(solution)/shard_map/ppermute | solution.py:22
  94.6 19.8 %collective-permute-start.20 = (bf16[1024,384]{1,0:T(8,128)(2,1)}, bf16[1024,384]{1,0:T(8,128)(2,1)}, u32[]{:S(2)}, u32[]{:S(2)}) collective-permute-start(bf16[1024,384]{1,0:T(8,128)(2,1)} %copy-done.2), channel_id=1, source_target_pairs={{0,8},{1,9},{2,10},{3,11},{4,12},{5,13},{6,14},{7,15},{8,16},{9,17... | collective-permute-start | bytes 2359304 | tf_op jit(solution)/shard_map/ppermute | solution.py:22
  100.2 31.6 %collective-permute-start.17 = (bf16[1024,512]{1,0:T(8,128)(2,1)}, bf16[1024,512]{1,0:T(8,128)(2,1)S(1)}, u32[]{:S(2)}, u32[]{:S(2)}) collective-permute-start(bf16[1024,512]{1,0:T(8,128)(2,1)} %collective-permute-done.15.refs_8_), channel_id=1, source_target_pairs={{0,7},{1,0},{2,1},{3,2},{4,3},{5,4},{6,5},{7,6},{8,15},{9,8},{10,9... | collective-permute-start | bytes 3145736 | tf_op jit(solution)/shard_map/ppermute | solution.py:22
  100.4 31.4 %collective-permute-start.16 = (bf16[1024,512]{1,0:T(8,128)(2,1)}, bf16[1024,512]{1,0:T(8,128)(2,1)S(1)}, u32[]{:S(2)}, u32[]{:S(2)}) collective-permute-start(bf16[1024,512]{1,0:T(8,128)(2,1)} %collective-permute-done.14.refs_7_), channel_id=1, source_target_pairs={{0,1},{1,2},{2,3},{3,4},{4,5},{5,6},{6,7},{7,0},{8,9},{9,10},{10,1... | collective-permute-start | bytes 3145736 | tf_op jit(solution)/shard_map/ppermute | solution.py:22
  114.5 17.4 %collective-permute-start.23 = (bf16[512,384]{1,0:T(8,128)(2,1)S(1)}, bf16[512,384]{1,0:T(8,128)(2,1)S(1)}, u32[]{:S(2)}, u32[]{:S(2)}) collective-permute-start(bf16[512,384]{1,0:T(8,128)(2,1)S(1)} %slice.28), channel_id=1, source_target_pairs={{0,24},{1,25},{2,26},{3,27},{4,28},{5,29},{6,30},{7,31},{8,0},{9,1... | collective-permute-start | bytes 1179656 | tf_op jit(solution)/shard_map/ppermute | solution.py:22
  116.5 15.3 %collective-permute-start.22 = (bf16[512,384]{1,0:T(8,128)(2,1)}, bf16[512,384]{1,0:T(8,128)(2,1)S(1)}, u32[]{:S(2)}, u32[]{:S(2)}) collective-permute-start(bf16[512,384]{1,0:T(8,128)(2,1)} %slice.27), channel_id=1, source_target_pairs={{0,8},{1,9},{2,10},{3,11},{4,12},{5,13},{6,14},{7,15},{8,16},{9,17... | collective-permute-start | bytes 1179656 | tf_op jit(solution)/shard_map/ppermute | solution.py:22
  132.7 11.6 %collective-permute-start.25 = (bf16[512,512]{1,0:T(8,128)(2,1)S(1)}, bf16[512,512]{1,0:T(8,128)(2,1)S(1)}, u32[]{:S(2)}, u32[]{:S(2)}) collective-permute-start(bf16[512,512]{1,0:T(8,128)(2,1)S(1)} %slice.29), channel_id=1, source_target_pairs={{0,7},{1,0},{2,1},{3,2},{4,3},{5,4},{6,5},{7,6},{8,15},{9,8},{10,9... | collective-permute-start | bytes 1572872 | tf_op jit(solution)/shard_map/ppermute | solution.py:22
  135.1 11.2 %collective-permute-start.24 = (bf16[512,512]{1,0:T(8,128)(2,1)S(1)}, bf16[512,512]{1,0:T(8,128)(2,1)}, u32[]{:S(2)}, u32[]{:S(2)}) collective-permute-start(bf16[512,512]{1,0:T(8,128)(2,1)S(1)} %slice.24), channel_id=1, source_target_pairs={{0,1},{1,2},{2,3},{3,4},{4,5},{5,6},{6,7},{7,0},{8,9},{9,10},{10,1... | collective-permute-start | bytes 1572872 | tf_op jit(solution)/shard_map/ppermute | solution.py:22
  (8 other events, 17.5 us)
Sparse Core Ops, SparseCore 0:
  9.2 46.1 all-gather.4
  57.2 43.5 all-gather.2

commit v9 on v8

--- a/solution.py
+++ b/solution.py
@@ -237,7 +237,7 @@
 
     labels = (here, sym_ij, sym_cd, amp_mask)
     near, far = (0, -1, 1, -2, 2), (-3, 3, 4)
-    tp = mask(*labels, raw_plus, plus(near, 0, -1, 1) + plus(far, 0), plus(far, -1, 1), plus(near, 2) + plus(far, 2))
+    tp = mask(*labels, raw_plus, plus(near, 0, -1, 1) + plus(far, 0), plus(near, 2) + plus(far, -1, 1, 2))
     z4 = (go(zu[2], tp[0], dz=1),)
     d0 = join([(zu[2],), (zd[2],), z4])
     c2 = (go(c1[0][:HALF], *c1, tp[0], dy=1), go(c1[1][HALF:], *c1, tp[0], dy=-1))
@@ -249,11 +249,9 @@
     wd.append(go(wd[1], wu[1], dz=-1))
     tm = mask(*labels, raw_minus, minus(0, -1, 1, -2, 2), minus(-3, 3), minus(4))
     d2 = (go(d1[0][:HALF], *d1, tm[0], dy=1), go(d1[1][HALF:], *d1, tm[0], dy=-1))
-    total = add(
-        [tm[0], tp[1]], [(w0,), (wu[0],), (wd[0],), (wu[1],), (wd[1],), d1[:1], d1[1:]], total
-    )
+    total = add(tm[:1], [(w0,), (wu[0],), (wd[0],), (wu[1],), (wd[1],)], total)
     w4 = (go(wu[2][:HALF], wd[2], *d2, total, dz=1), go(wd[2][HALF:], wu[2], *d2, total, dz=-1))
-    total = add([tp[2], tm[1]], [c2, d2, (wu[2],), (wd[2],)], total)
+    total = add([tp[1], tm[1]], [c2, d1[:1], d1[1:], d2, (wu[2],), (wd[2],)], total)
     return add(tm[2:], [w4], total, True)
 
 

time: 159 us -> 160 us (level)
  waiting for transfers between devices: 48.4 us -> 45.7 us
  starting transfers between devices: 37.1 us -> 39 us
    ppermute x26, waiting for transfers between devices: 32.2 us -> 30.1 us  [move(): return lax.ppermute(values, 'mem', perm_of(dy, dz))]
    ppermute x26, starting transfers between devices: 37.1 us -> 38.9 us  [move(): return lax.ppermute(values, 'mem', perm_of(dy, dz))]
    slice x1, local copies, waits for them, and re-layouts: 1.78 us -> 0.04 us  [body(): d1[0][:HALF]]
  transfers between devices with their start and end apart: 28 -> 28, of which waited for: 13 -> 12; matrix products, arithmetic and copies ran while one was open for 4% -> 4% of each run, Pallas kernels for 29% -> 29%
where the time goes in v9:
time: 160 us; the launch traced here: 159 us
  Pallas kernels  50.6 us (32%)
  waiting for transfers between devices  45.7 us (29%)
  starting transfers between devices  39 us (24%)
  between operations  13.7 us (9%)
  local copies, waits for them, and re-layouts  9.23 us (6%)
    ppermute x26, starting transfers between devices, move(): return lax.ppermute(values, 'mem', perm_of(dy, dz))  38.9 us
    pallas_call x4, Pallas kernels, product(): pl.pallas_call(kernel, out_shape=jax.ShapeDtypeStruct((768, 1024), BF16 i...  35.5 us
    ppermute x26, waiting for transfers between devices, move(): return lax.ppermute(values, 'mem', perm_of(dy, dz))  30.1 us
    pallas_call x2, Pallas kernels, mask(): pl.pallas_call(kernel, out_shape=[jax.ShapeDtypeStruct(shape, BF16) for s...  14.6 us
    all_gather x1, waiting for transfers between devices, body(): raw_plus = lax.all_gather(amp_plus, 'grp', axis=1, tiled=True)  14.2 us
  transfers between devices with their start and end apart: 28, of which 12 were waited for; matrix products, arithmetic and copies ran while one was open for 4% of the time, Pallas kernels for 29%

profile of v9, /device:TPU:24, one launch (start us, length us, event | category | flops | bytes accessed | tf_op | source)
XLA Modules:
  0.0 158.7 jit_solution(14116384098575420134)
XLA Ops:
  8.0 2.0 %collective-permute-start = (bf16[1024,128]{1,0:T(8,128)(2,1)}, bf16[1024,128]{1,0:T(8,128)(2,1)S(1)}, u32[]{:S(2)}, u32[]{:S(2)}) collective-permute-start(bf16[1024,128]{1,0:T(8,128)(2,1)} %refs_0_.6), channel_id=1, source_target_pairs={{0,8},{1,9},{2,10},{3,11},{4,12},{5,13},{6,14},{7,15},{8,16},{9,17... | collective-permute-start | bytes 786440 | tf_op jit(solution)/shard_map/ppermute | solution.py:22
  10.2 3.9 %collective-permute-start.3 = (bf16[1024,128]{1,0:T(8,128)(2,1)}, bf16[1024,128]{1,0:T(8,128)(2,1)S(1)}, u32[]{:S(2)}, u32[]{:S(2)}) collective-permute-start(bf16[1024,128]{1,0:T(8,128)(2,1)} %refs_0_.7), channel_id=1, source_target_pairs={{0,7},{1,0},{2,1},{3,2},{4,3},{5,4},{6,5},{7,6},{8,15},{9,8},{10,9... | collective-permute-start | bytes 786440 | tf_op jit(solution)/shard_map/ppermute | solution.py:22
  14.2 1.8 %collective-permute-start.1 = (bf16[1024,128]{1,0:T(8,128)(2,1)}, bf16[1024,128]{1,0:T(8,128)(2,1)S(1)}, u32[]{:S(2)}, u32[]{:S(2)}) collective-permute-start(bf16[1024,128]{1,0:T(8,128)(2,1)} %refs_0_.6), channel_id=1, source_target_pairs={{0,24},{1,25},{2,26},{3,27},{4,28},{5,29},{6,30},{7,31},{8,0},{9,1... | collective-permute-start | bytes 786440 | tf_op jit(solution)/shard_map/ppermute | solution.py:22
  16.3 4.2 %collective-permute-done.2.refs_1_ = bf16[1024,128]{1,0:T(8,128)(2,1)S(1)} collective-permute-done((bf16[1024,128]{1,0:T(8,128)(2,1)}, bf16[1024,128]{1,0:T(8,128)(2,1)S(1)}, u32[]{:S(2)}, u32[]{:S(2)}) %collective-permute-start.2) | collective-permute-done | bytes 262176 | tf_op jit(solution)/shard_map/ppermute | solution.py:22
  20.6 3.2 %collective-permute-start.6 = (bf16[1024,128]{1,0:T(8,128)(2,1)S(1)}, bf16[1024,128]{1,0:T(8,128)(2,1)S(1)}, u32[]{:S(2)}, u32[]{:S(2)}) collective-permute-start(bf16[1024,128]{1,0:T(8,128)(2,1)S(1)} %collective-permute-done.3.refs_2_), channel_id=1, source_target_pairs={{0,7},{1,0},{2,1},{3,2},{4,3},{5,4},{6,5},{7,6},{8,15},{9,8},{10,9... | collective-permute-start | bytes 786440 | tf_op jit(solution)/shard_map/ppermute | solution.py:22
  23.8 1.4 collective-permute-start.4
  25.2 3.9 %collective-permute-done.5.refs_3_ = bf16[1024,128]{1,0:T(8,128)(2,1)S(1)} collective-permute-done((bf16[1024,128]{1,0:T(8,128)(2,1)S(1)}, bf16[1024,128]{1,0:T(8,128)(2,1)S(1)}, u32[]{:S(2)}, u32[]{:S(2)}) %collective-permute-start.5) | collective-permute-done | bytes 262176 | tf_op jit(solution)/shard_map/ppermute | solution.py:22
  29.1 1.8 %collective-permute-start.7 = (bf16[1024,128]{1,0:T(8,128)(2,1)S(1)}, bf16[1024,128]{1,0:T(8,128)(2,1)S(1)}, u32[]{:S(2)}, u32[]{:S(2)}) collective-permute-start(bf16[1024,128]{1,0:T(8,128)(2,1)S(1)} %collective-permute-done.5.refs_3_), channel_id=1, source_target_pairs={{0,1},{1,2},{2,3},{3,4},{4,5},{5,6},{6,7},{7,0},{8,9},{9,10},{10,1... | collective-permute-start | bytes 786440 | tf_op jit(solution)/shard_map/ppermute | solution.py:22
  30.9 1.4 collective-permute-start.8
  33.5 1.3 collective-permute-start.12
  37.3 1.7 %collective-permute-start.9 = (bf16[1024,512]{1,0:T(8,128)(2,1)S(1)}, bf16[1024,512]{1,0:T(8,128)(2,1)}, u32[]{:S(2)}, u32[]{:S(2)}) collective-permute-start(bf16[1024,512]{1,0:T(8,128)(2,1)S(1)} %shard_map.83.refs_3_), channel_id=1, source_target_pairs={{0,1},{1,2},{2,3},{3,4},{4,5},{5,6},{6,7},{7,0},{8,9},{9,10},{10,1... | collective-permute-start | bytes 3145736 | tf_op jit(solution)/shard_map/ppermute | solution.py:22
  39.0 1.5 collective-permute-start.10
  41.1 14.2 %all-gather.5.cloned.1.call-done.refs_4_ = bf16[768,4096]{1,0:T(8,128)(2,1)} async-done(((bf16[768,512]{1,0:T(8,128)(2,1)}), bf16[768,4096]{1,0:T(8,128)(2,1)}) %all-gather.5.cloned.1.call-update) | async-done | bytes 6291472 | tf_op jit(solution)/shard_map/all_gather | solution.py:211
  55.4 7.2 %shard_map.84 = (bf16[768,2304]{1,0:T(8,128)(2,1)}, bf16[768,1792]{1,0:T(8,128)(2,1)}) custom-call(s32[2]{0:T(128)} %pad_add_fusion.refs_0_, s32[6]{0:T(128)} %refs_0_.11, s32[32]{0:T(128)} %refs_2_.3, s32[6,32]{1,0:T(8,128)} %refs_3_.3, bf16[768,4096]{1,0:T(8,128)(2,1)} %all-gather.5.cloned.1.call-done.refs_4_), custom_call_target="tpu_custom_call" | custom-call | bytes 12582912 | tf_op jit(solution)/shard_map/pallas_call | solution.py:104
  62.6 1.6 %collective-permute-start.11 = (bf16[1024,128]{1,0:T(8,128)(2,1)S(1)}, bf16[1024,128]{1,0:T(8,128)(2,1)S(1)}, u32[]{:S(2)}, u32[]{:S(2)}) collective-permute-start(bf16[1024,128]{1,0:T(8,128)(2,1)S(1)} %collective-permute-done.7.refs_0_), channel_id=1, source_target_pairs={{0,1},{1,2},{2,3},{3,4},{4,5},{5,6},{6,7},{7,0},{8,9},{9,10},{10,1... | collective-permute-start | bytes 786440 | tf_op jit(solution)/shard_map/ppermute | solution.py:22
  64.2 8.5 %collective-permute-done.11.refs_2_ = bf16[1024,128]{1,0:T(8,128)(2,1)S(1)} collective-permute-done((bf16[1024,128]{1,0:T(8,128)(2,1)S(1)}, bf16[1024,128]{1,0:T(8,128)(2,1)S(1)}, u32[]{:S(2)}, u32[]{:S(2)}) %collective-permute-start.11) | collective-permute-done | bytes 262176 | tf_op jit(solution)/shard_map/ppermute | solution.py:22
  72.7 3.2 %collective-permute-start.15 = (bf16[1024,512]{1,0:T(8,128)(2,1)}, bf16[1024,512]{1,0:T(8,128)(2,1)S(1)}, u32[]{:S(2)}, u32[]{:S(2)}) collective-permute-start(bf16[1024,512]{1,0:T(8,128)(2,1)} %collective-permute-done.10.refs_5_), channel_id=1, source_target_pairs={{0,7},{1,0},{2,1},{3,2},{4,3},{5,4},{6,5},{7,6},{8,15},{9,8},{10,9... | collective-permute-start | bytes 3145736 | tf_op jit(solution)/shard_map/ppermute | solution.py:22
  75.9 2.0 %slice.25 = bf16[512,640]{1,0:T(8,128)(2,1)} slice(bf16[1024,640]{1,0:T(8,128)(2,1)} %collective-permute-done.12.refs_4_), slice={[0:512], [0:640]} | slice | bytes 1310720 | tf_op jit(solution)/shard_map/slice | solution.py:243
  77.9 1.1 slice.26
  79.7 1.5 collective-permute-start.19
  82.2 9.4 %shard_map.87.refs_8_ = f32[768,1024]{1,0:T(8,128)} custom-call(s32[6]{0:T(128)} %refs_0_.11, s32[8]{0:T(128)} %refs_1_.11, bf16[768,2304]{1,0:T(8,128)(2,1)} %get-tuple-element.36.refs_2_, bf16[1024,640]{1,0:T(8,128)(2,1)} %copy-done.1, bf16[1024,640]{1,0:T(8,128)(2,1)} %collective-permute-done.12.refs_4_, ...), custom_call_target="tpu_custom_call" | custom-call | flops 3623878656 | bytes 16646144 | tf_op jit(solution)/shard_map/pallas_call | solution.py:193
  91.6 3.7 %collective-permute-done.18.refs_4_ = bf16[512,640]{1,0:T(8,128)(2,1)} collective-permute-done((bf16[512,640]{1,0:T(8,128)(2,1)}, bf16[512,640]{1,0:T(8,128)(2,1)}, u32[]{:S(2)}, u32[]{:S(2)}) %collective-permute-start.18) | collective-permute-done | bytes 655392 | tf_op jit(solution)/shard_map/ppermute | solution.py:22
  95.3 1.2 collective-permute-done.19.refs_5_
  97.0 1.5 collective-permute-start.21
  99.0 3.2 %collective-permute-start.17 = (bf16[1024,512]{1,0:T(8,128)(2,1)S(1)}, bf16[1024,512]{1,0:T(8,128)(2,1)}, u32[]{:S(2)}, u32[]{:S(2)}) collective-permute-start(bf16[1024,512]{1,0:T(8,128)(2,1)S(1)} %collective-permute-done.15.refs_7_), channel_id=1, source_target_pairs={{0,7},{1,0},{2,1},{3,2},{4,3},{5,4},{6,5},{7,6},{8,15},{9,8},{10,9... | collective-permute-start | bytes 3145736 | tf_op jit(solution)/shard_map/ppermute | solution.py:22
  102.3 7.4 %shard_map.82 = (bf16[768,2560]{1,0:T(8,128)(2,1)}, bf16[768,1024]{1,0:T(8,128)(2,1)}, bf16[768,512]{1,0:T(8,128)(2,1)}) custom-call(s32[2]{0:T(128)} %pad_add_fusion.refs_0_, s32[6]{0:T(128)} %refs_0_.11, s32[32]{0:T(128)} %refs_2_.3, s32[6,32]{1,0:T(8,128)} %refs_3_.3, bf16[768,4096]{1,0:T(8,128)(2,1)} %all-gather.3.cloned.1.call-done.refs_4_), custom_call_target="tpu_custom_call" | custom-call | bytes 12582912 | tf_op jit(solution)/shard_map/pallas_call | solution.py:104
  109.7 4.5 %collective-permute-done.20.refs_6_ = bf16[1024,384]{1,0:T(8,128)(2,1)S(1)} collective-permute-done((bf16[1024,384]{1,0:T(8,128)(2,1)}, bf16[1024,384]{1,0:T(8,128)(2,1)S(1)}, u32[]{:S(2)}, u32[]{:S(2)}) %collective-permute-start.20) | collective-permute-done | bytes 786464 | tf_op jit(solution)/shard_map/ppermute | solution.py:22
  114.2 1.8 %collective-permute-done.21.refs_7_ = bf16[1024,384]{1,0:T(8,128)(2,1)} collective-permute-done((bf16[1024,384]{1,0:T(8,128)(2,1)}, bf16[1024,384]{1,0:T(8,128)(2,1)}, u32[]{:S(2)}, u32[]{:S(2)}) %collective-permute-start.21) | collective-permute-done | bytes 786464 | tf_op jit(solution)/shard_map/ppermute | solution.py:22
  119.2 10.2 %shard_map.88.refs_12_ = f32[768,1024]{1,0:T(8,128)} custom-call(s32[6]{0:T(128)} %refs_0_.11, s32[8]{0:T(128)} %refs_1_.11, bf16[768,2560]{1,0:T(8,128)(2,1)} %get-tuple-element.46.refs_2_, bf16[1024,512]{1,0:T(8,128)(2,1)} %copy-done, bf16[1024,512]{1,0:T(8,128)(2,1)} %collective-permute-done.9.refs_4_, bf16[1024,512]{1,0:T(8,128)(2,1)} %collective-permute-done.10.refs_5_, ...), custom_call_target="tpu_custom_call" | custom-call | flops 4026531840 | bytes 17563648 | tf_op jit(solution)/shard_map/pallas_call | solution.py:193
  131.7 3.3 %collective-permute-start.25 = (bf16[512,512]{1,0:T(8,128)(2,1)S(1)}, bf16[512,512]{1,0:T(8,128)(2,1)S(1)}, u32[]{:S(2)}, u32[]{:S(2)}) collective-permute-start(bf16[512,512]{1,0:T(8,128)(2,1)S(1)} %slice.29), channel_id=1, source_target_pairs={{0,7},{1,0},{2,1},{3,2},{4,3},{5,4},{6,5},{7,6},{8,15},{9,8},{10,9... | collective-permute-start | bytes 1572872 | tf_op jit(solution)/shard_map/ppermute | solution.py:22
  135.0 10.8 %shard_map.89.refs_5_ = f32[768,1024]{1,0:T(8,128)} custom-call(s32[6]{0:T(128)} %refs_0_.11, s32[8]{0:T(128)} %refs_1_.11, bf16[768,1792]{1,0:T(8,128)(2,1)} %get-tuple-element.51.refs_2_, bf16[768,1024]{1,0:T(8,128)(2,1)} %get-tuple-element.52.refs_3_, bf16[512,640]{1,0:T(8,128)(2,1)} %collective-permute-done.18.refs_4_, ...), custom_call_target="tpu_custom_call" | custom-call | flops 4429185024 | bytes 18481152 | tf_op jit(solution)/shard_map/pallas_call | solution.py:193
  146.8 5.0 %shard_map.90 = bf16[768,1024]{1,0:T(8,128)(2,1)} custom-call(s32[6]{0:T(128)} %refs_0_.11, s32[8]{0:T(128)} %refs_1_.11, bf16[768,512]{1,0:T(8,128)(2,1)} %get-tuple-element.29.refs_2_, bf16[512,512]{1,0:T(8,128)(2,1)} %copy-done.7, bf16[512,512]{1,0:T(8,128)(2,1)} %copy-done.8, f32[768,1024]{1,0:T(8,128)} %shard_map.89.refs_5_), custom_call_target="tpu_custom_call" | custom-call | flops 805306368 | bytes 10223616 | tf_op jit(solution)/shard_map/pallas_call | solution.py:193
  (64 shorter events, 15.2 us)
Async XLA Ops:
  6.5 29.1 %copy-start.4 = (bf16[1024,128]{1,0:T(8,128)(2,1)S(1)}, bf16[1024,128]{1,0:T(8,128)(2,1)}, u32[]{:S(2)}) copy-start(bf16[1024,128]{1,0:T(8,128)(2,1)} %refs_0_.6) | copy-start | bytes 786436
  6.5 48.8 %all-gather.5.cloned.1.call-start = ((), (), s32[]{:S(2)}) async-start(), calls=%async_computation.1 | async-start | bytes 7077888 | tf_op jit(solution)/shard_map/all_gather | solution.py:211
  7.3 95.0 %all-gather.3.cloned.1.call-start = ((), (), s32[]{:S(2)}) async-start(), calls=%async_computation | async-start | bytes 7077888 | tf_op jit(solution)/shard_map/all_gather | solution.py:212
  8.0 8.3 %collective-permute-start = (bf16[1024,128]{1,0:T(8,128)(2,1)}, bf16[1024,128]{1,0:T(8,128)(2,1)S(1)}, u32[]{:S(2)}, u32[]{:S(2)}) collective-permute-start(bf16[1024,128]{1,0:T(8,128)(2,1)} %refs_0_.6), channel_id=1, source_target_pairs={{0,8},{1,9},{2,10},{3,11},{4,12},{5,13},{6,14},{7,15},{8,16},{9,17... | collective-permute-start | bytes 786440 | tf_op jit(solution)/shard_map/ppermute | solution.py:22
  10.0 10.5 %collective-permute-start.2 = (bf16[1024,128]{1,0:T(8,128)(2,1)}, bf16[1024,128]{1,0:T(8,128)(2,1)S(1)}, u32[]{:S(2)}, u32[]{:S(2)}) collective-permute-start(bf16[1024,128]{1,0:T(8,128)(2,1)} %refs_0_.7), channel_id=1, source_target_pairs={{0,1},{1,2},{2,3},{3,4},{4,5},{5,6},{6,7},{7,0},{8,9},{9,10},{10,1... | collective-permute-start | bytes 786440 | tf_op jit(solution)/shard_map/ppermute | solution.py:22
  10.2 10.3 %collective-permute-start.3 = (bf16[1024,128]{1,0:T(8,128)(2,1)}, bf16[1024,128]{1,0:T(8,128)(2,1)S(1)}, u32[]{:S(2)}, u32[]{:S(2)}) collective-permute-start(bf16[1024,128]{1,0:T(8,128)(2,1)} %refs_0_.7), channel_id=1, source_target_pairs={{0,7},{1,0},{2,1},{3,2},{4,3},{5,4},{6,5},{7,6},{8,15},{9,8},{10,9... | collective-permute-start | bytes 786440 | tf_op jit(solution)/shard_map/ppermute | solution.py:22
  14.2 9.6 %collective-permute-start.1 = (bf16[1024,128]{1,0:T(8,128)(2,1)}, bf16[1024,128]{1,0:T(8,128)(2,1)S(1)}, u32[]{:S(2)}, u32[]{:S(2)}) collective-permute-start(bf16[1024,128]{1,0:T(8,128)(2,1)} %refs_0_.6), channel_id=1, source_target_pairs={{0,24},{1,25},{2,26},{3,27},{4,28},{5,29},{6,30},{7,31},{8,0},{9,1... | collective-permute-start | bytes 786440 | tf_op jit(solution)/shard_map/ppermute | solution.py:22
  20.5 8.6 %collective-permute-start.5 = (bf16[1024,128]{1,0:T(8,128)(2,1)S(1)}, bf16[1024,128]{1,0:T(8,128)(2,1)S(1)}, u32[]{:S(2)}, u32[]{:S(2)}) collective-permute-start(bf16[1024,128]{1,0:T(8,128)(2,1)S(1)} %collective-permute-done.2.refs_1_), channel_id=1, source_target_pairs={{0,1},{1,2},{2,3},{3,4},{4,5},{5,6},{6,7},{7,0},{8,9},{9,10},{10,1... | collective-permute-start | bytes 786440 | tf_op jit(solution)/shard_map/ppermute | solution.py:22
  20.6 8.6 %collective-permute-start.6 = (bf16[1024,128]{1,0:T(8,128)(2,1)S(1)}, bf16[1024,128]{1,0:T(8,128)(2,1)S(1)}, u32[]{:S(2)}, u32[]{:S(2)}) collective-permute-start(bf16[1024,128]{1,0:T(8,128)(2,1)S(1)} %collective-permute-done.3.refs_2_), channel_id=1, source_target_pairs={{0,7},{1,0},{2,1},{3,2},{4,3},{5,4},{6,5},{7,6},{8,15},{9,8},{10,9... | collective-permute-start | bytes 786440 | tf_op jit(solution)/shard_map/ppermute | solution.py:22
  23.8 9.7 %collective-permute-start.4 = (bf16[1024,128]{1,0:T(8,128)(2,1)S(1)}, bf16[1024,128]{1,0:T(8,128)(2,1)S(1)}, u32[]{:S(2)}, u32[]{:S(2)}) collective-permute-start(bf16[1024,128]{1,0:T(8,128)(2,1)S(1)} %collective-permute-done.refs_1_), channel_id=1, source_target_pairs={{0,8},{1,9},{2,10},{3,11},{4,12},{5,13},{6,14},{7,15},{8,16},{9,17... | collective-permute-start | bytes 786440 | tf_op jit(solution)/shard_map/ppermute | solution.py:22
  29.1 7.6 %collective-permute-start.7 = (bf16[1024,128]{1,0:T(8,128)(2,1)S(1)}, bf16[1024,128]{1,0:T(8,128)(2,1)S(1)}, u32[]{:S(2)}, u32[]{:S(2)}) collective-permute-start(bf16[1024,128]{1,0:T(8,128)(2,1)S(1)} %collective-permute-done.5.refs_3_), channel_id=1, source_target_pairs={{0,1},{1,2},{2,3},{3,4},{4,5},{5,6},{6,7},{7,0},{8,9},{9,10},{10,1... | collective-permute-start | bytes 786440 | tf_op jit(solution)/shard_map/ppermute | solution.py:22
  30.9 6.4 %collective-permute-start.8 = (bf16[1024,128]{1,0:T(8,128)(2,1)S(1)}, bf16[1024,128]{1,0:T(8,128)(2,1)S(1)}, u32[]{:S(2)}, u32[]{:S(2)}) collective-permute-start(bf16[1024,128]{1,0:T(8,128)(2,1)S(1)} %collective-permute-done.6.refs_4_), channel_id=1, source_target_pairs={{0,7},{1,0},{2,1},{3,2},{4,3},{5,4},{6,5},{7,6},{8,15},{9,8},{10,9... | collective-permute-start | bytes 786440 | tf_op jit(solution)/shard_map/ppermute | solution.py:22
  33.5 29.0 %copy-start.1 = (bf16[1024,640]{1,0:T(8,128)(2,1)}, bf16[1024,640]{1,0:T(8,128)(2,1)S(1)}, u32[]{:S(2)}) copy-start(bf16[1024,640]{1,0:T(8,128)(2,1)S(1)} %shard_map.85.refs_3_) | copy-start | bytes 3932164
  33.5 30.7 %collective-permute-start.12 = (bf16[1024,640]{1,0:T(8,128)(2,1)S(1)}, bf16[1024,640]{1,0:T(8,128)(2,1)}, u32[]{:S(2)}, u32[]{:S(2)}) collective-permute-start(bf16[1024,640]{1,0:T(8,128)(2,1)S(1)} %shard_map.85.refs_3_), channel_id=1, source_target_pairs={{0,8},{1,9},{2,10},{3,11},{4,12},{5,13},{6,14},{7,15},{8,16},{9,17... | collective-permute-start | bytes 3932168 | tf_op jit(solution)/shard_map/ppermute | solution.py:22
  34.9 29.3 %collective-permute-start.13 = (bf16[1024,640]{1,0:T(8,128)(2,1)S(1)}, bf16[1024,640]{1,0:T(8,128)(2,1)}, u32[]{:S(2)}, u32[]{:S(2)}) collective-permute-start(bf16[1024,640]{1,0:T(8,128)(2,1)S(1)} %shard_map.85.refs_3_), channel_id=1, source_target_pairs={{0,24},{1,25},{2,26},{3,27},{4,28},{5,29},{6,30},{7,31},{8,0},{9,1... | collective-permute-start | bytes 3932168 | tf_op jit(solution)/shard_map/ppermute | solution.py:22
  35.8 26.7 %copy-start = (bf16[1024,512]{1,0:T(8,128)(2,1)}, bf16[1024,512]{1,0:T(8,128)(2,1)S(1)}, u32[]{:S(2)}) copy-start(bf16[1024,512]{1,0:T(8,128)(2,1)S(1)} %shard_map.83.refs_3_) | copy-start | bytes 3145732
  37.3 26.9 %collective-permute-start.9 = (bf16[1024,512]{1,0:T(8,128)(2,1)S(1)}, bf16[1024,512]{1,0:T(8,128)(2,1)}, u32[]{:S(2)}, u32[]{:S(2)}) collective-permute-start(bf16[1024,512]{1,0:T(8,128)(2,1)S(1)} %shard_map.83.refs_3_), channel_id=1, source_target_pairs={{0,1},{1,2},{2,3},{3,4},{4,5},{5,6},{6,7},{7,0},{8,9},{9,10},{10,1... | collective-permute-start | bytes 3145736 | tf_op jit(solution)/shard_map/ppermute | solution.py:22
  39.0 25.2 %collective-permute-start.10 = (bf16[1024,512]{1,0:T(8,128)(2,1)S(1)}, bf16[1024,512]{1,0:T(8,128)(2,1)}, u32[]{:S(2)}, u32[]{:S(2)}) collective-permute-start(bf16[1024,512]{1,0:T(8,128)(2,1)S(1)} %shard_map.83.refs_3_), channel_id=1, source_target_pairs={{0,7},{1,0},{2,1},{3,2},{4,3},{5,4},{6,5},{7,6},{8,15},{9,8},{10,9... | collective-permute-start | bytes 3145736 | tf_op jit(solution)/shard_map/ppermute | solution.py:22
  62.6 10.1 %collective-permute-start.11 = (bf16[1024,128]{1,0:T(8,128)(2,1)S(1)}, bf16[1024,128]{1,0:T(8,128)(2,1)S(1)}, u32[]{:S(2)}, u32[]{:S(2)}) collective-permute-start(bf16[1024,128]{1,0:T(8,128)(2,1)S(1)} %collective-permute-done.7.refs_0_), channel_id=1, source_target_pairs={{0,1},{1,2},{2,3},{3,4},{4,5},{5,6},{6,7},{7,0},{8,9},{9,10},{10,1... | collective-permute-start | bytes 786440 | tf_op jit(solution)/shard_map/ppermute | solution.py:22
  72.7 26.2 %collective-permute-start.14 = (bf16[1024,512]{1,0:T(8,128)(2,1)}, bf16[1024,512]{1,0:T(8,128)(2,1)S(1)}, u32[]{:S(2)}, u32[]{:S(2)}) collective-permute-start(bf16[1024,512]{1,0:T(8,128)(2,1)} %collective-permute-done.9.refs_4_), channel_id=1, source_target_pairs={{0,1},{1,2},{2,3},{3,4},{4,5},{5,6},{6,7},{7,0},{8,9},{9,10},{10,1... | collective-permute-start | bytes 3145736 | tf_op jit(solution)/shard_map/ppermute | solution.py:22
  72.7 26.3 %collective-permute-start.15 = (bf16[1024,512]{1,0:T(8,128)(2,1)}, bf16[1024,512]{1,0:T(8,128)(2,1)S(1)}, u32[]{:S(2)}, u32[]{:S(2)}) collective-permute-start(bf16[1024,512]{1,0:T(8,128)(2,1)} %collective-permute-done.10.refs_5_), channel_id=1, source_target_pairs={{0,7},{1,0},{2,1},{3,2},{4,3},{5,4},{6,5},{7,6},{8,15},{9,8},{10,9... | collective-permute-start | bytes 3145736 | tf_op jit(solution)/shard_map/ppermute | solution.py:22
  79.1 16.2 %collective-permute-start.18 = (bf16[512,640]{1,0:T(8,128)(2,1)}, bf16[512,640]{1,0:T(8,128)(2,1)}, u32[]{:S(2)}, u32[]{:S(2)}) collective-permute-start(bf16[512,640]{1,0:T(8,128)(2,1)} %slice.25), channel_id=1, source_target_pairs={{0,8},{1,9},{2,10},{3,11},{4,12},{5,13},{6,14},{7,15},{8,16},{9,17... | collective-permute-start | bytes 1966088 | tf_op jit(solution)/shard_map/ppermute | solution.py:22
  79.7 16.9 %collective-permute-start.19 = (bf16[512,640]{1,0:T(8,128)(2,1)S(1)}, bf16[512,640]{1,0:T(8,128)(2,1)}, u32[]{:S(2)}, u32[]{:S(2)}) collective-permute-start(bf16[512,640]{1,0:T(8,128)(2,1)S(1)} %slice.26), channel_id=1, source_target_pairs={{0,24},{1,25},{2,26},{3,27},{4,28},{5,29},{6,30},{7,31},{8,0},{9,1... | collective-permute-start | bytes 1966088 | tf_op jit(solution)/shard_map/ppermute | solution.py:22
  96.5 17.7 %collective-permute-start.20 = (bf16[1024,384]{1,0:T(8,128)(2,1)}, bf16[1024,384]{1,0:T(8,128)(2,1)S(1)}, u32[]{:S(2)}, u32[]{:S(2)}) collective-permute-start(bf16[1024,384]{1,0:T(8,128)(2,1)} %copy-done.2), channel_id=1, source_target_pairs={{0,8},{1,9},{2,10},{3,11},{4,12},{5,13},{6,14},{7,15},{8,16},{9,17... | collective-permute-start | bytes 2359304 | tf_op jit(solution)/shard_map/ppermute | solution.py:22
  97.0 19.0 %collective-permute-start.21 = (bf16[1024,384]{1,0:T(8,128)(2,1)}, bf16[1024,384]{1,0:T(8,128)(2,1)}, u32[]{:S(2)}, u32[]{:S(2)}) collective-permute-start(bf16[1024,384]{1,0:T(8,128)(2,1)} %copy-done.2), channel_id=1, source_target_pairs={{0,24},{1,25},{2,26},{3,27},{4,28},{5,29},{6,30},{7,31},{8,0},{9,1... | collective-permute-start | bytes 2359304 | tf_op jit(solution)/shard_map/ppermute | solution.py:22
  99.0 10.7 %copy-start.5 = (bf16[1024,512]{1,0:T(8,128)(2,1)}, bf16[1024,512]{1,0:T(8,128)(2,1)S(1)}, u32[]{:S(2)}) copy-start(bf16[1024,512]{1,0:T(8,128)(2,1)S(1)} %collective-permute-done.15.refs_7_) | copy-start | bytes 3145732
  99.0 30.4 %collective-permute-start.16 = (bf16[1024,512]{1,0:T(8,128)(2,1)S(1)}, bf16[1024,512]{1,0:T(8,128)(2,1)}, u32[]{:S(2)}, u32[]{:S(2)}) collective-permute-start(bf16[1024,512]{1,0:T(8,128)(2,1)S(1)} %collective-permute-done.14.refs_6_), channel_id=1, source_target_pairs={{0,1},{1,2},{2,3},{3,4},{4,5},{5,6},{6,7},{7,0},{8,9},{9,10},{10,1... | collective-permute-start | bytes 3145736 | tf_op jit(solution)/shard_map/ppermute | solution.py:22
  99.0 31.5 %collective-permute-start.17 = (bf16[1024,512]{1,0:T(8,128)(2,1)S(1)}, bf16[1024,512]{1,0:T(8,128)(2,1)}, u32[]{:S(2)}, u32[]{:S(2)}) collective-permute-start(bf16[1024,512]{1,0:T(8,128)(2,1)S(1)} %collective-permute-done.15.refs_7_), channel_id=1, source_target_pairs={{0,7},{1,0},{2,1},{3,2},{4,3},{5,4},{6,5},{7,6},{8,15},{9,8},{10,9... | collective-permute-start | bytes 3145736 | tf_op jit(solution)/shard_map/ppermute | solution.py:22
  116.0 14.5 %collective-permute-start.22 = (bf16[512,384]{1,0:T(8,128)(2,1)S(1)}, bf16[512,384]{1,0:T(8,128)(2,1)}, u32[]{:S(2)}, u32[]{:S(2)}) collective-permute-start(bf16[512,384]{1,0:T(8,128)(2,1)S(1)} %slice.27), channel_id=1, source_target_pairs={{0,8},{1,9},{2,10},{3,11},{4,12},{5,13},{6,14},{7,15},{8,16},{9,17... | collective-permute-start | bytes 1179656 | tf_op jit(solution)/shard_map/ppermute | solution.py:22
  118.2 12.3 %collective-permute-start.23 = (bf16[512,384]{1,0:T(8,128)(2,1)S(1)}, bf16[512,384]{1,0:T(8,128)(2,1)S(1)}, u32[]{:S(2)}, u32[]{:S(2)}) collective-permute-start(bf16[512,384]{1,0:T(8,128)(2,1)S(1)} %slice.28), channel_id=1, source_target_pairs={{0,24},{1,25},{2,26},{3,27},{4,28},{5,29},{6,30},{7,31},{8,0},{9,1... | collective-permute-start | bytes 1179656 | tf_op jit(solution)/shard_map/ppermute | solution.py:22
  130.5 15.3 %collective-permute-start.24 = (bf16[512,512]{1,0:T(8,128)(2,1)S(1)}, bf16[512,512]{1,0:T(8,128)(2,1)S(1)}, u32[]{:S(2)}, u32[]{:S(2)}) collective-permute-start(bf16[512,512]{1,0:T(8,128)(2,1)S(1)} %slice.24), channel_id=1, source_target_pairs={{0,1},{1,2},{2,3},{3,4},{4,5},{5,6},{6,7},{7,0},{8,9},{9,10},{10,1... | collective-permute-start | bytes 1572872 | tf_op jit(solution)/shard_map/ppermute | solution.py:22
  131.7 14.1 %collective-permute-start.25 = (bf16[512,512]{1,0:T(8,128)(2,1)S(1)}, bf16[512,512]{1,0:T(8,128)(2,1)S(1)}, u32[]{:S(2)}, u32[]{:S(2)}) collective-permute-start(bf16[512,512]{1,0:T(8,128)(2,1)S(1)} %slice.29), channel_id=1, source_target_pairs={{0,7},{1,0},{2,1},{3,2},{4,3},{5,4},{6,5},{7,6},{8,15},{9,8},{10,9... | collective-permute-start | bytes 1572872 | tf_op jit(solution)/shard_map/ppermute | solution.py:22
  (7 other events, 20.6 us)
Sparse Core Ops, SparseCore 0:
  9.2 46.1 all-gather.4
  57.2 43.5 all-gather.2

commit v10 on v9

--- a/solution.py
+++ b/solution.py
@@ -81,13 +81,13 @@
     fetch.wait()
     copies = []
     for p, (target, tiles) in enumerate(zip(laid, parts)):
-        for k, (off_y, off_z) in enumerate(tiles):
+        for k, (panel, off_y, off_z) in enumerate(tiles):
             tile = 8 * ((y + off_y) & (NY - 1)) + ((z + off_z) & (NZ - 1))
             cols = pl.ds(pl.multiple_of(tile * BLK, BLK), BLK)
             label = cd_ref[tile]
             for row in range(6):
                 on = (ij_ref[row] == label) & (mask_ref[row, tile] == 1)
-                kept = raw[row * BLK:(row + 1) * BLK, cols]
+                kept = raw[panel * 768 + row * BLK:panel * 768 + (row + 1) * BLK, cols]
                 target[row * BLK:(row + 1) * BLK, k * BLK:(k + 1) * BLK] = jnp.where(on, kept, jnp.zeros_like(kept))
         copies.append(pltpu.make_async_copy(target, outs[p], sem.at[p]))
         copies[-1].start()
@@ -106,11 +106,11 @@
         out_shape=[jax.ShapeDtypeStruct(shape, BF16) for shape in shapes],
         in_specs=[SMEM] * 4 + [HBM],
         out_specs=[HBM] * len(shapes),
-        scratch_shapes=[pltpu.VMEM((768, 4096), BF16)]
+        scratch_shapes=[pltpu.VMEM((1536, 4096), BF16)]
         + [pltpu.VMEM(shape, BF16) for shape in shapes]
         + [pltpu.SemaphoreType.DMA((len(shapes) + 1,))],
         compiler_params=params(60),
-        cost_estimate=cost(0, 12 * 2**20),
+        cost_estimate=cost(0, 25 * 2**20),
     )(here, sym_ij, sym_cd, amp_mask, raw)
 
 
@@ -208,8 +208,7 @@
     def go(value, *waits, **way):
         return move(after(value, *waits) if waits else value, **way)
 
-    raw_plus = lax.all_gather(amp_plus, "grp", axis=1, tiled=True)
-    raw_minus = lax.all_gather(amp_minus, "grp", axis=1, tiled=True)
+    raw = lax.all_gather(jnp.concatenate([amp_plus, amp_minus], axis=0), "grp", axis=1, tiled=True)
 
     z0, y0 = ints_plus, ints_minus
     zu, zd, yu, yd = [go(z0, dz=1)], [go(z0, dz=-1)], [go(y0, dy=1)], [go(y0, dy=-1)]
@@ -227,32 +226,36 @@
     wu, wd = [go(w0, *threes, dz=1)], [go(w0, *threes, dz=-1)]
 
     def plus(offs, *ys):
-        return [(y, z) for y in ys for z in offs]
+        return [(0, y, z) for y in ys for z in offs]
 
     def minus(*zs):
-        return [(y, z) for z in zs for y in (0, -1, 1, 2)]
+        return [(1, y, z) for z in zs for y in (0, -1, 1, 2)]
 
     def add(amps, blocks, *rest):
         return product(sym_ij, sym_ab, amps, blocks, *rest)
 
-    labels = (here, sym_ij, sym_cd, amp_mask)
     near, far = (0, -1, 1, -2, 2), (-3, 3, 4)
-    tp = mask(*labels, raw_plus, plus(near, 0, -1, 1) + plus(far, 0), plus(near, 2) + plus(far, -1, 1, 2))
-    z4 = (go(zu[2], tp[0], dz=1),)
+    z4 = (go(zu[2], dz=1),)
     d0 = join([(zu[2],), (zd[2],), z4])
-    c2 = (go(c1[0][:HALF], *c1, tp[0], dy=1), go(c1[1][HALF:], *c1, tp[0], dy=-1))
+    c2 = (go(c1[0][:HALF], *c1, dy=1), go(c1[1][HALF:], *c1, dy=-1))
     wu.append(go(wu[0], wd[0], *z4, *c1, dz=1))
     wd.append(go(wd[0], wu[0], *z4, *c1, dz=-1))
-    total = add(tp[:1], [(c0,), c1[:1], c1[1:], (d0,)])
-    d1 = (go(d0, *c2, total, dy=1), go(d0, *c2, total, dy=-1))
-    wu.append(go(wu[1], wd[1], dz=1))
-    wd.append(go(wd[1], wu[1], dz=-1))
-    tm = mask(*labels, raw_minus, minus(0, -1, 1, -2, 2), minus(-3, 3), minus(4))
-    d2 = (go(d1[0][:HALF], *d1, tm[0], dy=1), go(d1[1][HALF:], *d1, tm[0], dy=-1))
-    total = add(tm[:1], [(w0,), (wu[0],), (wd[0],), (wu[1],), (wd[1],)], total)
+    d1 = (go(d0, *c2, dy=1), go(d0, *c2, dy=-1))
+    amps = mask(
+        here, sym_ij, sym_cd, amp_mask, raw,
+        plus(near, 0, -1, 1) + plus(far, 0) + minus(0, -1, 1),
+        plus(near, 2) + plus(far, -1, 1) + minus(-2, 2),
+        plus(far, 2) + minus(-3, 3),
+        minus(4),
+    )
+    wu.append(go(wu[1], wd[1], amps[0], dz=1))
+    wd.append(go(wd[1], wu[1], amps[0], dz=-1))
+    total = add(amps[:1], [(c0,), c1[:1], c1[1:], (d0,), (w0,), (wu[0],), (wd[0],)])
+    d2 = (go(d1[0][:HALF], *d1, total, dy=1), go(d1[1][HALF:], *d1, total, dy=-1))
+    total = add(amps[1:2], [c2, d1[:1], d1[1:], (wu[1],), (wd[1],)], total)
     w4 = (go(wu[2][:HALF], wd[2], *d2, total, dz=1), go(wd[2][HALF:], wu[2], *d2, total, dz=-1))
-    total = add([tp[1], tm[1]], [c2, d1[:1], d1[1:], d2, (wu[2],), (wd[2],)], total)
-    return add(tm[2:], [w4], total, True)
+    total = add(amps[2:3], [d2, (wu[2],), (wd[2],)], total)
+    return add(amps[3:], [w4], total, True)
 
 
 def solution(mesh):

time: 160 us -> 156 us (0.975)
  waiting for transfers between devices: 45.7 us -> 50 us
  local copies, waits for them, and re-layouts: 9.23 us -> 5.76 us
  starting transfers between devices: 39 us -> 35.8 us
  Pallas kernels: 50.6 us -> 47.6 us
  other arithmetic: 0.58 us -> 3.32 us
    ppermute x26, waiting for transfers between devices: 30.1 us -> 50 us  [move(): return lax.ppermute(values, 'mem', perm_of(dy, dz))]
    all_gather x2 -> x1, waiting for transfers between devices: 14.2 us -> 0.01 us  [body(): lax.all_gather(jnp.concatenate([amp_plus, amp_minus], axis=0), 'grp', axi...]
    ppermute x26, starting transfers between devices: 38.9 us -> 35.8 us  [move(): return lax.ppermute(values, 'mem', perm_of(dy, dz))]
    pallas_call x2 -> x1, Pallas kernels: 14.6 us -> 11.5 us  [mask(): pl.pallas_call(kernel, out_shape=[jax.ShapeDtypeStruct(shape, BF16) for s...]
    slice x2, local copies, waits for them, and re-layouts: 3.14 us -> 0.11 us  [body(): c2 = (go(c1[0][:HALF], *c1, dy=1), go(c1[1][HALF:], *c1, dy=-1))]
    concatenate x0 -> x1, other arithmetic: none -> 2.67 us  [body(): jnp.concatenate([amp_plus, amp_minus], axis=0)]
  transfers between devices with their start and end apart: 28 -> 27, of which waited for: 12 -> 14; matrix products, arithmetic and copies ran while one was open for 4% -> 2% of each run, Pallas kernels for 29% -> 27%
where the time goes in v10:
time: 156 us
  waiting for transfers between devices  50 us (32%)
  Pallas kernels  47.6 us (31%)
  starting transfers between devices  35.8 us (23%)
  between operations  13.6 us (9%)
  local copies, waits for them, and re-layouts  5.76 us (4%)
  other arithmetic  3.32 us (2%)
    ppermute x26, waiting for transfers between devices, move(): return lax.ppermute(values, 'mem', perm_of(dy, dz))  50 us
    ppermute x26, starting transfers between devices, move(): return lax.ppermute(values, 'mem', perm_of(dy, dz))  35.8 us
    pallas_call x4, Pallas kernels, product(): pl.pallas_call(kernel, out_shape=jax.ShapeDtypeStruct((768, 1024), BF16 i...  35.6 us
    pallas_call x1, Pallas kernels, mask(): pl.pallas_call(kernel, out_shape=[jax.ShapeDtypeStruct(shape, BF16) for s...  11.5 us
  transfers between devices with their start and end apart: 27, of which 14 were waited for; matrix products, arithmetic and copies ran while one was open for 2% of the time, Pallas kernels for 27%

profile of v10, /device:TPU:24, one launch (start us, length us, event | category | flops | bytes accessed | tf_op | source)
XLA Modules:
  0.0 156.1 jit_solution(5183568629462206593)
XLA Ops:
  6.5 2.7 %pad_maximum_fusion = bf16[1536,512]{1,0:T(8,128)(2,1)} fusion(bf16[768,512]{1,0:T(8,128)(2,1)} %param.9, bf16[768,512]{1,0:T(8,128)(2,1)} %param.8), kind=kLoop, calls=%fused_computation | loop fusion | flops 3145728 | bytes 3145728 | tf_op jit(solution)/shard_map/concatenate | solution.py:211
  9.2 2.0 %collective-permute-start = (bf16[1024,128]{1,0:T(8,128)(2,1)S(1)}, bf16[1024,128]{1,0:T(8,128)(2,1)S(1)}, u32[]{:S(2)}, u32[]{:S(2)}) collective-permute-start(bf16[1024,128]{1,0:T(8,128)(2,1)S(1)} %copy-done.4), channel_id=1, source_target_pairs={{0,8},{1,9},{2,10},{3,11},{4,12},{5,13},{6,14},{7,15},{8,16},{9,17... | collective-permute-start | bytes 786440 | tf_op jit(solution)/shard_map/ppermute | solution.py:22
  11.5 3.9 %collective-permute-start.3 = (bf16[1024,128]{1,0:T(8,128)(2,1)S(1)}, bf16[1024,128]{1,0:T(8,128)(2,1)S(1)}, u32[]{:S(2)}, u32[]{:S(2)}) collective-permute-start(bf16[1024,128]{1,0:T(8,128)(2,1)S(1)} %copy-done.3), channel_id=1, source_target_pairs={{0,7},{1,0},{2,1},{3,2},{4,3},{5,4},{6,5},{7,6},{8,15},{9,8},{10,9... | collective-permute-start | bytes 786440 | tf_op jit(solution)/shard_map/ppermute | solution.py:22
  15.4 1.8 %collective-permute-start.1 = (bf16[1024,128]{1,0:T(8,128)(2,1)S(1)}, bf16[1024,128]{1,0:T(8,128)(2,1)S(1)}, u32[]{:S(2)}, u32[]{:S(2)}) collective-permute-start(bf16[1024,128]{1,0:T(8,128)(2,1)S(1)} %copy-done.4), channel_id=1, source_target_pairs={{0,24},{1,25},{2,26},{3,27},{4,28},{5,29},{6,30},{7,31},{8,0},{9,1... | collective-permute-start | bytes 786440 | tf_op jit(solution)/shard_map/ppermute | solution.py:22
  17.4 4.2 %collective-permute-done.2.refs_1_ = bf16[1024,128]{1,0:T(8,128)(2,1)S(1)} collective-permute-done((bf16[1024,128]{1,0:T(8,128)(2,1)S(1)}, bf16[1024,128]{1,0:T(8,128)(2,1)S(1)}, u32[]{:S(2)}, u32[]{:S(2)}) %collective-permute-start.2) | collective-permute-done | bytes 262176 | tf_op jit(solution)/shard_map/ppermute | solution.py:22
  21.6 3.2 %collective-permute-start.6 = (bf16[1024,128]{1,0:T(8,128)(2,1)S(1)}, bf16[1024,128]{1,0:T(8,128)(2,1)S(1)}, u32[]{:S(2)}, u32[]{:S(2)}) collective-permute-start(bf16[1024,128]{1,0:T(8,128)(2,1)S(1)} %collective-permute-done.3.refs_2_), channel_id=1, source_target_pairs={{0,7},{1,0},{2,1},{3,2},{4,3},{5,4},{6,5},{7,6},{8,15},{9,8},{10,9... | collective-permute-start | bytes 786440 | tf_op jit(solution)/shard_map/ppermute | solution.py:22
  24.8 1.4 collective-permute-start.4
  26.3 3.9 %collective-permute-done.5.refs_3_ = bf16[1024,128]{1,0:T(8,128)(2,1)S(1)} collective-permute-done((bf16[1024,128]{1,0:T(8,128)(2,1)S(1)}, bf16[1024,128]{1,0:T(8,128)(2,1)S(1)}, u32[]{:S(2)}, u32[]{:S(2)}) %collective-permute-start.5) | collective-permute-done | bytes 262176 | tf_op jit(solution)/shard_map/ppermute | solution.py:22
  30.4 1.2 collective-permute-done.4.refs_3_
  31.6 2.5 %collective-permute-start.12 = (bf16[1024,640]{1,0:T(8,128)(2,1)S(1)}, bf16[1024,640]{1,0:T(8,128)(2,1)S(1)}, u32[]{:S(2)}, u32[]{:S(2)}) collective-permute-start(bf16[1024,640]{1,0:T(8,128)(2,1)S(1)} %shard_map.84.refs_3_), channel_id=1, source_target_pairs={{0,8},{1,9},{2,10},{3,11},{4,12},{5,13},{6,14},{7,15},{8,16},{9,17... | collective-permute-start | bytes 3932168 | tf_op jit(solution)/shard_map/ppermute | solution.py:22
  34.3 3.0 %collective-permute-start.8 = (bf16[1024,128]{1,0:T(8,128)(2,1)S(1)}, bf16[1024,128]{1,0:T(8,128)(2,1)S(1)}, u32[]{:S(2)}, u32[]{:S(2)}) collective-permute-start(bf16[1024,128]{1,0:T(8,128)(2,1)S(1)} %collective-permute-done.6.refs_4_), channel_id=1, source_target_pairs={{0,7},{1,0},{2,1},{3,2},{4,3},{5,4},{6,5},{7,6},{8,15},{9,8},{10,9... | collective-permute-start | bytes 786440 | tf_op jit(solution)/shard_map/ppermute | solution.py:22
  37.5 4.2 %collective-permute-done.7.refs_0_ = bf16[1024,128]{1,0:T(8,128)(2,1)S(1)} collective-permute-done((bf16[1024,128]{1,0:T(8,128)(2,1)S(1)}, bf16[1024,128]{1,0:T(8,128)(2,1)S(1)}, u32[]{:S(2)}, u32[]{:S(2)}) %collective-permute-start.7) | collective-permute-done | bytes 262176 | tf_op jit(solution)/shard_map/ppermute | solution.py:22
  41.7 3.2 %collective-permute-start.10 = (bf16[1024,512]{1,0:T(8,128)(2,1)S(1)}, bf16[1024,512]{1,0:T(8,128)(2,1)}, u32[]{:S(2)}, u32[]{:S(2)}) collective-permute-start(bf16[1024,512]{1,0:T(8,128)(2,1)S(1)} %shard_map.83.refs_7_), channel_id=1, source_target_pairs={{0,7},{1,0},{2,1},{3,2},{4,3},{5,4},{6,5},{7,6},{8,15},{9,8},{10,9... | collective-permute-start | bytes 3145736 | tf_op jit(solution)/shard_map/ppermute | solution.py:22
  44.9 15.1 %collective-permute-done.12.refs_4_ = bf16[1024,640]{1,0:T(8,128)(2,1)S(1)} collective-permute-done((bf16[1024,640]{1,0:T(8,128)(2,1)S(1)}, bf16[1024,640]{1,0:T(8,128)(2,1)S(1)}, u32[]{:S(2)}, u32[]{:S(2)}) %collective-permute-start.12) | collective-permute-done | bytes 1310752 | tf_op jit(solution)/shard_map/ppermute | solution.py:22
  61.0 2.2 %collective-permute-done.13.refs_5_ = bf16[1024,640]{1,0:T(8,128)(2,1)S(1)} collective-permute-done((bf16[1024,640]{1,0:T(8,128)(2,1)S(1)}, bf16[1024,640]{1,0:T(8,128)(2,1)S(1)}, u32[]{:S(2)}, u32[]{:S(2)}) %collective-permute-start.13) | collective-permute-done | bytes 1310752 | tf_op jit(solution)/shard_map/ppermute | solution.py:22
  63.3 1.4 collective-permute-start.18
  65.6 7.6 %collective-permute-done.11.refs_2_ = bf16[1024,128]{1,0:T(8,128)(2,1)S(1)} collective-permute-done((bf16[1024,128]{1,0:T(8,128)(2,1)S(1)}, bf16[1024,128]{1,0:T(8,128)(2,1)S(1)}, u32[]{:S(2)}, u32[]{:S(2)}) %collective-permute-start.11) | collective-permute-done | bytes 262176 | tf_op jit(solution)/shard_map/ppermute | solution.py:22
  73.2 2.0 %collective-permute-start.14 = (bf16[1024,512]{1,0:T(8,128)(2,1)}, bf16[1024,512]{1,0:T(8,128)(2,1)}, u32[]{:S(2)}, u32[]{:S(2)}) collective-permute-start(bf16[1024,512]{1,0:T(8,128)(2,1)} %collective-permute-done.9.refs_8_), channel_id=1, source_target_pairs={{0,1},{1,2},{2,3},{3,4},{4,5},{5,6},{6,7},{7,0},{8,9},{9,10},{10,1... | collective-permute-start | bytes 3145736 | tf_op jit(solution)/shard_map/ppermute | solution.py:22
  76.4 3.4 %collective-permute-done.19.refs_4_ = bf16[512,640]{1,0:T(8,128)(2,1)S(1)} collective-permute-done((bf16[512,640]{1,0:T(8,128)(2,1)S(1)}, bf16[512,640]{1,0:T(8,128)(2,1)S(1)}, u32[]{:S(2)}, u32[]{:S(2)}) %collective-permute-start.19) | collective-permute-done | bytes 655392 | tf_op jit(solution)/shard_map/ppermute | solution.py:22
  80.6 2.4 %collective-permute-start.20 = (bf16[1024,384]{1,0:T(8,128)(2,1)S(1)}, bf16[1024,384]{1,0:T(8,128)(2,1)}, u32[]{:S(2)}, u32[]{:S(2)}) collective-permute-start(bf16[1024,384]{1,0:T(8,128)(2,1)S(1)} %shard_map.85.refs_6_), channel_id=1, source_target_pairs={{0,8},{1,9},{2,10},{3,11},{4,12},{5,13},{6,14},{7,15},{8,16},{9,17... | collective-permute-start | bytes 2359304 | tf_op jit(solution)/shard_map/ppermute | solution.py:22
  83.6 11.5 %shard_map.82 = (bf16[768,3840]{1,0:T(8,128)(2,1)}, bf16[768,2432]{1,0:T(8,128)(2,1)}, bf16[768,1408]{1,0:T(8,128)(2,1)}, bf16[768,512]{1,0:T(8,128)(2,1)}) custom-call(s32[2]{0:T(128)} %pad_add_fusion.refs_0_, s32[6]{0:T(128)} %refs_0_.11, s32[32]{0:T(128)} %refs_2_.1, s32[6,32]{1,0:T(8,128)} %refs_3_.1, bf16[1536,4096]{1,0:T(8,128)(2,1)} %all-gather.2.cloned.1.call-done.refs_4_), custom_call_target="tpu_custom_call" | custom-call | bytes 26214400 | tf_op jit(solution)/shard_map/pallas_call | solution.py:104
  95.6 1.3 collective-permute-done.14.refs_7_
  97.1 1.8 %collective-permute-start.16 = (bf16[1024,512]{1,0:T(8,128)(2,1)}, bf16[1024,512]{1,0:T(8,128)(2,1)S(1)}, u32[]{:S(2)}, u32[]{:S(2)}) collective-permute-start(bf16[1024,512]{1,0:T(8,128)(2,1)} %collective-permute-done.14.refs_7_), channel_id=1, source_target_pairs={{0,1},{1,2},{2,3},{3,4},{4,5},{5,6},{6,7},{7,0},{8,9},{9,10},{10,1... | collective-permute-start | bytes 3145736 | tf_op jit(solution)/shard_map/ppermute | solution.py:22
  98.9 1.8 %slice.28 = bf16[512,384]{1,0:T(8,128)(2,1)} slice(bf16[1024,384]{1,0:T(8,128)(2,1)} %collective-permute-done.21.refs_6_), slice={[512:1024], [0:384]} | slice | bytes 786432 | tf_op jit(solution)/shard_map/slice | solution.py:254
  101.7 12.7 %shard_map.86.refs_9_ = f32[768,1024]{1,0:T(8,128)} custom-call(s32[6]{0:T(128)} %refs_0_.11, s32[8]{0:T(128)} %refs_1_.9, bf16[768,3840]{1,0:T(8,128)(2,1)} %get-tuple-element.37.refs_2_, bf16[1024,640]{1,0:T(8,128)(2,1)} %copy-done, bf16[1024,640]{1,0:T(8,128)(2,1)} %copy-done.12, bf16[1024,640]{1,0:T(8,128)(2,1)} %copy-done.13, ...), custom_call_target="tpu_custom_call" | custom-call | flops 6039797760 | bytes 22151168 | tf_op jit(solution)/shard_map/pallas_call | solution.py:193
  115.5 2.3 %collective-permute-start.22 = (bf16[512,384]{1,0:T(8,128)(2,1)S(1)}, bf16[512,384]{1,0:T(8,128)(2,1)S(1)}, u32[]{:S(2)}, u32[]{:S(2)}) collective-permute-start(bf16[512,384]{1,0:T(8,128)(2,1)S(1)} %slice.27), channel_id=1, source_target_pairs={{0,8},{1,9},{2,10},{3,11},{4,12},{5,13},{6,14},{7,15},{8,16},{9,17... | collective-permute-start | bytes 1179656 | tf_op jit(solution)/shard_map/ppermute | solution.py:22
  117.8 10.1 %shard_map.87.refs_7_ = f32[768,1024]{1,0:T(8,128)} custom-call(s32[6]{0:T(128)} %refs_0_.11, s32[8]{0:T(128)} %refs_1_.9, bf16[768,2432]{1,0:T(8,128)(2,1)} %get-tuple-element.45.refs_2_, bf16[512,640]{1,0:T(8,128)(2,1)} %copy-done.7, bf16[512,640]{1,0:T(8,128)(2,1)} %copy-done.8, bf16[1024,384]{1,0:T(8,128)(2,1)} %collective-permute-done.20.refs_5_, ...), custom_call_target="tpu_custom_call" | custom-call | flops 3825205248 | bytes 17104896 | tf_op jit(solution)/shard_map/pallas_call | solution.py:193
  128.9 1.4 collective-permute-start.25
  131.1 7.7 %shard_map.88.refs_5_ = f32[768,1024]{1,0:T(8,128)} custom-call(s32[6]{0:T(128)} %refs_0_.11, s32[8]{0:T(128)} %refs_1_.9, bf16[768,1408]{1,0:T(8,128)(2,1)} %get-tuple-element.48.refs_2_, bf16[512,384]{1,0:T(8,128)(2,1)} %copy-done.11, bf16[512,384]{1,0:T(8,128)(2,1)} %copy-done.10, bf16[1024,512]{1,0:T(8,128)(2,1)} %copy-done.6, ...), custom_call_target="tpu_custom_call" | custom-call | flops 2214592512 | bytes 13434880 | tf_op jit(solution)/shard_map/pallas_call | solution.py:193
  138.8 1.8 %collective-permute-done.25.refs_4_ = bf16[512,512]{1,0:T(8,128)(2,1)S(1)} collective-permute-done((bf16[512,512]{1,0:T(8,128)(2,1)S(1)}, bf16[512,512]{1,0:T(8,128)(2,1)S(1)}, u32[]{:S(2)}, u32[]{:S(2)}) %collective-permute-start.25) | collective-permute-done | bytes 524320 | tf_op jit(solution)/shard_map/ppermute | solution.py:22
  140.6 3.6 %collective-permute-done.24.refs_3_ = bf16[512,512]{1,0:T(8,128)(2,1)} collective-permute-done((bf16[512,512]{1,0:T(8,128)(2,1)S(1)}, bf16[512,512]{1,0:T(8,128)(2,1)}, u32[]{:S(2)}, u32[]{:S(2)}) %collective-permute-start.24) | collective-permute-done | bytes 524320 | tf_op jit(solution)/shard_map/ppermute | solution.py:22
  144.2 5.0 %shard_map.89 = bf16[768,1024]{1,0:T(8,128)(2,1)} custom-call(s32[6]{0:T(128)} %refs_0_.11, s32[8]{0:T(128)} %refs_1_.9, bf16[768,512]{1,0:T(8,128)(2,1)} %get-tuple-element.27.refs_2_, bf16[512,512]{1,0:T(8,128)(2,1)} %collective-permute-done.24.refs_3_, bf16[512,512]{1,0:T(8,128)(2,1)} %copy-done.9, f32[768,1024]{1,0:T(8,128)} %shard_map.88.refs_5_), custom_call_target="tpu_custom_call" | custom-call | flops 805306368 | bytes 10223616 | tf_op jit(solution)/shard_map/pallas_call | solution.py:193
  (67 shorter events, 10.1 us)
Async XLA Ops:
  6.5 4.7 %copy-start.3 = (bf16[1024,128]{1,0:T(8,128)(2,1)S(1)}, bf16[1024,128]{1,0:T(8,128)(2,1)}, u32[]{:S(2)}) copy-start(bf16[1024,128]{1,0:T(8,128)(2,1)} %refs_0_.7) | copy-start | bytes 786436
  6.5 77.1 %all-gather.2.cloned.1.call-start = ((), (), s32[]{:S(2)}) async-start(), calls=%async_computation | async-start | bytes 14155776 | tf_op jit(solution)/shard_map/all_gather | solution.py:211
  9.2 8.1 %collective-permute-start = (bf16[1024,128]{1,0:T(8,128)(2,1)S(1)}, bf16[1024,128]{1,0:T(8,128)(2,1)S(1)}, u32[]{:S(2)}, u32[]{:S(2)}) collective-permute-start(bf16[1024,128]{1,0:T(8,128)(2,1)S(1)} %copy-done.4), channel_id=1, source_target_pairs={{0,8},{1,9},{2,10},{3,11},{4,12},{5,13},{6,14},{7,15},{8,16},{9,17... | collective-permute-start | bytes 786440 | tf_op jit(solution)/shard_map/ppermute | solution.py:22
  11.3 10.3 %collective-permute-start.2 = (bf16[1024,128]{1,0:T(8,128)(2,1)S(1)}, bf16[1024,128]{1,0:T(8,128)(2,1)S(1)}, u32[]{:S(2)}, u32[]{:S(2)}) collective-permute-start(bf16[1024,128]{1,0:T(8,128)(2,1)S(1)} %copy-done.3), channel_id=1, source_target_pairs={{0,1},{1,2},{2,3},{3,4},{4,5},{5,6},{6,7},{7,0},{8,9},{9,10},{10,1... | collective-permute-start | bytes 786440 | tf_op jit(solution)/shard_map/ppermute | solution.py:22
  11.5 10.1 %collective-permute-start.3 = (bf16[1024,128]{1,0:T(8,128)(2,1)S(1)}, bf16[1024,128]{1,0:T(8,128)(2,1)S(1)}, u32[]{:S(2)}, u32[]{:S(2)}) collective-permute-start(bf16[1024,128]{1,0:T(8,128)(2,1)S(1)} %copy-done.3), channel_id=1, source_target_pairs={{0,7},{1,0},{2,1},{3,2},{4,3},{5,4},{6,5},{7,6},{8,15},{9,8},{10,9... | collective-permute-start | bytes 786440 | tf_op jit(solution)/shard_map/ppermute | solution.py:22
  15.4 9.4 %collective-permute-start.1 = (bf16[1024,128]{1,0:T(8,128)(2,1)S(1)}, bf16[1024,128]{1,0:T(8,128)(2,1)S(1)}, u32[]{:S(2)}, u32[]{:S(2)}) collective-permute-start(bf16[1024,128]{1,0:T(8,128)(2,1)S(1)} %copy-done.4), channel_id=1, source_target_pairs={{0,24},{1,25},{2,26},{3,27},{4,28},{5,29},{6,30},{7,31},{8,0},{9,1... | collective-permute-start | bytes 786440 | tf_op jit(solution)/shard_map/ppermute | solution.py:22
  21.6 8.6 %collective-permute-start.5 = (bf16[1024,128]{1,0:T(8,128)(2,1)S(1)}, bf16[1024,128]{1,0:T(8,128)(2,1)S(1)}, u32[]{:S(2)}, u32[]{:S(2)}) collective-permute-start(bf16[1024,128]{1,0:T(8,128)(2,1)S(1)} %collective-permute-done.2.refs_1_), channel_id=1, source_target_pairs={{0,1},{1,2},{2,3},{3,4},{4,5},{5,6},{6,7},{7,0},{8,9},{9,10},{10,1... | collective-permute-start | bytes 786440 | tf_op jit(solution)/shard_map/ppermute | solution.py:22
  21.6 8.6 %collective-permute-start.6 = (bf16[1024,128]{1,0:T(8,128)(2,1)S(1)}, bf16[1024,128]{1,0:T(8,128)(2,1)S(1)}, u32[]{:S(2)}, u32[]{:S(2)}) collective-permute-start(bf16[1024,128]{1,0:T(8,128)(2,1)S(1)} %collective-permute-done.3.refs_2_), channel_id=1, source_target_pairs={{0,7},{1,0},{2,1},{3,2},{4,3},{5,4},{6,5},{7,6},{8,15},{9,8},{10,9... | collective-permute-start | bytes 786440 | tf_op jit(solution)/shard_map/ppermute | solution.py:22
  24.8 6.8 %collective-permute-start.4 = (bf16[1024,128]{1,0:T(8,128)(2,1)S(1)}, bf16[1024,128]{1,0:T(8,128)(2,1)S(1)}, u32[]{:S(2)}, u32[]{:S(2)}) collective-permute-start(bf16[1024,128]{1,0:T(8,128)(2,1)S(1)} %collective-permute-done.refs_1_), channel_id=1, source_target_pairs={{0,8},{1,9},{2,10},{3,11},{4,12},{5,13},{6,14},{7,15},{8,16},{9,17... | collective-permute-start | bytes 786440 | tf_op jit(solution)/shard_map/ppermute | solution.py:22
  30.4 45.0 %copy-start = (bf16[1024,640]{1,0:T(8,128)(2,1)}, bf16[1024,640]{1,0:T(8,128)(2,1)S(1)}, u32[]{:S(2)}) copy-start(bf16[1024,640]{1,0:T(8,128)(2,1)S(1)} %shard_map.84.refs_3_) | copy-start | bytes 3932164
  31.6 28.3 %collective-permute-start.12 = (bf16[1024,640]{1,0:T(8,128)(2,1)S(1)}, bf16[1024,640]{1,0:T(8,128)(2,1)S(1)}, u32[]{:S(2)}, u32[]{:S(2)}) collective-permute-start(bf16[1024,640]{1,0:T(8,128)(2,1)S(1)} %shard_map.84.refs_3_), channel_id=1, source_target_pairs={{0,8},{1,9},{2,10},{3,11},{4,12},{5,13},{6,14},{7,15},{8,16},{9,17... | collective-permute-start | bytes 3932168 | tf_op jit(solution)/shard_map/ppermute | solution.py:22
  34.1 29.2 %collective-permute-start.13 = (bf16[1024,640]{1,0:T(8,128)(2,1)S(1)}, bf16[1024,640]{1,0:T(8,128)(2,1)S(1)}, u32[]{:S(2)}, u32[]{:S(2)}) collective-permute-start(bf16[1024,640]{1,0:T(8,128)(2,1)S(1)} %shard_map.84.refs_3_), channel_id=1, source_target_pairs={{0,24},{1,25},{2,26},{3,27},{4,28},{5,29},{6,30},{7,31},{8,0},{9,1... | collective-permute-start | bytes 3932168 | tf_op jit(solution)/shard_map/ppermute | solution.py:22
  34.1 7.6 %collective-permute-start.7 = (bf16[1024,128]{1,0:T(8,128)(2,1)S(1)}, bf16[1024,128]{1,0:T(8,128)(2,1)S(1)}, u32[]{:S(2)}, u32[]{:S(2)}) collective-permute-start(bf16[1024,128]{1,0:T(8,128)(2,1)S(1)} %collective-permute-done.5.refs_3_), channel_id=1, source_target_pairs={{0,1},{1,2},{2,3},{3,4},{4,5},{5,6},{6,7},{7,0},{8,9},{9,10},{10,1... | collective-permute-start | bytes 786440 | tf_op jit(solution)/shard_map/ppermute | solution.py:22
  34.3 7.3 %collective-permute-start.8 = (bf16[1024,128]{1,0:T(8,128)(2,1)S(1)}, bf16[1024,128]{1,0:T(8,128)(2,1)S(1)}, u32[]{:S(2)}, u32[]{:S(2)}) collective-permute-start(bf16[1024,128]{1,0:T(8,128)(2,1)S(1)} %collective-permute-done.6.refs_4_), channel_id=1, source_target_pairs={{0,7},{1,0},{2,1},{3,2},{4,3},{5,4},{6,5},{7,6},{8,15},{9,8},{10,9... | collective-permute-start | bytes 786440 | tf_op jit(solution)/shard_map/ppermute | solution.py:22
  37.5 57.6 %copy-start.1 = (bf16[1024,512]{1,0:T(8,128)(2,1)}, bf16[1024,512]{1,0:T(8,128)(2,1)S(1)}, u32[]{:S(2)}) copy-start(bf16[1024,512]{1,0:T(8,128)(2,1)S(1)} %shard_map.83.refs_7_) | copy-start | bytes 3145732
  41.7 31.5 %collective-permute-start.10 = (bf16[1024,512]{1,0:T(8,128)(2,1)S(1)}, bf16[1024,512]{1,0:T(8,128)(2,1)}, u32[]{:S(2)}, u32[]{:S(2)}) collective-permute-start(bf16[1024,512]{1,0:T(8,128)(2,1)S(1)} %shard_map.83.refs_7_), channel_id=1, source_target_pairs={{0,7},{1,0},{2,1},{3,2},{4,3},{5,4},{6,5},{7,6},{8,15},{9,8},{10,9... | collective-permute-start | bytes 3145736 | tf_op jit(solution)/shard_map/ppermute | solution.py:22
  44.9 28.3 %collective-permute-start.9 = (bf16[1024,512]{1,0:T(8,128)(2,1)S(1)}, bf16[1024,512]{1,0:T(8,128)(2,1)}, u32[]{:S(2)}, u32[]{:S(2)}) collective-permute-start(bf16[1024,512]{1,0:T(8,128)(2,1)S(1)} %shard_map.83.refs_7_), channel_id=1, source_target_pairs={{0,1},{1,2},{2,3},{3,4},{4,5},{5,6},{6,7},{7,0},{8,9},{9,10},{10,1... | collective-permute-start | bytes 3145736 | tf_op jit(solution)/shard_map/ppermute | solution.py:22
  63.3 19.7 %copy-start.13 = (bf16[1024,640]{1,0:T(8,128)(2,1)}, bf16[1024,640]{1,0:T(8,128)(2,1)S(1)}, u32[]{:S(2)}) copy-start(bf16[1024,640]{1,0:T(8,128)(2,1)S(1)} %collective-permute-done.13.refs_5_) | copy-start | bytes 3932164
  63.3 13.1 %collective-permute-start.18 = (bf16[512,640]{1,0:T(8,128)(2,1)S(1)}, bf16[512,640]{1,0:T(8,128)(2,1)S(1)}, u32[]{:S(2)}, u32[]{:S(2)}) collective-permute-start(bf16[512,640]{1,0:T(8,128)(2,1)S(1)} %slice.25), channel_id=1, source_target_pairs={{0,8},{1,9},{2,10},{3,11},{4,12},{5,13},{6,14},{7,15},{8,16},{9,17... | collective-permute-start | bytes 1966088 | tf_op jit(solution)/shard_map/ppermute | solution.py:22
  64.7 15.0 %collective-permute-start.19 = (bf16[512,640]{1,0:T(8,128)(2,1)S(1)}, bf16[512,640]{1,0:T(8,128)(2,1)S(1)}, u32[]{:S(2)}, u32[]{:S(2)}) collective-permute-start(bf16[512,640]{1,0:T(8,128)(2,1)S(1)} %slice.26), channel_id=1, source_target_pairs={{0,24},{1,25},{2,26},{3,27},{4,28},{5,29},{6,30},{7,31},{8,0},{9,1... | collective-permute-start | bytes 1966088 | tf_op jit(solution)/shard_map/ppermute | solution.py:22
  65.6 7.6 %collective-permute-start.11 = (bf16[1024,128]{1,0:T(8,128)(2,1)S(1)}, bf16[1024,128]{1,0:T(8,128)(2,1)S(1)}, u32[]{:S(2)}, u32[]{:S(2)}) collective-permute-start(bf16[1024,128]{1,0:T(8,128)(2,1)S(1)} %collective-permute-done.7.refs_0_), channel_id=1, source_target_pairs={{0,1},{1,2},{2,3},{3,4},{4,5},{5,6},{6,7},{7,0},{8,9},{9,10},{10,1... | collective-permute-start | bytes 786440 | tf_op jit(solution)/shard_map/ppermute | solution.py:22
  73.2 22.4 %collective-permute-start.15 = (bf16[1024,512]{1,0:T(8,128)(2,1)}, bf16[1024,512]{1,0:T(8,128)(2,1)}, u32[]{:S(2)}, u32[]{:S(2)}) collective-permute-start(bf16[1024,512]{1,0:T(8,128)(2,1)} %collective-permute-done.10.refs_9_), channel_id=1, source_target_pairs={{0,7},{1,0},{2,1},{3,2},{4,3},{5,4},{6,5},{7,6},{8,15},{9,8},{10,9... | collective-permute-start | bytes 3145736 | tf_op jit(solution)/shard_map/ppermute | solution.py:22
  73.2 23.7 %collective-permute-start.14 = (bf16[1024,512]{1,0:T(8,128)(2,1)}, bf16[1024,512]{1,0:T(8,128)(2,1)}, u32[]{:S(2)}, u32[]{:S(2)}) collective-permute-start(bf16[1024,512]{1,0:T(8,128)(2,1)} %collective-permute-done.9.refs_8_), channel_id=1, source_target_pairs={{0,1},{1,2},{2,3},{3,4},{4,5},{5,6},{6,7},{7,0},{8,9},{9,10},{10,1... | collective-permute-start | bytes 3145736 | tf_op jit(solution)/shard_map/ppermute | solution.py:22
  75.4 19.8 %copy-start.2 = (bf16[1024,384]{1,0:T(8,128)(2,1)}, bf16[1024,384]{1,0:T(8,128)(2,1)S(1)}, u32[]{:S(2)}) copy-start(bf16[1024,384]{1,0:T(8,128)(2,1)S(1)} %shard_map.85.refs_6_) | copy-start | bytes 2359300
  79.7 19.2 %collective-permute-start.21 = (bf16[1024,384]{1,0:T(8,128)(2,1)S(1)}, bf16[1024,384]{1,0:T(8,128)(2,1)}, u32[]{:S(2)}, u32[]{:S(2)}) collective-permute-start(bf16[1024,384]{1,0:T(8,128)(2,1)S(1)} %shard_map.85.refs_6_), channel_id=1, source_target_pairs={{0,24},{1,25},{2,26},{3,27},{4,28},{5,29},{6,30},{7,31},{8,0},{9,1... | collective-permute-start | bytes 2359304 | tf_op jit(solution)/shard_map/ppermute | solution.py:22
  80.6 20.1 %collective-permute-start.20 = (bf16[1024,384]{1,0:T(8,128)(2,1)S(1)}, bf16[1024,384]{1,0:T(8,128)(2,1)}, u32[]{:S(2)}, u32[]{:S(2)}) collective-permute-start(bf16[1024,384]{1,0:T(8,128)(2,1)S(1)} %shard_map.85.refs_6_), channel_id=1, source_target_pairs={{0,8},{1,9},{2,10},{3,11},{4,12},{5,13},{6,14},{7,15},{8,16},{9,17... | collective-permute-start | bytes 2359304 | tf_op jit(solution)/shard_map/ppermute | solution.py:22
  96.9 31.1 %collective-permute-start.17 = (bf16[1024,512]{1,0:T(8,128)(2,1)}, bf16[1024,512]{1,0:T(8,128)(2,1)S(1)}, u32[]{:S(2)}, u32[]{:S(2)}) collective-permute-start(bf16[1024,512]{1,0:T(8,128)(2,1)} %collective-permute-done.15.refs_8_), channel_id=1, source_target_pairs={{0,7},{1,0},{2,1},{3,2},{4,3},{5,4},{6,5},{7,6},{8,15},{9,8},{10,9... | collective-permute-start | bytes 3145736 | tf_op jit(solution)/shard_map/ppermute | solution.py:22
  97.1 31.0 %collective-permute-start.16 = (bf16[1024,512]{1,0:T(8,128)(2,1)}, bf16[1024,512]{1,0:T(8,128)(2,1)S(1)}, u32[]{:S(2)}, u32[]{:S(2)}) collective-permute-start(bf16[1024,512]{1,0:T(8,128)(2,1)} %collective-permute-done.14.refs_7_), channel_id=1, source_target_pairs={{0,1},{1,2},{2,3},{3,4},{4,5},{5,6},{6,7},{7,0},{8,9},{9,10},{10,1... | collective-permute-start | bytes 3145736 | tf_op jit(solution)/shard_map/ppermute | solution.py:22
  114.5 13.6 %collective-permute-start.23 = (bf16[512,384]{1,0:T(8,128)(2,1)}, bf16[512,384]{1,0:T(8,128)(2,1)S(1)}, u32[]{:S(2)}, u32[]{:S(2)}) collective-permute-start(bf16[512,384]{1,0:T(8,128)(2,1)} %slice.28), channel_id=1, source_target_pairs={{0,24},{1,25},{2,26},{3,27},{4,28},{5,29},{6,30},{7,31},{8,0},{9,1... | collective-permute-start | bytes 1179656 | tf_op jit(solution)/shard_map/ppermute | solution.py:22
  115.5 12.5 %collective-permute-start.22 = (bf16[512,384]{1,0:T(8,128)(2,1)S(1)}, bf16[512,384]{1,0:T(8,128)(2,1)S(1)}, u32[]{:S(2)}, u32[]{:S(2)}) collective-permute-start(bf16[512,384]{1,0:T(8,128)(2,1)S(1)} %slice.27), channel_id=1, source_target_pairs={{0,8},{1,9},{2,10},{3,11},{4,12},{5,13},{6,14},{7,15},{8,16},{9,17... | collective-permute-start | bytes 1179656 | tf_op jit(solution)/shard_map/ppermute | solution.py:22
  128.9 11.6 %collective-permute-start.25 = (bf16[512,512]{1,0:T(8,128)(2,1)S(1)}, bf16[512,512]{1,0:T(8,128)(2,1)S(1)}, u32[]{:S(2)}, u32[]{:S(2)}) collective-permute-start(bf16[512,512]{1,0:T(8,128)(2,1)S(1)} %slice.29), channel_id=1, source_target_pairs={{0,7},{1,0},{2,1},{3,2},{4,3},{5,4},{6,5},{7,6},{8,15},{9,8},{10,9... | collective-permute-start | bytes 1572872 | tf_op jit(solution)/shard_map/ppermute | solution.py:22
  130.4 13.8 %collective-permute-start.24 = (bf16[512,512]{1,0:T(8,128)(2,1)S(1)}, bf16[512,512]{1,0:T(8,128)(2,1)}, u32[]{:S(2)}, u32[]{:S(2)}) collective-permute-start(bf16[512,512]{1,0:T(8,128)(2,1)S(1)} %slice.24), channel_id=1, source_target_pairs={{0,1},{1,2},{2,3},{3,4},{4,5},{5,6},{6,7},{7,0},{8,9},{9,10},{10,1... | collective-permute-start | bytes 1572872 | tf_op jit(solution)/shard_map/ppermute | solution.py:22
  (9 other events, 20.8 us)
Sparse Core Ops, SparseCore 0:
  9.4 72.5 all-gather.1

commit v11 on v10

--- a/solution.py
+++ b/solution.py
@@ -114,13 +114,12 @@
     )(here, sym_ij, sym_cd, amp_mask, raw)
 
 
-def product_kernel(pieces, sizes, first, last, ij_ref, ab_ref, *refs):
+def product_kernel(sizes, first, last, ij_ref, ab_ref, amps_hbm, *refs):
     n = sum(sizes)
-    amps_hbm, ints, refs = refs[:pieces], refs[pieces:pieces + n], refs[pieces + n:]
-    if first:
-        out, amps, rows_v, sem = refs
-    else:
-        total_hbm, out, amps, rows_v, sem, total = refs
+    ints, refs = refs[:n], refs[n:]
+    if not first:
+        total_hbm, refs = refs[0], refs[1:]
+    out_hbm, amps, rows_v, total, done, sem = refs
 
     def fetch(c, act):
         rows = pl.ds(pl.multiple_of(c * 256, 256), 256)
@@ -145,60 +144,78 @@
         if not first:
             act(pltpu.make_async_copy(total_hbm.at[:, rows], total.at[:, rows], sem.at[c, len(sizes)]))
 
-    whole, at = [], 0
-    for k, piece in enumerate(amps_hbm):
-        width = piece.shape[1]
-        whole.append(pltpu.make_async_copy(piece, amps.at[:, pl.ds(at, width)], sem.at[4, k]))
-        whole[-1].start()
-        at += width
-    for c in range(4):
+    chunks = []
+    for k, at in enumerate(range(0, amps.shape[1], 1024)):
+        cols = slice(at, min(at + 1024, amps.shape[1]))
+        chunks.append((cols, pltpu.make_async_copy(amps_hbm.at[:, cols], amps.at[:, cols], sem.at[4, k])))
+    fetch(jnp.int32(0), lambda copy: copy.start())
+    for _, copy in chunks:
+        copy.start()
+    for c in range(1, 4):
         fetch(jnp.int32(c), lambda copy: copy.start())
-    for copy in whole:
-        copy.wait()
-
-    def strip(c, carry):
-        fetch(c, lambda copy: copy.wait())
+
+    def drain(c):
         cols = pl.ds(pl.multiple_of(c * 256, 256), 256)
-
-        value = dot(amps[...], rows_v[cols, :])
+        return pltpu.make_async_copy(done.at[:, cols], out_hbm.at[:, cols], sem.at[5, c])
+
+    def finish(c, value):
+        cols = pl.ds(pl.multiple_of(c * 256, 256), 256)
         if not first:
             value = value + total[:, cols]
         if not last:
-            out[:, cols] = value
-            return carry
-        for i in range(6):
-            for j in range(2):
-                rows = slice(i * BLK, (i + 1) * BLK)
-                tile = value[rows, j * BLK:(j + 1) * BLK] * 0.5
-                on = ij_ref[i] == ab_ref[2 * c + j]
-                where = pl.ds(pl.multiple_of(c * 256 + j * BLK, BLK), BLK)
-                out[rows, where] = jnp.where(on, tile, jnp.zeros_like(tile)).astype(BF16)
+            done[:, cols] = value
+        else:
+            for i in range(6):
+                for j in range(2):
+                    rows = slice(i * BLK, (i + 1) * BLK)
+                    tile = value[rows, j * BLK:(j + 1) * BLK] * 0.5
+                    on = ij_ref[i] == ab_ref[2 * c + j]
+                    where = pl.ds(pl.multiple_of(c * 256 + j * BLK, BLK), BLK)
+                    done[rows, where] = jnp.where(on, tile, jnp.zeros_like(tile)).astype(BF16)
+        drain(c).start()
+
+    fetch(jnp.int32(0), lambda copy: copy.wait())
+    value = None
+    for cols, copy in chunks:
+        copy.wait()
+        part = dot(amps[:, cols], rows_v[:256, cols])
+        value = part if value is None else value + part
+    finish(jnp.int32(0), value)
+
+    def strip(c, carry):
+        fetch(c, lambda copy: copy.wait())
+        finish(c, dot(amps[...], rows_v[pl.ds(pl.multiple_of(c * 256, 256), 256), :]))
         return carry
 
-    lax.fori_loop(0, 4, strip, 0)
+    lax.fori_loop(1, 4, strip, 0)
+    for c in range(4):
+        drain(c).wait()
 
 
 def product(sym_ij, sym_ab, amps, blocks, total=None, last=False):
-    depth = sum(piece.shape[1] for piece in amps)
+    depth = amps.shape[1]
     first = total is None
     sizes = [len(block) for block in blocks]
-    n = sum(sizes)
+    kind = BF16 if last else F32
 
     def kernel(*refs):
-        product_kernel(len(amps), sizes, first, last, *refs)
-
-    scratch = [
-        pltpu.VMEM((768, depth), BF16), pltpu.VMEM((1024, depth), BF16), pltpu.SemaphoreType.DMA((5, len(sizes) + 1))
-    ]
+        product_kernel(sizes, first, last, *refs)
+
     return pl.pallas_call(
         kernel,
-        out_shape=jax.ShapeDtypeStruct((768, 1024), BF16 if last else F32),
-        in_specs=[SMEM] * 2 + [HBM] * (len(amps) + n + (not first)),
-        out_specs=VMEM,
-        scratch_shapes=scratch + ([] if first else [pltpu.VMEM((768, 1024), F32)]),
+        out_shape=jax.ShapeDtypeStruct((768, 1024), kind),
+        in_specs=[SMEM] * 2 + [HBM] * (1 + sum(sizes) + (not first)),
+        out_specs=HBM,
+        scratch_shapes=[
+            pltpu.VMEM((768, depth), BF16),
+            pltpu.VMEM((1024, depth), BF16),
+            pltpu.VMEM((8, BLK) if first else (768, 1024), F32),
+            pltpu.VMEM((768, 1024), kind),
+            pltpu.SemaphoreType.DMA((6, len(sizes) + 4)),
+        ],
         compiler_params=params(60),
         cost_estimate=cost(2 * 768 * 1024 * depth, 8 * 2**20 + 3584 * depth),
-    )(sym_ij, sym_ab, *amps, *[array for block in blocks for array in block], *([] if first else [total]))
+    )(sym_ij, sym_ab, amps, *[array for block in blocks for array in block], *([] if first else [total]))
 
 
 def body(amp_plus, amp_minus, ints_plus, ints_minus, sym_ij, sym_ab, sym_cd, amp_mask):
@@ -250,12 +267,12 @@
     )
     wu.append(go(wu[1], wd[1], amps[0], dz=1))
     wd.append(go(wd[1], wu[1], amps[0], dz=-1))
-    total = add(amps[:1], [(c0,), c1[:1], c1[1:], (d0,), (w0,), (wu[0],), (wd[0],)])
+    total = add(amps[0], [(c0,), c1[:1], c1[1:], (d0,), (w0,), (wu[0],), (wd[0],)])
     d2 = (go(d1[0][:HALF], *d1, total, dy=1), go(d1[1][HALF:], *d1, total, dy=-1))
-    total = add(amps[1:2], [c2, d1[:1], d1[1:], (wu[1],), (wd[1],)], total)
+    total = add(amps[1], [c2, d1[:1], d1[1:], (wu[1],), (wd[1],)], total)
     w4 = (go(wu[2][:HALF], wd[2], *d2, total, dz=1), go(wd[2][HALF:], wu[2], *d2, total, dz=-1))
-    total = add(amps[2:3], [d2, (wu[2],), (wd[2],)], total)
-    return add(amps[3:], [w4], total, True)
+    total = add(amps[2], [d2, (wu[2],), (wd[2],)], total)
+    return add(amps[3], [w4], total, True)
 
 
 def solution(mesh):

time: 156 us -> 157 us (level)
  no operation moved by 1% of the time
where the time goes in v11:
time: 157 us
  waiting for transfers between devices  50.5 us (32%)
  Pallas kernels  47.5 us (30%)
  starting transfers between devices  36 us (23%)
  between operations  13.6 us (9%)
  local copies, waits for them, and re-layouts  5.76 us (4%)
  other arithmetic  3.32 us (2%)
    ppermute x26, waiting for transfers between devices, move(): return lax.ppermute(values, 'mem', perm_of(dy, dz))  50.5 us
    ppermute x26, starting transfers between devices, move(): return lax.ppermute(values, 'mem', perm_of(dy, dz))  35.9 us
    pallas_call x4, Pallas kernels, product(): pl.pallas_call(kernel, out_shape=jax.ShapeDtypeStruct((768, 1024), kind),...  35.4 us
    pallas_call x1, Pallas kernels, mask(): pl.pallas_call(kernel, out_shape=[jax.ShapeDtypeStruct(shape, BF16) for s...  11.5 us
  transfers between devices with their start and end apart: 27, of which 14 were waited for; matrix products, arithmetic and copies ran while one was open for 2% of the time, Pallas kernels for 27%

profile of v11, /device:TPU:24, one launch (start us, length us, event | category | flops | bytes accessed | tf_op | source)
XLA Modules:
  0.0 156.6 jit_solution(12989954664062563601)
XLA Ops:
  6.5 2.7 %pad_maximum_fusion = bf16[1536,512]{1,0:T(8,128)(2,1)} fusion(bf16[768,512]{1,0:T(8,128)(2,1)} %param.9, bf16[768,512]{1,0:T(8,128)(2,1)} %param.8), kind=kLoop, calls=%fused_computation | loop fusion | flops 3145728 | bytes 3145728 | tf_op jit(solution)/shard_map/concatenate | solution.py:228
  9.2 2.0 %collective-permute-start = (bf16[1024,128]{1,0:T(8,128)(2,1)S(1)}, bf16[1024,128]{1,0:T(8,128)(2,1)S(1)}, u32[]{:S(2)}, u32[]{:S(2)}) collective-permute-start(bf16[1024,128]{1,0:T(8,128)(2,1)S(1)} %copy-done.4), channel_id=1, source_target_pairs={{0,8},{1,9},{2,10},{3,11},{4,12},{5,13},{6,14},{7,15},{8,16},{9,17... | collective-permute-start | bytes 786440 | tf_op jit(solution)/shard_map/ppermute | solution.py:22
  11.5 3.9 %collective-permute-start.3 = (bf16[1024,128]{1,0:T(8,128)(2,1)S(1)}, bf16[1024,128]{1,0:T(8,128)(2,1)S(1)}, u32[]{:S(2)}, u32[]{:S(2)}) collective-permute-start(bf16[1024,128]{1,0:T(8,128)(2,1)S(1)} %copy-done.3), channel_id=1, source_target_pairs={{0,7},{1,0},{2,1},{3,2},{4,3},{5,4},{6,5},{7,6},{8,15},{9,8},{10,9... | collective-permute-start | bytes 786440 | tf_op jit(solution)/shard_map/ppermute | solution.py:22
  15.4 1.8 %collective-permute-start.1 = (bf16[1024,128]{1,0:T(8,128)(2,1)S(1)}, bf16[1024,128]{1,0:T(8,128)(2,1)S(1)}, u32[]{:S(2)}, u32[]{:S(2)}) collective-permute-start(bf16[1024,128]{1,0:T(8,128)(2,1)S(1)} %copy-done.4), channel_id=1, source_target_pairs={{0,24},{1,25},{2,26},{3,27},{4,28},{5,29},{6,30},{7,31},{8,0},{9,1... | collective-permute-start | bytes 786440 | tf_op jit(solution)/shard_map/ppermute | solution.py:22
  17.4 4.2 %collective-permute-done.2.refs_1_ = bf16[1024,128]{1,0:T(8,128)(2,1)S(1)} collective-permute-done((bf16[1024,128]{1,0:T(8,128)(2,1)S(1)}, bf16[1024,128]{1,0:T(8,128)(2,1)S(1)}, u32[]{:S(2)}, u32[]{:S(2)}) %collective-permute-start.2) | collective-permute-done | bytes 262176 | tf_op jit(solution)/shard_map/ppermute | solution.py:22
  21.6 3.2 %collective-permute-start.6 = (bf16[1024,128]{1,0:T(8,128)(2,1)S(1)}, bf16[1024,128]{1,0:T(8,128)(2,1)S(1)}, u32[]{:S(2)}, u32[]{:S(2)}) collective-permute-start(bf16[1024,128]{1,0:T(8,128)(2,1)S(1)} %collective-permute-done.3.refs_2_), channel_id=1, source_target_pairs={{0,7},{1,0},{2,1},{3,2},{4,3},{5,4},{6,5},{7,6},{8,15},{9,8},{10,9... | collective-permute-start | bytes 786440 | tf_op jit(solution)/shard_map/ppermute | solution.py:22
  24.8 1.4 collective-permute-start.4
  26.3 3.9 %collective-permute-done.5.refs_3_ = bf16[1024,128]{1,0:T(8,128)(2,1)S(1)} collective-permute-done((bf16[1024,128]{1,0:T(8,128)(2,1)S(1)}, bf16[1024,128]{1,0:T(8,128)(2,1)S(1)}, u32[]{:S(2)}, u32[]{:S(2)}) %collective-permute-start.5) | collective-permute-done | bytes 262176 | tf_op jit(solution)/shard_map/ppermute | solution.py:22
  31.6 2.5 %collective-permute-start.12 = (bf16[1024,640]{1,0:T(8,128)(2,1)S(1)}, bf16[1024,640]{1,0:T(8,128)(2,1)S(1)}, u32[]{:S(2)}, u32[]{:S(2)}) collective-permute-start(bf16[1024,640]{1,0:T(8,128)(2,1)S(1)} %shard_map.84.refs_3_), channel_id=1, source_target_pairs={{0,8},{1,9},{2,10},{3,11},{4,12},{5,13},{6,14},{7,15},{8,16},{9,17... | collective-permute-start | bytes 3932168 | tf_op jit(solution)/shard_map/ppermute | solution.py:22
  34.3 3.0 %collective-permute-start.8 = (bf16[1024,128]{1,0:T(8,128)(2,1)S(1)}, bf16[1024,128]{1,0:T(8,128)(2,1)S(1)}, u32[]{:S(2)}, u32[]{:S(2)}) collective-permute-start(bf16[1024,128]{1,0:T(8,128)(2,1)S(1)} %collective-permute-done.6.refs_4_), channel_id=1, source_target_pairs={{0,7},{1,0},{2,1},{3,2},{4,3},{5,4},{6,5},{7,6},{8,15},{9,8},{10,9... | collective-permute-start | bytes 786440 | tf_op jit(solution)/shard_map/ppermute | solution.py:22
  37.5 4.2 %collective-permute-done.7.refs_0_ = bf16[1024,128]{1,0:T(8,128)(2,1)S(1)} collective-permute-done((bf16[1024,128]{1,0:T(8,128)(2,1)S(1)}, bf16[1024,128]{1,0:T(8,128)(2,1)S(1)}, u32[]{:S(2)}, u32[]{:S(2)}) %collective-permute-start.7) | collective-permute-done | bytes 262176 | tf_op jit(solution)/shard_map/ppermute | solution.py:22
  41.7 3.2 %collective-permute-start.10 = (bf16[1024,512]{1,0:T(8,128)(2,1)S(1)}, bf16[1024,512]{1,0:T(8,128)(2,1)}, u32[]{:S(2)}, u32[]{:S(2)}) collective-permute-start(bf16[1024,512]{1,0:T(8,128)(2,1)S(1)} %shard_map.83.refs_7_), channel_id=1, source_target_pairs={{0,7},{1,0},{2,1},{3,2},{4,3},{5,4},{6,5},{7,6},{8,15},{9,8},{10,9... | collective-permute-start | bytes 3145736 | tf_op jit(solution)/shard_map/ppermute | solution.py:22
  44.9 15.1 %collective-permute-done.12.refs_4_ = bf16[1024,640]{1,0:T(8,128)(2,1)S(1)} collective-permute-done((bf16[1024,640]{1,0:T(8,128)(2,1)S(1)}, bf16[1024,640]{1,0:T(8,128)(2,1)S(1)}, u32[]{:S(2)}, u32[]{:S(2)}) %collective-permute-start.12) | collective-permute-done | bytes 1310752 | tf_op jit(solution)/shard_map/ppermute | solution.py:22
  61.0 2.2 %collective-permute-done.13.refs_5_ = bf16[1024,640]{1,0:T(8,128)(2,1)S(1)} collective-permute-done((bf16[1024,640]{1,0:T(8,128)(2,1)S(1)}, bf16[1024,640]{1,0:T(8,128)(2,1)S(1)}, u32[]{:S(2)}, u32[]{:S(2)}) %collective-permute-start.13) | collective-permute-done | bytes 1310752 | tf_op jit(solution)/shard_map/ppermute | solution.py:22
  63.3 1.4 collective-permute-start.18
  65.6 7.6 %collective-permute-done.11.refs_2_ = bf16[1024,128]{1,0:T(8,128)(2,1)S(1)} collective-permute-done((bf16[1024,128]{1,0:T(8,128)(2,1)S(1)}, bf16[1024,128]{1,0:T(8,128)(2,1)S(1)}, u32[]{:S(2)}, u32[]{:S(2)}) %collective-permute-start.11) | collective-permute-done | bytes 262176 | tf_op jit(solution)/shard_map/ppermute | solution.py:22
  73.2 2.0 %collective-permute-start.14 = (bf16[1024,512]{1,0:T(8,128)(2,1)}, bf16[1024,512]{1,0:T(8,128)(2,1)}, u32[]{:S(2)}, u32[]{:S(2)}) collective-permute-start(bf16[1024,512]{1,0:T(8,128)(2,1)} %collective-permute-done.9.refs_8_), channel_id=1, source_target_pairs={{0,1},{1,2},{2,3},{3,4},{4,5},{5,6},{6,7},{7,0},{8,9},{9,10},{10,1... | collective-permute-start | bytes 3145736 | tf_op jit(solution)/shard_map/ppermute | solution.py:22
  76.4 3.4 %collective-permute-done.19.refs_4_ = bf16[512,640]{1,0:T(8,128)(2,1)S(1)} collective-permute-done((bf16[512,640]{1,0:T(8,128)(2,1)S(1)}, bf16[512,640]{1,0:T(8,128)(2,1)S(1)}, u32[]{:S(2)}, u32[]{:S(2)}) %collective-permute-start.19) | collective-permute-done | bytes 655392 | tf_op jit(solution)/shard_map/ppermute | solution.py:22
  80.6 2.4 %collective-permute-start.20 = (bf16[1024,384]{1,0:T(8,128)(2,1)S(1)}, bf16[1024,384]{1,0:T(8,128)(2,1)}, u32[]{:S(2)}, u32[]{:S(2)}) collective-permute-start(bf16[1024,384]{1,0:T(8,128)(2,1)S(1)} %shard_map.85.refs_6_), channel_id=1, source_target_pairs={{0,8},{1,9},{2,10},{3,11},{4,12},{5,13},{6,14},{7,15},{8,16},{9,17... | collective-permute-start | bytes 2359304 | tf_op jit(solution)/shard_map/ppermute | solution.py:22
  83.6 11.5 %shard_map.82 = (bf16[768,3840]{1,0:T(8,128)(2,1)}, bf16[768,2432]{1,0:T(8,128)(2,1)}, bf16[768,1408]{1,0:T(8,128)(2,1)}, bf16[768,512]{1,0:T(8,128)(2,1)}) custom-call(s32[2]{0:T(128)} %pad_add_fusion.refs_0_, s32[6]{0:T(128)} %refs_0_.11, s32[32]{0:T(128)} %refs_2_.1, s32[6,32]{1,0:T(8,128)} %refs_3_.1, bf16[1536,4096]{1,0:T(8,128)(2,1)} %all-gather.2.cloned.1.call-done.refs_4_), custom_call_target="tpu_custom_call" | custom-call | bytes 26214400 | tf_op jit(solution)/shard_map/pallas_call | solution.py:104
  95.6 1.3 collective-permute-done.14.refs_7_
  97.1 1.8 %collective-permute-start.16 = (bf16[1024,512]{1,0:T(8,128)(2,1)}, bf16[1024,512]{1,0:T(8,128)(2,1)S(1)}, u32[]{:S(2)}, u32[]{:S(2)}) collective-permute-start(bf16[1024,512]{1,0:T(8,128)(2,1)} %collective-permute-done.14.refs_7_), channel_id=1, source_target_pairs={{0,1},{1,2},{2,3},{3,4},{4,5},{5,6},{6,7},{7,0},{8,9},{9,10},{10,1... | collective-permute-start | bytes 3145736 | tf_op jit(solution)/shard_map/ppermute | solution.py:22
  98.9 1.8 %slice.28 = bf16[512,384]{1,0:T(8,128)(2,1)} slice(bf16[1024,384]{1,0:T(8,128)(2,1)} %collective-permute-done.21.refs_6_), slice={[512:1024], [0:384]} | slice | bytes 786432 | tf_op jit(solution)/shard_map/slice | solution.py:271
  101.7 13.3 %shard_map.86.refs_9_ = f32[768,1024]{1,0:T(8,128)} custom-call(s32[6]{0:T(128)} %refs_0_.11, s32[8]{0:T(128)} %refs_1_.9, bf16[768,3840]{1,0:T(8,128)(2,1)} %get-tuple-element.37.refs_2_, bf16[1024,640]{1,0:T(8,128)(2,1)} %copy-done, bf16[1024,640]{1,0:T(8,128)(2,1)} %copy-done.12, bf16[1024,640]{1,0:T(8,128)(2,1)} %copy-done.13, ...), custom_call_target="tpu_custom_call" | custom-call | flops 6039797760 | bytes 22151168 | tf_op jit(solution)/shard_map/pallas_call | solution.py:204
  115.0 1.3 collective-permute-start.23
  116.3 2.2 %collective-permute-start.22 = (bf16[512,384]{1,0:T(8,128)(2,1)S(1)}, bf16[512,384]{1,0:T(8,128)(2,1)S(1)}, u32[]{:S(2)}, u32[]{:S(2)}) collective-permute-start(bf16[512,384]{1,0:T(8,128)(2,1)S(1)} %slice.27), channel_id=1, source_target_pairs={{0,8},{1,9},{2,10},{3,11},{4,12},{5,13},{6,14},{7,15},{8,16},{9,17... | collective-permute-start | bytes 1179656 | tf_op jit(solution)/shard_map/ppermute | solution.py:22
  118.5 10.1 %shard_map.87.refs_7_ = f32[768,1024]{1,0:T(8,128)} custom-call(s32[6]{0:T(128)} %refs_0_.11, s32[8]{0:T(128)} %refs_1_.9, bf16[768,2432]{1,0:T(8,128)(2,1)} %get-tuple-element.45.refs_2_, bf16[512,640]{1,0:T(8,128)(2,1)} %copy-done.7, bf16[512,640]{1,0:T(8,128)(2,1)} %copy-done.8, bf16[1024,384]{1,0:T(8,128)(2,1)} %collective-permute-done.20.refs_5_, ...), custom_call_target="tpu_custom_call" | custom-call | flops 3825205248 | bytes 17104896 | tf_op jit(solution)/shard_map/pallas_call | solution.py:204
  129.6 1.4 collective-permute-start.25
  131.8 7.3 %shard_map.88.refs_5_ = f32[768,1024]{1,0:T(8,128)} custom-call(s32[6]{0:T(128)} %refs_0_.11, s32[8]{0:T(128)} %refs_1_.9, bf16[768,1408]{1,0:T(8,128)(2,1)} %get-tuple-element.48.refs_2_, bf16[512,384]{1,0:T(8,128)(2,1)} %copy-done.11, bf16[512,384]{1,0:T(8,128)(2,1)} %copy-done.10, bf16[1024,512]{1,0:T(8,128)(2,1)} %copy-done.6, ...), custom_call_target="tpu_custom_call" | custom-call | flops 2214592512 | bytes 13434880 | tf_op jit(solution)/shard_map/pallas_call | solution.py:204
  139.1 2.2 %collective-permute-done.25.refs_4_ = bf16[512,512]{1,0:T(8,128)(2,1)S(1)} collective-permute-done((bf16[512,512]{1,0:T(8,128)(2,1)S(1)}, bf16[512,512]{1,0:T(8,128)(2,1)S(1)}, u32[]{:S(2)}, u32[]{:S(2)}) %collective-permute-start.25) | collective-permute-done | bytes 524320 | tf_op jit(solution)/shard_map/ppermute | solution.py:22
  141.3 3.6 %collective-permute-done.24.refs_3_ = bf16[512,512]{1,0:T(8,128)(2,1)} collective-permute-done((bf16[512,512]{1,0:T(8,128)(2,1)S(1)}, bf16[512,512]{1,0:T(8,128)(2,1)}, u32[]{:S(2)}, u32[]{:S(2)}) %collective-permute-start.24) | collective-permute-done | bytes 524320 | tf_op jit(solution)/shard_map/ppermute | solution.py:22
  144.9 4.8 %shard_map.89 = bf16[768,1024]{1,0:T(8,128)(2,1)} custom-call(s32[6]{0:T(128)} %refs_0_.11, s32[8]{0:T(128)} %refs_1_.9, bf16[768,512]{1,0:T(8,128)(2,1)} %get-tuple-element.27.refs_2_, bf16[512,512]{1,0:T(8,128)(2,1)} %collective-permute-done.24.refs_3_, bf16[512,512]{1,0:T(8,128)(2,1)} %copy-done.9, f32[768,1024]{1,0:T(8,128)} %shard_map.88.refs_5_), custom_call_target="tpu_custom_call" | custom-call | flops 805306368 | bytes 10223616 | tf_op jit(solution)/shard_map/pallas_call | solution.py:204
  (67 shorter events, 10.3 us)
Async XLA Ops:
  6.5 4.7 %copy-start.3 = (bf16[1024,128]{1,0:T(8,128)(2,1)S(1)}, bf16[1024,128]{1,0:T(8,128)(2,1)}, u32[]{:S(2)}) copy-start(bf16[1024,128]{1,0:T(8,128)(2,1)} %refs_0_.7) | copy-start | bytes 786436
  6.5 77.1 %all-gather.2.cloned.1.call-start = ((), (), s32[]{:S(2)}) async-start(), calls=%async_computation | async-start | bytes 14155776 | tf_op jit(solution)/shard_map/all_gather | solution.py:228
  9.2 8.1 %collective-permute-start = (bf16[1024,128]{1,0:T(8,128)(2,1)S(1)}, bf16[1024,128]{1,0:T(8,128)(2,1)S(1)}, u32[]{:S(2)}, u32[]{:S(2)}) collective-permute-start(bf16[1024,128]{1,0:T(8,128)(2,1)S(1)} %copy-done.4), channel_id=1, source_target_pairs={{0,8},{1,9},{2,10},{3,11},{4,12},{5,13},{6,14},{7,15},{8,16},{9,17... | collective-permute-start | bytes 786440 | tf_op jit(solution)/shard_map/ppermute | solution.py:22
  11.3 10.3 %collective-permute-start.2 = (bf16[1024,128]{1,0:T(8,128)(2,1)S(1)}, bf16[1024,128]{1,0:T(8,128)(2,1)S(1)}, u32[]{:S(2)}, u32[]{:S(2)}) collective-permute-start(bf16[1024,128]{1,0:T(8,128)(2,1)S(1)} %copy-done.3), channel_id=1, source_target_pairs={{0,1},{1,2},{2,3},{3,4},{4,5},{5,6},{6,7},{7,0},{8,9},{9,10},{10,1... | collective-permute-start | bytes 786440 | tf_op jit(solution)/shard_map/ppermute | solution.py:22
  11.5 10.1 %collective-permute-start.3 = (bf16[1024,128]{1,0:T(8,128)(2,1)S(1)}, bf16[1024,128]{1,0:T(8,128)(2,1)S(1)}, u32[]{:S(2)}, u32[]{:S(2)}) collective-permute-start(bf16[1024,128]{1,0:T(8,128)(2,1)S(1)} %copy-done.3), channel_id=1, source_target_pairs={{0,7},{1,0},{2,1},{3,2},{4,3},{5,4},{6,5},{7,6},{8,15},{9,8},{10,9... | collective-permute-start | bytes 786440 | tf_op jit(solution)/shard_map/ppermute | solution.py:22
  15.4 9.4 %collective-permute-start.1 = (bf16[1024,128]{1,0:T(8,128)(2,1)S(1)}, bf16[1024,128]{1,0:T(8,128)(2,1)S(1)}, u32[]{:S(2)}, u32[]{:S(2)}) collective-permute-start(bf16[1024,128]{1,0:T(8,128)(2,1)S(1)} %copy-done.4), channel_id=1, source_target_pairs={{0,24},{1,25},{2,26},{3,27},{4,28},{5,29},{6,30},{7,31},{8,0},{9,1... | collective-permute-start | bytes 786440 | tf_op jit(solution)/shard_map/ppermute | solution.py:22
  21.6 8.6 %collective-permute-start.5 = (bf16[1024,128]{1,0:T(8,128)(2,1)S(1)}, bf16[1024,128]{1,0:T(8,128)(2,1)S(1)}, u32[]{:S(2)}, u32[]{:S(2)}) collective-permute-start(bf16[1024,128]{1,0:T(8,128)(2,1)S(1)} %collective-permute-done.2.refs_1_), channel_id=1, source_target_pairs={{0,1},{1,2},{2,3},{3,4},{4,5},{5,6},{6,7},{7,0},{8,9},{9,10},{10,1... | collective-permute-start | bytes 786440 | tf_op jit(solution)/shard_map/ppermute | solution.py:22
  21.6 8.6 %collective-permute-start.6 = (bf16[1024,128]{1,0:T(8,128)(2,1)S(1)}, bf16[1024,128]{1,0:T(8,128)(2,1)S(1)}, u32[]{:S(2)}, u32[]{:S(2)}) collective-permute-start(bf16[1024,128]{1,0:T(8,128)(2,1)S(1)} %collective-permute-done.3.refs_2_), channel_id=1, source_target_pairs={{0,7},{1,0},{2,1},{3,2},{4,3},{5,4},{6,5},{7,6},{8,15},{9,8},{10,9... | collective-permute-start | bytes 786440 | tf_op jit(solution)/shard_map/ppermute | solution.py:22
  24.8 6.8 %collective-permute-start.4 = (bf16[1024,128]{1,0:T(8,128)(2,1)S(1)}, bf16[1024,128]{1,0:T(8,128)(2,1)S(1)}, u32[]{:S(2)}, u32[]{:S(2)}) collective-permute-start(bf16[1024,128]{1,0:T(8,128)(2,1)S(1)} %collective-permute-done.refs_1_), channel_id=1, source_target_pairs={{0,8},{1,9},{2,10},{3,11},{4,12},{5,13},{6,14},{7,15},{8,16},{9,17... | collective-permute-start | bytes 786440 | tf_op jit(solution)/shard_map/ppermute | solution.py:22
  30.4 45.0 %copy-start = (bf16[1024,640]{1,0:T(8,128)(2,1)}, bf16[1024,640]{1,0:T(8,128)(2,1)S(1)}, u32[]{:S(2)}) copy-start(bf16[1024,640]{1,0:T(8,128)(2,1)S(1)} %shard_map.84.refs_3_) | copy-start | bytes 3932164
  31.6 28.3 %collective-permute-start.12 = (bf16[1024,640]{1,0:T(8,128)(2,1)S(1)}, bf16[1024,640]{1,0:T(8,128)(2,1)S(1)}, u32[]{:S(2)}, u32[]{:S(2)}) collective-permute-start(bf16[1024,640]{1,0:T(8,128)(2,1)S(1)} %shard_map.84.refs_3_), channel_id=1, source_target_pairs={{0,8},{1,9},{2,10},{3,11},{4,12},{5,13},{6,14},{7,15},{8,16},{9,17... | collective-permute-start | bytes 3932168 | tf_op jit(solution)/shard_map/ppermute | solution.py:22
  34.1 29.2 %collective-permute-start.13 = (bf16[1024,640]{1,0:T(8,128)(2,1)S(1)}, bf16[1024,640]{1,0:T(8,128)(2,1)S(1)}, u32[]{:S(2)}, u32[]{:S(2)}) collective-permute-start(bf16[1024,640]{1,0:T(8,128)(2,1)S(1)} %shard_map.84.refs_3_), channel_id=1, source_target_pairs={{0,24},{1,25},{2,26},{3,27},{4,28},{5,29},{6,30},{7,31},{8,0},{9,1... | collective-permute-start | bytes 3932168 | tf_op jit(solution)/shard_map/ppermute | solution.py:22
  34.1 7.6 %collective-permute-start.7 = (bf16[1024,128]{1,0:T(8,128)(2,1)S(1)}, bf16[1024,128]{1,0:T(8,128)(2,1)S(1)}, u32[]{:S(2)}, u32[]{:S(2)}) collective-permute-start(bf16[1024,128]{1,0:T(8,128)(2,1)S(1)} %collective-permute-done.5.refs_3_), channel_id=1, source_target_pairs={{0,1},{1,2},{2,3},{3,4},{4,5},{5,6},{6,7},{7,0},{8,9},{9,10},{10,1... | collective-permute-start | bytes 786440 | tf_op jit(solution)/shard_map/ppermute | solution.py:22
  34.3 7.3 %collective-permute-start.8 = (bf16[1024,128]{1,0:T(8,128)(2,1)S(1)}, bf16[1024,128]{1,0:T(8,128)(2,1)S(1)}, u32[]{:S(2)}, u32[]{:S(2)}) collective-permute-start(bf16[1024,128]{1,0:T(8,128)(2,1)S(1)} %collective-permute-done.6.refs_4_), channel_id=1, source_target_pairs={{0,7},{1,0},{2,1},{3,2},{4,3},{5,4},{6,5},{7,6},{8,15},{9,8},{10,9... | collective-permute-start | bytes 786440 | tf_op jit(solution)/shard_map/ppermute | solution.py:22
  37.5 57.6 %copy-start.1 = (bf16[1024,512]{1,0:T(8,128)(2,1)}, bf16[1024,512]{1,0:T(8,128)(2,1)S(1)}, u32[]{:S(2)}) copy-start(bf16[1024,512]{1,0:T(8,128)(2,1)S(1)} %shard_map.83.refs_7_) | copy-start | bytes 3145732
  41.7 31.5 %collective-permute-start.10 = (bf16[1024,512]{1,0:T(8,128)(2,1)S(1)}, bf16[1024,512]{1,0:T(8,128)(2,1)}, u32[]{:S(2)}, u32[]{:S(2)}) collective-permute-start(bf16[1024,512]{1,0:T(8,128)(2,1)S(1)} %shard_map.83.refs_7_), channel_id=1, source_target_pairs={{0,7},{1,0},{2,1},{3,2},{4,3},{5,4},{6,5},{7,6},{8,15},{9,8},{10,9... | collective-permute-start | bytes 3145736 | tf_op jit(solution)/shard_map/ppermute | solution.py:22
  44.9 28.3 %collective-permute-start.9 = (bf16[1024,512]{1,0:T(8,128)(2,1)S(1)}, bf16[1024,512]{1,0:T(8,128)(2,1)}, u32[]{:S(2)}, u32[]{:S(2)}) collective-permute-start(bf16[1024,512]{1,0:T(8,128)(2,1)S(1)} %shard_map.83.refs_7_), channel_id=1, source_target_pairs={{0,1},{1,2},{2,3},{3,4},{4,5},{5,6},{6,7},{7,0},{8,9},{9,10},{10,1... | collective-permute-start | bytes 3145736 | tf_op jit(solution)/shard_map/ppermute | solution.py:22
  63.3 19.7 %copy-start.13 = (bf16[1024,640]{1,0:T(8,128)(2,1)}, bf16[1024,640]{1,0:T(8,128)(2,1)S(1)}, u32[]{:S(2)}) copy-start(bf16[1024,640]{1,0:T(8,128)(2,1)S(1)} %collective-permute-done.13.refs_5_) | copy-start | bytes 3932164
  63.3 13.1 %collective-permute-start.18 = (bf16[512,640]{1,0:T(8,128)(2,1)S(1)}, bf16[512,640]{1,0:T(8,128)(2,1)S(1)}, u32[]{:S(2)}, u32[]{:S(2)}) collective-permute-start(bf16[512,640]{1,0:T(8,128)(2,1)S(1)} %slice.25), channel_id=1, source_target_pairs={{0,8},{1,9},{2,10},{3,11},{4,12},{5,13},{6,14},{7,15},{8,16},{9,17... | collective-permute-start | bytes 1966088 | tf_op jit(solution)/shard_map/ppermute | solution.py:22
  64.7 15.0 %collective-permute-start.19 = (bf16[512,640]{1,0:T(8,128)(2,1)S(1)}, bf16[512,640]{1,0:T(8,128)(2,1)S(1)}, u32[]{:S(2)}, u32[]{:S(2)}) collective-permute-start(bf16[512,640]{1,0:T(8,128)(2,1)S(1)} %slice.26), channel_id=1, source_target_pairs={{0,24},{1,25},{2,26},{3,27},{4,28},{5,29},{6,30},{7,31},{8,0},{9,1... | collective-permute-start | bytes 1966088 | tf_op jit(solution)/shard_map/ppermute | solution.py:22
  65.6 7.6 %collective-permute-start.11 = (bf16[1024,128]{1,0:T(8,128)(2,1)S(1)}, bf16[1024,128]{1,0:T(8,128)(2,1)S(1)}, u32[]{:S(2)}, u32[]{:S(2)}) collective-permute-start(bf16[1024,128]{1,0:T(8,128)(2,1)S(1)} %collective-permute-done.7.refs_0_), channel_id=1, source_target_pairs={{0,1},{1,2},{2,3},{3,4},{4,5},{5,6},{6,7},{7,0},{8,9},{9,10},{10,1... | collective-permute-start | bytes 786440 | tf_op jit(solution)/shard_map/ppermute | solution.py:22
  73.2 22.4 %collective-permute-start.15 = (bf16[1024,512]{1,0:T(8,128)(2,1)}, bf16[1024,512]{1,0:T(8,128)(2,1)}, u32[]{:S(2)}, u32[]{:S(2)}) collective-permute-start(bf16[1024,512]{1,0:T(8,128)(2,1)} %collective-permute-done.10.refs_9_), channel_id=1, source_target_pairs={{0,7},{1,0},{2,1},{3,2},{4,3},{5,4},{6,5},{7,6},{8,15},{9,8},{10,9... | collective-permute-start | bytes 3145736 | tf_op jit(solution)/shard_map/ppermute | solution.py:22
  73.2 23.7 %collective-permute-start.14 = (bf16[1024,512]{1,0:T(8,128)(2,1)}, bf16[1024,512]{1,0:T(8,128)(2,1)}, u32[]{:S(2)}, u32[]{:S(2)}) collective-permute-start(bf16[1024,512]{1,0:T(8,128)(2,1)} %collective-permute-done.9.refs_8_), channel_id=1, source_target_pairs={{0,1},{1,2},{2,3},{3,4},{4,5},{5,6},{6,7},{7,0},{8,9},{9,10},{10,1... | collective-permute-start | bytes 3145736 | tf_op jit(solution)/shard_map/ppermute | solution.py:22
  75.4 19.8 %copy-start.2 = (bf16[1024,384]{1,0:T(8,128)(2,1)}, bf16[1024,384]{1,0:T(8,128)(2,1)S(1)}, u32[]{:S(2)}) copy-start(bf16[1024,384]{1,0:T(8,128)(2,1)S(1)} %shard_map.85.refs_6_) | copy-start | bytes 2359300
  79.7 19.2 %collective-permute-start.21 = (bf16[1024,384]{1,0:T(8,128)(2,1)S(1)}, bf16[1024,384]{1,0:T(8,128)(2,1)}, u32[]{:S(2)}, u32[]{:S(2)}) collective-permute-start(bf16[1024,384]{1,0:T(8,128)(2,1)S(1)} %shard_map.85.refs_6_), channel_id=1, source_target_pairs={{0,24},{1,25},{2,26},{3,27},{4,28},{5,29},{6,30},{7,31},{8,0},{9,1... | collective-permute-start | bytes 2359304 | tf_op jit(solution)/shard_map/ppermute | solution.py:22
  80.6 20.1 %collective-permute-start.20 = (bf16[1024,384]{1,0:T(8,128)(2,1)S(1)}, bf16[1024,384]{1,0:T(8,128)(2,1)}, u32[]{:S(2)}, u32[]{:S(2)}) collective-permute-start(bf16[1024,384]{1,0:T(8,128)(2,1)S(1)} %shard_map.85.refs_6_), channel_id=1, source_target_pairs={{0,8},{1,9},{2,10},{3,11},{4,12},{5,13},{6,14},{7,15},{8,16},{9,17... | collective-permute-start | bytes 2359304 | tf_op jit(solution)/shard_map/ppermute | solution.py:22
  96.9 31.8 %collective-permute-start.17 = (bf16[1024,512]{1,0:T(8,128)(2,1)}, bf16[1024,512]{1,0:T(8,128)(2,1)S(1)}, u32[]{:S(2)}, u32[]{:S(2)}) collective-permute-start(bf16[1024,512]{1,0:T(8,128)(2,1)} %collective-permute-done.15.refs_8_), channel_id=1, source_target_pairs={{0,7},{1,0},{2,1},{3,2},{4,3},{5,4},{6,5},{7,6},{8,15},{9,8},{10,9... | collective-permute-start | bytes 3145736 | tf_op jit(solution)/shard_map/ppermute | solution.py:22
  97.1 31.7 %collective-permute-start.16 = (bf16[1024,512]{1,0:T(8,128)(2,1)}, bf16[1024,512]{1,0:T(8,128)(2,1)S(1)}, u32[]{:S(2)}, u32[]{:S(2)}) collective-permute-start(bf16[1024,512]{1,0:T(8,128)(2,1)} %collective-permute-done.14.refs_7_), channel_id=1, source_target_pairs={{0,1},{1,2},{2,3},{3,4},{4,5},{5,6},{6,7},{7,0},{8,9},{9,10},{10,1... | collective-permute-start | bytes 3145736 | tf_op jit(solution)/shard_map/ppermute | solution.py:22
  115.0 13.7 %collective-permute-start.23 = (bf16[512,384]{1,0:T(8,128)(2,1)}, bf16[512,384]{1,0:T(8,128)(2,1)S(1)}, u32[]{:S(2)}, u32[]{:S(2)}) collective-permute-start(bf16[512,384]{1,0:T(8,128)(2,1)} %slice.28), channel_id=1, source_target_pairs={{0,24},{1,25},{2,26},{3,27},{4,28},{5,29},{6,30},{7,31},{8,0},{9,1... | collective-permute-start | bytes 1179656 | tf_op jit(solution)/shard_map/ppermute | solution.py:22
  116.3 12.4 %collective-permute-start.22 = (bf16[512,384]{1,0:T(8,128)(2,1)S(1)}, bf16[512,384]{1,0:T(8,128)(2,1)S(1)}, u32[]{:S(2)}, u32[]{:S(2)}) collective-permute-start(bf16[512,384]{1,0:T(8,128)(2,1)S(1)} %slice.27), channel_id=1, source_target_pairs={{0,8},{1,9},{2,10},{3,11},{4,12},{5,13},{6,14},{7,15},{8,16},{9,17... | collective-permute-start | bytes 1179656 | tf_op jit(solution)/shard_map/ppermute | solution.py:22
  129.6 11.7 %collective-permute-start.25 = (bf16[512,512]{1,0:T(8,128)(2,1)S(1)}, bf16[512,512]{1,0:T(8,128)(2,1)S(1)}, u32[]{:S(2)}, u32[]{:S(2)}) collective-permute-start(bf16[512,512]{1,0:T(8,128)(2,1)S(1)} %slice.29), channel_id=1, source_target_pairs={{0,7},{1,0},{2,1},{3,2},{4,3},{5,4},{6,5},{7,6},{8,15},{9,8},{10,9... | collective-permute-start | bytes 1572872 | tf_op jit(solution)/shard_map/ppermute | solution.py:22
  131.1 13.9 %collective-permute-start.24 = (bf16[512,512]{1,0:T(8,128)(2,1)S(1)}, bf16[512,512]{1,0:T(8,128)(2,1)}, u32[]{:S(2)}, u32[]{:S(2)}) collective-permute-start(bf16[512,512]{1,0:T(8,128)(2,1)S(1)} %slice.24), channel_id=1, source_target_pairs={{0,1},{1,2},{2,3},{3,4},{4,5},{5,6},{6,7},{7,0},{8,9},{9,10},{10,1... | collective-permute-start | bytes 1572872 | tf_op jit(solution)/shard_map/ppermute | solution.py:22
  (9 other events, 20.8 us)
Sparse Core Ops, SparseCore 0:
  9.4 72.5 all-gather.1

commit v12 on v11

--- a/solution.py
+++ b/solution.py
@@ -261,18 +261,16 @@
     amps = mask(
         here, sym_ij, sym_cd, amp_mask, raw,
         plus(near, 0, -1, 1) + plus(far, 0) + minus(0, -1, 1),
-        plus(near, 2) + plus(far, -1, 1) + minus(-2, 2),
-        plus(far, 2) + minus(-3, 3),
+        plus(near, 2) + plus(far, -1, 1, 2) + minus(-2, 2, -3, 3),
         minus(4),
     )
     wu.append(go(wu[1], wd[1], amps[0], dz=1))
     wd.append(go(wd[1], wu[1], amps[0], dz=-1))
     total = add(amps[0], [(c0,), c1[:1], c1[1:], (d0,), (w0,), (wu[0],), (wd[0],)])
-    d2 = (go(d1[0][:HALF], *d1, total, dy=1), go(d1[1][HALF:], *d1, total, dy=-1))
-    total = add(amps[1], [c2, d1[:1], d1[1:], (wu[1],), (wd[1],)], total)
+    d2 = (go(d1[0][:HALF], *d1, dy=1), go(d1[1][HALF:], *d1, dy=-1))
     w4 = (go(wu[2][:HALF], wd[2], *d2, total, dz=1), go(wd[2][HALF:], wu[2], *d2, total, dz=-1))
-    total = add(amps[2], [d2, (wu[2],), (wd[2],)], total)
-    return add(amps[3], [w4], total, True)
+    total = add(amps[1], [c2, d1[:1], d1[1:], d2, (wu[1],), (wd[1],), (wu[2],), (wd[2],)], total)
+    return add(amps[2], [w4], total, True)
 
 
 def solution(mesh):

time: 157 us -> 156 us (level)
  Pallas kernels: 47.5 us -> 43.8 us
  starting transfers between devices: 36 us -> 37.9 us
    pallas_call x4 -> x3, Pallas kernels: 35.4 us -> 31.7 us  [product(): pl.pallas_call(kernel, out_shape=jax.ShapeDtypeStruct((768, 1024), kind),...]
    ppermute x26, starting transfers between devices: 35.9 us -> 37.9 us  [move(): return lax.ppermute(values, 'mem', perm_of(dy, dz))]
  transfers between devices with their start and end apart: 27 -> 27, of which waited for: 14 -> 8; matrix products, arithmetic and copies ran while one was open for 2% -> 3% of each run, Pallas kernels for 27% -> 25%
where the time goes in v12:
time: 156 us
  waiting for transfers between devices  51.8 us (33%)
  Pallas kernels  43.8 us (28%)
  starting transfers between devices  37.9 us (24%)
  between operations  13.7 us (9%)
  local copies, waits for them, and re-layouts  5.19 us (3%)
  other arithmetic  3.32 us (2%)
    ppermute x26, waiting for transfers between devices, move(): return lax.ppermute(values, 'mem', perm_of(dy, dz))  51.8 us
    ppermute x26, starting transfers between devices, move(): return lax.ppermute(values, 'mem', perm_of(dy, dz))  37.9 us
    pallas_call x3, Pallas kernels, product(): pl.pallas_call(kernel, out_shape=jax.ShapeDtypeStruct((768, 1024), kind),...  31.7 us
    pallas_call x1, Pallas kernels, mask(): pl.pallas_call(kernel, out_shape=[jax.ShapeDtypeStruct(shape, BF16) for s...  11.5 us
  transfers between devices with their start and end apart: 27, of which 8 were waited for; matrix products, arithmetic and copies ran while one was open for 3% of the time, Pallas kernels for 25%

profile of v12, /device:TPU:24, one launch (start us, length us, event | category | flops | bytes accessed | tf_op | source)
XLA Modules:
  0.0 155.8 jit_solution(6602641972011177951)
XLA Ops:
  6.5 2.7 %pad_maximum_fusion = bf16[1536,512]{1,0:T(8,128)(2,1)} fusion(bf16[768,512]{1,0:T(8,128)(2,1)} %param.9, bf16[768,512]{1,0:T(8,128)(2,1)} %param.8), kind=kLoop, calls=%fused_computation | loop fusion | flops 3145728 | bytes 3145728 | tf_op jit(solution)/shard_map/concatenate | solution.py:228
  9.2 2.0 %collective-permute-start = (bf16[1024,128]{1,0:T(8,128)(2,1)S(1)}, bf16[1024,128]{1,0:T(8,128)(2,1)S(1)}, u32[]{:S(2)}, u32[]{:S(2)}) collective-permute-start(bf16[1024,128]{1,0:T(8,128)(2,1)S(1)} %copy-done.4), channel_id=1, source_target_pairs={{0,8},{1,9},{2,10},{3,11},{4,12},{5,13},{6,14},{7,15},{8,16},{9,17... | collective-permute-start | bytes 786440 | tf_op jit(solution)/shard_map/ppermute | solution.py:22
  11.5 3.9 %collective-permute-start.3 = (bf16[1024,128]{1,0:T(8,128)(2,1)S(1)}, bf16[1024,128]{1,0:T(8,128)(2,1)S(1)}, u32[]{:S(2)}, u32[]{:S(2)}) collective-permute-start(bf16[1024,128]{1,0:T(8,128)(2,1)S(1)} %copy-done.3), channel_id=1, source_target_pairs={{0,7},{1,0},{2,1},{3,2},{4,3},{5,4},{6,5},{7,6},{8,15},{9,8},{10,9... | collective-permute-start | bytes 786440 | tf_op jit(solution)/shard_map/ppermute | solution.py:22
  15.4 1.8 %collective-permute-start.1 = (bf16[1024,128]{1,0:T(8,128)(2,1)S(1)}, bf16[1024,128]{1,0:T(8,128)(2,1)S(1)}, u32[]{:S(2)}, u32[]{:S(2)}) collective-permute-start(bf16[1024,128]{1,0:T(8,128)(2,1)S(1)} %copy-done.4), channel_id=1, source_target_pairs={{0,24},{1,25},{2,26},{3,27},{4,28},{5,29},{6,30},{7,31},{8,0},{9,1... | collective-permute-start | bytes 786440 | tf_op jit(solution)/shard_map/ppermute | solution.py:22
  17.4 4.2 %collective-permute-done.2.refs_1_ = bf16[1024,128]{1,0:T(8,128)(2,1)S(1)} collective-permute-done((bf16[1024,128]{1,0:T(8,128)(2,1)S(1)}, bf16[1024,128]{1,0:T(8,128)(2,1)S(1)}, u32[]{:S(2)}, u32[]{:S(2)}) %collective-permute-start.2) | collective-permute-done | bytes 262176 | tf_op jit(solution)/shard_map/ppermute | solution.py:22
  21.6 3.2 %collective-permute-start.6 = (bf16[1024,128]{1,0:T(8,128)(2,1)S(1)}, bf16[1024,128]{1,0:T(8,128)(2,1)S(1)}, u32[]{:S(2)}, u32[]{:S(2)}) collective-permute-start(bf16[1024,128]{1,0:T(8,128)(2,1)S(1)} %collective-permute-done.3.refs_2_), channel_id=1, source_target_pairs={{0,7},{1,0},{2,1},{3,2},{4,3},{5,4},{6,5},{7,6},{8,15},{9,8},{10,9... | collective-permute-start | bytes 786440 | tf_op jit(solution)/shard_map/ppermute | solution.py:22
  24.8 1.4 collective-permute-start.4
  26.3 3.9 %collective-permute-done.5.refs_3_ = bf16[1024,128]{1,0:T(8,128)(2,1)S(1)} collective-permute-done((bf16[1024,128]{1,0:T(8,128)(2,1)S(1)}, bf16[1024,128]{1,0:T(8,128)(2,1)S(1)}, u32[]{:S(2)}, u32[]{:S(2)}) %collective-permute-start.5) | collective-permute-done | bytes 262176 | tf_op jit(solution)/shard_map/ppermute | solution.py:22
  30.2 1.8 %collective-permute-start.7 = (bf16[1024,128]{1,0:T(8,128)(2,1)S(1)}, bf16[1024,128]{1,0:T(8,128)(2,1)S(1)}, u32[]{:S(2)}, u32[]{:S(2)}) collective-permute-start(bf16[1024,128]{1,0:T(8,128)(2,1)S(1)} %collective-permute-done.5.refs_3_), channel_id=1, source_target_pairs={{0,1},{1,2},{2,3},{3,4},{4,5},{5,6},{6,7},{7,0},{8,9},{9,10},{10,1... | collective-permute-start | bytes 786440 | tf_op jit(solution)/shard_map/ppermute | solution.py:22
  32.0 1.4 collective-permute-start.8
  33.6 1.3 collective-permute-start.12
  35.9 1.9 %collective-permute-done.7.refs_0_ = bf16[1024,128]{1,0:T(8,128)(2,1)S(1)} collective-permute-done((bf16[1024,128]{1,0:T(8,128)(2,1)S(1)}, bf16[1024,128]{1,0:T(8,128)(2,1)S(1)}, u32[]{:S(2)}, u32[]{:S(2)}) %collective-permute-start.7) | collective-permute-done | bytes 262176 | tf_op jit(solution)/shard_map/ppermute | solution.py:22
  37.8 1.0 collective-permute-done.8.refs_1_
  38.8 2.1 %collective-permute-start.10 = (bf16[1024,512]{1,0:T(8,128)(2,1)S(1)}, bf16[1024,512]{1,0:T(8,128)(2,1)}, u32[]{:S(2)}, u32[]{:S(2)}) collective-permute-start(bf16[1024,512]{1,0:T(8,128)(2,1)S(1)} %shard_map.83.refs_7_), channel_id=1, source_target_pairs={{0,7},{1,0},{2,1},{3,2},{4,3},{5,4},{6,5},{7,6},{8,15},{9,8},{10,9... | collective-permute-start | bytes 3145736 | tf_op jit(solution)/shard_map/ppermute | solution.py:22
  41.0 1.8 %collective-permute-start.11 = (bf16[1024,128]{1,0:T(8,128)(2,1)S(1)}, bf16[1024,128]{1,0:T(8,128)(2,1)S(1)}, u32[]{:S(2)}, u32[]{:S(2)}) collective-permute-start(bf16[1024,128]{1,0:T(8,128)(2,1)S(1)} %collective-permute-done.7.refs_0_), channel_id=1, source_target_pairs={{0,1},{1,2},{2,3},{3,4},{4,5},{5,6},{6,7},{7,0},{8,9},{9,10},{10,1... | collective-permute-start | bytes 786440 | tf_op jit(solution)/shard_map/ppermute | solution.py:22
  42.8 27.0 %collective-permute-done.11.refs_2_ = bf16[1024,128]{1,0:T(8,128)(2,1)S(1)} collective-permute-done((bf16[1024,128]{1,0:T(8,128)(2,1)S(1)}, bf16[1024,128]{1,0:T(8,128)(2,1)S(1)}, u32[]{:S(2)}, u32[]{:S(2)}) %collective-permute-start.11) | collective-permute-done | bytes 262176 | tf_op jit(solution)/shard_map/ppermute | solution.py:22
  70.1 2.0 %collective-permute-start.14 = (bf16[1024,512]{1,0:T(8,128)(2,1)}, bf16[1024,512]{1,0:T(8,128)(2,1)}, u32[]{:S(2)}, u32[]{:S(2)}) collective-permute-start(bf16[1024,512]{1,0:T(8,128)(2,1)} %collective-permute-done.9.refs_8_), channel_id=1, source_target_pairs={{0,1},{1,2},{2,3},{3,4},{4,5},{5,6},{6,7},{7,0},{8,9},{9,10},{10,1... | collective-permute-start | bytes 3145736 | tf_op jit(solution)/shard_map/ppermute | solution.py:22
  72.2 1.1 collective-permute-start.18
  73.4 1.1 collective-permute-start.19
  74.6 10.9 %collective-permute-done.18.refs_3_ = bf16[512,640]{1,0:T(8,128)(2,1)S(1)} collective-permute-done((bf16[512,640]{1,0:T(8,128)(2,1)S(1)}, bf16[512,640]{1,0:T(8,128)(2,1)S(1)}, u32[]{:S(2)}, u32[]{:S(2)}) %collective-permute-start.18) | collective-permute-done | bytes 655392 | tf_op jit(solution)/shard_map/ppermute | solution.py:22
  85.5 2.7 %collective-permute-done.19.refs_4_ = bf16[512,640]{1,0:T(8,128)(2,1)S(1)} collective-permute-done((bf16[512,640]{1,0:T(8,128)(2,1)S(1)}, bf16[512,640]{1,0:T(8,128)(2,1)S(1)}, u32[]{:S(2)}, u32[]{:S(2)}) %collective-permute-start.19) | collective-permute-done | bytes 655392 | tf_op jit(solution)/shard_map/ppermute | solution.py:22
  89.1 2.4 %collective-permute-start.20 = (bf16[1024,384]{1,0:T(8,128)(2,1)S(1)}, bf16[1024,384]{1,0:T(8,128)(2,1)}, u32[]{:S(2)}, u32[]{:S(2)}) collective-permute-start(bf16[1024,384]{1,0:T(8,128)(2,1)S(1)} %shard_map.85.refs_6_), channel_id=1, source_target_pairs={{0,8},{1,9},{2,10},{3,11},{4,12},{5,13},{6,14},{7,15},{8,16},{9,17... | collective-permute-start | bytes 2359304 | tf_op jit(solution)/shard_map/ppermute | solution.py:22
  92.1 11.5 %shard_map.82 = (bf16[768,3840]{1,0:T(8,128)(2,1)}, bf16[768,3840]{1,0:T(8,128)(2,1)}, bf16[768,512]{1,0:T(8,128)(2,1)}) custom-call(s32[2]{0:T(128)} %pad_add_fusion.refs_0_, s32[6]{0:T(128)} %refs_0_.9, s32[32]{0:T(128)} %refs_2_.1, s32[6,32]{1,0:T(8,128)} %refs_3_.1, bf16[1536,4096]{1,0:T(8,128)(2,1)} %all-gather.2.cloned.1.call-done.refs_4_), custom_call_target="tpu_custom_call" | custom-call | bytes 26214400 | tf_op jit(solution)/shard_map/pallas_call | solution.py:104
  103.7 1.4 collective-permute-start.17
  105.8 1.0 slice.28
  107.0 1.0 slice.27
  108.0 3.5 %collective-permute-start.22 = (bf16[512,384]{1,0:T(8,128)(2,1)S(1)}, bf16[512,384]{1,0:T(8,128)(2,1)S(1)}, u32[]{:S(2)}, u32[]{:S(2)}) collective-permute-start(bf16[512,384]{1,0:T(8,128)(2,1)S(1)} %slice.27), channel_id=1, source_target_pairs={{0,8},{1,9},{2,10},{3,11},{4,12},{5,13},{6,14},{7,15},{8,16},{9,17... | collective-permute-start | bytes 1179656 | tf_op jit(solution)/shard_map/ppermute | solution.py:22
  111.5 13.3 %shard_map.86.refs_13_ = f32[768,1024]{1,0:T(8,128)} custom-call(s32[6]{0:T(128)} %refs_0_.9, s32[8]{0:T(128)} %refs_1_.7, bf16[768,3840]{1,0:T(8,128)(2,1)} %get-tuple-element.36.refs_2_, bf16[1024,640]{1,0:T(8,128)(2,1)} %copy-done, bf16[1024,640]{1,0:T(8,128)(2,1)} %copy-done.7, bf16[1024,640]{1,0:T(8,128)(2,1)} %copy-done.8, ...), custom_call_target="tpu_custom_call" | custom-call | flops 6039797760 | bytes 22151168 | tf_op jit(solution)/shard_map/pallas_call | solution.py:204
  125.8 2.5 %collective-permute-start.25 = (bf16[512,512]{1,0:T(8,128)(2,1)S(1)}, bf16[512,512]{1,0:T(8,128)(2,1)S(1)}, u32[]{:S(2)}, u32[]{:S(2)}) collective-permute-start(bf16[512,512]{1,0:T(8,128)(2,1)S(1)} %slice.29), channel_id=1, source_target_pairs={{0,7},{1,0},{2,1},{3,2},{4,3},{5,4},{6,5},{7,6},{8,15},{9,8},{10,9... | collective-permute-start | bytes 1572872 | tf_op jit(solution)/shard_map/ppermute | solution.py:22
  128.3 1.1 slice.24
  129.5 13.6 %shard_map.87.refs_5_ = f32[768,1024]{1,0:T(8,128)} custom-call(s32[6]{0:T(128)} %refs_0_.9, s32[8]{0:T(128)} %refs_1_.7, bf16[768,3840]{1,0:T(8,128)(2,1)} %get-tuple-element.46.refs_2_, bf16[512,640]{1,0:T(8,128)(2,1)} %copy-done.10, bf16[512,640]{1,0:T(8,128)(2,1)} %copy-done.11, bf16[1024,384]{1,0:T(8,128)(2,1)} %collective-permute-done.20.refs_5_, ...), custom_call_target="tpu_custom_call" | custom-call | flops 6039797760 | bytes 22151168 | tf_op jit(solution)/shard_map/pallas_call | solution.py:204
  144.1 4.8 %shard_map.88 = bf16[768,1024]{1,0:T(8,128)(2,1)} custom-call(s32[6]{0:T(128)} %refs_0_.9, s32[8]{0:T(128)} %refs_1_.7, bf16[768,512]{1,0:T(8,128)(2,1)} %get-tuple-element.26.refs_2_, bf16[512,512]{1,0:T(8,128)(2,1)} %copy-done.6, bf16[512,512]{1,0:T(8,128)(2,1)} %copy-done.5, f32[768,1024]{1,0:T(8,128)} %shard_map.87.refs_5_), custom_call_target="tpu_custom_call" | custom-call | flops 805306368 | bytes 10223616 | tf_op jit(solution)/shard_map/pallas_call | solution.py:204
  (66 shorter events, 6.4 us)
Async XLA Ops:
  6.5 4.7 %copy-start.3 = (bf16[1024,128]{1,0:T(8,128)(2,1)S(1)}, bf16[1024,128]{1,0:T(8,128)(2,1)}, u32[]{:S(2)}) copy-start(bf16[1024,128]{1,0:T(8,128)(2,1)} %refs_0_.6) | copy-start | bytes 786436
  6.5 85.6 %all-gather.2.cloned.1.call-start = ((), (), s32[]{:S(2)}) async-start(), calls=%async_computation | async-start | bytes 14155776 | tf_op jit(solution)/shard_map/all_gather | solution.py:228
  9.2 8.1 %collective-permute-start = (bf16[1024,128]{1,0:T(8,128)(2,1)S(1)}, bf16[1024,128]{1,0:T(8,128)(2,1)S(1)}, u32[]{:S(2)}, u32[]{:S(2)}) collective-permute-start(bf16[1024,128]{1,0:T(8,128)(2,1)S(1)} %copy-done.4), channel_id=1, source_target_pairs={{0,8},{1,9},{2,10},{3,11},{4,12},{5,13},{6,14},{7,15},{8,16},{9,17... | collective-permute-start | bytes 786440 | tf_op jit(solution)/shard_map/ppermute | solution.py:22
  11.3 10.3 %collective-permute-start.2 = (bf16[1024,128]{1,0:T(8,128)(2,1)S(1)}, bf16[1024,128]{1,0:T(8,128)(2,1)S(1)}, u32[]{:S(2)}, u32[]{:S(2)}) collective-permute-start(bf16[1024,128]{1,0:T(8,128)(2,1)S(1)} %copy-done.3), channel_id=1, source_target_pairs={{0,1},{1,2},{2,3},{3,4},{4,5},{5,6},{6,7},{7,0},{8,9},{9,10},{10,1... | collective-permute-start | bytes 786440 | tf_op jit(solution)/shard_map/ppermute | solution.py:22
  11.5 10.1 %collective-permute-start.3 = (bf16[1024,128]{1,0:T(8,128)(2,1)S(1)}, bf16[1024,128]{1,0:T(8,128)(2,1)S(1)}, u32[]{:S(2)}, u32[]{:S(2)}) collective-permute-start(bf16[1024,128]{1,0:T(8,128)(2,1)S(1)} %copy-done.3), channel_id=1, source_target_pairs={{0,7},{1,0},{2,1},{3,2},{4,3},{5,4},{6,5},{7,6},{8,15},{9,8},{10,9... | collective-permute-start | bytes 786440 | tf_op jit(solution)/shard_map/ppermute | solution.py:22
  15.4 9.4 %collective-permute-start.1 = (bf16[1024,128]{1,0:T(8,128)(2,1)S(1)}, bf16[1024,128]{1,0:T(8,128)(2,1)S(1)}, u32[]{:S(2)}, u32[]{:S(2)}) collective-permute-start(bf16[1024,128]{1,0:T(8,128)(2,1)S(1)} %copy-done.4), channel_id=1, source_target_pairs={{0,24},{1,25},{2,26},{3,27},{4,28},{5,29},{6,30},{7,31},{8,0},{9,1... | collective-permute-start | bytes 786440 | tf_op jit(solution)/shard_map/ppermute | solution.py:22
  21.6 8.6 %collective-permute-start.5 = (bf16[1024,128]{1,0:T(8,128)(2,1)S(1)}, bf16[1024,128]{1,0:T(8,128)(2,1)S(1)}, u32[]{:S(2)}, u32[]{:S(2)}) collective-permute-start(bf16[1024,128]{1,0:T(8,128)(2,1)S(1)} %collective-permute-done.2.refs_1_), channel_id=1, source_target_pairs={{0,1},{1,2},{2,3},{3,4},{4,5},{5,6},{6,7},{7,0},{8,9},{9,10},{10,1... | collective-permute-start | bytes 786440 | tf_op jit(solution)/shard_map/ppermute | solution.py:22
  21.6 8.6 %collective-permute-start.6 = (bf16[1024,128]{1,0:T(8,128)(2,1)S(1)}, bf16[1024,128]{1,0:T(8,128)(2,1)S(1)}, u32[]{:S(2)}, u32[]{:S(2)}) collective-permute-start(bf16[1024,128]{1,0:T(8,128)(2,1)S(1)} %collective-permute-done.3.refs_2_), channel_id=1, source_target_pairs={{0,7},{1,0},{2,1},{3,2},{4,3},{5,4},{6,5},{7,6},{8,15},{9,8},{10,9... | collective-permute-start | bytes 786440 | tf_op jit(solution)/shard_map/ppermute | solution.py:22
  24.8 8.8 %collective-permute-start.4 = (bf16[1024,128]{1,0:T(8,128)(2,1)S(1)}, bf16[1024,128]{1,0:T(8,128)(2,1)S(1)}, u32[]{:S(2)}, u32[]{:S(2)}) collective-permute-start(bf16[1024,128]{1,0:T(8,128)(2,1)S(1)} %collective-permute-done.refs_1_), channel_id=1, source_target_pairs={{0,8},{1,9},{2,10},{3,11},{4,12},{5,13},{6,14},{7,15},{8,16},{9,17... | collective-permute-start | bytes 786440 | tf_op jit(solution)/shard_map/ppermute | solution.py:22
  30.2 7.6 %collective-permute-start.7 = (bf16[1024,128]{1,0:T(8,128)(2,1)S(1)}, bf16[1024,128]{1,0:T(8,128)(2,1)S(1)}, u32[]{:S(2)}, u32[]{:S(2)}) collective-permute-start(bf16[1024,128]{1,0:T(8,128)(2,1)S(1)} %collective-permute-done.5.refs_3_), channel_id=1, source_target_pairs={{0,1},{1,2},{2,3},{3,4},{4,5},{5,6},{6,7},{7,0},{8,9},{9,10},{10,1... | collective-permute-start | bytes 786440 | tf_op jit(solution)/shard_map/ppermute | solution.py:22
  32.0 6.9 %collective-permute-start.8 = (bf16[1024,128]{1,0:T(8,128)(2,1)S(1)}, bf16[1024,128]{1,0:T(8,128)(2,1)S(1)}, u32[]{:S(2)}, u32[]{:S(2)}) collective-permute-start(bf16[1024,128]{1,0:T(8,128)(2,1)S(1)} %collective-permute-done.6.refs_4_), channel_id=1, source_target_pairs={{0,7},{1,0},{2,1},{3,2},{4,3},{5,4},{6,5},{7,6},{8,15},{9,8},{10,9... | collective-permute-start | bytes 786440 | tf_op jit(solution)/shard_map/ppermute | solution.py:22
  33.6 40.9 %copy-start = (bf16[1024,640]{1,0:T(8,128)(2,1)}, bf16[1024,640]{1,0:T(8,128)(2,1)S(1)}, u32[]{:S(2)}) copy-start(bf16[1024,640]{1,0:T(8,128)(2,1)S(1)} %shard_map.84.refs_3_) | copy-start | bytes 3932164
  33.6 36.1 %collective-permute-start.12 = (bf16[1024,640]{1,0:T(8,128)(2,1)S(1)}, bf16[1024,640]{1,0:T(8,128)(2,1)S(1)}, u32[]{:S(2)}, u32[]{:S(2)}) collective-permute-start(bf16[1024,640]{1,0:T(8,128)(2,1)S(1)} %shard_map.84.refs_3_), channel_id=1, source_target_pairs={{0,8},{1,9},{2,10},{3,11},{4,12},{5,13},{6,14},{7,15},{8,16},{9,17... | collective-permute-start | bytes 3932168 | tf_op jit(solution)/shard_map/ppermute | solution.py:22
  35.0 34.8 %collective-permute-start.13 = (bf16[1024,640]{1,0:T(8,128)(2,1)S(1)}, bf16[1024,640]{1,0:T(8,128)(2,1)S(1)}, u32[]{:S(2)}, u32[]{:S(2)}) collective-permute-start(bf16[1024,640]{1,0:T(8,128)(2,1)S(1)} %shard_map.84.refs_3_), channel_id=1, source_target_pairs={{0,24},{1,25},{2,26},{3,27},{4,28},{5,29},{6,30},{7,31},{8,0},{9,1... | collective-permute-start | bytes 3932168 | tf_op jit(solution)/shard_map/ppermute | solution.py:22
  35.9 67.7 %copy-start.1 = (bf16[1024,512]{1,0:T(8,128)(2,1)}, bf16[1024,512]{1,0:T(8,128)(2,1)S(1)}, u32[]{:S(2)}) copy-start(bf16[1024,512]{1,0:T(8,128)(2,1)S(1)} %shard_map.83.refs_7_) | copy-start | bytes 3145732
  38.8 30.9 %collective-permute-start.10 = (bf16[1024,512]{1,0:T(8,128)(2,1)S(1)}, bf16[1024,512]{1,0:T(8,128)(2,1)}, u32[]{:S(2)}, u32[]{:S(2)}) collective-permute-start(bf16[1024,512]{1,0:T(8,128)(2,1)S(1)} %shard_map.83.refs_7_), channel_id=1, source_target_pairs={{0,7},{1,0},{2,1},{3,2},{4,3},{5,4},{6,5},{7,6},{8,15},{9,8},{10,9... | collective-permute-start | bytes 3145736 | tf_op jit(solution)/shard_map/ppermute | solution.py:22
  41.0 28.8 %collective-permute-start.9 = (bf16[1024,512]{1,0:T(8,128)(2,1)S(1)}, bf16[1024,512]{1,0:T(8,128)(2,1)}, u32[]{:S(2)}, u32[]{:S(2)}) collective-permute-start(bf16[1024,512]{1,0:T(8,128)(2,1)S(1)} %shard_map.83.refs_7_), channel_id=1, source_target_pairs={{0,1},{1,2},{2,3},{3,4},{4,5},{5,6},{6,7},{7,0},{8,9},{9,10},{10,1... | collective-permute-start | bytes 3145736 | tf_op jit(solution)/shard_map/ppermute | solution.py:22
  41.0 28.8 %collective-permute-start.11 = (bf16[1024,128]{1,0:T(8,128)(2,1)S(1)}, bf16[1024,128]{1,0:T(8,128)(2,1)S(1)}, u32[]{:S(2)}, u32[]{:S(2)}) collective-permute-start(bf16[1024,128]{1,0:T(8,128)(2,1)S(1)} %collective-permute-done.7.refs_0_), channel_id=1, source_target_pairs={{0,1},{1,2},{2,3},{3,4},{4,5},{5,6},{6,7},{7,0},{8,9},{9,10},{10,1... | collective-permute-start | bytes 786440 | tf_op jit(solution)/shard_map/ppermute | solution.py:22
  69.8 18.4 %copy-start.8 = (bf16[1024,640]{1,0:T(8,128)(2,1)}, bf16[1024,640]{1,0:T(8,128)(2,1)S(1)}, u32[]{:S(2)}) copy-start(bf16[1024,640]{1,0:T(8,128)(2,1)S(1)} %collective-permute-done.13.refs_5_) | copy-start | bytes 3932164
  69.8 33.9 %collective-permute-start.15 = (bf16[1024,512]{1,0:T(8,128)(2,1)}, bf16[1024,512]{1,0:T(8,128)(2,1)}, u32[]{:S(2)}, u32[]{:S(2)}) collective-permute-start(bf16[1024,512]{1,0:T(8,128)(2,1)} %collective-permute-done.10.refs_9_), channel_id=1, source_target_pairs={{0,7},{1,0},{2,1},{3,2},{4,3},{5,4},{6,5},{7,6},{8,15},{9,8},{10,9... | collective-permute-start | bytes 3145736 | tf_op jit(solution)/shard_map/ppermute | solution.py:22
  70.1 33.6 %collective-permute-start.14 = (bf16[1024,512]{1,0:T(8,128)(2,1)}, bf16[1024,512]{1,0:T(8,128)(2,1)}, u32[]{:S(2)}, u32[]{:S(2)}) collective-permute-start(bf16[1024,512]{1,0:T(8,128)(2,1)} %collective-permute-done.9.refs_8_), channel_id=1, source_target_pairs={{0,1},{1,2},{2,3},{3,4},{4,5},{5,6},{6,7},{7,0},{8,9},{9,10},{10,1... | collective-permute-start | bytes 3145736 | tf_op jit(solution)/shard_map/ppermute | solution.py:22
  72.2 13.3 %collective-permute-start.18 = (bf16[512,640]{1,0:T(8,128)(2,1)S(1)}, bf16[512,640]{1,0:T(8,128)(2,1)S(1)}, u32[]{:S(2)}, u32[]{:S(2)}) collective-permute-start(bf16[512,640]{1,0:T(8,128)(2,1)S(1)} %slice.25), channel_id=1, source_target_pairs={{0,8},{1,9},{2,10},{3,11},{4,12},{5,13},{6,14},{7,15},{8,16},{9,17... | collective-permute-start | bytes 1966088 | tf_op jit(solution)/shard_map/ppermute | solution.py:22
  73.4 14.9 %collective-permute-start.19 = (bf16[512,640]{1,0:T(8,128)(2,1)S(1)}, bf16[512,640]{1,0:T(8,128)(2,1)S(1)}, u32[]{:S(2)}, u32[]{:S(2)}) collective-permute-start(bf16[512,640]{1,0:T(8,128)(2,1)S(1)} %slice.26), channel_id=1, source_target_pairs={{0,24},{1,25},{2,26},{3,27},{4,28},{5,29},{6,30},{7,31},{8,0},{9,1... | collective-permute-start | bytes 1966088 | tf_op jit(solution)/shard_map/ppermute | solution.py:22
  74.6 29.1 %copy-start.2 = (bf16[1024,384]{1,0:T(8,128)(2,1)}, bf16[1024,384]{1,0:T(8,128)(2,1)S(1)}, u32[]{:S(2)}) copy-start(bf16[1024,384]{1,0:T(8,128)(2,1)S(1)} %shard_map.85.refs_6_) | copy-start | bytes 2359300
  88.2 17.6 %collective-permute-start.21 = (bf16[1024,384]{1,0:T(8,128)(2,1)S(1)}, bf16[1024,384]{1,0:T(8,128)(2,1)}, u32[]{:S(2)}, u32[]{:S(2)}) collective-permute-start(bf16[1024,384]{1,0:T(8,128)(2,1)S(1)} %shard_map.85.refs_6_), channel_id=1, source_target_pairs={{0,24},{1,25},{2,26},{3,27},{4,28},{5,29},{6,30},{7,31},{8,0},{9,1... | collective-permute-start | bytes 2359304 | tf_op jit(solution)/shard_map/ppermute | solution.py:22
  89.1 17.8 %collective-permute-start.20 = (bf16[1024,384]{1,0:T(8,128)(2,1)S(1)}, bf16[1024,384]{1,0:T(8,128)(2,1)}, u32[]{:S(2)}, u32[]{:S(2)}) collective-permute-start(bf16[1024,384]{1,0:T(8,128)(2,1)S(1)} %shard_map.85.refs_6_), channel_id=1, source_target_pairs={{0,8},{1,9},{2,10},{3,11},{4,12},{5,13},{6,14},{7,15},{8,16},{9,17... | collective-permute-start | bytes 2359304 | tf_op jit(solution)/shard_map/ppermute | solution.py:22
  103.7 21.1 %collective-permute-start.17 = (bf16[1024,512]{1,0:T(8,128)(2,1)}, bf16[1024,512]{1,0:T(8,128)(2,1)S(1)}, u32[]{:S(2)}, u32[]{:S(2)}) collective-permute-start(bf16[1024,512]{1,0:T(8,128)(2,1)} %collective-permute-done.15.refs_10_), channel_id=1, source_target_pairs={{0,7},{1,0},{2,1},{3,2},{4,3},{5,4},{6,5},{7,6},{8,15},{9,8},{10,9... | collective-permute-start | bytes 3145736 | tf_op jit(solution)/shard_map/ppermute | solution.py:22
  105.1 20.7 %collective-permute-start.16 = (bf16[1024,512]{1,0:T(8,128)(2,1)}, bf16[1024,512]{1,0:T(8,128)(2,1)}, u32[]{:S(2)}, u32[]{:S(2)}) collective-permute-start(bf16[1024,512]{1,0:T(8,128)(2,1)} %collective-permute-done.14.refs_9_), channel_id=1, source_target_pairs={{0,1},{1,2},{2,3},{3,4},{4,5},{5,6},{6,7},{7,0},{8,9},{9,10},{10,1... | collective-permute-start | bytes 3145736 | tf_op jit(solution)/shard_map/ppermute | solution.py:22
  106.9 18.0 %collective-permute-start.23 = (bf16[512,384]{1,0:T(8,128)(2,1)S(1)}, bf16[512,384]{1,0:T(8,128)(2,1)S(1)}, u32[]{:S(2)}, u32[]{:S(2)}) collective-permute-start(bf16[512,384]{1,0:T(8,128)(2,1)S(1)} %slice.28), channel_id=1, source_target_pairs={{0,24},{1,25},{2,26},{3,27},{4,28},{5,29},{6,30},{7,31},{8,0},{9,1... | collective-permute-start | bytes 1179656 | tf_op jit(solution)/shard_map/ppermute | solution.py:22
  108.0 16.9 %collective-permute-start.22 = (bf16[512,384]{1,0:T(8,128)(2,1)S(1)}, bf16[512,384]{1,0:T(8,128)(2,1)S(1)}, u32[]{:S(2)}, u32[]{:S(2)}) collective-permute-start(bf16[512,384]{1,0:T(8,128)(2,1)S(1)} %slice.27), channel_id=1, source_target_pairs={{0,8},{1,9},{2,10},{3,11},{4,12},{5,13},{6,14},{7,15},{8,16},{9,17... | collective-permute-start | bytes 1179656 | tf_op jit(solution)/shard_map/ppermute | solution.py:22
  125.8 17.3 %collective-permute-start.25 = (bf16[512,512]{1,0:T(8,128)(2,1)S(1)}, bf16[512,512]{1,0:T(8,128)(2,1)S(1)}, u32[]{:S(2)}, u32[]{:S(2)}) collective-permute-start(bf16[512,512]{1,0:T(8,128)(2,1)S(1)} %slice.29), channel_id=1, source_target_pairs={{0,7},{1,0},{2,1},{3,2},{4,3},{5,4},{6,5},{7,6},{8,15},{9,8},{10,9... | collective-permute-start | bytes 1572872 | tf_op jit(solution)/shard_map/ppermute | solution.py:22
  129.4 13.8 %collective-permute-start.24 = (bf16[512,512]{1,0:T(8,128)(2,1)S(1)}, bf16[512,512]{1,0:T(8,128)(2,1)S(1)}, u32[]{:S(2)}, u32[]{:S(2)}) collective-permute-start(bf16[512,512]{1,0:T(8,128)(2,1)S(1)} %slice.24), channel_id=1, source_target_pairs={{0,1},{1,2},{2,3},{3,4},{4,5},{5,6},{6,7},{7,0},{8,9},{9,10},{10,1... | collective-permute-start | bytes 1572872 | tf_op jit(solution)/shard_map/ppermute | solution.py:22
  (9 other events, 23.0 us)
Sparse Core Ops, SparseCore 0:
  9.4 72.5 all-gather.1

commit v13 on v12

--- a/solution.py
+++ b/solution.py
@@ -259,7 +259,7 @@
     wd.append(go(wd[0], wu[0], *z4, *c1, dz=-1))
     d1 = (go(d0, *c2, dy=1), go(d0, *c2, dy=-1))
     amps = mask(
-        here, sym_ij, sym_cd, amp_mask, raw,
+        here, sym_ij, sym_cd, amp_mask, after(raw, *c2),
         plus(near, 0, -1, 1) + plus(far, 0) + minus(0, -1, 1),
         plus(near, 2) + plus(far, -1, 1, 2) + minus(-2, 2, -3, 3),
         minus(4),

time: 156 us -> 157 us (level); the launches traced: 156 us -> 155 us
  waiting for transfers between devices: 51.8 us -> 45.6 us
  starting transfers between devices: 37.9 us -> 42.6 us
    ppermute x26, waiting for transfers between devices: 51.8 us -> 45.5 us  [move(): return lax.ppermute(values, 'mem', perm_of(dy, dz))]
    ppermute x26, starting transfers between devices: 37.9 us -> 42.6 us  [move(): return lax.ppermute(values, 'mem', perm_of(dy, dz))]
  transfers between devices with their start and end apart: 27 -> 27, of which waited for: 8 -> 6; matrix products, arithmetic and copies ran while one was open for 3% -> 3% of each run, Pallas kernels for 25% -> 25%
where the time goes in v13:
time: 157 us; the launch traced here: 155 us
  waiting for transfers between devices  45.6 us (29%)
  Pallas kernels  43.8 us (28%)
  starting transfers between devices  42.6 us (27%)
  between operations  13.7 us (9%)
  local copies, waits for them, and re-layouts  5.9 us (4%)
  other arithmetic  3.32 us (2%)
    ppermute x26, waiting for transfers between devices, move(): return lax.ppermute(values, 'mem', perm_of(dy, dz))  45.5 us
    ppermute x26, starting transfers between devices, move(): return lax.ppermute(values, 'mem', perm_of(dy, dz))  42.6 us
    pallas_call x3, Pallas kernels, product(): pl.pallas_call(kernel, out_shape=jax.ShapeDtypeStruct((768, 1024), kind),...  31.7 us
    pallas_call x1, Pallas kernels, mask(): pl.pallas_call(kernel, out_shape=[jax.ShapeDtypeStruct(shape, BF16) for s...  11.5 us
  transfers between devices with their start and end apart: 27, of which 6 were waited for; matrix products, arithmetic and copies ran while one was open for 3% of the time, Pallas kernels for 25%

profile of v13, /device:TPU:24, one launch (start us, length us, event | category | flops | bytes accessed | tf_op | source)
XLA Modules:
  0.0 154.9 jit_solution(13117524829249861780)
XLA Ops:
  6.5 2.7 %pad_maximum_fusion = bf16[1536,512]{1,0:T(8,128)(2,1)} fusion(bf16[768,512]{1,0:T(8,128)(2,1)} %param.9, bf16[768,512]{1,0:T(8,128)(2,1)} %param.8), kind=kLoop, calls=%fused_computation | loop fusion | flops 3145728 | bytes 3145728 | tf_op jit(solution)/shard_map/concatenate | solution.py:228
  9.2 2.0 %collective-permute-start = (bf16[1024,128]{1,0:T(8,128)(2,1)S(1)}, bf16[1024,128]{1,0:T(8,128)(2,1)S(1)}, u32[]{:S(2)}, u32[]{:S(2)}) collective-permute-start(bf16[1024,128]{1,0:T(8,128)(2,1)S(1)} %copy-done.3), channel_id=1, source_target_pairs={{0,1},{1,2},{2,3},{3,4},{4,5},{5,6},{6,7},{7,0},{8,9},{9,10},{10,1... | collective-permute-start | bytes 786440 | tf_op jit(solution)/shard_map/ppermute | solution.py:22
  11.2 4.0 %collective-permute-start.1 = (bf16[1024,128]{1,0:T(8,128)(2,1)S(1)}, bf16[1024,128]{1,0:T(8,128)(2,1)S(1)}, u32[]{:S(2)}, u32[]{:S(2)}) collective-permute-start(bf16[1024,128]{1,0:T(8,128)(2,1)S(1)} %copy-done.3), channel_id=1, source_target_pairs={{0,7},{1,0},{2,1},{3,2},{4,3},{5,4},{6,5},{7,6},{8,15},{9,8},{10,9... | collective-permute-start | bytes 786440 | tf_op jit(solution)/shard_map/ppermute | solution.py:22
  15.5 1.8 %collective-permute-start.5 = (bf16[1024,128]{1,0:T(8,128)(2,1)S(1)}, bf16[1024,128]{1,0:T(8,128)(2,1)S(1)}, u32[]{:S(2)}, u32[]{:S(2)}) collective-permute-start(bf16[1024,128]{1,0:T(8,128)(2,1)S(1)} %copy-done.4), channel_id=1, source_target_pairs={{0,24},{1,25},{2,26},{3,27},{4,28},{5,29},{6,30},{7,31},{8,0},{9,1... | collective-permute-start | bytes 786440 | tf_op jit(solution)/shard_map/ppermute | solution.py:22
  17.3 4.2 %collective-permute-done.refs_1_ = bf16[1024,128]{1,0:T(8,128)(2,1)S(1)} collective-permute-done((bf16[1024,128]{1,0:T(8,128)(2,1)S(1)}, bf16[1024,128]{1,0:T(8,128)(2,1)S(1)}, u32[]{:S(2)}, u32[]{:S(2)}) %collective-permute-start) | collective-permute-done | bytes 262176 | tf_op jit(solution)/shard_map/ppermute | solution.py:22
  21.5 1.5 %collective-permute-done.2.refs_1_ = bf16[1024,128]{1,0:T(8,128)(2,1)S(1)} collective-permute-done((bf16[1024,128]{1,0:T(8,128)(2,1)S(1)}, bf16[1024,128]{1,0:T(8,128)(2,1)S(1)}, u32[]{:S(2)}, u32[]{:S(2)}) %collective-permute-start.2) | collective-permute-done | bytes 262176 | tf_op jit(solution)/shard_map/ppermute | solution.py:22
  23.0 3.2 %collective-permute-start.4 = (bf16[1024,128]{1,0:T(8,128)(2,1)S(1)}, bf16[1024,128]{1,0:T(8,128)(2,1)S(1)}, u32[]{:S(2)}, u32[]{:S(2)}) collective-permute-start(bf16[1024,128]{1,0:T(8,128)(2,1)S(1)} %collective-permute-done.1.refs_2_), channel_id=1, source_target_pairs={{0,7},{1,0},{2,1},{3,2},{4,3},{5,4},{6,5},{7,6},{8,15},{9,8},{10,9... | collective-permute-start | bytes 786440 | tf_op jit(solution)/shard_map/ppermute | solution.py:22
  26.3 1.5 collective-permute-start.6
  27.8 3.3 %collective-permute-done.3.refs_3_ = bf16[1024,128]{1,0:T(8,128)(2,1)S(1)} collective-permute-done((bf16[1024,128]{1,0:T(8,128)(2,1)S(1)}, bf16[1024,128]{1,0:T(8,128)(2,1)S(1)}, u32[]{:S(2)}, u32[]{:S(2)}) %collective-permute-start.3) | collective-permute-done | bytes 262176 | tf_op jit(solution)/shard_map/ppermute | solution.py:22
  31.1 0.9 collective-permute-start.11
  32.0 2.3 %collective-permute-start.12 = (bf16[1024,128]{1,0:T(8,128)(2,1)S(1)}, bf16[1024,128]{1,0:T(8,128)(2,1)S(1)}, u32[]{:S(2)}, u32[]{:S(2)}) collective-permute-start(bf16[1024,128]{1,0:T(8,128)(2,1)S(1)} %collective-permute-done.4.refs_4_), channel_id=1, source_target_pairs={{0,7},{1,0},{2,1},{3,2},{4,3},{5,4},{6,5},{7,6},{8,15},{9,8},{10,9... | collective-permute-start | bytes 786440 | tf_op jit(solution)/shard_map/ppermute | solution.py:22
  34.6 0.8 collective-permute-start.8
  35.4 2.5 %collective-permute-start.7 = (bf16[1024,640]{1,0:T(8,128)(2,1)S(1)}, bf16[1024,640]{1,0:T(8,128)(2,1)S(1)}, u32[]{:S(2)}, u32[]{:S(2)}) collective-permute-start(bf16[1024,640]{1,0:T(8,128)(2,1)S(1)} %shard_map.82.refs_3_), channel_id=1, source_target_pairs={{0,8},{1,9},{2,10},{3,11},{4,12},{5,13},{6,14},{7,15},{8,16},{9,17... | collective-permute-start | bytes 3932168 | tf_op jit(solution)/shard_map/ppermute | solution.py:22
  38.7 2.2 %collective-permute-start.13 = (bf16[1024,512]{1,0:T(8,128)(2,1)S(1)}, bf16[1024,512]{1,0:T(8,128)(2,1)}, u32[]{:S(2)}, u32[]{:S(2)}) collective-permute-start(bf16[1024,512]{1,0:T(8,128)(2,1)S(1)} %shard_map.84.refs_7_), channel_id=1, source_target_pairs={{0,1},{1,2},{2,3},{3,4},{4,5},{5,6},{6,7},{7,0},{8,9},{9,10},{10,1... | collective-permute-start | bytes 3145736 | tf_op jit(solution)/shard_map/ppermute | solution.py:22
  40.9 1.1 collective-permute-start.14
  41.9 1.0 collective-permute-start.15
  42.9 24.7 %collective-permute-done.15.refs_2_ = bf16[1024,128]{1,0:T(8,128)(2,1)S(1)} collective-permute-done((bf16[1024,128]{1,0:T(8,128)(2,1)S(1)}, bf16[1024,128]{1,0:T(8,128)(2,1)S(1)}, u32[]{:S(2)}, u32[]{:S(2)}) %collective-permute-start.15) | collective-permute-done | bytes 262176 | tf_op jit(solution)/shard_map/ppermute | solution.py:22
  67.6 2.9 %collective-permute-start.17 = (bf16[1024,512]{1,0:T(8,128)(2,1)}, bf16[1024,512]{1,0:T(8,128)(2,1)}, u32[]{:S(2)}, u32[]{:S(2)}) collective-permute-start(bf16[1024,512]{1,0:T(8,128)(2,1)} %collective-permute-done.14.refs_9_), channel_id=1, source_target_pairs={{0,7},{1,0},{2,1},{3,2},{4,3},{5,4},{6,5},{7,6},{8,15},{9,8},{10,9... | collective-permute-start | bytes 3145736 | tf_op jit(solution)/shard_map/ppermute | solution.py:22
  71.4 2.6 %collective-permute-start.9 = (bf16[512,640]{1,0:T(8,128)(2,1)S(1)}, bf16[512,640]{1,0:T(8,128)(2,1)S(1)}, u32[]{:S(2)}, u32[]{:S(2)}) collective-permute-start(bf16[512,640]{1,0:T(8,128)(2,1)S(1)} %slice.24), channel_id=1, source_target_pairs={{0,8},{1,9},{2,10},{3,11},{4,12},{5,13},{6,14},{7,15},{8,16},{9,17... | collective-permute-start | bytes 1966088 | tf_op jit(solution)/shard_map/ppermute | solution.py:22
  74.2 11.2 %collective-permute-done.10.refs_4_ = bf16[512,640]{1,0:T(8,128)(2,1)S(1)} collective-permute-done((bf16[512,640]{1,0:T(8,128)(2,1)S(1)}, bf16[512,640]{1,0:T(8,128)(2,1)S(1)}, u32[]{:S(2)}, u32[]{:S(2)}) %collective-permute-start.10) | collective-permute-done | bytes 655392 | tf_op jit(solution)/shard_map/ppermute | solution.py:22
  86.1 2.5 %collective-permute-start.20 = (bf16[1024,384]{1,0:T(8,128)(2,1)S(1)}, bf16[1024,384]{1,0:T(8,128)(2,1)}, u32[]{:S(2)}, u32[]{:S(2)}) collective-permute-start(bf16[1024,384]{1,0:T(8,128)(2,1)S(1)} %shard_map.85.refs_6_), channel_id=1, source_target_pairs={{0,8},{1,9},{2,10},{3,11},{4,12},{5,13},{6,14},{7,15},{8,16},{9,17... | collective-permute-start | bytes 2359304 | tf_op jit(solution)/shard_map/ppermute | solution.py:22
  89.3 11.5 %shard_map.83 = (bf16[768,3840]{1,0:T(8,128)(2,1)}, bf16[768,3840]{1,0:T(8,128)(2,1)}, bf16[768,512]{1,0:T(8,128)(2,1)}) custom-call(s32[2]{0:T(128)} %pad_add_fusion.refs_0_, s32[6]{0:T(128)} %refs_0_.9, s32[32]{0:T(128)} %refs_2_.1, s32[6,32]{1,0:T(8,128)} %refs_3_.1, bf16[1536,4096]{1,0:T(8,128)(2,1)} %all-gather.2.cloned.1.call-done.refs_4_), custom_call_target="tpu_custom_call" | custom-call | bytes 26214400 | tf_op jit(solution)/shard_map/pallas_call | solution.py:104
  100.9 3.3 %collective-permute-start.19 = (bf16[1024,512]{1,0:T(8,128)(2,1)}, bf16[1024,512]{1,0:T(8,128)(2,1)S(1)}, u32[]{:S(2)}, u32[]{:S(2)}) collective-permute-start(bf16[1024,512]{1,0:T(8,128)(2,1)} %collective-permute-done.17.refs_10_), channel_id=1, source_target_pairs={{0,7},{1,0},{2,1},{3,2},{4,3},{5,4},{6,5},{7,6},{8,15},{9,8},{10,9... | collective-permute-start | bytes 3145736 | tf_op jit(solution)/shard_map/ppermute | solution.py:22
  104.2 1.0 slice.28
  105.3 1.0 slice.27
  106.4 3.5 %collective-permute-start.22 = (bf16[512,384]{1,0:T(8,128)(2,1)S(1)}, bf16[512,384]{1,0:T(8,128)(2,1)S(1)}, u32[]{:S(2)}, u32[]{:S(2)}) collective-permute-start(bf16[512,384]{1,0:T(8,128)(2,1)S(1)} %slice.27), channel_id=1, source_target_pairs={{0,8},{1,9},{2,10},{3,11},{4,12},{5,13},{6,14},{7,15},{8,16},{9,17... | collective-permute-start | bytes 1179656 | tf_op jit(solution)/shard_map/ppermute | solution.py:22
  109.9 13.3 %shard_map.86.refs_13_ = f32[768,1024]{1,0:T(8,128)} custom-call(s32[6]{0:T(128)} %refs_0_.9, s32[8]{0:T(128)} %refs_1_.7, bf16[768,3840]{1,0:T(8,128)(2,1)} %get-tuple-element.40.refs_2_, bf16[1024,640]{1,0:T(8,128)(2,1)} %copy-done, bf16[1024,640]{1,0:T(8,128)(2,1)} %copy-done.8, bf16[1024,640]{1,0:T(8,128)(2,1)} %copy-done.7, ...), custom_call_target="tpu_custom_call" | custom-call | flops 6039797760 | bytes 22151168 | tf_op jit(solution)/shard_map/pallas_call | solution.py:204
  123.3 0.9 copy-done.9
  124.2 3.2 %collective-permute-start.25 = (bf16[512,512]{1,0:T(8,128)(2,1)S(1)}, bf16[512,512]{1,0:T(8,128)(2,1)S(1)}, u32[]{:S(2)}, u32[]{:S(2)}) collective-permute-start(bf16[512,512]{1,0:T(8,128)(2,1)S(1)} %slice.29), channel_id=1, source_target_pairs={{0,7},{1,0},{2,1},{3,2},{4,3},{5,4},{6,5},{7,6},{8,15},{9,8},{10,9... | collective-permute-start | bytes 1572872 | tf_op jit(solution)/shard_map/ppermute | solution.py:22
  127.4 1.1 slice.26
  128.6 13.6 %shard_map.87.refs_5_ = f32[768,1024]{1,0:T(8,128)} custom-call(s32[6]{0:T(128)} %refs_0_.9, s32[8]{0:T(128)} %refs_1_.7, bf16[768,3840]{1,0:T(8,128)(2,1)} %get-tuple-element.48.refs_2_, bf16[512,640]{1,0:T(8,128)(2,1)} %copy-done.11, bf16[512,640]{1,0:T(8,128)(2,1)} %copy-done.10, bf16[1024,384]{1,0:T(8,128)(2,1)} %collective-permute-done.20.refs_5_, ...), custom_call_target="tpu_custom_call" | custom-call | flops 6039797760 | bytes 22151168 | tf_op jit(solution)/shard_map/pallas_call | solution.py:204
  143.2 4.8 %shard_map.88 = bf16[768,1024]{1,0:T(8,128)(2,1)} custom-call(s32[6]{0:T(128)} %refs_0_.9, s32[8]{0:T(128)} %refs_1_.7, bf16[768,512]{1,0:T(8,128)(2,1)} %get-tuple-element.34.refs_2_, bf16[512,512]{1,0:T(8,128)(2,1)} %copy-done.6, bf16[512,512]{1,0:T(8,128)(2,1)} %copy-done.5, f32[768,1024]{1,0:T(8,128)} %shard_map.87.refs_5_), custom_call_target="tpu_custom_call" | custom-call | flops 805306368 | bytes 10223616 | tf_op jit(solution)/shard_map/pallas_call | solution.py:204
  (66 shorter events, 5.0 us)
Async XLA Ops:
  6.5 8.7 %copy-start.4 = (bf16[1024,128]{1,0:T(8,128)(2,1)S(1)}, bf16[1024,128]{1,0:T(8,128)(2,1)}, u32[]{:S(2)}) copy-start(bf16[1024,128]{1,0:T(8,128)(2,1)} %refs_0_.6) | copy-start | bytes 786436
  6.5 82.8 %all-gather.2.cloned.1.call-start = ((), (), s32[]{:S(2)}) async-start(), calls=%async_computation | async-start | bytes 14155776 | tf_op jit(solution)/shard_map/all_gather | solution.py:228
  9.2 12.2 %collective-permute-start = (bf16[1024,128]{1,0:T(8,128)(2,1)S(1)}, bf16[1024,128]{1,0:T(8,128)(2,1)S(1)}, u32[]{:S(2)}, u32[]{:S(2)}) collective-permute-start(bf16[1024,128]{1,0:T(8,128)(2,1)S(1)} %copy-done.3), channel_id=1, source_target_pairs={{0,1},{1,2},{2,3},{3,4},{4,5},{5,6},{6,7},{7,0},{8,9},{9,10},{10,1... | collective-permute-start | bytes 786440 | tf_op jit(solution)/shard_map/ppermute | solution.py:22
  11.2 10.2 %collective-permute-start.1 = (bf16[1024,128]{1,0:T(8,128)(2,1)S(1)}, bf16[1024,128]{1,0:T(8,128)(2,1)S(1)}, u32[]{:S(2)}, u32[]{:S(2)}) collective-permute-start(bf16[1024,128]{1,0:T(8,128)(2,1)S(1)} %copy-done.3), channel_id=1, source_target_pairs={{0,7},{1,0},{2,1},{3,2},{4,3},{5,4},{6,5},{7,6},{8,15},{9,8},{10,9... | collective-permute-start | bytes 786440 | tf_op jit(solution)/shard_map/ppermute | solution.py:22
  15.3 7.8 %collective-permute-start.2 = (bf16[1024,128]{1,0:T(8,128)(2,1)S(1)}, bf16[1024,128]{1,0:T(8,128)(2,1)S(1)}, u32[]{:S(2)}, u32[]{:S(2)}) collective-permute-start(bf16[1024,128]{1,0:T(8,128)(2,1)S(1)} %copy-done.4), channel_id=1, source_target_pairs={{0,8},{1,9},{2,10},{3,11},{4,12},{5,13},{6,14},{7,15},{8,16},{9,17... | collective-permute-start | bytes 786440 | tf_op jit(solution)/shard_map/ppermute | solution.py:22
  15.5 10.8 %collective-permute-start.5 = (bf16[1024,128]{1,0:T(8,128)(2,1)S(1)}, bf16[1024,128]{1,0:T(8,128)(2,1)S(1)}, u32[]{:S(2)}, u32[]{:S(2)}) collective-permute-start(bf16[1024,128]{1,0:T(8,128)(2,1)S(1)} %copy-done.4), channel_id=1, source_target_pairs={{0,24},{1,25},{2,26},{3,27},{4,28},{5,29},{6,30},{7,31},{8,0},{9,1... | collective-permute-start | bytes 786440 | tf_op jit(solution)/shard_map/ppermute | solution.py:22
  23.0 8.1 %collective-permute-start.3 = (bf16[1024,128]{1,0:T(8,128)(2,1)S(1)}, bf16[1024,128]{1,0:T(8,128)(2,1)S(1)}, u32[]{:S(2)}, u32[]{:S(2)}) collective-permute-start(bf16[1024,128]{1,0:T(8,128)(2,1)S(1)} %collective-permute-done.refs_1_), channel_id=1, source_target_pairs={{0,1},{1,2},{2,3},{3,4},{4,5},{5,6},{6,7},{7,0},{8,9},{9,10},{10,1... | collective-permute-start | bytes 786440 | tf_op jit(solution)/shard_map/ppermute | solution.py:22
  23.0 8.1 %collective-permute-start.4 = (bf16[1024,128]{1,0:T(8,128)(2,1)S(1)}, bf16[1024,128]{1,0:T(8,128)(2,1)S(1)}, u32[]{:S(2)}, u32[]{:S(2)}) collective-permute-start(bf16[1024,128]{1,0:T(8,128)(2,1)S(1)} %collective-permute-done.1.refs_2_), channel_id=1, source_target_pairs={{0,7},{1,0},{2,1},{3,2},{4,3},{5,4},{6,5},{7,6},{8,15},{9,8},{10,9... | collective-permute-start | bytes 786440 | tf_op jit(solution)/shard_map/ppermute | solution.py:22
  26.3 8.3 %collective-permute-start.6 = (bf16[1024,128]{1,0:T(8,128)(2,1)S(1)}, bf16[1024,128]{1,0:T(8,128)(2,1)S(1)}, u32[]{:S(2)}, u32[]{:S(2)}) collective-permute-start(bf16[1024,128]{1,0:T(8,128)(2,1)S(1)} %collective-permute-done.2.refs_1_), channel_id=1, source_target_pairs={{0,8},{1,9},{2,10},{3,11},{4,12},{5,13},{6,14},{7,15},{8,16},{9,17... | collective-permute-start | bytes 786440 | tf_op jit(solution)/shard_map/ppermute | solution.py:22
  31.1 7.6 %collective-permute-start.11 = (bf16[1024,128]{1,0:T(8,128)(2,1)S(1)}, bf16[1024,128]{1,0:T(8,128)(2,1)S(1)}, u32[]{:S(2)}, u32[]{:S(2)}) collective-permute-start(bf16[1024,128]{1,0:T(8,128)(2,1)S(1)} %collective-permute-done.3.refs_3_), channel_id=1, source_target_pairs={{0,1},{1,2},{2,3},{3,4},{4,5},{5,6},{6,7},{7,0},{8,9},{9,10},{10,1... | collective-permute-start | bytes 786440 | tf_op jit(solution)/shard_map/ppermute | solution.py:22
  32.0 6.7 %collective-permute-start.12 = (bf16[1024,128]{1,0:T(8,128)(2,1)S(1)}, bf16[1024,128]{1,0:T(8,128)(2,1)S(1)}, u32[]{:S(2)}, u32[]{:S(2)}) collective-permute-start(bf16[1024,128]{1,0:T(8,128)(2,1)S(1)} %collective-permute-done.4.refs_4_), channel_id=1, source_target_pairs={{0,7},{1,0},{2,1},{3,2},{4,3},{5,4},{6,5},{7,6},{8,15},{9,8},{10,9... | collective-permute-start | bytes 786440 | tf_op jit(solution)/shard_map/ppermute | solution.py:22
  34.6 39.6 %copy-start = (bf16[1024,640]{1,0:T(8,128)(2,1)}, bf16[1024,640]{1,0:T(8,128)(2,1)S(1)}, u32[]{:S(2)}) copy-start(bf16[1024,640]{1,0:T(8,128)(2,1)S(1)} %shard_map.82.refs_3_) | copy-start | bytes 3932164
  34.6 33.0 %collective-permute-start.8 = (bf16[1024,640]{1,0:T(8,128)(2,1)S(1)}, bf16[1024,640]{1,0:T(8,128)(2,1)S(1)}, u32[]{:S(2)}, u32[]{:S(2)}) collective-permute-start(bf16[1024,640]{1,0:T(8,128)(2,1)S(1)} %shard_map.82.refs_3_), channel_id=1, source_target_pairs={{0,24},{1,25},{2,26},{3,27},{4,28},{5,29},{6,30},{7,31},{8,0},{9,1... | collective-permute-start | bytes 3932168 | tf_op jit(solution)/shard_map/ppermute | solution.py:22
  35.4 32.2 %collective-permute-start.7 = (bf16[1024,640]{1,0:T(8,128)(2,1)S(1)}, bf16[1024,640]{1,0:T(8,128)(2,1)S(1)}, u32[]{:S(2)}, u32[]{:S(2)}) collective-permute-start(bf16[1024,640]{1,0:T(8,128)(2,1)S(1)} %shard_map.82.refs_3_), channel_id=1, source_target_pairs={{0,8},{1,9},{2,10},{3,11},{4,12},{5,13},{6,14},{7,15},{8,16},{9,17... | collective-permute-start | bytes 3932168 | tf_op jit(solution)/shard_map/ppermute | solution.py:22
  38.1 62.8 %copy-start.1 = (bf16[1024,512]{1,0:T(8,128)(2,1)}, bf16[1024,512]{1,0:T(8,128)(2,1)S(1)}, u32[]{:S(2)}) copy-start(bf16[1024,512]{1,0:T(8,128)(2,1)S(1)} %shard_map.84.refs_7_) | copy-start | bytes 3145732
  38.7 28.9 %collective-permute-start.13 = (bf16[1024,512]{1,0:T(8,128)(2,1)S(1)}, bf16[1024,512]{1,0:T(8,128)(2,1)}, u32[]{:S(2)}, u32[]{:S(2)}) collective-permute-start(bf16[1024,512]{1,0:T(8,128)(2,1)S(1)} %shard_map.84.refs_7_), channel_id=1, source_target_pairs={{0,1},{1,2},{2,3},{3,4},{4,5},{5,6},{6,7},{7,0},{8,9},{9,10},{10,1... | collective-permute-start | bytes 3145736 | tf_op jit(solution)/shard_map/ppermute | solution.py:22
  40.9 26.7 %collective-permute-start.14 = (bf16[1024,512]{1,0:T(8,128)(2,1)S(1)}, bf16[1024,512]{1,0:T(8,128)(2,1)}, u32[]{:S(2)}, u32[]{:S(2)}) collective-permute-start(bf16[1024,512]{1,0:T(8,128)(2,1)S(1)} %shard_map.84.refs_7_), channel_id=1, source_target_pairs={{0,7},{1,0},{2,1},{3,2},{4,3},{5,4},{6,5},{7,6},{8,15},{9,8},{10,9... | collective-permute-start | bytes 3145736 | tf_op jit(solution)/shard_map/ppermute | solution.py:22
  41.9 25.6 %collective-permute-start.15 = (bf16[1024,128]{1,0:T(8,128)(2,1)S(1)}, bf16[1024,128]{1,0:T(8,128)(2,1)S(1)}, u32[]{:S(2)}, u32[]{:S(2)}) collective-permute-start(bf16[1024,128]{1,0:T(8,128)(2,1)S(1)} %collective-permute-done.11.refs_0_), channel_id=1, source_target_pairs={{0,1},{1,2},{2,3},{3,4},{4,5},{5,6},{6,7},{7,0},{8,9},{9,10},{10,1... | collective-permute-start | bytes 786440 | tf_op jit(solution)/shard_map/ppermute | solution.py:22
  67.6 17.7 %copy-start.8 = (bf16[1024,640]{1,0:T(8,128)(2,1)}, bf16[1024,640]{1,0:T(8,128)(2,1)S(1)}, u32[]{:S(2)}) copy-start(bf16[1024,640]{1,0:T(8,128)(2,1)S(1)} %collective-permute-done.7.refs_4_) | copy-start | bytes 3932164
  67.6 33.3 %collective-permute-start.17 = (bf16[1024,512]{1,0:T(8,128)(2,1)}, bf16[1024,512]{1,0:T(8,128)(2,1)}, u32[]{:S(2)}, u32[]{:S(2)}) collective-permute-start(bf16[1024,512]{1,0:T(8,128)(2,1)} %collective-permute-done.14.refs_9_), channel_id=1, source_target_pairs={{0,7},{1,0},{2,1},{3,2},{4,3},{5,4},{6,5},{7,6},{8,15},{9,8},{10,9... | collective-permute-start | bytes 3145736 | tf_op jit(solution)/shard_map/ppermute | solution.py:22
  70.5 30.4 %collective-permute-start.16 = (bf16[1024,512]{1,0:T(8,128)(2,1)}, bf16[1024,512]{1,0:T(8,128)(2,1)}, u32[]{:S(2)}, u32[]{:S(2)}) collective-permute-start(bf16[1024,512]{1,0:T(8,128)(2,1)} %collective-permute-done.13.refs_8_), channel_id=1, source_target_pairs={{0,1},{1,2},{2,3},{3,4},{4,5},{5,6},{6,7},{7,0},{8,9},{9,10},{10,1... | collective-permute-start | bytes 3145736 | tf_op jit(solution)/shard_map/ppermute | solution.py:22
  70.5 14.8 %collective-permute-start.10 = (bf16[512,640]{1,0:T(8,128)(2,1)S(1)}, bf16[512,640]{1,0:T(8,128)(2,1)S(1)}, u32[]{:S(2)}, u32[]{:S(2)}) collective-permute-start(bf16[512,640]{1,0:T(8,128)(2,1)S(1)} %slice.25), channel_id=1, source_target_pairs={{0,24},{1,25},{2,26},{3,27},{4,28},{5,29},{6,30},{7,31},{8,0},{9,1... | collective-permute-start | bytes 1966088 | tf_op jit(solution)/shard_map/ppermute | solution.py:22
  71.4 13.9 %collective-permute-start.9 = (bf16[512,640]{1,0:T(8,128)(2,1)S(1)}, bf16[512,640]{1,0:T(8,128)(2,1)S(1)}, u32[]{:S(2)}, u32[]{:S(2)}) collective-permute-start(bf16[512,640]{1,0:T(8,128)(2,1)S(1)} %slice.24), channel_id=1, source_target_pairs={{0,8},{1,9},{2,10},{3,11},{4,12},{5,13},{6,14},{7,15},{8,16},{9,17... | collective-permute-start | bytes 1966088 | tf_op jit(solution)/shard_map/ppermute | solution.py:22
  74.1 26.7 %copy-start.2 = (bf16[1024,384]{1,0:T(8,128)(2,1)}, bf16[1024,384]{1,0:T(8,128)(2,1)S(1)}, u32[]{:S(2)}) copy-start(bf16[1024,384]{1,0:T(8,128)(2,1)S(1)} %shard_map.85.refs_6_) | copy-start | bytes 2359300
  85.3 18.9 %collective-permute-start.21 = (bf16[1024,384]{1,0:T(8,128)(2,1)S(1)}, bf16[1024,384]{1,0:T(8,128)(2,1)}, u32[]{:S(2)}, u32[]{:S(2)}) collective-permute-start(bf16[1024,384]{1,0:T(8,128)(2,1)S(1)} %shard_map.85.refs_6_), channel_id=1, source_target_pairs={{0,24},{1,25},{2,26},{3,27},{4,28},{5,29},{6,30},{7,31},{8,0},{9,1... | collective-permute-start | bytes 2359304 | tf_op jit(solution)/shard_map/ppermute | solution.py:22
  86.1 19.1 %collective-permute-start.20 = (bf16[1024,384]{1,0:T(8,128)(2,1)S(1)}, bf16[1024,384]{1,0:T(8,128)(2,1)}, u32[]{:S(2)}, u32[]{:S(2)}) collective-permute-start(bf16[1024,384]{1,0:T(8,128)(2,1)S(1)} %shard_map.85.refs_6_), channel_id=1, source_target_pairs={{0,8},{1,9},{2,10},{3,11},{4,12},{5,13},{6,14},{7,15},{8,16},{9,17... | collective-permute-start | bytes 2359304 | tf_op jit(solution)/shard_map/ppermute | solution.py:22
  100.9 22.3 %collective-permute-start.19 = (bf16[1024,512]{1,0:T(8,128)(2,1)}, bf16[1024,512]{1,0:T(8,128)(2,1)S(1)}, u32[]{:S(2)}, u32[]{:S(2)}) collective-permute-start(bf16[1024,512]{1,0:T(8,128)(2,1)} %collective-permute-done.17.refs_10_), channel_id=1, source_target_pairs={{0,7},{1,0},{2,1},{3,2},{4,3},{5,4},{6,5},{7,6},{8,15},{9,8},{10,9... | collective-permute-start | bytes 3145736 | tf_op jit(solution)/shard_map/ppermute | solution.py:22
  104.2 20.0 %collective-permute-start.18 = (bf16[1024,512]{1,0:T(8,128)(2,1)}, bf16[1024,512]{1,0:T(8,128)(2,1)}, u32[]{:S(2)}, u32[]{:S(2)}) collective-permute-start(bf16[1024,512]{1,0:T(8,128)(2,1)} %collective-permute-done.16.refs_9_), channel_id=1, source_target_pairs={{0,1},{1,2},{2,3},{3,4},{4,5},{5,6},{6,7},{7,0},{8,9},{9,10},{10,1... | collective-permute-start | bytes 3145736 | tf_op jit(solution)/shard_map/ppermute | solution.py:22
  105.3 18.0 %collective-permute-start.23 = (bf16[512,384]{1,0:T(8,128)(2,1)S(1)}, bf16[512,384]{1,0:T(8,128)(2,1)S(1)}, u32[]{:S(2)}, u32[]{:S(2)}) collective-permute-start(bf16[512,384]{1,0:T(8,128)(2,1)S(1)} %slice.28), channel_id=1, source_target_pairs={{0,24},{1,25},{2,26},{3,27},{4,28},{5,29},{6,30},{7,31},{8,0},{9,1... | collective-permute-start | bytes 1179656 | tf_op jit(solution)/shard_map/ppermute | solution.py:22
  106.4 16.9 %collective-permute-start.22 = (bf16[512,384]{1,0:T(8,128)(2,1)S(1)}, bf16[512,384]{1,0:T(8,128)(2,1)S(1)}, u32[]{:S(2)}, u32[]{:S(2)}) collective-permute-start(bf16[512,384]{1,0:T(8,128)(2,1)S(1)} %slice.27), channel_id=1, source_target_pairs={{0,8},{1,9},{2,10},{3,11},{4,12},{5,13},{6,14},{7,15},{8,16},{9,17... | collective-permute-start | bytes 1179656 | tf_op jit(solution)/shard_map/ppermute | solution.py:22
  124.2 18.1 %collective-permute-start.25 = (bf16[512,512]{1,0:T(8,128)(2,1)S(1)}, bf16[512,512]{1,0:T(8,128)(2,1)S(1)}, u32[]{:S(2)}, u32[]{:S(2)}) collective-permute-start(bf16[512,512]{1,0:T(8,128)(2,1)S(1)} %slice.29), channel_id=1, source_target_pairs={{0,7},{1,0},{2,1},{3,2},{4,3},{5,4},{6,5},{7,6},{8,15},{9,8},{10,9... | collective-permute-start | bytes 1572872 | tf_op jit(solution)/shard_map/ppermute | solution.py:22
  128.5 13.8 %collective-permute-start.24 = (bf16[512,512]{1,0:T(8,128)(2,1)S(1)}, bf16[512,512]{1,0:T(8,128)(2,1)S(1)}, u32[]{:S(2)}, u32[]{:S(2)}) collective-permute-start(bf16[512,512]{1,0:T(8,128)(2,1)S(1)} %slice.26), channel_id=1, source_target_pairs={{0,1},{1,2},{2,3},{3,4},{4,5},{5,6},{6,7},{7,0},{8,9},{9,10},{10,1... | collective-permute-start | bytes 1572872 | tf_op jit(solution)/shard_map/ppermute | solution.py:22
  (9 other events, 22.3 us)
Sparse Core Ops, SparseCore 0:
  9.4 72.5 all-gather.1

commit v14 on v6

--- a/solution.py
+++ b/solution.py
@@ -240,8 +240,8 @@
     near, far = (0, -1, 1, -2, 2), (-3, 3, 4)
     groups = [
         [plus(near, y) for y in (0, -1, 1)],
-        [plus(near, 2)] + [plus(far, y) for y in (0, -1, 1)] + [minus(z) for z in (0, -1, 1, -2, 2)],
-        [plus(far, 2)] + [minus(z) for z in (-3, 3)],
+        [plus(near, 2)] + [plus(far, y) for y in (0, -1, 1)] + [minus(z) for z in (0, -1, 1)],
+        [plus(far, 2)] + [minus(z) for z in (-2, 2, -3, 3)],
         [minus(4)],
     ]
     amps = mask(here, sym_ij, sym_cd, amp_mask, raw, groups)
@@ -250,10 +250,10 @@
     blocks = [(c0,), c1[:1], c1[1:]]
     total = product(sym_ij, sym_ab, amps[0], [(None, block) for block in blocks])
     d2 = (go(d1[0][:HALF], *d1, total, dy=1), go(d1[1][HALF:], *d1, total, dy=-1))
-    blocks = [c2, (d0,), d1[:1], d1[1:], (w0,), (wu[0],), (wd[0],), (wu[1],), (wd[1],)]
+    blocks = [c2, (d0,), d1[:1], d1[1:], (w0,), (wu[0],), (wd[0],)]
     total = product(sym_ij, sym_ab, amps[1], [(None, block) for block in blocks], total)
     w4 = (go(wu[2][:HALF], wd[2], *d2, total, dz=1), go(wd[2][HALF:], wu[2], *d2, total, dz=-1))
-    blocks = [d2, (wu[2],), (wd[2],)]
+    blocks = [d2, (wu[1],), (wd[1],), (wu[2],), (wd[2],)]
     total = product(sym_ij, sym_ab, amps[2], [(None, block) for block in blocks], total)
     return product(sym_ij, sym_ab, amps[3], [(None, w4)], total, True)
 

time: 157 us -> 153 us (0.975)
  waiting for transfers between devices: 50.9 us -> 47.1 us
    ppermute x26, waiting for transfers between devices: 50.9 us -> 47.1 us  [move(): return lax.ppermute(values, 'mem', perm_of(dy, dz))]
  transfers between devices with their start and end apart: 27 -> 27, of which waited for: 14 -> 13; matrix products, arithmetic and copies ran while one was open for 2% -> 2% of each run, Pallas kernels for 27% -> 28%
where the time goes in v14:
time: 153 us
  Pallas kernels  47.6 us (31%)
  waiting for transfers between devices  47.1 us (31%)
  starting transfers between devices  38 us (25%)
  between operations  13.7 us (9%)
  other arithmetic  3.33 us (2%)
  local copies, waits for them, and re-layouts  3.14 us (2%)
    ppermute x26, waiting for transfers between devices, move(): return lax.ppermute(values, 'mem', perm_of(dy, dz))  47.1 us
    ppermute x26, starting transfers between devices, move(): return lax.ppermute(values, 'mem', perm_of(dy, dz))  38 us
    pallas_call x4, Pallas kernels, product(): pl.pallas_call(kernel, out_shape=jax.ShapeDtypeStruct((768, 1024), BF16 i...  35.8 us
    pallas_call x1, Pallas kernels, mask(): pl.pallas_call(kernel, out_shape=[jax.ShapeDtypeStruct(shape, BF16) for s...  11.3 us
  transfers between devices with their start and end apart: 27, of which 13 were waited for; matrix products, arithmetic and copies ran while one was open for 2% of the time, Pallas kernels for 28%

profile of v14, /device:TPU:24, one launch (start us, length us, event | category | flops | bytes accessed | tf_op | source)
XLA Modules:
  0.0 152.9 jit_solution(12573163204180239815)
XLA Ops:
  6.5 2.7 %pad_maximum_fusion = bf16[1536,512]{1,0:T(8,128)(2,1)} fusion(bf16[768,512]{1,0:T(8,128)(2,1)} %param.9, bf16[768,512]{1,0:T(8,128)(2,1)} %param.8), kind=kLoop, calls=%fused_computation | loop fusion | flops 3145728 | bytes 3145728 | tf_op jit(solution)/shard_map/concatenate | solution.py:211
  9.2 2.0 %collective-permute-start = (bf16[1024,128]{1,0:T(8,128)(2,1)S(1)}, bf16[1024,128]{1,0:T(8,128)(2,1)S(1)}, u32[]{:S(2)}, u32[]{:S(2)}) collective-permute-start(bf16[1024,128]{1,0:T(8,128)(2,1)S(1)} %copy-done.4), channel_id=1, source_target_pairs={{0,8},{1,9},{2,10},{3,11},{4,12},{5,13},{6,14},{7,15},{8,16},{9,17... | collective-permute-start | bytes 786440 | tf_op jit(solution)/shard_map/ppermute | solution.py:22
  11.5 3.9 %collective-permute-start.3 = (bf16[1024,128]{1,0:T(8,128)(2,1)S(1)}, bf16[1024,128]{1,0:T(8,128)(2,1)S(1)}, u32[]{:S(2)}, u32[]{:S(2)}) collective-permute-start(bf16[1024,128]{1,0:T(8,128)(2,1)S(1)} %copy-done.3), channel_id=1, source_target_pairs={{0,7},{1,0},{2,1},{3,2},{4,3},{5,4},{6,5},{7,6},{8,15},{9,8},{10,9... | collective-permute-start | bytes 786440 | tf_op jit(solution)/shard_map/ppermute | solution.py:22
  15.4 1.8 %collective-permute-start.1 = (bf16[1024,128]{1,0:T(8,128)(2,1)S(1)}, bf16[1024,128]{1,0:T(8,128)(2,1)S(1)}, u32[]{:S(2)}, u32[]{:S(2)}) collective-permute-start(bf16[1024,128]{1,0:T(8,128)(2,1)S(1)} %copy-done.4), channel_id=1, source_target_pairs={{0,24},{1,25},{2,26},{3,27},{4,28},{5,29},{6,30},{7,31},{8,0},{9,1... | collective-permute-start | bytes 786440 | tf_op jit(solution)/shard_map/ppermute | solution.py:22
  17.4 4.2 %collective-permute-done.2.refs_1_ = bf16[1024,128]{1,0:T(8,128)(2,1)S(1)} collective-permute-done((bf16[1024,128]{1,0:T(8,128)(2,1)S(1)}, bf16[1024,128]{1,0:T(8,128)(2,1)S(1)}, u32[]{:S(2)}, u32[]{:S(2)}) %collective-permute-start.2) | collective-permute-done | bytes 262176 | tf_op jit(solution)/shard_map/ppermute | solution.py:22
  21.6 3.2 %collective-permute-start.6 = (bf16[1024,128]{1,0:T(8,128)(2,1)S(1)}, bf16[1024,128]{1,0:T(8,128)(2,1)S(1)}, u32[]{:S(2)}, u32[]{:S(2)}) collective-permute-start(bf16[1024,128]{1,0:T(8,128)(2,1)S(1)} %collective-permute-done.3.refs_2_), channel_id=1, source_target_pairs={{0,7},{1,0},{2,1},{3,2},{4,3},{5,4},{6,5},{7,6},{8,15},{9,8},{10,9... | collective-permute-start | bytes 786440 | tf_op jit(solution)/shard_map/ppermute | solution.py:22
  24.8 1.4 collective-permute-start.4
  26.3 3.9 %collective-permute-done.5.refs_3_ = bf16[1024,128]{1,0:T(8,128)(2,1)S(1)} collective-permute-done((bf16[1024,128]{1,0:T(8,128)(2,1)S(1)}, bf16[1024,128]{1,0:T(8,128)(2,1)S(1)}, u32[]{:S(2)}, u32[]{:S(2)}) %collective-permute-start.5) | collective-permute-done | bytes 262176 | tf_op jit(solution)/shard_map/ppermute | solution.py:22
  30.4 1.2 collective-permute-done.4.refs_3_
  31.6 2.5 %collective-permute-start.16 = (bf16[1024,640]{1,0:T(8,128)(2,1)S(1)}, bf16[1024,640]{1,0:T(8,128)(2,1)S(1)}, u32[]{:S(2)}, u32[]{:S(2)}) collective-permute-start(bf16[1024,640]{1,0:T(8,128)(2,1)S(1)} %shard_map.85.refs_3_), channel_id=1, source_target_pairs={{0,8},{1,9},{2,10},{3,11},{4,12},{5,13},{6,14},{7,15},{8,16},{9,17... | collective-permute-start | bytes 3932168 | tf_op jit(solution)/shard_map/ppermute | solution.py:22
  34.3 3.0 %collective-permute-start.8 = (bf16[1024,128]{1,0:T(8,128)(2,1)S(1)}, bf16[1024,128]{1,0:T(8,128)(2,1)S(1)}, u32[]{:S(2)}, u32[]{:S(2)}) collective-permute-start(bf16[1024,128]{1,0:T(8,128)(2,1)S(1)} %collective-permute-done.6.refs_4_), channel_id=1, source_target_pairs={{0,7},{1,0},{2,1},{3,2},{4,3},{5,4},{6,5},{7,6},{8,15},{9,8},{10,9... | collective-permute-start | bytes 786440 | tf_op jit(solution)/shard_map/ppermute | solution.py:22
  37.5 4.2 %collective-permute-done.7.refs_0_ = bf16[1024,128]{1,0:T(8,128)(2,1)S(1)} collective-permute-done((bf16[1024,128]{1,0:T(8,128)(2,1)S(1)}, bf16[1024,128]{1,0:T(8,128)(2,1)S(1)}, u32[]{:S(2)}, u32[]{:S(2)}) %collective-permute-start.7) | collective-permute-done | bytes 262176 | tf_op jit(solution)/shard_map/ppermute | solution.py:22
  41.7 3.2 %collective-permute-start.10 = (bf16[1024,512]{1,0:T(8,128)(2,1)S(1)}, bf16[1024,512]{1,0:T(8,128)(2,1)}, u32[]{:S(2)}, u32[]{:S(2)}) collective-permute-start(bf16[1024,512]{1,0:T(8,128)(2,1)S(1)} %shard_map.83.refs_8_), channel_id=1, source_target_pairs={{0,7},{1,0},{2,1},{3,2},{4,3},{5,4},{6,5},{7,6},{8,15},{9,8},{10,9... | collective-permute-start | bytes 3145736 | tf_op jit(solution)/shard_map/ppermute | solution.py:22
  44.9 1.1 collective-permute-start.11
  46.0 13.9 %collective-permute-done.16.refs_4_ = bf16[1024,640]{1,0:T(8,128)(2,1)S(1)} collective-permute-done((bf16[1024,640]{1,0:T(8,128)(2,1)S(1)}, bf16[1024,640]{1,0:T(8,128)(2,1)S(1)}, u32[]{:S(2)}, u32[]{:S(2)}) %collective-permute-start.16) | collective-permute-done | bytes 1310752 | tf_op jit(solution)/shard_map/ppermute | solution.py:22
  60.0 3.2 %collective-permute-done.17.refs_5_ = bf16[1024,640]{1,0:T(8,128)(2,1)S(1)} collective-permute-done((bf16[1024,640]{1,0:T(8,128)(2,1)S(1)}, bf16[1024,640]{1,0:T(8,128)(2,1)S(1)}, u32[]{:S(2)}, u32[]{:S(2)}) %collective-permute-start.17) | collective-permute-done | bytes 1310752 | tf_op jit(solution)/shard_map/ppermute | solution.py:22
  63.3 1.4 collective-permute-start.18
  65.4 8.0 %collective-permute-done.11.refs_2_ = bf16[1024,128]{1,0:T(8,128)(2,1)S(1)} collective-permute-done((bf16[1024,128]{1,0:T(8,128)(2,1)S(1)}, bf16[1024,128]{1,0:T(8,128)(2,1)S(1)}, u32[]{:S(2)}, u32[]{:S(2)}) %collective-permute-start.11) | collective-permute-done | bytes 262176 | tf_op jit(solution)/shard_map/ppermute | solution.py:22
  73.4 2.0 %collective-permute-start.12 = (bf16[1024,512]{1,0:T(8,128)(2,1)}, bf16[1024,512]{1,0:T(8,128)(2,1)}, u32[]{:S(2)}, u32[]{:S(2)}) collective-permute-start(bf16[1024,512]{1,0:T(8,128)(2,1)} %collective-permute-done.9.refs_9_), channel_id=1, source_target_pairs={{0,1},{1,2},{2,3},{3,4},{4,5},{5,6},{6,7},{7,0},{8,9},{9,10},{10,1... | collective-permute-start | bytes 3145736 | tf_op jit(solution)/shard_map/ppermute | solution.py:22
  76.4 3.2 %collective-permute-done.19.refs_4_ = bf16[512,640]{1,0:T(8,128)(2,1)S(1)} collective-permute-done((bf16[512,640]{1,0:T(8,128)(2,1)S(1)}, bf16[512,640]{1,0:T(8,128)(2,1)S(1)}, u32[]{:S(2)}, u32[]{:S(2)}) %collective-permute-start.19) | collective-permute-done | bytes 655392 | tf_op jit(solution)/shard_map/ppermute | solution.py:22
  79.6 3.2 %collective-permute-start.20 = (bf16[1024,384]{1,0:T(8,128)(2,1)S(1)}, bf16[1024,384]{1,0:T(8,128)(2,1)}, u32[]{:S(2)}, u32[]{:S(2)}) collective-permute-start(bf16[1024,384]{1,0:T(8,128)(2,1)S(1)} %shard_map.84.refs_5_), channel_id=1, source_target_pairs={{0,8},{1,9},{2,10},{3,11},{4,12},{5,13},{6,14},{7,15},{8,16},{9,17... | collective-permute-start | bytes 2359304 | tf_op jit(solution)/shard_map/ppermute | solution.py:22
  83.5 11.3 %shard_map.82 = (bf16[768,1920]{1,0:T(8,128)(2,1)}, bf16[768,3328]{1,0:T(8,128)(2,1)}, bf16[768,2432]{1,0:T(8,128)(2,1)}, bf16[768,512]{1,0:T(8,128)(2,1)}) custom-call(s32[2]{0:T(128)} %pad_add_fusion.refs_0_, s32[6]{0:T(128)} %refs_0_.11, s32[32]{0:T(128)} %refs_2_.1, s32[6,32]{1,0:T(8,128)} %refs_3_.1, bf16[1536,4096]{1,0:T(8,128)(2,1)} %all-gather.2.cloned.1.call-done.refs_4_), custom_call_target="tpu_custom_call" | custom-call | bytes 26214400 | tf_op jit(solution)/shard_map/pallas_call | solution.py:109
  95.3 1.3 collective-permute-start.15
  97.4 1.0 slice.28
  98.4 1.0 slice.27
  99.5 8.7 %shard_map.86.refs_11_ = f32[768,1024]{1,0:T(8,128)} custom-call(s32[6]{0:T(128)} %refs_0_.11, s32[8]{0:T(128)} %refs_1_.9, bf16[768,1920]{1,0:T(8,128)(2,1)} %get-tuple-element.36.refs_2_, bf16[1024,640]{1,0:T(8,128)(2,1)} %copy-done, bf16[1024,640]{1,0:T(8,128)(2,1)} %copy-done.9, bf16[1024,640]{1,0:T(8,128)(2,1)} %copy-done.10), custom_call_target="tpu_custom_call" | custom-call | flops 3019898880 | bytes 15269888 | tf_op jit(solution)/shard_map/pallas_call | solution.py:193
  109.0 2.5 %collective-permute-start.22 = (bf16[512,384]{1,0:T(8,128)(2,1)S(1)}, bf16[512,384]{1,0:T(8,128)(2,1)}, u32[]{:S(2)}, u32[]{:S(2)}) collective-permute-start(bf16[512,384]{1,0:T(8,128)(2,1)S(1)} %slice.27), channel_id=1, source_target_pairs={{0,8},{1,9},{2,10},{3,11},{4,12},{5,13},{6,14},{7,15},{8,16},{9,17... | collective-permute-start | bytes 1179656 | tf_op jit(solution)/shard_map/ppermute | solution.py:22
  111.5 11.9 %shard_map.87.refs_9_ = f32[768,1024]{1,0:T(8,128)} custom-call(s32[6]{0:T(128)} %refs_0_.11, s32[8]{0:T(128)} %refs_1_.9, bf16[768,3328]{1,0:T(8,128)(2,1)} %get-tuple-element.45.refs_2_, bf16[512,640]{1,0:T(8,128)(2,1)} %copy-done.11, bf16[512,640]{1,0:T(8,128)(2,1)} %copy-done.12, bf16[1024,384]{1,0:T(8,128)(2,1)} %copy-done.2, ...), custom_call_target="tpu_custom_call" | custom-call | flops 5234491392 | bytes 20316160 | tf_op jit(solution)/shard_map/pallas_call | solution.py:193
  124.4 2.5 %collective-permute-start.25 = (bf16[512,512]{1,0:T(8,128)(2,1)S(1)}, bf16[512,512]{1,0:T(8,128)(2,1)S(1)}, u32[]{:S(2)}, u32[]{:S(2)}) collective-permute-start(bf16[512,512]{1,0:T(8,128)(2,1)S(1)} %slice.29), channel_id=1, source_target_pairs={{0,7},{1,0},{2,1},{3,2},{4,3},{5,4},{6,5},{7,6},{8,15},{9,8},{10,9... | collective-permute-start | bytes 1572872 | tf_op jit(solution)/shard_map/ppermute | solution.py:22
  127.0 10.1 %shard_map.88.refs_5_ = f32[768,1024]{1,0:T(8,128)} custom-call(s32[6]{0:T(128)} %refs_0_.11, s32[8]{0:T(128)} %refs_1_.9, bf16[768,2432]{1,0:T(8,128)(2,1)} %get-tuple-element.48.refs_2_, bf16[512,384]{1,0:T(8,128)(2,1)} %collective-permute-done.22.refs_3_, bf16[512,384]{1,0:T(8,128)(2,1)} %copy-done.8, bf16[1024,512]{1,0:T(8,128)(2,1)} %collective-permute-done.12.refs_5_, ...), custom_call_target="tpu_custom_call" | custom-call | flops 3825205248 | bytes 17104896 | tf_op jit(solution)/shard_map/pallas_call | solution.py:193
  137.3 3.6 %collective-permute-done.24.refs_3_ = bf16[512,512]{1,0:T(8,128)(2,1)} collective-permute-done((bf16[512,512]{1,0:T(8,128)(2,1)S(1)}, bf16[512,512]{1,0:T(8,128)(2,1)}, u32[]{:S(2)}, u32[]{:S(2)}) %collective-permute-start.24) | collective-permute-done | bytes 524320 | tf_op jit(solution)/shard_map/ppermute | solution.py:22
  141.0 5.0 %shard_map.89 = bf16[768,1024]{1,0:T(8,128)(2,1)} custom-call(s32[6]{0:T(128)} %refs_0_.11, s32[8]{0:T(128)} %refs_1_.9, bf16[768,512]{1,0:T(8,128)(2,1)} %get-tuple-element.27.refs_2_, bf16[512,512]{1,0:T(8,128)(2,1)} %collective-permute-done.24.refs_3_, bf16[512,512]{1,0:T(8,128)(2,1)} %copy-done.7, f32[768,1024]{1,0:T(8,128)} %shard_map.88.refs_5_), custom_call_target="tpu_custom_call" | custom-call | flops 805306368 | bytes 10223616 | tf_op jit(solution)/shard_map/pallas_call | solution.py:193
  (65 shorter events, 6.9 us)
Async XLA Ops:
  6.5 4.7 %copy-start.3 = (bf16[1024,128]{1,0:T(8,128)(2,1)S(1)}, bf16[1024,128]{1,0:T(8,128)(2,1)}, u32[]{:S(2)}) copy-start(bf16[1024,128]{1,0:T(8,128)(2,1)} %refs_0_.7) | copy-start | bytes 786436
  6.5 76.9 %all-gather.2.cloned.1.call-start = ((), (), s32[]{:S(2)}) async-start(), calls=%async_computation | async-start | bytes 14155776 | tf_op jit(solution)/shard_map/all_gather | solution.py:211
  9.2 8.1 %collective-permute-start = (bf16[1024,128]{1,0:T(8,128)(2,1)S(1)}, bf16[1024,128]{1,0:T(8,128)(2,1)S(1)}, u32[]{:S(2)}, u32[]{:S(2)}) collective-permute-start(bf16[1024,128]{1,0:T(8,128)(2,1)S(1)} %copy-done.4), channel_id=1, source_target_pairs={{0,8},{1,9},{2,10},{3,11},{4,12},{5,13},{6,14},{7,15},{8,16},{9,17... | collective-permute-start | bytes 786440 | tf_op jit(solution)/shard_map/ppermute | solution.py:22
  11.3 10.3 %collective-permute-start.2 = (bf16[1024,128]{1,0:T(8,128)(2,1)S(1)}, bf16[1024,128]{1,0:T(8,128)(2,1)S(1)}, u32[]{:S(2)}, u32[]{:S(2)}) collective-permute-start(bf16[1024,128]{1,0:T(8,128)(2,1)S(1)} %copy-done.3), channel_id=1, source_target_pairs={{0,1},{1,2},{2,3},{3,4},{4,5},{5,6},{6,7},{7,0},{8,9},{9,10},{10,1... | collective-permute-start | bytes 786440 | tf_op jit(solution)/shard_map/ppermute | solution.py:22
  11.5 10.1 %collective-permute-start.3 = (bf16[1024,128]{1,0:T(8,128)(2,1)S(1)}, bf16[1024,128]{1,0:T(8,128)(2,1)S(1)}, u32[]{:S(2)}, u32[]{:S(2)}) collective-permute-start(bf16[1024,128]{1,0:T(8,128)(2,1)S(1)} %copy-done.3), channel_id=1, source_target_pairs={{0,7},{1,0},{2,1},{3,2},{4,3},{5,4},{6,5},{7,6},{8,15},{9,8},{10,9... | collective-permute-start | bytes 786440 | tf_op jit(solution)/shard_map/ppermute | solution.py:22
  15.4 9.4 %collective-permute-start.1 = (bf16[1024,128]{1,0:T(8,128)(2,1)S(1)}, bf16[1024,128]{1,0:T(8,128)(2,1)S(1)}, u32[]{:S(2)}, u32[]{:S(2)}) collective-permute-start(bf16[1024,128]{1,0:T(8,128)(2,1)S(1)} %copy-done.4), channel_id=1, source_target_pairs={{0,24},{1,25},{2,26},{3,27},{4,28},{5,29},{6,30},{7,31},{8,0},{9,1... | collective-permute-start | bytes 786440 | tf_op jit(solution)/shard_map/ppermute | solution.py:22
  21.6 8.6 %collective-permute-start.5 = (bf16[1024,128]{1,0:T(8,128)(2,1)S(1)}, bf16[1024,128]{1,0:T(8,128)(2,1)S(1)}, u32[]{:S(2)}, u32[]{:S(2)}) collective-permute-start(bf16[1024,128]{1,0:T(8,128)(2,1)S(1)} %collective-permute-done.2.refs_1_), channel_id=1, source_target_pairs={{0,1},{1,2},{2,3},{3,4},{4,5},{5,6},{6,7},{7,0},{8,9},{9,10},{10,1... | collective-permute-start | bytes 786440 | tf_op jit(solution)/shard_map/ppermute | solution.py:22
  21.6 8.6 %collective-permute-start.6 = (bf16[1024,128]{1,0:T(8,128)(2,1)S(1)}, bf16[1024,128]{1,0:T(8,128)(2,1)S(1)}, u32[]{:S(2)}, u32[]{:S(2)}) collective-permute-start(bf16[1024,128]{1,0:T(8,128)(2,1)S(1)} %collective-permute-done.3.refs_2_), channel_id=1, source_target_pairs={{0,7},{1,0},{2,1},{3,2},{4,3},{5,4},{6,5},{7,6},{8,15},{9,8},{10,9... | collective-permute-start | bytes 786440 | tf_op jit(solution)/shard_map/ppermute | solution.py:22
  24.8 6.8 %collective-permute-start.4 = (bf16[1024,128]{1,0:T(8,128)(2,1)S(1)}, bf16[1024,128]{1,0:T(8,128)(2,1)S(1)}, u32[]{:S(2)}, u32[]{:S(2)}) collective-permute-start(bf16[1024,128]{1,0:T(8,128)(2,1)S(1)} %collective-permute-done.refs_1_), channel_id=1, source_target_pairs={{0,8},{1,9},{2,10},{3,11},{4,12},{5,13},{6,14},{7,15},{8,16},{9,17... | collective-permute-start | bytes 786440 | tf_op jit(solution)/shard_map/ppermute | solution.py:22
  30.4 45.2 %copy-start = (bf16[1024,640]{1,0:T(8,128)(2,1)}, bf16[1024,640]{1,0:T(8,128)(2,1)S(1)}, u32[]{:S(2)}) copy-start(bf16[1024,640]{1,0:T(8,128)(2,1)S(1)} %shard_map.85.refs_3_) | copy-start | bytes 3932164
  31.6 28.3 %collective-permute-start.16 = (bf16[1024,640]{1,0:T(8,128)(2,1)S(1)}, bf16[1024,640]{1,0:T(8,128)(2,1)S(1)}, u32[]{:S(2)}, u32[]{:S(2)}) collective-permute-start(bf16[1024,640]{1,0:T(8,128)(2,1)S(1)} %shard_map.85.refs_3_), channel_id=1, source_target_pairs={{0,8},{1,9},{2,10},{3,11},{4,12},{5,13},{6,14},{7,15},{8,16},{9,17... | collective-permute-start | bytes 3932168 | tf_op jit(solution)/shard_map/ppermute | solution.py:22
  34.1 29.2 %collective-permute-start.17 = (bf16[1024,640]{1,0:T(8,128)(2,1)S(1)}, bf16[1024,640]{1,0:T(8,128)(2,1)S(1)}, u32[]{:S(2)}, u32[]{:S(2)}) collective-permute-start(bf16[1024,640]{1,0:T(8,128)(2,1)S(1)} %shard_map.85.refs_3_), channel_id=1, source_target_pairs={{0,24},{1,25},{2,26},{3,27},{4,28},{5,29},{6,30},{7,31},{8,0},{9,1... | collective-permute-start | bytes 3932168 | tf_op jit(solution)/shard_map/ppermute | solution.py:22
  34.1 7.6 %collective-permute-start.7 = (bf16[1024,128]{1,0:T(8,128)(2,1)S(1)}, bf16[1024,128]{1,0:T(8,128)(2,1)S(1)}, u32[]{:S(2)}, u32[]{:S(2)}) collective-permute-start(bf16[1024,128]{1,0:T(8,128)(2,1)S(1)} %collective-permute-done.5.refs_3_), channel_id=1, source_target_pairs={{0,1},{1,2},{2,3},{3,4},{4,5},{5,6},{6,7},{7,0},{8,9},{9,10},{10,1... | collective-permute-start | bytes 786440 | tf_op jit(solution)/shard_map/ppermute | solution.py:22
  34.3 7.3 %collective-permute-start.8 = (bf16[1024,128]{1,0:T(8,128)(2,1)S(1)}, bf16[1024,128]{1,0:T(8,128)(2,1)S(1)}, u32[]{:S(2)}, u32[]{:S(2)}) collective-permute-start(bf16[1024,128]{1,0:T(8,128)(2,1)S(1)} %collective-permute-done.6.refs_4_), channel_id=1, source_target_pairs={{0,7},{1,0},{2,1},{3,2},{4,3},{5,4},{6,5},{7,6},{8,15},{9,8},{10,9... | collective-permute-start | bytes 786440 | tf_op jit(solution)/shard_map/ppermute | solution.py:22
  37.5 57.2 %copy-start.1 = (bf16[1024,512]{1,0:T(8,128)(2,1)}, bf16[1024,512]{1,0:T(8,128)(2,1)S(1)}, u32[]{:S(2)}) copy-start(bf16[1024,512]{1,0:T(8,128)(2,1)S(1)} %shard_map.83.refs_8_) | copy-start | bytes 3145732
  41.7 31.8 %collective-permute-start.10 = (bf16[1024,512]{1,0:T(8,128)(2,1)S(1)}, bf16[1024,512]{1,0:T(8,128)(2,1)}, u32[]{:S(2)}, u32[]{:S(2)}) collective-permute-start(bf16[1024,512]{1,0:T(8,128)(2,1)S(1)} %shard_map.83.refs_8_), channel_id=1, source_target_pairs={{0,7},{1,0},{2,1},{3,2},{4,3},{5,4},{6,5},{7,6},{8,15},{9,8},{10,9... | collective-permute-start | bytes 3145736 | tf_op jit(solution)/shard_map/ppermute | solution.py:22
  44.9 28.5 %collective-permute-start.9 = (bf16[1024,512]{1,0:T(8,128)(2,1)S(1)}, bf16[1024,512]{1,0:T(8,128)(2,1)}, u32[]{:S(2)}, u32[]{:S(2)}) collective-permute-start(bf16[1024,512]{1,0:T(8,128)(2,1)S(1)} %shard_map.83.refs_8_), channel_id=1, source_target_pairs={{0,1},{1,2},{2,3},{3,4},{4,5},{5,6},{6,7},{7,0},{8,9},{9,10},{10,1... | collective-permute-start | bytes 3145736 | tf_op jit(solution)/shard_map/ppermute | solution.py:22
  44.9 28.5 %collective-permute-start.11 = (bf16[1024,128]{1,0:T(8,128)(2,1)S(1)}, bf16[1024,128]{1,0:T(8,128)(2,1)S(1)}, u32[]{:S(2)}, u32[]{:S(2)}) collective-permute-start(bf16[1024,128]{1,0:T(8,128)(2,1)S(1)} %collective-permute-done.7.refs_0_), channel_id=1, source_target_pairs={{0,1},{1,2},{2,3},{3,4},{4,5},{5,6},{6,7},{7,0},{8,9},{9,10},{10,1... | collective-permute-start | bytes 786440 | tf_op jit(solution)/shard_map/ppermute | solution.py:22
  63.3 16.3 %copy-start.10 = (bf16[1024,640]{1,0:T(8,128)(2,1)}, bf16[1024,640]{1,0:T(8,128)(2,1)S(1)}, u32[]{:S(2)}) copy-start(bf16[1024,640]{1,0:T(8,128)(2,1)S(1)} %collective-permute-done.17.refs_5_) | copy-start | bytes 3932164
  63.3 13.1 %collective-permute-start.18 = (bf16[512,640]{1,0:T(8,128)(2,1)S(1)}, bf16[512,640]{1,0:T(8,128)(2,1)S(1)}, u32[]{:S(2)}, u32[]{:S(2)}) collective-permute-start(bf16[512,640]{1,0:T(8,128)(2,1)S(1)} %slice.25), channel_id=1, source_target_pairs={{0,8},{1,9},{2,10},{3,11},{4,12},{5,13},{6,14},{7,15},{8,16},{9,17... | collective-permute-start | bytes 1966088 | tf_op jit(solution)/shard_map/ppermute | solution.py:22
  64.7 14.9 %collective-permute-start.19 = (bf16[512,640]{1,0:T(8,128)(2,1)S(1)}, bf16[512,640]{1,0:T(8,128)(2,1)S(1)}, u32[]{:S(2)}, u32[]{:S(2)}) collective-permute-start(bf16[512,640]{1,0:T(8,128)(2,1)S(1)} %slice.26), channel_id=1, source_target_pairs={{0,24},{1,25},{2,26},{3,27},{4,28},{5,29},{6,30},{7,31},{8,0},{9,1... | collective-permute-start | bytes 1966088 | tf_op jit(solution)/shard_map/ppermute | solution.py:22
  73.4 21.3 %collective-permute-start.13 = (bf16[1024,512]{1,0:T(8,128)(2,1)}, bf16[1024,512]{1,0:T(8,128)(2,1)}, u32[]{:S(2)}, u32[]{:S(2)}) collective-permute-start(bf16[1024,512]{1,0:T(8,128)(2,1)} %collective-permute-done.10.refs_10_), channel_id=1, source_target_pairs={{0,7},{1,0},{2,1},{3,2},{4,3},{5,4},{6,5},{7,6},{8,15},{9,8},{10,9... | collective-permute-start | bytes 3145736 | tf_op jit(solution)/shard_map/ppermute | solution.py:22
  73.4 21.9 %collective-permute-start.12 = (bf16[1024,512]{1,0:T(8,128)(2,1)}, bf16[1024,512]{1,0:T(8,128)(2,1)}, u32[]{:S(2)}, u32[]{:S(2)}) collective-permute-start(bf16[1024,512]{1,0:T(8,128)(2,1)} %collective-permute-done.9.refs_9_), channel_id=1, source_target_pairs={{0,1},{1,2},{2,3},{3,4},{4,5},{5,6},{6,7},{7,0},{8,9},{9,10},{10,1... | collective-permute-start | bytes 3145736 | tf_op jit(solution)/shard_map/ppermute | solution.py:22
  75.6 19.1 %copy-start.2 = (bf16[1024,384]{1,0:T(8,128)(2,1)}, bf16[1024,384]{1,0:T(8,128)(2,1)S(1)}, u32[]{:S(2)}) copy-start(bf16[1024,384]{1,0:T(8,128)(2,1)S(1)} %shard_map.84.refs_5_) | copy-start | bytes 2359300
  79.5 17.8 %collective-permute-start.21 = (bf16[1024,384]{1,0:T(8,128)(2,1)S(1)}, bf16[1024,384]{1,0:T(8,128)(2,1)}, u32[]{:S(2)}, u32[]{:S(2)}) collective-permute-start(bf16[1024,384]{1,0:T(8,128)(2,1)S(1)} %shard_map.84.refs_5_), channel_id=1, source_target_pairs={{0,24},{1,25},{2,26},{3,27},{4,28},{5,29},{6,30},{7,31},{8,0},{9,1... | collective-permute-start | bytes 2359304 | tf_op jit(solution)/shard_map/ppermute | solution.py:22
  79.6 18.9 %collective-permute-start.20 = (bf16[1024,384]{1,0:T(8,128)(2,1)S(1)}, bf16[1024,384]{1,0:T(8,128)(2,1)}, u32[]{:S(2)}, u32[]{:S(2)}) collective-permute-start(bf16[1024,384]{1,0:T(8,128)(2,1)S(1)} %shard_map.84.refs_5_), channel_id=1, source_target_pairs={{0,8},{1,9},{2,10},{3,11},{4,12},{5,13},{6,14},{7,15},{8,16},{9,17... | collective-permute-start | bytes 2359304 | tf_op jit(solution)/shard_map/ppermute | solution.py:22
  95.3 28.1 %collective-permute-start.15 = (bf16[1024,512]{1,0:T(8,128)(2,1)}, bf16[1024,512]{1,0:T(8,128)(2,1)S(1)}, u32[]{:S(2)}, u32[]{:S(2)}) collective-permute-start(bf16[1024,512]{1,0:T(8,128)(2,1)} %collective-permute-done.13.refs_6_), channel_id=1, source_target_pairs={{0,7},{1,0},{2,1},{3,2},{4,3},{5,4},{6,5},{7,6},{8,15},{9,8},{10,9... | collective-permute-start | bytes 3145736 | tf_op jit(solution)/shard_map/ppermute | solution.py:22
  96.6 27.7 %collective-permute-start.14 = (bf16[1024,512]{1,0:T(8,128)(2,1)}, bf16[1024,512]{1,0:T(8,128)(2,1)S(1)}, u32[]{:S(2)}, u32[]{:S(2)}) collective-permute-start(bf16[1024,512]{1,0:T(8,128)(2,1)} %collective-permute-done.12.refs_5_), channel_id=1, source_target_pairs={{0,1},{1,2},{2,3},{3,4},{4,5},{5,6},{6,7},{7,0},{8,9},{9,10},{10,1... | collective-permute-start | bytes 3145736 | tf_op jit(solution)/shard_map/ppermute | solution.py:22
  108.1 15.4 %collective-permute-start.23 = (bf16[512,384]{1,0:T(8,128)(2,1)S(1)}, bf16[512,384]{1,0:T(8,128)(2,1)S(1)}, u32[]{:S(2)}, u32[]{:S(2)}) collective-permute-start(bf16[512,384]{1,0:T(8,128)(2,1)S(1)} %slice.28), channel_id=1, source_target_pairs={{0,24},{1,25},{2,26},{3,27},{4,28},{5,29},{6,30},{7,31},{8,0},{9,1... | collective-permute-start | bytes 1179656 | tf_op jit(solution)/shard_map/ppermute | solution.py:22
  109.0 14.5 %collective-permute-start.22 = (bf16[512,384]{1,0:T(8,128)(2,1)S(1)}, bf16[512,384]{1,0:T(8,128)(2,1)}, u32[]{:S(2)}, u32[]{:S(2)}) collective-permute-start(bf16[512,384]{1,0:T(8,128)(2,1)S(1)} %slice.27), channel_id=1, source_target_pairs={{0,8},{1,9},{2,10},{3,11},{4,12},{5,13},{6,14},{7,15},{8,16},{9,17... | collective-permute-start | bytes 1179656 | tf_op jit(solution)/shard_map/ppermute | solution.py:22
  124.4 13.0 %collective-permute-start.25 = (bf16[512,512]{1,0:T(8,128)(2,1)S(1)}, bf16[512,512]{1,0:T(8,128)(2,1)S(1)}, u32[]{:S(2)}, u32[]{:S(2)}) collective-permute-start(bf16[512,512]{1,0:T(8,128)(2,1)S(1)} %slice.29), channel_id=1, source_target_pairs={{0,7},{1,0},{2,1},{3,2},{4,3},{5,4},{6,5},{7,6},{8,15},{9,8},{10,9... | collective-permute-start | bytes 1572872 | tf_op jit(solution)/shard_map/ppermute | solution.py:22
  126.9 14.1 %collective-permute-start.24 = (bf16[512,512]{1,0:T(8,128)(2,1)S(1)}, bf16[512,512]{1,0:T(8,128)(2,1)}, u32[]{:S(2)}, u32[]{:S(2)}) collective-permute-start(bf16[512,512]{1,0:T(8,128)(2,1)S(1)} %slice.24), channel_id=1, source_target_pairs={{0,1},{1,2},{2,3},{3,4},{4,5},{5,6},{6,7},{7,0},{8,9},{9,10},{10,1... | collective-permute-start | bytes 1572872 | tf_op jit(solution)/shard_map/ppermute | solution.py:22
  (8 other events, 23.1 us)
Sparse Core Ops, SparseCore 0:
  9.4 72.5 all-gather.1
